TPU v7x, 128 devices: a whole 4x4x4 slice. The times are simulated.
128 devices in a mesh: dp: 16 (over x_hi, z, core), fsdp: 8 (over y, x_lo).
Axes of the slice: x: 4 (x_hi: 2, x_lo: 2; x = x_hi * 2 + x_lo), y: 4, z: 4, core: 2. Of those that a mesh axis runs over, the one named last changes fastest.
Arguments:
- tokens: bfloat16 [16, 2048, 1152], P('dp', 'fsdp'), may hold values from -6 to 6
- text_states: bfloat16 [16, 480, 4096], P('dp', 'fsdp'), may hold values from -6 to 6
- seg_lengths: int32 [16, 3], P('dp'), may hold values from 1 to 1793, as said below
- caption_of_segment: int32 [16, 3], P('dp'), may hold values from 0 to 3
- text_lengths: int32 [16, 4], P('dp'), may hold values from 1 to 120, as said below
- ln1_gain: float32 [1152], replicated, may hold values from 0.1 to 1.9
- ln1_bias: float32 [1152], replicated, may hold values from -3 to 3
- w_query: bfloat16 [1152, 1152], P('fsdp'), may hold values from -0.1875 to 0.1875
- w_key: bfloat16 [1152, 1152], P('fsdp'), may hold values from -0.1875 to 0.1875
- w_value: bfloat16 [1152, 1152], P('fsdp'), may hold values from -0.1875 to 0.1875
- w_out: bfloat16 [1152, 1152], P('fsdp'), may hold values from -0.5 to 0.5
- ln2_gain: float32 [1152], replicated, may hold values from 0.1 to 1.9
- ln2_bias: float32 [1152], replicated, may hold values from -3 to 3
- c_query: bfloat16 [1152, 1152], P('fsdp'), may hold values from -0.1875 to 0.1875
- w_text: bfloat16 [4096, 1152], P('fsdp'), may hold values from -0.09375 to 0.09375
- c_key: bfloat16 [1152, 1152], P('fsdp'), may hold values from -0.1875 to 0.1875
- c_value: bfloat16 [1152, 1152], P('fsdp'), may hold values from -0.1875 to 0.1875
- c_out: bfloat16 [1152, 1152], P('fsdp'), may hold values from -0.5 to 0.5
- ln3_gain: float32 [1152], replicated, may hold values from 0.1 to 1.9
- ln3_bias: float32 [1152], replicated, may hold values from -3 to 3
- w_up: bfloat16 [1152, 4608], P('fsdp'), may hold values from -0.1875 to 0.1875
- w_down: bfloat16 [4608, 1152], P('fsdp'), may hold values from -0.09375 to 0.09375
- cotangent: float32 [16, 2048, 1152], P('dp', 'fsdp'), may hold values from -6 to 6
Outputs:
- outputs: float32 [16, 2048, 1152], P('dp', 'fsdp')
- grad_tokens: float32 [16, 2048, 1152], P('dp', 'fsdp')
- grad_text: float32 [16, 480, 4096], P('dp', 'fsdp')
- grad_ln1_gain: float32 [1152], replicated
- grad_ln1_bias: float32 [1152], replicated
- grad_w_query: float32 [1152, 1152], P('fsdp')
- grad_w_key: float32 [1152, 1152], P('fsdp')
- grad_w_value: float32 [1152, 1152], P('fsdp')
- grad_w_out: float32 [1152, 1152], P('fsdp')
- grad_ln2_gain: float32 [1152], replicated
- grad_ln2_bias: float32 [1152], replicated
- grad_c_query: float32 [1152, 1152], P('fsdp')
- grad_w_text: float32 [4096, 1152], P('fsdp')
- grad_c_key: float32 [1152, 1152], P('fsdp')
- grad_c_value: float32 [1152, 1152], P('fsdp')
- grad_c_out: float32 [1152, 1152], P('fsdp')
- grad_ln3_gain: float32 [1152], replicated
- grad_ln3_bias: float32 [1152], replicated
- grad_w_up: float32 [1152, 4608], P('fsdp')
- grad_w_down: float32 [4608, 1152], P('fsdp')
Inputs may be any that keep to these rules, and one draw needn't show every extreme that they name: `seg_lengths`: each row's 3 lengths sum to 2048, and one item of every row holds exactly 1793 positions. `text_lengths`: every row has a caption of 120 live tokens.
All inputs are finite; a program needn't handle non-finite values.
Results may differ from a plain program's by a relative error of at most 0.03.
Values may be sent and summed in bfloat16 or wider, within the bound.
No kernel may reach another device: no remote copies, remote signals or barrier semaphores. Data moves between devices by JAX's collectives and lax.ppermute only.
A program may use at most 320 MiB of HBM per device.

v0:
```python
import jax
import jax.numpy as jnp
from jax import lax
from jax.sharding import PartitionSpec as P

HEADS = 16
HEAD = 72
CAP_LEN = 120
SEGS = 3
CAPS = 4


norm_eps = 1e-06
masked_score = -1e30


def split_up(x, dim, peers):
    before, after = (x.shape[:dim], x.shape[dim + 1 :])
    return jnp.moveaxis(x.reshape(*before, peers, -1, *after), dim, 0)


def sum_at_owner(x, axis, dim):
    pieces = split_up(x, dim, lax.axis_size(axis))
    arrived = lax.all_to_all(pieces, axis, split_axis=0, concat_axis=0, tiled=True)
    return arrived.astype(jnp.float32).sum(axis=0)


def in_one_piece(arrays, axis, dim, along):
    ends, at = ([], 0)
    for a in arrays[:-1]:
        at += a.shape[along]
        ends.append(at)
    both = jnp.concatenate(arrays, axis=along)
    return tuple(jnp.split(sum_at_owner(both, axis, dim), ends, axis=along))


def norm_layer(values, norm_gain, norm_shift):
    center = values - jnp.mean(values, axis=-1, keepdims=True)
    spread = jnp.mean(center * center, axis=-1, keepdims=True)
    return center * lax.rsqrt(spread + norm_eps) * norm_gain + norm_shift


def fetch_weight(shard):
    return lax.all_gather(shard, "fsdp", axis=0, tiled=True)


def reduce_grad(left_side, right_side):
    return lax.psum_scatter(
        jnp.einsum("ti,to->io", left_side, right_side, preferred_element_type=jnp.float32).astype(
            jnp.bfloat16
        ),
        "fsdp",
        scatter_dimension=0,
        tiled=True,
    ).astype(jnp.float32)


def head_view(values):
    return values.reshape(values.shape[0], HEADS, HEAD)


def back_product(grad_rows, weight_full):
    return jnp.einsum("tj,ij->ti", grad_rows, weight_full, preferred_element_type=jnp.float32)


def score_rows(query_rows, key_rows, allowed):
    scores = jnp.einsum(
        "qhe,khe->hqk",
        head_view(query_rows),
        head_view(key_rows),
        preferred_element_type=jnp.float32,
    ) * HEAD ** (-0.5)
    return jnp.where(allowed[None], scores, masked_score)


def attend_forward(query_rows, key_rows, value_rows, allowed):
    scores = score_rows(query_rows, key_rows, allowed)
    log_total = jax.nn.logsumexp(scores, axis=-1, keepdims=True)
    weights = jnp.exp(scores - log_total).astype(jnp.bfloat16)
    mixed_rows = jnp.einsum(
        "hqk,khe->qhe", weights, head_view(value_rows), preferred_element_type=jnp.float32
    )
    return (mixed_rows.reshape(query_rows.shape[0], HEADS * HEAD).astype(jnp.bfloat16), log_total)


def attend_backward(query_rows, key_rows, value_rows, allowed, log_total, grad_mixed):
    scores = score_rows(query_rows, key_rows, allowed)
    probs = jnp.exp(scores - log_total)
    grad_heads = head_view(grad_mixed)
    grad_probs = jnp.einsum(
        "qhe,khe->hqk", grad_heads, head_view(value_rows), preferred_element_type=jnp.float32
    )
    grad_values = jnp.einsum(
        "hqk,qhe->khe", probs.astype(jnp.bfloat16), grad_heads, preferred_element_type=jnp.float32
    )
    grad_scores = (
        probs * (grad_probs - jnp.sum(grad_probs * probs, axis=-1, keepdims=True))
    ).astype(jnp.bfloat16)
    scale = HEAD ** (-0.5)
    grad_queries = (
        jnp.einsum(
            "hqk,khe->qhe", grad_scores, head_view(key_rows), preferred_element_type=jnp.float32
        )
        * scale
    )
    grad_keys = (
        jnp.einsum(
            "hqk,qhe->khe", grad_scores, head_view(query_rows), preferred_element_type=jnp.float32
        )
        * scale
    )
    width = HEADS * HEAD
    return (
        grad_queries.reshape(-1, width),
        grad_keys.reshape(-1, width),
        grad_values.reshape(-1, width),
    )


def local(
    tokens,
    text_states,
    seg_lengths,
    caption_of_segment,
    text_lengths,
    ln1_gain,
    ln1_bias,
    w_query,
    w_key,
    w_value,
    w_out,
    ln2_gain,
    ln2_bias,
    c_query,
    w_text,
    c_key,
    c_value,
    c_out,
    ln3_gain,
    ln3_bias,
    w_up,
    w_down,
    cotangent,
):
    low_type = jnp.bfloat16
    local_rows = tokens.shape[1]
    fsdp_size = lax.axis_size("fsdp")
    row_length = local_rows * fsdp_size
    first_row = lax.axis_index("fsdp") * local_rows
    positions_all = jnp.arange(row_length, dtype=jnp.int32)
    positions_own = first_row + jnp.arange(local_rows, dtype=jnp.int32)
    segment_ends = jnp.cumsum(seg_lengths[0])
    segment_all = jnp.sum(
        (positions_all[:, None] >= segment_ends[None, :]).astype(jnp.int32), axis=1
    )
    segment_own = jnp.sum(
        (positions_own[:, None] >= segment_ends[None, :]).astype(jnp.int32), axis=1
    )
    self_allowed = segment_own[:, None] == segment_all[None, :]
    text_total = text_states.shape[1] * fsdp_size
    text_pos = jnp.arange(text_total, dtype=jnp.int32)
    text_caption = text_pos // CAP_LEN
    cap_numbers = jnp.arange(CAPS, dtype=jnp.int32)
    seg_numbers = jnp.arange(SEGS, dtype=jnp.int32)
    live_length = jnp.sum(
        jnp.where(text_caption[:, None] == cap_numbers[None, :], text_lengths[0][None, :], 0),
        axis=1,
    )
    query_caption = jnp.sum(
        jnp.where(segment_own[:, None] == seg_numbers[None, :], caption_of_segment[0][None, :], 0),
        axis=1,
    )
    text_live = text_pos % CAP_LEN < live_length
    cross_allowed = (query_caption[:, None] == text_caption[None, :]) & text_live[None, :]
    rows_in = tokens[0].astype(jnp.float32)
    normed_one, pull_one = jax.vjp(norm_layer, rows_in, ln1_gain, ln1_bias)
    normed_one = normed_one.astype(low_type)
    full_query = fetch_weight(w_query)
    full_key = fetch_weight(w_key)
    full_value = fetch_weight(w_value)
    query_rows = jnp.dot(normed_one, full_query, preferred_element_type=jnp.float32).astype(
        low_type
    )
    key_rows = jnp.dot(normed_one, full_key, preferred_element_type=jnp.float32).astype(low_type)
    value_rows = jnp.dot(normed_one, full_value, preferred_element_type=jnp.float32).astype(
        low_type
    )
    key_all, value_all = (
        lax.all_gather(key_rows, "fsdp", axis=0, tiled=True),
        lax.all_gather(value_rows, "fsdp", axis=0, tiled=True),
    )
    attended, self_total = attend_forward(query_rows, key_all, value_all, self_allowed)
    full_out = fetch_weight(w_out)
    after_self = rows_in + jnp.dot(attended, full_out, preferred_element_type=jnp.float32)
    normed_two, pull_two = jax.vjp(norm_layer, after_self, ln2_gain, ln2_bias)
    normed_two = normed_two.astype(low_type)
    full_cquery = fetch_weight(c_query)
    cross_query = jnp.dot(normed_two, full_cquery, preferred_element_type=jnp.float32).astype(
        low_type
    )
    text_rows = text_states[0]
    text_columns = lax.all_to_all(text_rows, "fsdp", split_axis=1, concat_axis=0, tiled=True)
    context = lax.psum_scatter(
        jnp.dot(text_columns, w_text, preferred_element_type=jnp.float32),
        "fsdp",
        scatter_dimension=0,
        tiled=True,
    ).astype(low_type)
    full_ckey = fetch_weight(c_key)
    full_cvalue = fetch_weight(c_value)
    cross_key = jnp.dot(context, full_ckey, preferred_element_type=jnp.float32).astype(low_type)
    cross_value = jnp.dot(context, full_cvalue, preferred_element_type=jnp.float32).astype(low_type)
    ckey_all, cvalue_all = (
        lax.all_gather(cross_key, "fsdp", axis=0, tiled=True),
        lax.all_gather(cross_value, "fsdp", axis=0, tiled=True),
    )
    cross_mixed, cross_total = attend_forward(cross_query, ckey_all, cvalue_all, cross_allowed)
    full_cout = fetch_weight(c_out)
    after_cross = after_self + jnp.dot(cross_mixed, full_cout, preferred_element_type=jnp.float32)
    normed_three, pull_three = jax.vjp(norm_layer, after_cross, ln3_gain, ln3_bias)
    normed_three = normed_three.astype(low_type)
    full_up = fetch_weight(w_up)
    full_down = fetch_weight(w_down)
    hidden_pre = jnp.dot(normed_three, full_up, preferred_element_type=jnp.float32)
    hidden_act, pull_gelu = jax.vjp(
        lambda pre_act: jax.nn.gelu(pre_act, approximate=False), hidden_pre
    )
    hidden_act = hidden_act.astype(low_type)
    outputs = after_cross + jnp.dot(hidden_act, full_down, preferred_element_type=jnp.float32)
    grad_out = cotangent[0]
    grad_mlp = grad_out.astype(low_type)
    grad_w_down = reduce_grad(hidden_act, grad_mlp)
    grad_act = back_product(grad_mlp, full_down)
    grad_pre = pull_gelu(grad_act)[0].astype(low_type)
    grad_w_up = reduce_grad(normed_three, grad_pre)
    grad_cross_in, grad_ln3_gain, grad_ln3_bias = pull_three(back_product(grad_pre, full_up))
    grad_after_cross = grad_out + grad_cross_in
    grad_cross_branch = grad_after_cross.astype(low_type)
    grad_c_out = reduce_grad(cross_mixed, grad_cross_branch)
    grad_cross_mixed = back_product(grad_cross_branch, full_cout).astype(low_type)
    grad_cquery_rows, grad_ckey_all, grad_cvalue_all = attend_backward(
        cross_query, ckey_all, cvalue_all, cross_allowed, cross_total, grad_cross_mixed
    )
    grad_ckey_own, grad_cvalue_own = in_one_piece(
        (grad_ckey_all.astype(jnp.bfloat16), grad_cvalue_all.astype(jnp.bfloat16)), "fsdp", 0, 1
    )
    grad_ckey_own = grad_ckey_own.astype(low_type)
    grad_cvalue_own = grad_cvalue_own.astype(low_type)
    grad_c_key = reduce_grad(context, grad_ckey_own)
    grad_c_value = reduce_grad(context, grad_cvalue_own)
    grad_context = (
        back_product(grad_ckey_own, full_ckey) + back_product(grad_cvalue_own, full_cvalue)
    ).astype(low_type)
    context_grad_all = lax.all_gather(grad_context, "fsdp", axis=0, tiled=True)
    grad_w_text = jnp.einsum(
        "ti,to->io", text_columns, context_grad_all, preferred_element_type=jnp.float32
    )
    text_part = back_product(context_grad_all, w_text)
    grad_text = lax.all_to_all(
        text_part.astype(jnp.bfloat16), "fsdp", split_axis=0, concat_axis=1, tiled=True
    ).astype(text_part.dtype)
    grad_cquery_rows = grad_cquery_rows.astype(low_type)
    grad_c_query = reduce_grad(normed_two, grad_cquery_rows)
    grad_self_in, grad_ln2_gain, grad_ln2_bias = pull_two(
        back_product(grad_cquery_rows, full_cquery)
    )
    grad_after_self = grad_after_cross + grad_self_in
    grad_self_branch = grad_after_self.astype(low_type)
    grad_w_out = reduce_grad(attended, grad_self_branch)
    grad_attended = back_product(grad_self_branch, full_out).astype(low_type)
    grad_query_rows, grad_key_all, grad_value_all = attend_backward(
        query_rows, key_all, value_all, self_allowed, self_total, grad_attended
    )
    grad_key_own, grad_value_own = (
        lax.psum_scatter(
            grad_key_all.astype(jnp.bfloat16), "fsdp", scatter_dimension=0, tiled=True
        ).astype(jnp.float32),
        lax.psum_scatter(
            grad_value_all.astype(jnp.bfloat16), "fsdp", scatter_dimension=0, tiled=True
        ).astype(jnp.float32),
    )
    grad_key_own = grad_key_own.astype(low_type)
    grad_value_own = grad_value_own.astype(low_type)
    grad_query_rows = grad_query_rows.astype(low_type)
    grad_w_query = reduce_grad(normed_one, grad_query_rows)
    grad_w_key = reduce_grad(normed_one, grad_key_own)
    grad_w_value = reduce_grad(normed_one, grad_value_own)
    grad_normed_one = (
        back_product(grad_query_rows, full_query)
        + back_product(grad_key_own, full_key)
        + back_product(grad_value_own, full_value)
    )
    grad_rows_in, grad_ln1_gain, grad_ln1_bias = pull_one(grad_normed_one)
    grad_tokens = grad_after_self + grad_rows_in
    grad_ln1_gain, grad_ln1_bias, grad_ln2_gain, grad_ln2_bias, grad_ln3_gain, grad_ln3_bias = (
        lax.psum(
            (
                grad_ln1_gain,
                grad_ln1_bias,
                grad_ln2_gain,
                grad_ln2_bias,
                grad_ln3_gain,
                grad_ln3_bias,
            ),
            ("dp", "fsdp"),
        )
    )
    (
        grad_w_query,
        grad_w_key,
        grad_w_value,
        grad_w_out,
        grad_c_query,
        grad_w_text,
        grad_c_key,
        grad_c_value,
        grad_c_out,
        grad_w_up,
        grad_w_down,
    ) = (
        lax.psum(grad_w_query.astype(jnp.bfloat16), "dp").astype(jnp.float32),
        lax.psum(grad_w_key.astype(jnp.bfloat16), "dp").astype(jnp.float32),
        lax.psum(grad_w_value.astype(jnp.bfloat16), "dp").astype(jnp.float32),
        lax.psum(grad_w_out.astype(jnp.bfloat16), "dp").astype(jnp.float32),
        lax.psum(grad_c_query.astype(jnp.bfloat16), "dp").astype(jnp.float32),
        lax.psum(grad_w_text.astype(jnp.bfloat16), "dp").astype(jnp.float32),
        lax.psum(grad_c_key.astype(jnp.bfloat16), "dp").astype(jnp.float32),
        lax.psum(grad_c_value.astype(jnp.bfloat16), "dp").astype(jnp.float32),
        lax.psum(grad_c_out.astype(jnp.bfloat16), "dp").astype(jnp.float32),
        lax.psum(grad_w_up.astype(jnp.bfloat16), "dp").astype(jnp.float32),
        lax.psum(grad_w_down.astype(jnp.bfloat16), "dp").astype(jnp.float32),
    )
    return (
        outputs[None],
        grad_tokens[None],
        grad_text[None],
        grad_ln1_gain,
        grad_ln1_bias,
        grad_w_query,
        grad_w_key,
        grad_w_value,
        grad_w_out,
        grad_ln2_gain,
        grad_ln2_bias,
        grad_c_query,
        grad_w_text,
        grad_c_key,
        grad_c_value,
        grad_c_out,
        grad_ln3_gain,
        grad_ln3_bias,
        grad_w_up,
        grad_w_down,
    )


def solution(mesh):
    in_specs = (
        P("dp", "fsdp", None),
        P("dp", "fsdp", None),
        P("dp", None),
        P("dp", None),
        P("dp", None),
        P(),
        P(),
        P("fsdp", None),
        P("fsdp", None),
        P("fsdp", None),
        P("fsdp", None),
        P(),
        P(),
        P("fsdp", None),
        P("fsdp", None),
        P("fsdp", None),
        P("fsdp", None),
        P("fsdp", None),
        P(),
        P(),
        P("fsdp", None),
        P("fsdp", None),
        P("dp", "fsdp", None),
    )
    out_specs = (
        P("dp", "fsdp", None),
        P("dp", "fsdp", None),
        P("dp", "fsdp", None),
        P(),
        P(),
        P("fsdp", None),
        P("fsdp", None),
        P("fsdp", None),
        P("fsdp", None),
        P(),
        P(),
        P("fsdp", None),
        P("fsdp", None),
        P("fsdp", None),
        P("fsdp", None),
        P("fsdp", None),
        P(),
        P(),
        P("fsdp", None),
        P("fsdp", None),
    )
    return jax.shard_map(local, mesh=mesh, in_specs=in_specs, out_specs=out_specs, check_vma=False)
```

profile of v0, /device:TPU:1, one launch (start us, length us, event | category | flops | bytes accessed | tf_op | source)
XLA Modules:
  0.0 2738.0 jit_solution(16386332290813971306)
XLA Ops:
  30.7 90.7 %fusion = f32[64,1152]{1,0:T(8,128)} fusion(f32[480,1152]{1,0:T(8,128)S(1)} %fusion.96), kind=kCustom, calls=%all-reduce-scatter | all-reduce-scatter fusion | flops 589825 | bytes 2507264
  129.4 51.9 %all-gather.35.cloned.1.call-done = bf16[1152,1152]{1,0:T(8,128)(2,1)} async-done(((bf16[144,1152]{1,0:T(8,128)(2,1)}), bf16[1152,1152]{1,0:T(8,128)(2,1)}) %all-gather.35.cloned.1.call-update) | async-done | bytes 2654224 | tf_op jit(solution)/shard_map/all_gather | solution.py:44
  184.8 60.1 %all-gather.25.cloned.1.call-done = bf16[1152,1152]{1,0:T(8,128)(2,1)} async-done(((bf16[144,1152]{1,0:T(8,128)(2,1)}), bf16[1152,1152]{1,0:T(8,128)(2,1)}) %all-gather.25.cloned.1.call-update) | async-done | bytes 2654224 | tf_op jit(solution)/shard_map/all_gather | solution.py:44
  248.6 59.6 %all-gather.19.cloned.1.call-done = bf16[1152,1152]{1,0:T(8,128)(2,1)} async-done(((bf16[144,1152]{1,0:T(8,128)(2,1)}), bf16[1152,1152]{1,0:T(8,128)(2,1)}) %all-gather.19.cloned.1.call-update) | async-done | bytes 2654224 | tf_op jit(solution)/shard_map/all_gather | solution.py:44
  317.4 54.2 %all-gather.23.cloned.1.call-done = bf16[1152,1152]{1,0:T(8,128)(2,1)} async-done(((bf16[144,1152]{1,0:T(8,128)(2,1)}), bf16[1152,1152]{1,0:T(8,128)(2,1)}) %all-gather.23.cloned.1.call-update) | async-done | bytes 2654224 | tf_op jit(solution)/shard_map/all_gather | solution.py:44
  460.4 97.9 %all-gather.27.cloned.1.call-done = bf16[2048,1152]{1,0:T(8,128)(2,1)} async-done(((bf16[256,1152]{1,0:T(8,128)(2,1)}), bf16[2048,1152]{1,0:T(8,128)(2,1)}) %all-gather.27.cloned.1.call-update) | async-done | bytes 4718608 | tf_op jit(solution)/shard_map/all_gather | solution.py:189
  565.0 96.1 %all-gather.21.cloned.1.call-done = bf16[2048,1152]{1,0:T(8,128)(2,1)} async-done(((bf16[256,1152]{1,0:T(8,128)(2,1)}), bf16[2048,1152]{1,0:T(8,128)(2,1)}) %all-gather.21.cloned.1.call-update) | async-done | bytes 4718608 | tf_op jit(solution)/shard_map/all_gather | solution.py:190
  728.6 60.1 %all-gather.33.cloned.1.call-done = bf16[1152,1152]{1,0:T(8,128)(2,1)} async-done(((bf16[144,1152]{1,0:T(8,128)(2,1)}), bf16[1152,1152]{1,0:T(8,128)(2,1)}) %all-gather.33.cloned.1.call-update) | async-done | bytes 2654224 | tf_op jit(solution)/shard_map/all_gather | solution.py:44
  801.8 50.2 %all-gather.37.cloned.1.call-done = bf16[1152,1152]{1,0:T(8,128)(2,1)} async-done(((bf16[144,1152]{1,0:T(8,128)(2,1)}), bf16[1152,1152]{1,0:T(8,128)(2,1)}) %all-gather.37.cloned.1.call-update) | async-done | bytes 2654224 | tf_op jit(solution)/shard_map/all_gather | solution.py:44
  855.5 207.9 %all-gather.39.cloned.1.call-done = bf16[1152,4608]{1,0:T(8,128)(2,1)} async-done(((bf16[144,4608]{1,0:T(8,128)(2,1)}), bf16[1152,4608]{1,0:T(8,128)(2,1)}) %all-gather.39.cloned.1.call-update) | async-done | bytes 10616848 | tf_op jit(solution)/shard_map/all_gather | solution.py:44
  1080.7 195.4 %all-gather.41.cloned.1.call-done = bf16[4608,1152]{1,0:T(8,128)(2,1)} async-done(((bf16[576,1152]{1,0:T(8,128)(2,1)}), bf16[4608,1152]{1,0:T(8,128)(2,1)}) %all-gather.41.cloned.1.call-update) | async-done | bytes 10616848 | tf_op jit(solution)/shard_map/all_gather | solution.py:44
  1434.6 44.6 %all_to_all.38 = bf16[8,60,2304]{2,1,0:T(8,128)(2,1)} all-to-all(bf16[8,60,2304]{2,1,0:T(8,128)(2,1)S(1)} %pad_maximum_fusion), channel_id=1, replica_groups=mesh['dp'=16,'fsdp'=8] {'fsdp'}, dimensions={0} | all-to-all | bytes 4423680 | tf_op jit(solution)/shard_map/all_to_all | solution.py:24
  1601.0 64.4 %reduce-scatter.33.cloned.1.call-done = bf16[144,1152]{1,0:T(8,128)(2,1)} async-done(((bf16[1152,1152]{1,0:T(8,128)(2,1)}), bf16[144,1152]{1,0:T(8,128)(2,1)}) %reduce-scatter.33.cloned.1.call-update) | async-done | bytes 331792 | tf_op jit(solution)/shard_map/reduce_scatter | solution.py:48
  1665.5 65.2 %reduce-scatter.27.cloned.1.call-done = bf16[144,1152]{1,0:T(8,128)(2,1)} async-done(((bf16[1152,1152]{1,0:T(8,128)(2,1)}), bf16[144,1152]{1,0:T(8,128)(2,1)}) %reduce-scatter.27.cloned.1.call-update) | async-done | bytes 331792 | tf_op jit(solution)/shard_map/reduce_scatter | solution.py:48
  1730.7 65.0 %reduce-scatter.25.cloned.1.call-done = bf16[144,1152]{1,0:T(8,128)(2,1)} async-done(((bf16[1152,1152]{1,0:T(8,128)(2,1)}), bf16[144,1152]{1,0:T(8,128)(2,1)}) %reduce-scatter.25.cloned.1.call-update) | async-done | bytes 331792 | tf_op jit(solution)/shard_map/reduce_scatter | solution.py:48
  1795.7 65.8 %reduce-scatter.19.cloned.1.call-done = bf16[144,1152]{1,0:T(8,128)(2,1)} async-done(((bf16[1152,1152]{1,0:T(8,128)(2,1)}), bf16[144,1152]{1,0:T(8,128)(2,1)}) %reduce-scatter.19.cloned.1.call-update) | async-done | bytes 331792 | tf_op jit(solution)/shard_map/reduce_scatter | solution.py:48
  1861.5 65.2 %reduce-scatter.29.cloned.1.call-done = bf16[144,1152]{1,0:T(8,128)(2,1)} async-done(((bf16[1152,1152]{1,0:T(8,128)(2,1)}), bf16[144,1152]{1,0:T(8,128)(2,1)}) %reduce-scatter.29.cloned.1.call-update) | async-done | bytes 331792 | tf_op jit(solution)/shard_map/reduce_scatter | solution.py:48
  1926.7 65.2 %reduce-scatter.31.cloned.1.call-done = bf16[144,1152]{1,0:T(8,128)(2,1)} async-done(((bf16[1152,1152]{1,0:T(8,128)(2,1)}), bf16[144,1152]{1,0:T(8,128)(2,1)}) %reduce-scatter.31.cloned.1.call-update) | async-done | bytes 331792 | tf_op jit(solution)/shard_map/reduce_scatter | solution.py:48
  1991.9 65.1 %reduce-scatter.23.cloned.1.call-done = bf16[144,1152]{1,0:T(8,128)(2,1)} async-done(((bf16[1152,1152]{1,0:T(8,128)(2,1)}), bf16[144,1152]{1,0:T(8,128)(2,1)}) %reduce-scatter.23.cloned.1.call-update) | async-done | bytes 331792 | tf_op jit(solution)/shard_map/reduce_scatter | solution.py:48
  2057.0 65.8 %reduce-scatter.21.cloned.1.call-done = bf16[144,1152]{1,0:T(8,128)(2,1)} async-done(((bf16[1152,1152]{1,0:T(8,128)(2,1)}), bf16[144,1152]{1,0:T(8,128)(2,1)}) %reduce-scatter.21.cloned.1.call-update) | async-done | bytes 331792 | tf_op jit(solution)/shard_map/reduce_scatter | solution.py:48
  2122.7 213.1 %reduce-scatter.35.cloned.1.call-done = bf16[144,4608]{1,0:T(8,128)(2,1)} async-done(((bf16[1152,4608]{1,0:T(8,128)(2,1)}), bf16[144,4608]{1,0:T(8,128)(2,1)}) %reduce-scatter.35.cloned.1.call-update) | async-done | bytes 1327120 | tf_op jit(solution)/shard_map/reduce_scatter | solution.py:48
  2335.8 214.5 %reduce-scatter.37.cloned.1.call-done = bf16[576,1152]{1,0:T(8,128)(2,1)} async-done(((bf16[4608,1152]{1,0:T(8,128)(2,1)}), bf16[576,1152]{1,0:T(8,128)(2,1)}) %reduce-scatter.37.cloned.1.call-update) | async-done | bytes 1327120 | tf_op jit(solution)/shard_map/reduce_scatter | solution.py:48
  2577.5 70.2 %all-reduce.2 = (f32[1152]{0:T(1024)}, f32[1152]{0:T(1024)}, f32[1152]{0:T(1024)}, f32[1152]{0:T(1024)}, f32[1152]{0:T(1024)}, /*index=5*/f32[1152]{0:T(1024)}) all-reduce(f32[1152]{0:T(1024)S(1)} %get-tuple-element.124, f32[1152]{0:T(1024)S(1)} %get-tuple-element.128, ...), channel_id=1, replica_groups=mesh['dp'=16,'fsdp'=8] {'dp','fsdp'}, use_global_device_ids=true, to_apply=%region_28.29 | all-reduce | flops 6912 | bytes 55296 | tf_op jit(solution)/shard_map/psum | solution.py:296
  2650.5 64.1 %all-reduce.6.cloned.1.call-done = (bf16[144,1152]{1,0:T(8,128)(2,1)}, bf16[144,1152]{1,0:T(8,128)(2,1)}, bf16[144,1152]{1,0:T(8,128)(2,1)}, bf16[144,1152]{1,0:...) async-done(((bf16[144,1152]{1,0:T(8,128)(2,1)}, ...) | async-done | bytes 6488080 | tf_op jit(solution)/shard_map/psum | solution.py:321
  (343 shorter events, 569.4 us)
Async XLA Ops:
  8.7 236.2 %all-gather.25.cloned.1.call-start = ((), (), s32[]{:S(2)}) async-start(), calls=%async_computation.18 | async-start | bytes 2985984 | tf_op jit(solution)/shard_map/all_gather | solution.py:44
  9.4 298.8 %all-gather.19.cloned.1.call-start = ((), (), s32[]{:S(2)}) async-start(), calls=%async_computation.15 | async-start | bytes 2985984 | tf_op jit(solution)/shard_map/all_gather | solution.py:44
  10.0 361.6 %all-gather.23.cloned.1.call-start = ((), (), s32[]{:S(2)}) async-start(), calls=%async_computation.17 | async-start | bytes 2985984 | tf_op jit(solution)/shard_map/all_gather | solution.py:44
  10.6 398.6 %all-gather.43.cloned.1.call-start = ((), (), s32[]{:S(2)}) async-start(), calls=%async_computation.39 | async-start | bytes 1327104 | tf_op jit(solution)/shard_map/all_gather | solution.py:215
  129.3 322.3 %all-gather.45.cloned.1.call-start = ((), (), s32[]{:S(2)}) async-start(), calls=%async_computation.40 | async-start | bytes 1327104 | tf_op jit(solution)/shard_map/all_gather | solution.py:214
  184.2 374.1 %all-gather.27.cloned.1.call-start = ((), (), s32[]{:S(2)}) async-start(), calls=%async_computation.19 | async-start | bytes 5308416 | tf_op jit(solution)/shard_map/all_gather | solution.py:189
  248.5 412.6 %all-gather.21.cloned.1.call-start = ((), (), s32[]{:S(2)}) async-start(), calls=%async_computation.16 | async-start | bytes 5308416 | tf_op jit(solution)/shard_map/all_gather | solution.py:190
  311.9 413.3 %all-gather.29.cloned.1.call-start = ((), (), s32[]{:S(2)}) async-start(), calls=%async_computation.20 | async-start | bytes 2985984 | tf_op jit(solution)/shard_map/all_gather | solution.py:44
  312.5 476.2 %all-gather.33.cloned.1.call-start = ((), (), s32[]{:S(2)}) async-start(), calls=%async_computation.22 | async-start | bytes 2985984 | tf_op jit(solution)/shard_map/all_gather | solution.py:44
  313.2 538.8 %all-gather.37.cloned.1.call-start = ((), (), s32[]{:S(2)}) async-start(), calls=%async_computation.24 | async-start | bytes 2985984 | tf_op jit(solution)/shard_map/all_gather | solution.py:44
  313.8 749.6 %all-gather.39.cloned.1.call-start = ((), (), s32[]{:S(2)}) async-start(), calls=%async_computation.25 | async-start | bytes 11943936 | tf_op jit(solution)/shard_map/all_gather | solution.py:44
  314.5 961.6 %all-gather.41.cloned.1.call-start = ((), (), s32[]{:S(2)}) async-start(), calls=%async_computation.26 | async-start | bytes 11943936 | tf_op jit(solution)/shard_map/all_gather | solution.py:44
  315.1 1207.0 %reduce-scatter.17.cloned.1.call-start = ((), (), s32[]{:S(2)}) async-start(), calls=%async_computation.28 | async-start | bytes 5308416 | tf_op jit(solution)/shard_map/reduce_scatter | solution.py:278
  1339.4 218.2 %reduce-scatter.15.cloned.1.call-start = ((), (), s32[]{:S(2)}) async-start(), calls=%async_computation.27 | async-start | bytes 5308416 | tf_op jit(solution)/shard_map/reduce_scatter | solution.py:275
  1489.7 241.0 %reduce-scatter.27.cloned.1.call-start = ((), (), s32[]{:S(2)}) async-start(), calls=%async_computation.33 | async-start | bytes 2985984 | tf_op jit(solution)/shard_map/reduce_scatter | solution.py:48
  1494.8 300.9 %reduce-scatter.25.cloned.1.call-start = ((), (), s32[]{:S(2)}) async-start(), calls=%async_computation.32 | async-start | bytes 2985984 | tf_op jit(solution)/shard_map/reduce_scatter | solution.py:48
  1499.6 361.9 %reduce-scatter.19.cloned.1.call-start = ((), (), s32[]{:S(2)}) async-start(), calls=%async_computation.29 | async-start | bytes 2985984 | tf_op jit(solution)/shard_map/reduce_scatter | solution.py:48
  1517.1 409.6 %reduce-scatter.29.cloned.1.call-start = ((), (), s32[]{:S(2)}) async-start(), calls=%async_computation.34 | async-start | bytes 2985984 | tf_op jit(solution)/shard_map/reduce_scatter | solution.py:48
  1519.6 472.3 %reduce-scatter.31.cloned.1.call-start = ((), (), s32[]{:S(2)}) async-start(), calls=%async_computation.35 | async-start | bytes 2985984 | tf_op jit(solution)/shard_map/reduce_scatter | solution.py:48
  1522.0 534.9 %reduce-scatter.23.cloned.1.call-start = ((), (), s32[]{:S(2)}) async-start(), calls=%async_computation.31 | async-start | bytes 2985984 | tf_op jit(solution)/shard_map/reduce_scatter | solution.py:48
  1525.9 596.9 %reduce-scatter.21.cloned.1.call-start = ((), (), s32[]{:S(2)}) async-start(), calls=%async_computation.30 | async-start | bytes 2985984 | tf_op jit(solution)/shard_map/reduce_scatter | solution.py:48
  1561.4 774.5 %reduce-scatter.35.cloned.1.call-start = ((), (), s32[]{:S(2)}) async-start(), calls=%async_computation.37 | async-start | bytes 11943936 | tf_op jit(solution)/shard_map/reduce_scatter | solution.py:48
  1570.7 979.6 %reduce-scatter.37.cloned.1.call-start = ((), (), s32[]{:S(2)}) async-start(), calls=%async_computation.38 | async-start | bytes 11943936 | tf_op jit(solution)/shard_map/reduce_scatter | solution.py:48
  1580.0 1134.6 %all-reduce.6.cloned.1.call-start = ((), (), s32[]{:S(2)}) async-start(), calls=%async_computation.42 | async-start | bytes 12976128 | tf_op jit(solution)/shard_map/psum | solution.py:321
  (81 other events, 4017.2 us)
Sparse Core Ops, SparseCore 0:
  9.7 106.0 all-gather.30
  117.4 63.7 all-gather.34
  182.9 61.9 all-gather.24
  309.7 61.7 all-gather.22
  453.9 104.4 all-gather.26
  560.6 100.5 all-gather.20
  662.6 62.4 all-gather.28
  726.8 61.7 all-gather.32
  790.2 61.7 all-gather.36
  853.6 209.7 all-gather.38
  1064.9 211.1 all-gather.40
  1339.5 101.7 reduce-scatter.16
  1443.6 114.0 reduce-scatter.14
  1598.1 67.3 reduce-scatter.32
  1667.9 62.7 reduce-scatter.26
  1732.9 62.7 reduce-scatter.24
  1798.7 62.7 reduce-scatter.18
  1863.9 62.7 reduce-scatter.28
  1929.1 62.7 reduce-scatter.30
  1994.2 62.7 reduce-scatter.22
  2060.0 62.7 reduce-scatter.20
  2125.0 210.7 reduce-scatter.34
  2338.2 212.0 reduce-scatter.36
  2553.8 160.7 all-reduce.5
  (4 shorter events, 173.4 us)
where the time goes:
time: 2750 us; the launch traced here: 2740 us
  waiting for transfers between devices  2080 us (76%)
  matrix products  266 us (10%)
  blocking collectives  221 us (8%)
  local copies, waits for them, and re-layouts  75.9 us (3%)
  other arithmetic  72.6 us (3%)
    reduce_scatter x10, waiting for transfers between devices, reduce_grad(): lax.psum_scatter(jnp.einsum('ti,to->io', left_side, right_side, preferred...  949 us
    all_gather x10, waiting for transfers between devices, fetch_weight(): return lax.all_gather(shard, 'fsdp', axis=0, tiled=True)  747 us
    all_gather x1, waiting for transfers between devices, local(): lax.all_gather(key_rows, 'fsdp', axis=0, tiled=True)  97.9 us
    all_gather x1, waiting for transfers between devices, local(): lax.all_gather(value_rows, 'fsdp', axis=0, tiled=True)  96.1 us
    unnamed x1, blocking collectives  90.7 us
    psum x1, blocking collectives, local(): lax.psum((grad_ln1_gain, grad_ln1_bias, grad_ln2_gain, grad_ln2_bias, gra...  70.2 us
    psum x1, waiting for transfers between devices, local(): lax.psum(grad_w_query.astype(jnp.bfloat16), 'dp').astype(jnp.float32)  64.1 us
  transfers between devices with their start and end apart: 30, of which 27 were waited for; matrix products, arithmetic and copies ran while one was open for 15% of the time, Pallas kernels for 0%

commit v1 on v0

v1 whole, which is shorter than its diff:
```python
import functools

import jax
import jax.numpy as jnp
from jax import lax
from jax.experimental import pallas as pl
from jax.experimental.pallas import tpu as pltpu
from jax.sharding import Mesh
from jax.sharding import PartitionSpec as P

HEADS = 16
HEAD = 72
D = 1152
FF = 4608
TXT = 480
TOK = 256
ROW = 2048
CAP_LEN = 120
SEGS = 3
CAPS = 4
SHARD = 144
SLOT = 128
HID = 72
HIDP = 80
BLK = 8 * HIDP
WIN = 640
STEP = 512

bf16 = jnp.bfloat16
f32 = jnp.float32
norm_eps = 1e-06
masked_score = -1e30
scale = HEAD ** (-0.5)
log2e = 1.4426950408889634
FS = ("y", "xl")
VMEM = 60 * 1024 * 1024


def dot_nn(a, b):
    return lax.dot_general(a, b, (((1,), (0,)), ((), ())), preferred_element_type=f32)


def dot_nt(a, b):
    return lax.dot_general(a, b, (((1,), (1,)), ((), ())), preferred_element_type=f32)


def dot_tn(a, b):
    return lax.dot_general(a, b, (((0,), (0,)), ((), ())), preferred_element_type=f32)


def params():
    return pltpu.CompilerParams(vmem_limit_bytes=VMEM)


def shift(x, axis, by):
    n = lax.axis_size(axis)
    return lax.ppermute(x, axis, [(i, (i + by) % n) for i in range(n)])


def halves(x):
    h = (x.shape[0] // 2 + 15) // 16 * 16
    return x[:h], x[h:]


def gather3(x):
    x01 = shift(x, "xl", 1)
    x10 = shift(x, "y", -1)
    x30 = shift(x, "y", 1)
    x31 = shift(x01, "y", 1)
    x20 = shift(x10, "y", -1)
    x11 = shift(x10, "xl", 1)
    lo = shift(halves(x11)[0], "y", -1)
    hi = shift(halves(x31)[1], "y", 1)
    return {
        (0, 0): x, (0, 1): x01, (1, 0): x10, (3, 0): x30, (3, 1): x31, (2, 0): x20, (1, 1): x11,
        (2, 1): (lo, hi),
    }


def reduce3(chunk):
    far = chunk(2, 1)
    lo, hi = halves(far)
    lo = shift(lo, "y", 1)
    hi = shift(hi, "y", -1)
    c20 = shift(chunk(2, 0), "y", 1)
    c11 = chunk(1, 1)
    h = lo.shape[0]
    c11 = jnp.concatenate([c11[:h] + lo, c11[h:]], axis=0)
    c31 = chunk(3, 1)
    c31 = jnp.concatenate([c31[:h], c31[h:] + hi], axis=0)
    c11 = shift(c11, "xl", 1)
    c31 = shift(c31, "y", -1)
    c10 = shift(chunk(1, 0) + c20 + c11, "y", 1)
    c01 = shift(chunk(0, 1) + c31, "xl", 1)
    c30 = shift(chunk(3, 0), "y", -1)
    return (
        chunk(0, 0).astype(f32) + c10.astype(f32) + c01.astype(f32) + c30.astype(f32)
    )


def peer(dy, dx):
    return ((lax.axis_index("y") + dy) % 4) * 2 + (lax.axis_index("xl") ^ dx)


def place(pieces, parts):
    flat, whose, at = [], [], []
    for (dy, dx), piece in pieces.items():
        first = 0
        for one in piece if isinstance(piece, tuple) else (piece,):
            flat.append(one)
            whose.append(peer(dy, dx))
            at.append(first)
            first += one.shape[0]
    n_in, n_out = len(flat), len(parts)
    copies = []
    for i, one in enumerate(flat):
        for o, (r0, rows, c0, cols) in enumerate(parts):
            lo, hi = max(r0, at[i]), min(r0 + rows, at[i] + one.shape[0])
            if hi > lo:
                copies.append((i, o, lo - at[i], hi - lo, c0, cols, lo - r0, rows))

    def body(where, *refs):
        ins, outs, sem = refs[:n_in], refs[n_in : n_in + n_out], refs[-1]
        started = []
        for k, (i, o, r, n, c0, cols, off, rows) in enumerate(copies):
            to = pl.multiple_of(where[i] * rows + off, 16)
            one = pltpu.make_async_copy(
                ins[i].at[pl.ds(r, n), pl.ds(c0, cols)], outs[o].at[pl.ds(to, n), :], sem.at[k]
            )
            one.start()
            started.append(one)
        for one in started:
            one.wait()

    any_spec = pl.BlockSpec(memory_space=pl.ANY)
    return pl.pallas_call(
        body,
        in_specs=[pl.BlockSpec(memory_space=pltpu.SMEM)] + [any_spec] * n_in,
        out_specs=[pl.BlockSpec(memory_space=pltpu.VMEM)] * n_out,
        out_shape=[jax.ShapeDtypeStruct((8 * p[1], p[3]), flat[0].dtype) for p in parts],
        scratch_shapes=[pltpu.SemaphoreType.DMA((len(copies),))],
        compiler_params=params(),
    )(jnp.stack(whose).astype(jnp.int32), *flat)


def sort_cores(mine, other):
    def body(core, m, o, w_out, c_key, c_query, c_value, c_out, sem):
        def run(first, second):
            moves = (
                (first, 0, D, w_out, 0), (first, D, D, c_key, 0), (first, 2 * D, WIN, c_out, 0),
                (second, 0, D, c_query, 0), (second, D, D, c_value, 0),
                (second, 2 * D + 128, STEP, c_out, WIN),
            )
            started = []
            for k, (src, c0, cols, dst, to) in enumerate(moves):
                one = pltpu.make_async_copy(
                    src.at[:, pl.ds(c0, cols)], dst.at[:, pl.ds(to, cols)], sem.at[k]
                )
                one.start()
                started.append(one)
            for one in started:
                one.wait()

        @pl.when(core[0] == 0)
        def _():
            run(m, o)

        @pl.when(core[0] != 0)
        def _():
            run(o, m)

    any_spec = pl.BlockSpec(memory_space=pl.ANY)
    return pl.pallas_call(
        body,
        in_specs=[pl.BlockSpec(memory_space=pltpu.SMEM), any_spec, any_spec],
        out_specs=[pl.BlockSpec(memory_space=pltpu.VMEM)] * 5,
        out_shape=[jax.ShapeDtypeStruct((D, D), bf16)] * 5,
        scratch_shapes=[pltpu.SemaphoreType.DMA((6,))],
        compiler_params=params(),
    )(lax.axis_index("c").astype(jnp.int32)[None], mine, other)


def self_forward_body(seg_q, seg_k, q, kv, out, total):
    mixed = []
    for h in range(2):
        base = 3 * SLOT * h
        s = dot_nt(q[:, base : base + SLOT], kv[:, base + SLOT : base + 2 * SLOT])
        s = jnp.where(seg_q[...] == seg_k[...], s, masked_score)
        top = jnp.max(s, axis=1, keepdims=True)
        p = jnp.exp2((s - top) * (scale * log2e))
        mass = jnp.sum(p, axis=1, keepdims=True)
        value = kv[:, base + 2 * SLOT : base + 3 * SLOT]
        mixed.append((dot_nn(p.astype(bf16), value) / mass)[:, :HEAD])
        log_total = top * (scale * log2e) + jnp.log2(mass)
        total[h] = jnp.transpose(jnp.broadcast_to(log_total, (TOK, SLOT)))[0:1, :]
    out[...] = jnp.concatenate(mixed, axis=1).astype(bf16)


def self_forward(seg_q, seg_k, qkv):
    return pl.pallas_call(
        self_forward_body,
        grid=(ROW // TOK,),
        in_specs=[
            pl.BlockSpec((TOK, 1), lambda i: (i, 0)),
            pl.BlockSpec((1, ROW), lambda i: (0, 0)),
            pl.BlockSpec((TOK, 6 * SLOT), lambda i: (i, 0)),
            pl.BlockSpec((ROW, 6 * SLOT), lambda i: (0, 0)),
        ],
        out_specs=[
            pl.BlockSpec((TOK, SHARD), lambda i: (i, 0)),
            pl.BlockSpec((2, 1, TOK), lambda i: (0, 0, i)),
        ],
        out_shape=[
            jax.ShapeDtypeStruct((ROW, SHARD), bf16),
            jax.ShapeDtypeStruct((2, 1, ROW), f32),
        ],
        compiler_params=params(),
    )(seg_q, seg_k, qkv, qkv)


def self_backward_body(head, seg_k, seg_q, total, q, kv, g, grad, key_sum, value_sum, key_t):
    i = pl.program_id(0)

    @pl.when(i == 0)
    def _():
        key_sum[...] = jnp.zeros_like(key_sum)
        value_sum[...] = jnp.zeros_like(value_sum)
        key_t[...] = jnp.transpose(kv[:, SLOT : 2 * SLOT])

    rows = pl.ds(pl.multiple_of(i * TOK, TOK), TOK)
    q_h, k_h, v_h = q[:, :SLOT], kv[:, SLOT : 2 * SLOT], kv[:, 2 * SLOT :]
    g_both = g[...]
    g_h = jnp.concatenate(
        [g_both[:, HEAD * head : HEAD * (head + 1)], jnp.zeros((TOK, SLOT - HEAD), bf16)], axis=1
    )
    p = jnp.exp2(dot_nt(k_h, q_h) * (scale * log2e) - total[0])
    p = jnp.where(seg_k[...] == seg_q[...], p, 0.0)
    dp = dot_nt(v_h, g_h)
    ds = (p * (dp - jnp.sum(p * dp, axis=0, keepdims=True))).astype(bf16)
    value_sum[...] += dot_nn(p.astype(bf16), g_h)
    key_sum[...] += dot_nn(ds, q_h)
    grad[rows, :SLOT] = (jnp.transpose(dot_nn(key_t[...], ds)) * scale).astype(bf16)

    @pl.when(i == pl.num_programs(0) - 1)
    def _():
        grad[:, SLOT : 2 * SLOT] = (key_sum[...] * scale).astype(bf16)
        grad[:, 2 * SLOT :] = value_sum[...].astype(bf16)


def self_backward(head, seg_k, seg_q, total, qkv, g):
    return pl.pallas_call(
        functools.partial(self_backward_body, head),
        grid=(ROW // TOK,),
        in_specs=[
            pl.BlockSpec((ROW, 1), lambda i: (0, 0)),
            pl.BlockSpec((1, TOK), lambda i: (0, i)),
            pl.BlockSpec((1, 1, TOK), lambda i: (head, 0, i)),
            pl.BlockSpec((TOK, 3 * SLOT), lambda i: (i, head)),
            pl.BlockSpec((ROW, 3 * SLOT), lambda i: (0, head)),
            pl.BlockSpec((TOK, SHARD), lambda i: (i, 0)),
        ],
        out_specs=pl.BlockSpec((ROW, 3 * SLOT), lambda i: (0, 0)),
        out_shape=jax.ShapeDtypeStruct((ROW, 3 * SLOT), bf16),
        scratch_shapes=[
            pltpu.VMEM((ROW, SLOT), f32),
            pltpu.VMEM((ROW, SLOT), f32),
            pltpu.VMEM((SLOT, ROW), bf16),
        ],
        compiler_params=params(),
    )(seg_k, seg_q, total, qkv, qkv, g)


def cross_forward_body(cap_q, cap_t, q, k, v, out):
    allowed = cap_q[...] == cap_t[...]
    mixed = []
    for h in range(HEADS):
        a, b = HEAD * h, HEAD * (h + 1)
        s = dot_nt(q[:, a:b], k[:, a:b])
        s = jnp.where(allowed, s, masked_score)
        top = jnp.max(s, axis=1, keepdims=True)
        p = jnp.exp2((s - top) * (scale * log2e))
        mass = jnp.sum(p, axis=1, keepdims=True)
        mixed.append(dot_nn(p.astype(bf16), v[:, a:b]) / mass)
    out[...] = jnp.concatenate(mixed, axis=1).astype(bf16)


def cross_forward(cap_q, cap_t, q, k, v):
    return pl.pallas_call(
        cross_forward_body,
        out_shape=jax.ShapeDtypeStruct((TOK, D), bf16),
        compiler_params=params(),
    )(cap_q, cap_t, q, k, v)


def cross_backward_body(cap_t, cap_q, q, k, v, g, grad_q, grad_k, grad_v):
    allowed = cap_t[...] == cap_q[...]
    dq, dk, dv = [], [], []
    for h in range(HEADS):
        a, b = HEAD * h, HEAD * (h + 1)
        q_h, k_h, v_h, g_h = q[:, a:b], k[:, a:b], v[:, a:b], g[:, a:b]
        s = jnp.where(allowed, dot_nt(k_h, q_h), masked_score)
        top = jnp.max(s, axis=0, keepdims=True)
        p = jnp.exp2((s - top) * (scale * log2e))
        p = p / jnp.sum(p, axis=0, keepdims=True)
        dp = dot_nt(v_h, g_h)
        ds = (p * (dp - jnp.sum(p * dp, axis=0, keepdims=True))).astype(bf16)
        dv.append(dot_nn(p.astype(bf16), g_h))
        dk.append(dot_nn(ds, q_h) * scale)
        dq.append(dot_tn(ds, k_h) * scale)
    grad_q[...] = jnp.concatenate(dq, axis=1).astype(bf16)
    grad_k[...] = jnp.concatenate(dk, axis=1).astype(bf16)
    grad_v[...] = jnp.concatenate(dv, axis=1).astype(bf16)


def cross_backward(cap_t, cap_q, q, k, v, g):
    return pl.pallas_call(
        cross_backward_body,
        out_shape=[
            jax.ShapeDtypeStruct((TOK, D), bf16),
            jax.ShapeDtypeStruct((TXT, D), bf16),
            jax.ShapeDtypeStruct((TXT, D), bf16),
        ],
        compiler_params=params(),
    )(cap_t, cap_q, q, k, v, g)


def mlp_body(*refs):
    x, g = refs[:2]
    ups, downs = refs[2:10], refs[10:18]
    out, act_out, pre_out, grad_x = refs[18:22]
    up_buf, down_buf, sem = refs[22:]

    def fetch(k):
        return (
            pltpu.make_async_copy(ups[k], up_buf.at[k % 2], sem.at[0, k % 2]),
            pltpu.make_async_copy(downs[k], down_buf.at[k % 2], sem.at[1, k % 2]),
        )

    for one in fetch(0):
        one.start()
    out[...] = jnp.zeros_like(out)
    grad_x[...] = jnp.zeros_like(grad_x)

    def step(h, carry):
        for k in range(8):

            @pl.when(h == k)
            def _(k=k):
                if k < 7:
                    for one in fetch(k + 1):
                        one.start()
                for one in fetch(k):
                    one.wait()

        slot = lax.rem(h, 2)
        up, down = up_buf[slot], down_buf[slot]
        cols = pl.ds(pl.multiple_of(h * BLK, BLK), BLK)
        pre = dot_nn(x[...], up)
        grad_act = dot_nt(g[...], down)
        cdf = 0.5 * (1.0 + lax.erf(pre * (0.5**0.5)))
        density = jnp.exp2(pre * pre * (-0.5 * log2e)) * 0.3989422804014327
        act = (pre * cdf).astype(bf16)
        grad_pre = (grad_act * (cdf + pre * density)).astype(bf16)
        act_out[:, cols] = act
        pre_out[:, cols] = grad_pre
        out[...] += dot_nn(act, down)
        grad_x[...] += dot_nt(grad_pre, up)
        return carry

    lax.fori_loop(0, 8, step, 0)


def mlp(x, g, ups, downs):
    vmem = pl.BlockSpec(memory_space=pltpu.VMEM)
    hbm = pl.BlockSpec(memory_space=pl.ANY)
    return pl.pallas_call(
        mlp_body,
        in_specs=[vmem] * 2 + [hbm] * 16,
        out_specs=[vmem] * 4,
        out_shape=[
            jax.ShapeDtypeStruct((TOK, D), f32),
            jax.ShapeDtypeStruct((TOK, 8 * BLK), bf16),
            jax.ShapeDtypeStruct((TOK, 8 * BLK), bf16),
            jax.ShapeDtypeStruct((TOK, D), f32),
        ],
        scratch_shapes=[
            pltpu.VMEM((2, D, BLK), bf16),
            pltpu.VMEM((2, BLK, D), bf16),
            pltpu.SemaphoreType.DMA((2, 2)),
        ],
        compiler_params=params(),
    )(x, g, *ups, *downs)


def sort_hidden_body(x, up, down):
    for f in range(8):
        lanes = slice(HIDP * f, HIDP * f + HID)
        up[:, 8 * HID * f : 8 * HID * (f + 1)] = jnp.concatenate(
            [x[h, :SHARD, lanes] for h in range(8)], axis=1
        ).astype(f32)
    for h in range(8):
        rows = slice(HID * h, HID * (h + 1))
        down[rows, :BLK] = x[h, SHARD : SHARD + HID].astype(f32)
        down[rows, BLK:] = x[h, SHARD + HIDP : SHARD + HIDP + HID, : D - BLK].astype(f32)


def sort_hidden(x):
    return pl.pallas_call(
        sort_hidden_body,
        out_shape=[
            jax.ShapeDtypeStruct((SHARD, FF), f32),
            jax.ShapeDtypeStruct((8 * HID, D), f32),
        ],
        compiler_params=params(),
    )(x)


def norm_layer(values, norm_gain, norm_shift):
    center = values - jnp.mean(values, axis=-1, keepdims=True)
    spread = jnp.mean(center * center, axis=-1, keepdims=True)
    return center * lax.rsqrt(spread + norm_eps) * norm_gain + norm_shift


def row_block(x, index, rows):
    return lax.dynamic_slice_in_dim(x, index * rows, rows, axis=0)


def core_window(x, core):
    return lax.dynamic_slice_in_dim(x, core * STEP, WIN, axis=1)


def both_cores(x):
    return jnp.concatenate([x, shift(x, "c", 1)], axis=0)


def window_grad(left, right):
    core = lax.axis_index("c")
    sent = shift(core_window(right, 1 - core), "c", 1)
    rights = jnp.concatenate([core_window(right, core), sent], axis=0)
    return dot_tn(both_cores(left), rights).astype(bf16)


def scatter_grads(grads, rows):
    packed = grads[0] if len(grads) == 1 else jnp.concatenate(grads, axis=1)
    return reduce3(lambda dy, dx: row_block(packed, peer(dy, dx), rows)).astype(bf16)


def whole_columns(mine, count):
    other = shift(mine, "c", 1)
    first = lax.axis_index("c") == 0
    low = jnp.where(first, mine, other).astype(f32)
    high = jnp.where(first, other, mine).astype(f32)
    return [
        jnp.concatenate(
            [low[:, WIN * k : WIN * (k + 1)], high[:, WIN * k + 128 : WIN * (k + 1)]], axis=1
        )
        for k in range(count)
    ]


def sum_rows_over_dp(x):
    core = lax.axis_index("c")
    rows = x.shape[0] // 2
    mine = row_block(x, core, rows) + shift(row_block(x, 1 - core, rows), "c", 1)
    mine = lax.psum(mine, ("xh", "z"))
    other = shift(mine, "c", 1)
    first = core == 0
    low = jnp.where(first, mine, other)
    high = jnp.where(first, other, mine)
    return jnp.concatenate([low, high], axis=0).astype(f32)


def sum_everywhere(x):
    for axis in ("y", "xl", "z", "xh", "c"):
        n = lax.axis_size(axis)
        x = sum([shift(x, axis, k) for k in range(1, n)], x)
    return x


def after(x, *others):
    return lax.optimization_barrier((x, *others))[0]


def local(
    tokens,
    text_states,
    seg_lengths,
    caption_of_segment,
    text_lengths,
    ln1_gain,
    ln1_bias,
    w_query,
    w_key,
    w_value,
    w_out,
    ln2_gain,
    ln2_bias,
    c_query,
    w_text,
    c_key,
    c_value,
    c_out,
    ln3_gain,
    ln3_bias,
    w_up,
    w_down,
    cotangent,
):
    core = lax.axis_index("c")
    first_core = core == 0
    eighth = lax.axis_index("z") * 2 + core
    first_row = peer(0, 0) * TOK

    ends = jnp.cumsum(seg_lengths[0])
    positions = jnp.arange(ROW, dtype=jnp.int32)
    segment = jnp.sum((positions[:, None] >= ends[None, :]).astype(jnp.int32), axis=1)
    own_segment = lax.dynamic_slice_in_dim(segment, first_row, TOK)
    text_pos = jnp.arange(TXT, dtype=jnp.int32)
    text_caption = text_pos // CAP_LEN
    live = jnp.sum(
        jnp.where(
            text_caption[:, None] == jnp.arange(CAPS, dtype=jnp.int32)[None, :],
            text_lengths[0][None, :],
            0,
        ),
        axis=1,
    )
    query_caption = jnp.sum(
        jnp.where(
            own_segment[:, None] == jnp.arange(SEGS, dtype=jnp.int32)[None, :],
            caption_of_segment[0][None, :],
            0,
        ),
        axis=1,
    )
    text_key = jnp.where(text_pos % CAP_LEN < live, text_caption, -1)

    rows_in = tokens[0].astype(f32)
    normed_one, pull_one = jax.vjp(norm_layer, rows_in, ln1_gain, ln1_bias)
    normed_one = normed_one.astype(bf16)
    (normed_all,) = place(gather3(normed_one), [(0, TOK, 0, D)])

    packed = jnp.concatenate(
        [
            jnp.concatenate([w[:, SHARD * k : SHARD * (k + 1)] for k in range(8)], axis=0)
            for w in (w_query, w_key, w_value)
        ],
        axis=1,
    )
    heads_w = lax.all_to_all(packed, FS, 0, 0, tiled=True)
    blank = jnp.zeros((D, SLOT - HEAD), bf16)
    heads_w = jnp.concatenate(
        [
            part
            for h in range(2)
            for k in range(3)
            for part in (heads_w[:, SHARD * k + HEAD * h : SHARD * k + HEAD * (h + 1)], blank)
        ],
        axis=1,
    )

    text_columns = lax.all_to_all(text_states[0], FS, split_axis=1, concat_axis=0, tiled=True)
    context = lax.psum(dot_nn(text_columns, w_text).astype(bf16), FS)

    pack = jnp.where(
        first_core,
        jnp.concatenate([w_out, c_key, c_out[:, :WIN]], axis=1),
        jnp.concatenate([c_query, c_value, c_out[:, STEP:]], axis=1),
    )
    (square_mine,) = place(gather3(after(pack, normed_all)), [(0, SHARD, 0, 2 * D + WIN)])
    square_other = shift(square_mine, "c", 1)
    full_out, full_ckey, full_cquery, full_cvalue, full_cout = sort_cores(
        square_mine, square_other
    )

    gap = jnp.zeros((SHARD, HIDP - HID), bf16)
    up_own = jnp.concatenate(
        [
            part
            for k in range(8)
            for part in (
                lax.dynamic_slice(w_up, (0, 8 * HID * k + HID * eighth), (SHARD, HID)),
                gap,
            )
        ],
        axis=1,
    )
    down_own = row_block(w_down, eighth, HID)
    down_own = jnp.pad(down_own, ((0, HIDP - HID), (0, 2 * BLK - D)))
    hidden_pack = jnp.concatenate([up_own, down_own[:, :BLK], down_own[:, BLK:]], axis=0)
    up_mine, low_mine, high_mine = place(
        gather3(hidden_pack),
        [(0, SHARD, 0, BLK), (SHARD, HIDP, 0, BLK), (SHARD + HIDP, HIDP, 0, D - BLK)],
    )
    down_mine = jnp.concatenate([low_mine, high_mine], axis=1)
    ups = [up_mine, shift(up_mine, "z", 1), shift(up_mine, "z", -1)]
    downs = [down_mine, shift(down_mine, "z", 1), shift(down_mine, "z", -1)]
    ups.append(shift(ups[1], "z", 1))
    downs.append(shift(downs[2], "z", -1))
    ups += [shift(w, "c", 1) for w in ups]
    downs += [shift(w, "c", 1) for w in downs]

    qkv = dot_nn(normed_all, heads_w).astype(bf16)
    attended_heads, self_total = self_forward(segment[:, None], segment[None, :], qkv)
    attended = lax.all_to_all(attended_heads, FS, split_axis=0, concat_axis=1, tiled=True)
    after_self = rows_in + dot_nn(attended, full_out)

    normed_two, pull_two = jax.vjp(norm_layer, after_self, ln2_gain, ln2_bias)
    normed_two = normed_two.astype(bf16)
    cross_query = dot_nn(normed_two, full_cquery).astype(bf16)
    cross_key = dot_nn(context, full_ckey).astype(bf16)
    cross_value = dot_nn(context, full_cvalue).astype(bf16)
    cross_mixed = cross_forward(
        query_caption[:, None], text_key[None, :], cross_query, cross_key, cross_value
    )
    after_cross = after_self + dot_nn(cross_mixed, full_cout)

    normed_three, pull_three = jax.vjp(norm_layer, after_cross, ln3_gain, ln3_bias)
    normed_three = normed_three.astype(bf16)
    grad_out = cotangent[0]
    grad_mlp = grad_out.astype(bf16)
    mlp_out, hidden_act, grad_pre, grad_three = mlp(normed_three, grad_mlp, ups, downs)
    outputs = after_cross + mlp_out
    grad_cross_in, grad_ln3_gain, grad_ln3_bias = pull_three(grad_three)
    grad_after_cross = grad_out + grad_cross_in

    half = 4 * BLK
    both_three = both_cores(normed_three)
    both_mlp = both_cores(grad_mlp)

    def own_blocks(x):
        mine = jnp.where(first_core, x[:, :half], x[:, half:])
        theirs = jnp.where(first_core, x[:, half:], x[:, :half])
        return mine, theirs

    act_mine, act_theirs = hidden_act[:, :half], hidden_act[:, half:]
    pre_mine, pre_theirs = grad_pre[:, :half], grad_pre[:, half:]
    act_both = jnp.concatenate([act_mine, shift(act_theirs, "c", 1)], axis=0)
    pre_both = jnp.concatenate([pre_mine, shift(pre_theirs, "c", 1)], axis=0)
    grad_up = dot_tn(both_three, pre_both).astype(bf16)
    grad_down = dot_tn(act_both, both_mlp).astype(bf16)

    def up_block(k):
        return grad_up[:, BLK * k : BLK * (k + 1)]

    def down_block(k):
        return grad_down[BLK * k : BLK * (k + 1)]

    far_up = shift(up_block(3), "z", -1)
    far_down = shift(down_block(3), "z", 1)
    up_minus = shift(up_block(1) + far_up, "z", -1)
    down_minus = shift(down_block(1), "z", -1)
    up_plus = shift(up_block(2), "z", 1)
    down_plus = shift(down_block(2) + far_down, "z", 1)
    up_sum = (
        up_block(0).astype(f32) + up_minus.astype(f32) + up_plus.astype(f32)
    ).astype(bf16)
    down_sum = (
        down_block(0).astype(f32) + down_minus.astype(f32) + down_plus.astype(f32)
    ).astype(bf16)

    def hidden_chunk(dy, dx):
        p = peer(dy, dx)
        down = jnp.pad(row_block(down_sum, p, HIDP), ((0, 0), (0, 2 * BLK - D)))
        return jnp.concatenate(
            [row_block(up_sum, p, SHARD), down[:, :BLK], down[:, BLK:]], axis=0
        )

    hidden_grad = reduce3(hidden_chunk).astype(bf16)
    hidden_grad = hidden_grad + shift(hidden_grad, "xh", 1)
    hidden_grad = lax.all_gather(hidden_grad, ("z", "c"), axis=0)
    grad_w_up, grad_w_down = sort_hidden(hidden_grad)

    grad_cross_branch = grad_after_cross.astype(bf16)
    grad_cross_mixed = dot_nt(grad_cross_branch, full_cout).astype(bf16)
    grad_cquery_rows, grad_key_part, grad_value_part = cross_backward(
        text_key[:, None],
        query_caption[None, :],
        cross_query,
        cross_key,
        cross_value,
        grad_cross_mixed,
    )
    context_grad_all = lax.psum(
        (dot_nt(grad_key_part, full_ckey) + dot_nt(grad_value_part, full_cvalue)).astype(bf16), FS
    )
    grad_w_text = dot_tn(text_columns, context_grad_all).astype(bf16)
    text_part = dot_nt(context_grad_all, w_text).astype(bf16)
    grad_text = lax.all_to_all(text_part, FS, split_axis=0, concat_axis=1, tiled=True).astype(f32)
    square_cross = scatter_grads(
        [
            window_grad(cross_mixed, grad_cross_branch),
            window_grad(normed_two, grad_cquery_rows),
            window_grad(context, grad_key_part),
            window_grad(context, grad_value_part),
        ],
        SHARD,
    )
    grad_self_in, grad_ln2_gain, grad_ln2_bias = pull_two(dot_nt(grad_cquery_rows, full_cquery))
    grad_after_self = grad_after_cross + grad_self_in

    grad_self_branch = grad_after_self.astype(bf16)
    square_out = scatter_grads([window_grad(attended, grad_self_branch)], SHARD)
    grad_attended = dot_nt(grad_self_branch, full_out).astype(bf16)
    grad_heads = lax.all_to_all(grad_attended, FS, split_axis=1, concat_axis=0, tiled=True)
    grad_qkv = jnp.concatenate(
        [
            self_backward(h, segment[:, None], segment[None, :], self_total, qkv, grad_heads)
            for h in range(2)
        ],
        axis=1,
    )
    normed_part = dot_nt(grad_qkv, heads_w).astype(bf16)
    grad_heads_w = dot_tn(normed_all, grad_qkv).astype(bf16)
    grad_heads_w = jnp.concatenate(
        [
            grad_heads_w[:, SLOT * (3 * h + k) : SLOT * (3 * h + k) + HEAD]
            for k in range(3)
            for h in range(2)
        ],
        axis=1,
    )
    grad_normed_one = reduce3(lambda dy, dx: row_block(normed_part, peer(dy, dx), TOK))
    grad_rows_in, grad_ln1_gain, grad_ln1_bias = pull_one(grad_normed_one)
    grad_tokens = grad_after_self + grad_rows_in

    square = jnp.concatenate([square_cross, square_out], axis=1)
    square = lax.psum(square, ("xh", "z"))
    grad_c_out, grad_c_query, grad_c_key, grad_c_value, grad_w_out = whole_columns(square, 5)
    grad_w_text = sum_rows_over_dp(grad_w_text)
    grad_qkv_w = lax.all_to_all(grad_heads_w, FS, 0, 0, tiled=True)
    grad_qkv_w = jnp.concatenate(
        [
            grad_qkv_w[SHARD * p : SHARD * (p + 1), SHARD * k : SHARD * (k + 1)]
            for k in range(3)
            for p in range(8)
        ],
        axis=1,
    )
    grad_qkv_w = sum_rows_over_dp(after(grad_qkv_w, square))
    grad_w_query, grad_w_key, grad_w_value = (
        grad_qkv_w[:, :D],
        grad_qkv_w[:, D : 2 * D],
        grad_qkv_w[:, 2 * D :],
    )
    norms = sum_everywhere(
        jnp.stack(
            [
                grad_ln1_gain,
                grad_ln1_bias,
                grad_ln2_gain,
                grad_ln2_bias,
                grad_ln3_gain,
                grad_ln3_bias,
            ]
        )
    )
    return (
        outputs[None],
        grad_tokens[None],
        grad_text[None],
        norms[0],
        norms[1],
        grad_w_query,
        grad_w_key,
        grad_w_value,
        grad_w_out,
        norms[2],
        norms[3],
        grad_c_query,
        grad_w_text,
        grad_c_key,
        grad_c_value,
        grad_c_out,
        norms[4],
        norms[5],
        grad_w_up,
        grad_w_down,
    )


def solution(mesh):
    split = Mesh(mesh.devices.reshape(2, 4, 2, 4, 2), ("xh", "z", "c", "y", "xl"))
    dp = ("xh", "z", "c")
    rows = P(dp, FS, None)
    per_row = P(dp, None)
    weight = P(FS, None)
    rep = P()
    in_specs = (
        rows, rows, per_row, per_row, per_row,
        rep, rep, weight, weight, weight, weight,
        rep, rep, weight, weight, weight, weight, weight,
        rep, rep, weight, weight, rows,
    )
    out_specs = (
        rows, rows, rows,
        rep, rep, weight, weight, weight, weight,
        rep, rep, weight, weight, weight, weight, weight,
        rep, rep, weight, weight,
    )
    return jax.shard_map(
        local, mesh=split, in_specs=in_specs, out_specs=out_specs, check_vma=False
    )
```

time: 2750 us -> 982 us (0.36)
  waiting for transfers between devices: 2080 us -> 392 us
  blocking collectives: 221 us -> 0 us
  matrix products: 266 us -> 76.7 us
  starting transfers between devices: 8.45 us -> 188 us
  Pallas kernels: 0 us -> 139 us
    all_gather x15 -> x1, waiting for transfers between devices: 1030 us -> 19 us  [local(): hidden_grad = lax.all_gather(hidden_grad, ('z', 'c'), axis=0)]
    reduce_scatter x12 -> x0, waiting for transfers between devices: 981 us -> none  [the longest x10 949 us: reduce_grad(): lax.psum_scatter(jnp.einsum('ti,to->io', left_side, right_side, preferred...]
    ppermute x0 -> x105, waiting for transfers between devices: none -> 207 us  [shift(): return lax.ppermute(x, axis, [(i, (i + by) % n) for i in range(n)])]
    dot_general x45 -> x23, matrix products: 266 us -> 76.7 us  [the longest x9 31.1 us: dot_tn(): lax.dot_general(a, b, (((0,), (0,)), ((), ())), preferred_element_type=f32)]
    ppermute x0 -> x105, starting transfers between devices: none -> 164 us  [shift(): return lax.ppermute(x, axis, [(i, (i + by) % n) for i in range(n)])]
    pallas_call x0 -> x11, Pallas kernels: none -> 139 us  [the longest x2 37.1 us: self_backward(): pl.pallas_call(functools.partial(self_backward_body, head), grid=(ROW //...]
    psum x1 -> x4, waiting for transfers between devices: 64.1 us -> 166 us  [the longest x1 67.5 us: local(): square = lax.psum(square, ('xh', 'z'))]
    unnamed x1 -> x0, blocking collectives: 90.7 us -> none
  transfers between devices with their start and end apart: 30 -> 116, of which waited for: 27 -> 36; matrix products, arithmetic and copies ran while one was open for 15% -> 22% of each run, Pallas kernels for 0% -> 14%
where the time goes in v1:
time: 982 us; the launch traced here: 971 us
  waiting for transfers between devices  392 us (40%)
  starting transfers between devices  188 us (19%)
  Pallas kernels  139 us (14%)
  local copies, waits for them, and re-layouts  91.1 us (9%)
  matrix products  76.7 us (8%)
  other arithmetic  67.3 us (7%)
  between operations  16.1 us (2%)
    ppermute x105, waiting for transfers between devices, shift(): return lax.ppermute(x, axis, [(i, (i + by) % n) for i in range(n)])  207 us
    ppermute x105, starting transfers between devices, shift(): return lax.ppermute(x, axis, [(i, (i + by) % n) for i in range(n)])  164 us
    psum x1, waiting for transfers between devices, local(): square = lax.psum(square, ('xh', 'z'))  67.5 us
    psum x1, waiting for transfers between devices, sum_rows_over_dp(): mine = lax.psum(mine, ('xh', 'z'))  54.5 us
    psum x1, waiting for transfers between devices, local(): context = lax.psum(dot_nn(text_columns, w_text).astype(bf16), FS)  44.1 us
    pallas_call x2, Pallas kernels, self_backward(): pl.pallas_call(functools.partial(self_backward_body, head), grid=(ROW //...  37.1 us
    dot_general x9, matrix products, dot_tn(): lax.dot_general(a, b, (((0,), (0,)), ((), ())), preferred_element_type=f32)  31.1 us
    unnamed x194, local copies, waits for them, and re-layouts  29.6 us
  transfers between devices with their start and end apart: 116, of which 36 were waited for; matrix products, arithmetic and copies ran while one was open for 22% of the time, Pallas kernels for 14%

profile of v1, /device:TPU:1, one launch (start us, length us, event | category | flops | bytes accessed | tf_op | source)
XLA Modules:
  0.0 970.7 jit_solution(16221276311687593429)
XLA Ops:
  17.5 9.1 collective-permute-done.1.refs_2_
  47.4 9.5 collective-permute-done.4.refs_5_
  76.0 11.9 %collective-permute-done.9.refs_2_ = bf16[144,2944]{1,0:T(8,128)(2,1)} collective-permute-done((bf16[144,2944]{1,0:T(8,128)(2,1)S(1)}, bf16[144,2944]{1,0:T(8,128)(2,1)}, u32[]{:S(2)}, u32[]{:S(2)}) %collective-permute-start.9) | collective-permute-done | bytes 847904 | tf_op jit(solution)/shard_map/ppermute | solution.py:57
  95.1 14.1 %collective-permute-done.13.refs_6_ = bf16[144,2944]{1,0:T(8,128)(2,1)} collective-permute-done((bf16[144,2944]{1,0:T(8,128)(2,1)}, bf16[144,2944]{1,0:T(8,128)(2,1)}, u32[]{:S(2)}, u32[]{:S(2)}) %collective-permute-start.13) | collective-permute-done | bytes 847904 | tf_op jit(solution)/shard_map/ppermute | solution.py:57
  115.3 9.6 collective-permute-done.10.refs_3_
  140.3 10.2 %collective-permute-start.16 = (bf16[1152,2944]{1,0:T(8,128)(2,1)}, bf16[1152,2944]{1,0:T(8,128)(2,1)}, u32[]{:S(2)}, u32[]{:S(2)}) collective-permute-start(bf16[1152,2944]{1,0:T(8,128)(2,1)} %shard_map.376.m), channel_id=1, source_target_pairs={{0,8},{8,0},{1,9},{9,1},{2,10},{10,2},{3,11},{11,3},{4,12},{12,4},... | collective-permute-start | bytes 20348936 | tf_op jit(solution)/shard_map/ppermute | solution.py:57
  175.0 19.8 %collective-permute-done.22.refs_6_ = bf16[304,640]{1,0:T(8,128)(2,1)S(1)} collective-permute-done((bf16[304,640]{1,0:T(8,128)(2,1)}, bf16[304,640]{1,0:T(8,128)(2,1)S(1)}, u32[]{:S(2)}, u32[]{:S(2)}) %collective-permute-start.22) | collective-permute-done | bytes 389152 | tf_op jit(solution)/shard_map/ppermute | solution.py:57
  208.4 44.1 %all-reduce.15.cloned.1.call-done = bf16[480,1152]{1,0:T(8,128)(2,1)} async-done(((bf16[480,1152]{1,0:T(8,128)(2,1)}), bf16[480,1152]{1,0:T(8,128)(2,1)}) %all-reduce.15.cloned.1.call-update) | async-done | bytes 1105936 | tf_op jit(solution)/shard_map/psum | solution.py:563
  271.1 20.0 %shard_map.375 = (bf16[2048,144]{1,0:T(8,128)(2,1)}, f32[2,1,2048]{2,1,0:T(1,128)}) custom-call(s32[2048,1]{1,0:T(8,128)} %copy.165.seg_q.seg_k, s32[1,2048]{1,0:T(1,128)} %bitcast.131, bf16[2048,768]{1,0:T(8,128)(2,1)} %convolution_convert_fusion.3.q.kv, bf16[2048,768]{1,0:T(8,128)(2,1)} %convolution_convert_fusion.3.q.kv), custom_call_target="tpu_custom_call" | custom-call | tf_op jit(solution)/shard_map/pallas_call | solution.py:200
  302.3 9.7 shard_map.377
  316.0 13.7 %collective-permute-start.34 = (bf16[640,1152]{1,0:T(8,128)(2,1)}, bf16[640,1152]{1,0:T(8,128)(2,1)}, u32[]{:S(2)}, u32[]{:S(2)}) collective-permute-start(bf16[640,1152]{1,0:T(8,128)(2,1)} %collective-permute-done.33.refs_12_), channel_id=1, source_target_pairs={{0,48},{16,0},{32,16},{48,32},{1,49},{17,1},{33,17},{49,33},{2,50}... | collective-permute-start | bytes 4423688 | tf_op jit(solution)/shard_map/ppermute | solution.py:57
  343.2 13.1 %shard_map.378 = bf16[256,1152]{1,0:T(8,128)(2,1)} custom-call(s32[256,1]{1,0:T(8,128)} %copy.168.cap_q, s32[1,480]{1,0:T(1,128)} %compare_select_fusion.cap_t, bf16[256,1152]{1,0:T(8,128)(2,1)} %convolution_convert_fusion.16.q, bf16[480,1152]{1,0:T(8,128)(2,1)} %convolution_convert_fusion.12.k, bf16[480,1152]{1,0:T(8,128)(2,1)} %convolution_convert_fusion.11.v), custom_call_target="tpu_custom_call" | custom-call | tf_op jit(solution)/shard_map/pallas_call | solution.py:288
  374.8 22.6 %shard_map.380 = (f32[256,1152]{1,0:T(8,128)}, bf16[256,5120]{1,0:T(8,128)(2,1)}, bf16[256,5120]{1,0:T(8,128)(2,1)}, f32[256,1152]{1,0:T(8,128)}) custom-call(bf16[256,1152]{1,0:T(8,128)(2,1)} %add_convert_fusion.3.refs_0_, bf16[256,1152]{1,0:T(8,128)(2,1)} %bitcast_convert_fusion.refs_1_, bf16[1152,640]{1,0:T(8,128)(2,1)} %get-tuple-element.48.refs_2_, ...), custom_call_target="tpu_custom_call" | custom-call | tf_op jit(solution)/shard_map/pallas_call | solution.py:376
  405.3 14.8 %shard_map.381 = (bf16[256,1152]{1,0:T(8,128)(2,1)}, bf16[480,1152]{1,0:T(8,128)(2,1)}, bf16[480,1152]{1,0:T(8,128)(2,1)}) custom-call(s32[480,1]{1,0:T(8,128)} %fusion.56.cap_t, s32[1,256]{1,0:T(1,128)} %bitcast.137, bf16[256,1152]{1,0:T(8,128)(2,1)} %convolution_convert_fusion.16.q, bf16[480,1152]{1,0:T(8,128)(2,1)} %convolution_convert_fusion.12.k, ...), custom_call_target="tpu_custom_call" | custom-call | tf_op jit(solution)/shard_map/pallas_call | solution.py:316
  469.6 18.5 %shard_map.382 = bf16[2048,384]{1,0:T(8,128)(2,1)} custom-call(s32[2048,1]{1,0:T(8,128)} %copy.165.seg_q.seg_k, s32[1,2048]{1,0:T(1,128)} %bitcast.132, f32[2,1,2048]{2,1,0:T(1,128)} %get-tuple-element.54.total, bf16[2048,768]{1,0:T(8,128)(2,1)} %convolution_convert_fusion.3.q.kv, bf16[2048,768]{1,0:T(8,128)(2,1)} %convolution_convert_fusion.3.q.kv, ...), custom_call_target="tpu_custom_call" | custom-call | tf_op jit(solution)/shard_map/pallas_call | solution.py:251
  488.2 18.6 %shard_map.383 = bf16[2048,384]{1,0:T(8,128)(2,1)} custom-call(s32[2048,1]{1,0:T(8,128)} %copy.165.seg_q.seg_k, s32[1,2048]{1,0:T(1,128)} %bitcast.133, f32[2,1,2048]{2,1,0:T(1,128)} %get-tuple-element.54.total, bf16[2048,768]{1,0:T(8,128)(2,1)} %convolution_convert_fusion.3.q.kv, bf16[2048,768]{1,0:T(8,128)(2,1)} %convolution_convert_fusion.3.q.kv, ...), custom_call_target="tpu_custom_call" | custom-call | tf_op jit(solution)/shard_map/pallas_call | solution.py:251
  571.0 11.9 %collective-permute-done.64 = bf16[80,2560]{1,0:T(8,128)(2,1)S(1)} collective-permute-done((bf16[80,2560]{1,0:T(8,128)(2,1)S(1)}, bf16[80,2560]{1,0:T(8,128)(2,1)S(1)}, u32[]{:S(2)}, u32[]{:S(2)}) %collective-permute-start.64) | collective-permute-done | bytes 409632 | tf_op jit(solution)/shard_map/ppermute | solution.py:57
  662.9 25.4 %collective-permute-done.51 = f32[6,1152]{1,0:T(8,128)S(1)} collective-permute-done((f32[6,1152]{1,0:T(8,128)S(1)}, f32[6,1152]{1,0:T(8,128)S(1)}, u32[]{:S(2)}, u32[]{:S(2)}) %collective-permute-start.51) | collective-permute-done | bytes 27680 | tf_op jit(solution)/shard_map/ppermute | solution.py:57
  697.1 9.6 collective-permute-done.70
  713.9 9.5 collective-permute-done.88
  729.9 67.5 %all-reduce.19.cloned.1.call-done = bf16[144,3200]{1,0:T(8,128)(2,1)} async-done(((bf16[144,3200]{1,0:T(8,128)(2,1)}), bf16[144,3200]{1,0:T(8,128)(2,1)}) %all-reduce.19.cloned.1.call-update) | async-done | bytes 921616 | tf_op jit(solution)/shard_map/psum | solution.py:728
  855.0 9.7 collective-permute-done.104
  870.1 54.5 %all-reduce.21.cloned.1.call-done = (bf16[72,3456]{1,0:T(8,128)(2,1)}, bf16[256,1152]{0,1:T(8,128)(2,1)}) async-done(((bf16[72,3456]{1,0:T(8,128)(2,1)}, bf16[256,1152]{0,1:T(8,128)(2,1)}), (bf16[72,3456]{1,0:T(8,128)(2,1)}, bf16[256,1152]{0,1:T(8,128)(2,1)})) %all-reduce.21.cloned.1.call-update) | async-done | bytes 1087504 | tf_op jit(solution)/shard_map/psum | solution.py:465
  939.0 19.0 %all-gather.3.cloned.1.call-done = bf16[2432,640]{1,0:T(8,128)(2,1)} async-done(((bf16[304,640]{1,0:T(8,128)(2,1)}), bf16[2432,640]{1,0:T(8,128)(2,1)}) %all-gather.3.cloned.1.call-update) | async-done | bytes 3112976 | tf_op jit(solution)/shard_map/all_gather | solution.py:671
  (611 shorter events, 488.1 us)
Async XLA Ops:
  28.8 141.4 %collective-permute-start.18 = (bf16[304,640]{1,0:T(8,128)(2,1)S(1)}, bf16[304,640]{1,0:T(8,128)(2,1)}, u32[]{:S(2)}, u32[]{:S(2)}) collective-permute-start(bf16[304,640]{1,0:T(8,128)(2,1)S(1)} %pad_maximum_fusion.15.refs_0_), channel_id=1, source_target_pairs={{0,6},{2,0},{4,2},{6,4},{1,7},{3,1},{5,3},{7,5},{8,14},{10,8},{12,... | collective-permute-start | bytes 1167368 | tf_op jit(solution)/shard_map/ppermute | solution.py:57
  33.7 126.1 %all-to-all-start.2 = ((bf16[60,8,512]{2,0,1:T(8,128)(2,1)}), bf16[60,8,512]{2,0,1:T(8,128)(2,1)S(1)}, u32[]{:S(2)}, u32[]{:S(2)}) async-start(bf16[60,8,512]{2,0,1:T(8,128)(2,1)} %copy.167), calls=%async_computation.2 | async-start | bytes 1048576 | tf_op jit(solution)/shard_map/all_to_all | solution.py:562
  126.1 77.6 %collective-permute-start.19 = (bf16[304,640]{1,0:T(8,128)(2,1)S(1)}, bf16[304,640]{1,0:T(8,128)(2,1)}, u32[]{:S(2)}, u32[]{:S(2)}) collective-permute-start(bf16[304,640]{1,0:T(8,128)(2,1)S(1)} %pad_maximum_fusion.15.refs_0_), channel_id=1, source_target_pairs={{0,2},{2,4},{4,6},{6,0},{1,3},{3,5},{5,7},{7,1},{8,10},{10,12},{12... | collective-permute-start | bytes 1167368 | tf_op jit(solution)/shard_map/ppermute | solution.py:57
  140.3 159.4 %collective-permute-start.16 = (bf16[1152,2944]{1,0:T(8,128)(2,1)}, bf16[1152,2944]{1,0:T(8,128)(2,1)}, u32[]{:S(2)}, u32[]{:S(2)}) collective-permute-start(bf16[1152,2944]{1,0:T(8,128)(2,1)} %shard_map.376.m), channel_id=1, source_target_pairs={{0,8},{8,0},{1,9},{9,1},{2,10},{10,2},{3,11},{11,3},{4,12},{12,4},... | collective-permute-start | bytes 20348936 | tf_op jit(solution)/shard_map/ppermute | solution.py:57
  163.4 89.1 %all-reduce.15.cloned.1.call-start = ((), (), s32[]{:S(2)}) async-start(), calls=%async_computation.6 | async-start | bytes 2211840 | tf_op jit(solution)/shard_map/psum | solution.py:563
  262.8 66.9 %collective-permute-start.35 = (bf16[640,1152]{1,0:T(8,128)(2,1)}, bf16[640,1152]{1,0:T(8,128)(2,1)}, u32[]{:S(2)}, u32[]{:S(2)}) collective-permute-start(bf16[640,1152]{1,0:T(8,128)(2,1)} %constant_dynamic-update-slice_fusion.refs_10_), channel_id=1, source_target_pairs={{0,8},{8,0},{1,9},{9,1},{2,10},{10,2},{3,11},{11,3},{4,12},{12,4},... | collective-permute-start | bytes 4423688 | tf_op jit(solution)/shard_map/ppermute | solution.py:57
  297.6 287.4 %all-reduce.17.cloned.1.call-start = ((), (), s32[]{:S(2)}) async-start(), calls=%async_computation.7 | async-start | bytes 2211840 | tf_op jit(solution)/shard_map/psum | solution.py:684
  299.7 56.6 %collective-permute-start.26 = (bf16[1152,640]{1,0:T(8,128)(2,1)}, bf16[1152,640]{1,0:T(8,128)(2,1)}, u32[]{:S(2)}, u32[]{:S(2)}) collective-permute-start(bf16[1152,640]{1,0:T(8,128)(2,1)} %get-tuple-element.48.refs_2_), channel_id=1, source_target_pairs={{0,48},{16,0},{32,16},{48,32},{1,49},{17,1},{33,17},{49,33},{2,50}... | collective-permute-start | bytes 4423688 | tf_op jit(solution)/shard_map/ppermute | solution.py:57
  374.2 75.6 %collective-permute-start.71 = (bf16[256,1152]{0,1:T(8,128)(2,1)}, bf16[256,1152]{0,1:T(8,128)(2,1)}, u32[]{:S(2)}, u32[]{:S(2)}) collective-permute-start(bf16[256,1152]{0,1:T(8,128)(2,1)} %bitcast.17), channel_id=1, source_target_pairs={{0,8},{8,0},{1,9},{9,1},{2,10},{10,2},{3,11},{11,3},{4,12},{12,4},... | collective-permute-start | bytes 1769480 | tf_op jit(solution)/shard_map/ppermute | solution.py:57
  374.2 154.4 %collective-permute-start.56 = (bf16[256,1152]{1,0:T(8,128)(2,1)}, bf16[256,1152]{1,0:T(8,128)(2,1)}, u32[]{:S(2)}, u32[]{:S(2)}) collective-permute-start(bf16[256,1152]{1,0:T(8,128)(2,1)} %shard_map.378), channel_id=1, source_target_pairs={{0,8},{8,0},{1,9},{9,1},{2,10},{10,2},{3,11},{11,3},{4,12},{12,4},... | collective-permute-start | bytes 1769480 | tf_op jit(solution)/shard_map/ppermute | solution.py:57
  374.7 159.7 %collective-permute-start.58 = (bf16[256,1152]{1,0:T(8,128)(2,1)}, bf16[256,1152]{1,0:T(8,128)(2,1)}, u32[]{:S(2)}, u32[]{:S(2)}) collective-permute-start(bf16[256,1152]{1,0:T(8,128)(2,1)} %add_convert_fusion.4), channel_id=1, source_target_pairs={{0,8},{8,0},{1,9},{9,1},{2,10},{10,2},{3,11},{11,3},{4,12},{12,4},... | collective-permute-start | bytes 1769480 | tf_op jit(solution)/shard_map/ppermute | solution.py:57
  433.9 94.6 %collective-permute-start.57 = (bf16[256,640]{1,0:T(8,128)(2,1)}, bf16[256,640]{1,0:T(8,128)(2,1)}, u32[]{:S(2)}, u32[]{:S(2)}) collective-permute-start(bf16[256,640]{1,0:T(8,128)(2,1)} %get-tuple-element.325), channel_id=1, source_target_pairs={{0,8},{8,0},{1,9},{9,1},{2,10},{10,2},{3,11},{11,3},{4,12},{12,4},... | collective-permute-start | bytes 983048 | tf_op jit(solution)/shard_map/ppermute | solution.py:57
  449.8 83.3 %collective-permute-start.59 = (bf16[256,640]{1,0:T(8,128)(2,1)}, bf16[256,640]{1,0:T(8,128)(2,1)}, u32[]{:S(2)}, u32[]{:S(2)}) collective-permute-start(bf16[256,640]{1,0:T(8,128)(2,1)} %get-tuple-element.327), channel_id=1, source_target_pairs={{0,8},{8,0},{1,9},{9,1},{2,10},{10,2},{3,11},{11,3},{4,12},{12,4},... | collective-permute-start | bytes 983048 | tf_op jit(solution)/shard_map/ppermute | solution.py:57
  465.4 73.0 %collective-permute-start.61 = (bf16[480,640]{1,0:T(8,128)(2,1)}, bf16[480,640]{1,0:T(8,128)(2,1)}, u32[]{:S(2)}, u32[]{:S(2)}) collective-permute-start(bf16[480,640]{1,0:T(8,128)(2,1)} %get-tuple-element.319), channel_id=1, source_target_pairs={{0,8},{8,0},{1,9},{9,1},{2,10},{10,2},{3,11},{11,3},{4,12},{12,4},... | collective-permute-start | bytes 1843208 | tf_op jit(solution)/shard_map/ppermute | solution.py:57
  521.8 101.4 %all-to-all-start.5 = ((bf16[8,144,432]{2,1,0:T(8,128)(2,1)}), bf16[8,144,432]{2,1,0:T(8,128)(2,1)S(1)}, u32[]{:S(2)}, u32[]{:S(2)}) async-start(bf16[8,144,432]{2,1,0:T(8,128)(2,1)} %bitcast.121), calls=%async_computation.5 | async-start | bytes 2359296 | tf_op jit(solution)/shard_map/all_to_all | solution.py:731
  627.8 169.7 %all-reduce.19.cloned.1.call-start = ((), (), s32[]{:S(2)}) async-start(), calls=%async_computation.8 | async-start | bytes 1843200 | tf_op jit(solution)/shard_map/psum | solution.py:728
  652.4 55.9 %collective-permute-start.94 = (bf16[640,1152]{1,0:T(8,128)(2,1)}, bf16[640,1152]{1,0:T(8,128)(2,1)S(1)}, u32[]{:S(2)}, u32[]{:S(2)}) collective-permute-start(bf16[640,1152]{1,0:T(8,128)(2,1)} %get-tuple-element.210), channel_id=1, source_target_pairs={{0,16},{16,32},{32,48},{48,0},{1,17},{17,33},{33,49},{49,1},{2,18}... | collective-permute-start | bytes 4423688 | tf_op jit(solution)/shard_map/ppermute | solution.py:57
  694.6 102.9 %collective-permute-start.93 = (bf16[640,1152]{1,0:T(8,128)(2,1)}, bf16[640,1152]{1,0:T(8,128)(2,1)}, u32[]{:S(2)}, u32[]{:S(2)}) collective-permute-start(bf16[640,1152]{1,0:T(8,128)(2,1)} %get-tuple-element.209), channel_id=1, source_target_pairs={{0,48},{16,0},{32,16},{48,32},{1,49},{17,1},{33,17},{49,33},{2,50}... | collective-permute-start | bytes 4423688 | tf_op jit(solution)/shard_map/ppermute | solution.py:57
  711.1 92.4 %collective-permute-start.95 = (bf16[640,1152]{1,0:T(8,128)(2,1)}, bf16[640,1152]{1,0:T(8,128)(2,1)}, u32[]{:S(2)}, u32[]{:S(2)}) collective-permute-start(bf16[640,1152]{1,0:T(8,128)(2,1)} %slice_add_fusion), channel_id=1, source_target_pairs={{0,16},{16,32},{32,48},{48,0},{1,17},{17,33},{33,49},{49,1},{2,18}... | collective-permute-start | bytes 4423688 | tf_op jit(solution)/shard_map/ppermute | solution.py:57
  712.2 212.5 %all-reduce.21.cloned.1.call-start = ((), (), s32[]{:S(2)}) async-start(), calls=%async_computation.10 | async-start | bytes 2174976 | tf_op jit(solution)/shard_map/psum | solution.py:465
  712.3 142.1 %collective-permute-start.55 = (f32[6,1152]{1,0:T(8,128)S(1)}, f32[6,1152]{1,0:T(8,128)S(1)}, u32[]{:S(2)}, u32[]{:S(2)}) collective-permute-start(f32[6,1152]{1,0:T(8,128)S(1)} %add.719), channel_id=1, source_target_pairs={{0,8},{8,0},{1,9},{9,1},{2,10},{10,2},{3,11},{11,3},{4,12},{12,4},... | collective-permute-start | bytes 82952 | tf_op jit(solution)/shard_map/ppermute | solution.py:57
  727.5 79.7 %collective-permute-start.89 = (bf16[1152,640]{1,0:T(8,128)(2,1)}, bf16[1152,640]{1,0:T(8,128)(2,1)}, u32[]{:S(2)}, u32[]{:S(2)}) collective-permute-start(bf16[1152,640]{1,0:T(8,128)(2,1)} %get-tuple-element.207), channel_id=1, source_target_pairs={{0,48},{16,0},{32,16},{48,32},{1,49},{17,1},{33,17},{49,33},{2,50}... | collective-permute-start | bytes 4423688 | tf_op jit(solution)/shard_map/ppermute | solution.py:57
  729.9 77.3 %collective-permute-start.90 = (bf16[1152,640]{1,0:T(8,128)(2,1)}, bf16[1152,640]{1,0:T(8,128)(2,1)}, u32[]{:S(2)}, u32[]{:S(2)}) collective-permute-start(bf16[1152,640]{1,0:T(8,128)(2,1)} %get-tuple-element.208), channel_id=1, source_target_pairs={{0,16},{16,32},{32,48},{48,0},{1,17},{17,33},{33,49},{49,1},{2,18}... | collective-permute-start | bytes 4423688 | tf_op jit(solution)/shard_map/ppermute | solution.py:57
  838.3 119.7 %all-gather.3.cloned.1.call-start = ((), (), s32[]{:S(2)}) async-start(), calls=%async_computation.9 | async-start | bytes 3502080 | tf_op jit(solution)/shard_map/all_gather | solution.py:671
  (174 other events, 2999.2 us)
Sparse Core Ops, SparseCore 0:
  167.9 84.5 all-reduce.14
  440.5 80.5 all-reduce.16
  712.3 85.1 all-reduce.18
  838.4 86.1 all-reduce.20
  926.7 31.2 all-gather.2

commit v2 on v1

v2 whole, which is shorter than its diff:
```python
import functools

import jax
import jax.numpy as jnp
from jax import lax
from jax.experimental import pallas as pl
from jax.experimental.pallas import tpu as pltpu
from jax.sharding import Mesh
from jax.sharding import PartitionSpec as P

HEADS = 16
HEAD = 72
D = 1152
FF = 4608
CAP_TOK = 60
TXT_OWN = 64
TXT = 8 * TXT_OWN
TOK = 256
ROW = 2048
CAP_LEN = 120
SEGS = 3
CAPS = 4
SHARD = 144
SLOT = 128
HID = 72
HIDP = 80
BLK = 8 * HIDP
PACK = D + 2 * BLK
OWN = SHARD + 2 * HIDP
WIN = 640
STEP = 512

bf16 = jnp.bfloat16
f32 = jnp.float32
norm_eps = 1e-06
masked_score = -1e30
scale = HEAD ** (-0.5)
log2e = 1.4426950408889634
FS = ("y", "xl")
VMEM = 60 * 1024 * 1024


def dot_nn(a, b):
    return lax.dot_general(a, b, (((1,), (0,)), ((), ())), preferred_element_type=f32)


def dot_nt(a, b):
    return lax.dot_general(a, b, (((1,), (1,)), ((), ())), preferred_element_type=f32)


def dot_tn(a, b):
    return lax.dot_general(a, b, (((0,), (0,)), ((), ())), preferred_element_type=f32)


def params():
    return pltpu.CompilerParams(vmem_limit_bytes=VMEM)


def shift(x, axis, by):
    n = lax.axis_size(axis)
    return lax.ppermute(x, axis, [(i, (i + by) % n) for i in range(n)])


def halves(x):
    h = (x.shape[0] // 2 + 15) // 16 * 16
    return x[:h], x[h:]


def after(x, *others):
    return lax.optimization_barrier((x, *others))[0] if others else x


def gather3(x, second=(), third=()):
    x01 = shift(x, "xl", 1)
    x10 = shift(x, "y", -1)
    x30 = shift(x, "y", 1)
    near = after(x10, *second)
    x31 = shift(after(x01, *second), "y", 1)
    x20 = shift(near, "y", -1)
    x11 = shift(near, "xl", 1)
    lo = shift(after(halves(x11)[0], *third), "y", -1)
    hi = shift(after(halves(x31)[1], *third), "y", 1)
    return {
        (0, 0): x, (0, 1): x01, (1, 0): x10, (3, 0): x30, (3, 1): x31, (2, 0): x20, (1, 1): x11,
        (2, 1): (lo, hi),
    }


def reduce3(chunk, second=(), third=()):
    lo, hi = halves(chunk(2, 1))
    lo = after(shift(lo, "y", 1), *second)
    hi = shift(hi, "y", -1)
    h = lo.shape[0]
    c20 = shift(after(chunk(2, 0), *second), "y", 1)
    c11 = chunk(1, 1)
    c11 = jnp.concatenate([c11[:h] + lo, c11[h:]], axis=0)
    c31 = chunk(3, 1)
    c31 = jnp.concatenate([c31[:h], c31[h:] + hi], axis=0)
    c11 = after(shift(c11, "xl", 1), *third)
    c31 = shift(c31, "y", -1)
    c10 = shift(chunk(1, 0) + c20 + c11, "y", 1)
    c01 = shift(chunk(0, 1) + c31, "xl", 1)
    c30 = shift(after(chunk(3, 0), *third), "y", -1)
    return (
        chunk(0, 0).astype(f32) + c10.astype(f32) + c01.astype(f32) + c30.astype(f32)
    )


def peer(dy, dx):
    return ((lax.axis_index("y") + dy) % 4) * 2 + (lax.axis_index("xl") ^ dx)


def place(pieces, parts):
    flat, whose, at = [], [], []
    for (dy, dx), piece in pieces.items():
        first = 0
        for one in piece if isinstance(piece, tuple) else (piece,):
            flat.append(one)
            whose.append(peer(dy, dx))
            at.append(first)
            first += one.shape[0]
    n_in, cols = len(flat), flat[0].shape[1]
    copies = []
    for i, one in enumerate(flat):
        for r0, rows, base in parts:
            lo, hi = max(r0, at[i]), min(r0 + rows, at[i] + one.shape[0])
            if hi > lo:
                copies.append((i, lo - at[i], hi - lo, rows, base + lo - r0))

    def body(where, *refs):
        ins, out, sem = refs[:n_in], refs[n_in], refs[-1]
        started = []
        for k, (i, r, n, rows, base) in enumerate(copies):
            to = pl.multiple_of(where[i] * rows + base, 16)
            one = pltpu.make_async_copy(ins[i].at[pl.ds(r, n)], out.at[pl.ds(to, n)], sem.at[k])
            one.start()
            started.append(one)
        for one in started:
            one.wait()

    any_spec = pl.BlockSpec(memory_space=pl.ANY)
    total = 8 * sum(rows for _, rows, _ in parts)
    return pl.pallas_call(
        body,
        in_specs=[pl.BlockSpec(memory_space=pltpu.SMEM)] + [any_spec] * n_in,
        out_specs=pl.BlockSpec(memory_space=pltpu.VMEM),
        out_shape=jax.ShapeDtypeStruct((total, cols), flat[0].dtype),
        scratch_shapes=[pltpu.SemaphoreType.DMA((len(copies),))],
        compiler_params=params(),
    )(jnp.stack(whose).astype(jnp.int32), *flat)


def sort_cores(mine, other, moves, count):
    def body(core, m, o, *refs):
        outs, sem = refs[:count], refs[-1]

        def run(sides):
            started = []
            for k, (side, c0, cols, dst, to) in enumerate(moves):
                one = pltpu.make_async_copy(
                    sides[side].at[:, pl.ds(c0, cols)], outs[dst].at[:, pl.ds(to, cols)], sem.at[k]
                )
                one.start()
                started.append(one)
            for one in started:
                one.wait()

        @pl.when(core[0] == 0)
        def _():
            run((m, o))

        @pl.when(core[0] != 0)
        def _():
            run((o, m))

    any_spec = pl.BlockSpec(memory_space=pl.ANY)
    return pl.pallas_call(
        body,
        in_specs=[pl.BlockSpec(memory_space=pltpu.SMEM), any_spec, any_spec],
        out_specs=[pl.BlockSpec(memory_space=pltpu.VMEM)] * count,
        out_shape=[jax.ShapeDtypeStruct((D, D), bf16)] * count,
        scratch_shapes=[pltpu.SemaphoreType.DMA((len(moves),))],
        compiler_params=params(),
    )(lax.axis_index("c").astype(jnp.int32)[None], mine, other)


def self_forward_body(seg_q, seg_k, q, kv, out, total):
    s = dot_nt(q[:, :SLOT], kv[:, SLOT : 2 * SLOT])
    s = jnp.where(seg_q[...] == seg_k[...], s, masked_score)
    top = jnp.max(s, axis=1, keepdims=True)
    p = jnp.exp2((s - top) * (scale * log2e))
    mass = jnp.sum(p, axis=1, keepdims=True)
    out[...] = (dot_nn(p.astype(bf16), kv[:, 2 * SLOT :]) / mass)[:, :HEAD].astype(bf16)
    log_total = top * (scale * log2e) + jnp.log2(mass)
    total[...] = jnp.transpose(jnp.broadcast_to(log_total, (TOK, SLOT)))[0:1, :]


def self_forward(head, seg_q, seg_k, qkv):
    return pl.pallas_call(
        self_forward_body,
        grid=(ROW // TOK,),
        in_specs=[
            pl.BlockSpec((TOK, 1), lambda i: (i, 0)),
            pl.BlockSpec((1, ROW), lambda i: (0, 0)),
            pl.BlockSpec((TOK, 3 * SLOT), lambda i: (i, head)),
            pl.BlockSpec((ROW, 3 * SLOT), lambda i: (0, head)),
        ],
        out_specs=[
            pl.BlockSpec((TOK, HEAD), lambda i: (i, 0)),
            pl.BlockSpec((1, TOK), lambda i: (0, i)),
        ],
        out_shape=[
            jax.ShapeDtypeStruct((ROW, HEAD), bf16),
            jax.ShapeDtypeStruct((1, ROW), f32),
        ],
        compiler_params=params(),
    )(seg_q, seg_k, qkv, qkv)


def self_backward_body(head, seg_k, seg_q, total, q, kv, g, grad, key_sum, value_sum, key_t):
    i = pl.program_id(0)

    @pl.when(i == 0)
    def _():
        key_sum[...] = jnp.zeros_like(key_sum)
        value_sum[...] = jnp.zeros_like(value_sum)
        key_t[...] = jnp.transpose(kv[:, SLOT : 2 * SLOT])

    rows = pl.ds(pl.multiple_of(i * TOK, TOK), TOK)
    q_h, k_h, v_h = q[:, :SLOT], kv[:, SLOT : 2 * SLOT], kv[:, 2 * SLOT :]
    g_both = g[...]
    g_h = jnp.concatenate(
        [g_both[:, HEAD * head : HEAD * (head + 1)], jnp.zeros((TOK, SLOT - HEAD), bf16)], axis=1
    )
    p = jnp.exp2(dot_nt(k_h, q_h) * (scale * log2e) - total[...])
    p = jnp.where(seg_k[...] == seg_q[...], p, 0.0)
    dp = dot_nt(v_h, g_h)
    ds = (p * (dp - jnp.sum(p * dp, axis=0, keepdims=True))).astype(bf16)
    value_sum[...] += dot_nn(p.astype(bf16), g_h)
    key_sum[...] += dot_nn(ds, q_h)
    grad[rows, :SLOT] = (jnp.transpose(dot_nn(key_t[...], ds)) * scale).astype(bf16)

    @pl.when(i == pl.num_programs(0) - 1)
    def _():
        grad[:, SLOT : 2 * SLOT] = (key_sum[...] * scale).astype(bf16)
        grad[:, 2 * SLOT :] = value_sum[...].astype(bf16)


def self_backward(head, seg_k, seg_q, total, qkv, g):
    return pl.pallas_call(
        functools.partial(self_backward_body, head),
        grid=(ROW // TOK,),
        in_specs=[
            pl.BlockSpec((ROW, 1), lambda i: (0, 0)),
            pl.BlockSpec((1, TOK), lambda i: (0, i)),
            pl.BlockSpec((1, TOK), lambda i: (0, i)),
            pl.BlockSpec((TOK, 3 * SLOT), lambda i: (i, head)),
            pl.BlockSpec((ROW, 3 * SLOT), lambda i: (0, head)),
            pl.BlockSpec((TOK, SHARD), lambda i: (i, 0)),
        ],
        out_specs=pl.BlockSpec((ROW, 3 * SLOT), lambda i: (0, 0)),
        out_shape=jax.ShapeDtypeStruct((ROW, 3 * SLOT), bf16),
        scratch_shapes=[
            pltpu.VMEM((ROW, SLOT), f32),
            pltpu.VMEM((ROW, SLOT), f32),
            pltpu.VMEM((SLOT, ROW), bf16),
        ],
        compiler_params=params(),
    )(seg_k, seg_q, total, qkv, qkv, g)


def cross_forward_body(cap_q, cap_t, q, k, v, out):
    allowed = cap_q[...] == cap_t[...]
    mixed = []
    for h in range(HEADS):
        a, b = HEAD * h, HEAD * (h + 1)
        s = dot_nt(q[:, a:b], k[:, a:b])
        s = jnp.where(allowed, s, masked_score)
        top = jnp.max(s, axis=1, keepdims=True)
        p = jnp.exp2((s - top) * (scale * log2e))
        mass = jnp.sum(p, axis=1, keepdims=True)
        mixed.append(dot_nn(p.astype(bf16), v[:, a:b]) / mass)
    out[...] = jnp.concatenate(mixed, axis=1).astype(bf16)


def cross_forward(cap_q, cap_t, q, k, v):
    return pl.pallas_call(
        cross_forward_body,
        out_shape=jax.ShapeDtypeStruct((TOK, D), bf16),
        compiler_params=params(),
    )(cap_q, cap_t, q, k, v)


def cross_backward_body(cap_t, cap_q, q, k, v, g, grad_q, grad_k, grad_v):
    allowed = cap_t[...] == cap_q[...]
    dq, dk, dv = [], [], []
    for h in range(HEADS):
        a, b = HEAD * h, HEAD * (h + 1)
        q_h, k_h, v_h, g_h = q[:, a:b], k[:, a:b], v[:, a:b], g[:, a:b]
        s = jnp.where(allowed, dot_nt(k_h, q_h), masked_score)
        top = jnp.max(s, axis=0, keepdims=True)
        p = jnp.exp2((s - top) * (scale * log2e))
        p = p / jnp.sum(p, axis=0, keepdims=True)
        dp = dot_nt(v_h, g_h)
        ds = (p * (dp - jnp.sum(p * dp, axis=0, keepdims=True))).astype(bf16)
        dv.append(dot_nn(p.astype(bf16), g_h))
        dk.append(dot_nn(ds, q_h) * scale)
        dq.append(dot_tn(ds, k_h) * scale)
    grad_q[...] = jnp.concatenate(dq, axis=1).astype(bf16)
    grad_k[...] = jnp.concatenate(dk, axis=1).astype(bf16)
    grad_v[...] = jnp.concatenate(dv, axis=1).astype(bf16)


def cross_backward(cap_t, cap_q, q, k, v, g):
    return pl.pallas_call(
        cross_backward_body,
        out_shape=[
            jax.ShapeDtypeStruct((TOK, D), bf16),
            jax.ShapeDtypeStruct((TXT, D), bf16),
            jax.ShapeDtypeStruct((TXT, D), bf16),
        ],
        compiler_params=params(),
    )(cap_t, cap_q, q, k, v, g)


def mlp_body(count, first, *refs):
    x, g = refs[:2]
    blocks = refs[2 : 2 + count]
    refs = refs[2 + count :]
    if not first:
        out_before, grad_before = refs[:2]
        refs = refs[2:]
    out, act_out, pre_out, grad_x, up_buf, down_buf, sem = refs

    def fetch(k):
        slot = k % 2
        return (
            pltpu.make_async_copy(blocks[k].at[:D], up_buf.at[slot], sem.at[0, slot]),
            pltpu.make_async_copy(
                blocks[k].at[D : D + BLK], down_buf.at[slot, :, :BLK], sem.at[1, slot]
            ),
            pltpu.make_async_copy(
                blocks[k].at[D + BLK :, : D - BLK], down_buf.at[slot, :, BLK:], sem.at[2, slot]
            ),
        )

    for one in fetch(0):
        one.start()
    out[...] = jnp.zeros_like(out) if first else out_before[...]
    grad_x[...] = jnp.zeros_like(grad_x) if first else grad_before[...]

    def step(h, carry):
        for k in range(count):

            @pl.when(h == k)
            def _(k=k):
                if k < count - 1:
                    for one in fetch(k + 1):
                        one.start()
                for one in fetch(k):
                    one.wait()

        slot = lax.rem(h, 2)
        up, down = up_buf[slot], down_buf[slot]
        cols = pl.ds(pl.multiple_of(h * BLK, BLK), BLK)
        pre = dot_nn(x[...], up)
        grad_act = dot_nt(g[...], down)
        cdf = 0.5 * (1.0 + lax.erf(pre * (0.5**0.5)))
        density = jnp.exp2(pre * pre * (-0.5 * log2e)) * 0.3989422804014327
        act = (pre * cdf).astype(bf16)
        grad_pre = (grad_act * (cdf + pre * density)).astype(bf16)
        act_out[:, cols] = act
        pre_out[:, cols] = grad_pre
        out[...] += dot_nn(act, down)
        grad_x[...] += dot_nt(grad_pre, up)
        return carry

    lax.fori_loop(0, count, step, 0)


def mlp(x, g, blocks, before=()):
    vmem = pl.BlockSpec(memory_space=pltpu.VMEM)
    hbm = pl.BlockSpec(memory_space=pl.ANY)
    count = len(blocks)
    return pl.pallas_call(
        functools.partial(mlp_body, count, not before),
        in_specs=[vmem] * 2 + [hbm] * count + [vmem] * len(before),
        out_specs=[vmem] * 4,
        out_shape=[
            jax.ShapeDtypeStruct((TOK, D), f32),
            jax.ShapeDtypeStruct((TOK, count * BLK), bf16),
            jax.ShapeDtypeStruct((TOK, count * BLK), bf16),
            jax.ShapeDtypeStruct((TOK, D), f32),
        ],
        scratch_shapes=[
            pltpu.VMEM((2, D, BLK), bf16),
            pltpu.VMEM((2, BLK, D), bf16),
            pltpu.SemaphoreType.DMA((3, 2)),
        ],
        compiler_params=params(),
    )(x, g, *blocks, *before)


def mlp_grads_body(x0, x1, g0, g1, pre0, pre1, act0, act1, out):
    up = dot_tn(x0[...], pre0[...]) + dot_tn(x1[...], pre1[...])
    down = dot_tn(act0[...], g0[...]) + dot_tn(act1[...], g1[...])
    out[0, :D] = up.astype(bf16)
    out[0, D : D + BLK] = down[:, :BLK].astype(bf16)
    out[0, D + BLK :, : D - BLK] = down[:, BLK:].astype(bf16)
    out[0, D + BLK :, D - BLK :] = jnp.zeros((BLK, 2 * BLK - D), bf16)


def mlp_grads(x0, x1, g0, g1, pre0, pre1, act0, act1):
    whole = pl.BlockSpec((TOK, D), lambda k: (0, 0))
    block = pl.BlockSpec((TOK, BLK), lambda k: (0, k))
    return pl.pallas_call(
        mlp_grads_body,
        grid=(4,),
        in_specs=[whole] * 4 + [block] * 4,
        out_specs=pl.BlockSpec((1, PACK, BLK), lambda k: (k, 0, 0)),
        out_shape=jax.ShapeDtypeStruct((4, PACK, BLK), bf16),
        compiler_params=params(),
    )(x0, x1, g0, g1, pre0, pre1, act0, act1)


def sort_hidden_body(x, up, down):
    for f in range(8):
        lanes = slice(HIDP * f, HIDP * f + HID)
        up[:, 8 * HID * f : 8 * HID * (f + 1)] = jnp.concatenate(
            [x[h, :SHARD, lanes] for h in range(8)], axis=1
        ).astype(f32)
    for h in range(8):
        rows = slice(HID * h, HID * (h + 1))
        down[rows, :BLK] = x[h, SHARD : SHARD + HID].astype(f32)
        down[rows, BLK:] = x[h, SHARD + HIDP : SHARD + HIDP + HID, : D - BLK].astype(f32)


def sort_hidden(x):
    return pl.pallas_call(
        sort_hidden_body,
        out_shape=[
            jax.ShapeDtypeStruct((SHARD, FF), f32),
            jax.ShapeDtypeStruct((8 * HID, D), f32),
        ],
        compiler_params=params(),
    )(x)


def norm_layer(values, norm_gain, norm_shift):
    center = values - jnp.mean(values, axis=-1, keepdims=True)
    spread = jnp.mean(center * center, axis=-1, keepdims=True)
    return center * lax.rsqrt(spread + norm_eps) * norm_gain + norm_shift


def row_block(x, index, rows):
    return lax.dynamic_slice_in_dim(x, index * rows, rows, axis=0)


def core_window(x, core):
    return lax.dynamic_slice_in_dim(x, core * STEP, WIN, axis=1)


def both_cores(x):
    return jnp.concatenate([x, shift(x, "c", 1)], axis=0)


def window_grad(left, right):
    core = lax.axis_index("c")
    sent = shift(core_window(right, 1 - core), "c", 1)
    rights = jnp.concatenate([core_window(right, core), sent], axis=0)
    return dot_tn(both_cores(left), rights).astype(bf16)


def sum_over_dp(x):
    part = lax.psum_scatter(x, "z", scatter_dimension=0, tiled=True)
    part = part + shift(part, "xh", 1)
    return lax.all_gather(part, "z", axis=0, tiled=True)


def whole_columns(mine, count):
    other = shift(mine, "c", 1)
    first = lax.axis_index("c") == 0
    low = jnp.where(first, mine, other).astype(f32)
    high = jnp.where(first, other, mine).astype(f32)
    return [
        jnp.concatenate(
            [low[SHARD * k : SHARD * (k + 1)], high[SHARD * k : SHARD * (k + 1), 128:]], axis=1
        )
        for k in range(count)
    ]


def sum_rows_over_dp(x):
    core = lax.axis_index("c")
    rows = x.shape[0] // 2
    mine = row_block(x, core, rows) + shift(row_block(x, 1 - core, rows), "c", 1)
    mine = sum_over_dp(mine)
    other = shift(mine, "c", 1)
    first = core == 0
    low = jnp.where(first, mine, other)
    high = jnp.where(first, other, mine)
    return jnp.concatenate([low, high], axis=0).astype(f32)


def sum_everywhere(x):
    for axis in ("y", "xl", "z", "xh", "c"):
        n = lax.axis_size(axis)
        x = sum([shift(x, axis, k) for k in range(1, n)], x)
    return x


def local(
    tokens,
    text_states,
    seg_lengths,
    caption_of_segment,
    text_lengths,
    ln1_gain,
    ln1_bias,
    w_query,
    w_key,
    w_value,
    w_out,
    ln2_gain,
    ln2_bias,
    c_query,
    w_text,
    c_key,
    c_value,
    c_out,
    ln3_gain,
    ln3_bias,
    w_up,
    w_down,
    cotangent,
):
    core = lax.axis_index("c")
    first_core = core == 0
    eighth = lax.axis_index("z") * 2 + core
    first_row = peer(0, 0) * TOK

    ends = jnp.cumsum(seg_lengths[0])
    positions = jnp.arange(ROW, dtype=jnp.int32)
    segment = jnp.sum((positions[:, None] >= ends[None, :]).astype(jnp.int32), axis=1)
    own_segment = lax.dynamic_slice_in_dim(segment, first_row, TOK)
    text_row = jnp.arange(TXT, dtype=jnp.int32)
    text_pos = text_row // TXT_OWN * CAP_TOK + text_row % TXT_OWN
    text_caption = text_pos // CAP_LEN
    live = jnp.sum(
        jnp.where(
            text_caption[:, None] == jnp.arange(CAPS, dtype=jnp.int32)[None, :],
            text_lengths[0][None, :],
            0,
        ),
        axis=1,
    )
    query_caption = jnp.sum(
        jnp.where(
            own_segment[:, None] == jnp.arange(SEGS, dtype=jnp.int32)[None, :],
            caption_of_segment[0][None, :],
            0,
        ),
        axis=1,
    )
    text_live = (text_row % TXT_OWN < CAP_TOK) & (text_pos % CAP_LEN < live)
    text_key = jnp.where(text_live, text_caption, -1)

    rows_in = tokens[0].astype(f32)
    normed_one, pull_one = jax.vjp(norm_layer, rows_in, ln1_gain, ln1_bias)
    normed_one = normed_one.astype(bf16)
    normed_all = place(gather3(normed_one), [(0, TOK, 0)])

    gap = jnp.zeros((SHARD, HIDP - HID), bf16)
    up_shard = after(w_up, normed_one)
    up_own = jnp.concatenate(
        [
            part
            for k in range(8)
            for part in (
                lax.dynamic_slice(up_shard, (0, 8 * HID * k + HID * eighth), (SHARD, HID)),
                gap,
            )
        ],
        axis=1,
    )
    down_own = row_block(w_down, eighth, HID)
    down_own = jnp.pad(down_own, ((0, HIDP - HID), (0, 2 * BLK - D)))
    hidden_own = jnp.concatenate([up_own, down_own[:, :BLK], down_own[:, BLK:]], axis=0)
    hidden = place(
        gather3(hidden_own),
        [(0, SHARD, 0), (SHARD, HIDP, D), (SHARD + HIDP, HIDP, D + BLK)],
    )

    text_own = jnp.pad(after(text_states[0], normed_one), ((0, TXT_OWN - CAP_TOK), (0, 0)))
    text_columns = lax.all_to_all(text_own, FS, split_axis=1, concat_axis=0, tiled=True)
    context_own = lax.psum_scatter(
        dot_nn(text_columns, w_text).astype(bf16), FS, scatter_dimension=0, tiled=True
    )
    context = lax.all_gather(context_own, FS, axis=0, tiled=True)

    packed = jnp.concatenate(
        [
            jnp.concatenate([w[:, SHARD * k : SHARD * (k + 1)] for k in range(8)], axis=0)
            for w in (w_query, w_key, w_value)
        ],
        axis=1,
    )
    heads_w = lax.all_to_all(after(packed, text_columns), FS, 0, 0, tiled=True)
    blank = jnp.zeros((D, SLOT - HEAD), bf16)
    heads_w = jnp.concatenate(
        [
            part
            for h in range(2)
            for k in range(3)
            for part in (heads_w[:, SHARD * k + HEAD * h : SHARD * k + HEAD * (h + 1)], blank)
        ],
        axis=1,
    )

    seg_col, seg_row = segment[:, None], segment[None, :]
    qkv = dot_nn(normed_all, heads_w).astype(bf16)
    head0, total0 = self_forward(0, seg_col, seg_row, qkv)
    head1, total1 = self_forward(1, seg_col, seg_row, after(qkv, head0))
    attended = lax.all_to_all(
        jnp.concatenate([head0, head1], axis=1), FS, split_axis=0, concat_axis=1, tiled=True
    )

    pack = after(jnp.where(first_core, w_out, c_query), normed_all)
    square_mine = place(gather3(pack, (qkv,), (head0,)), [(0, SHARD, 0)])
    full_out, full_cquery = sort_cores(
        square_mine, shift(square_mine, "c", 1), [(0, 0, D, 0, 0), (1, 0, D, 1, 0)], 2
    )
    pack = jnp.where(
        first_core,
        jnp.concatenate([c_key, c_out[:, :WIN]], axis=1),
        jnp.concatenate([c_value, c_out[:, STEP:]], axis=1),
    )
    square_mine = place(
        gather3(after(pack, qkv), (head0,), (head1,)), [(0, SHARD, 0)]
    )
    full_ckey, full_cvalue, full_cout = sort_cores(
        square_mine,
        shift(square_mine, "c", 1),
        [(0, 0, D, 0, 0), (1, 0, D, 1, 0), (0, D, WIN, 2, 0), (1, D + 128, STEP, 2, WIN)],
        3,
    )

    after_self = rows_in + dot_nn(attended, full_out)

    normed_two, pull_two = jax.vjp(norm_layer, after_self, ln2_gain, ln2_bias)
    normed_two = normed_two.astype(bf16)
    cross_query = dot_nn(normed_two, full_cquery).astype(bf16)
    context = after(context, after_self)
    cross_key = dot_nn(context, full_ckey).astype(bf16)
    cross_value = dot_nn(context, full_cvalue).astype(bf16)
    cross_mixed = cross_forward(
        query_caption[:, None], text_key[None, :], cross_query, cross_key, cross_value
    )
    after_cross = after_self + dot_nn(cross_mixed, full_cout)

    minus, plus = shift(hidden, "z", 1), shift(hidden, "z", -1)
    half = PACK // 2
    far = jnp.concatenate(
        [
            shift(after(minus[:half], cross_query), "z", 1),
            shift(after(plus[half:], cross_query), "z", -1),
        ],
        axis=0,
    )
    near = [hidden, minus, plus]
    near += [shift(w, "c", 1) for w in near]
    far = [far, shift(far, "c", 1)]

    normed_three, pull_three = jax.vjp(norm_layer, after_cross, ln3_gain, ln3_bias)
    normed_three = normed_three.astype(bf16)
    grad_out = cotangent[0]
    grad_mlp = grad_out.astype(bf16)
    part_out, act_near, pre_near, part_grad = mlp(normed_three, grad_mlp, near)
    mlp_out, act_far, pre_far, grad_three = mlp(
        normed_three, grad_mlp, far, (part_out, part_grad)
    )
    outputs = after_cross + mlp_out
    grad_cross_in, grad_ln3_gain, grad_ln3_bias = pull_three(grad_three)
    grad_after_cross = grad_out + grad_cross_in
    grad_cross_branch = grad_after_cross.astype(bf16)
    grad_cross_mixed = dot_nt(grad_cross_branch, full_cout).astype(bf16)

    def mine(near, far):
        return jnp.concatenate([near[:, : 3 * BLK], far[:, :BLK]], axis=1)

    def theirs(near, far):
        return shift(jnp.concatenate([near[:, 3 * BLK :], far[:, BLK:]], axis=1), "c", 1)

    hidden_grads = mlp_grads(
        normed_three,
        shift(normed_three, "c", 1),
        grad_mlp,
        shift(grad_mlp, "c", 1),
        mine(pre_near, pre_far),
        theirs(pre_near, pre_far),
        mine(act_near, act_far),
        theirs(act_near, act_far),
    )

    grad_cquery_rows, grad_key_part, grad_value_part = cross_backward(
        text_key[:, None],
        query_caption[None, :],
        cross_query,
        cross_key,
        cross_value,
        after(grad_cross_mixed, hidden_grads),
    )
    grad_self_in, grad_ln2_gain, grad_ln2_bias = pull_two(dot_nt(grad_cquery_rows, full_cquery))
    grad_after_self = grad_after_cross + grad_self_in
    grad_self_branch = grad_after_self.astype(bf16)
    grad_attended = dot_nt(grad_self_branch, full_out).astype(bf16)
    grad_heads = lax.all_to_all(grad_attended, FS, split_axis=1, concat_axis=0, tiled=True)

    grad_head0 = self_backward(0, seg_col, seg_row, total0, qkv, grad_heads)
    grad_head1 = self_backward(1, seg_col, seg_row, total1, qkv, after(grad_heads, grad_head0))
    grad_qkv = jnp.concatenate([grad_head0, grad_head1], axis=1)
    normed_part = dot_nt(grad_qkv, heads_w).astype(bf16)
    grad_heads_w = dot_tn(normed_all, grad_qkv).astype(bf16)
    grad_heads_w = jnp.concatenate(
        [
            grad_heads_w[:, SLOT * (3 * h + k) : SLOT * (3 * h + k) + HEAD]
            for k in range(3)
            for h in range(2)
        ],
        axis=1,
    )

    far_minus = shift(hidden_grads[3, :half], "z", -1)
    far_plus = shift(hidden_grads[3, half:], "z", 1)
    far_minus, far_plus, _ = lax.optimization_barrier((far_minus, far_plus, grad_heads))
    minus = jnp.concatenate(
        [hidden_grads[1, :half] + far_minus, hidden_grads[1, half:]], axis=0
    )
    plus = jnp.concatenate([hidden_grads[2, :half], hidden_grads[2, half:] + far_plus], axis=0)
    minus, plus = shift(minus, "z", -1), shift(plus, "z", 1)
    minus, plus, _ = lax.optimization_barrier((minus, plus, grad_head1))
    hidden_sum = (
        hidden_grads[0].astype(f32) + minus.astype(f32) + plus.astype(f32)
    ).astype(bf16)

    def hidden_chunk(dy, dx):
        p = peer(dy, dx)
        return jnp.concatenate(
            [
                row_block(hidden_sum[:D], p, SHARD),
                row_block(hidden_sum[D : D + BLK], p, HIDP),
                row_block(hidden_sum[D + BLK :], p, HIDP),
            ],
            axis=0,
        )

    hidden_grad = reduce3(hidden_chunk).astype(bf16)
    hidden_grad = hidden_grad + shift(hidden_grad, "xh", 1)
    hidden_grad = lax.all_gather(hidden_grad, ("z", "c"), axis=0)
    grad_w_up, grad_w_down = sort_hidden(hidden_grad)

    square = jnp.concatenate(
        [
            window_grad(cross_mixed, grad_cross_branch),
            window_grad(normed_two, grad_cquery_rows),
            window_grad(attended, grad_self_branch),
            window_grad(context, grad_key_part),
            window_grad(context, grad_value_part),
        ],
        axis=1,
    )
    square = after(square, grad_heads)
    square = reduce3(
        lambda dy, dx: row_block(square, peer(dy, dx), SHARD), (grad_head0,), (grad_head1,)
    ).astype(bf16)
    square = jnp.concatenate(
        [square[:, WIN * k : WIN * (k + 1)] for k in range(5)]
        + [jnp.zeros((768 - 5 * SHARD, WIN), bf16)],
        axis=0,
    )
    square = sum_over_dp(square)
    grad_c_out, grad_c_query, grad_w_out, grad_c_key, grad_c_value = whole_columns(square, 5)

    context_part = dot_nt(grad_key_part, full_ckey) + dot_nt(grad_value_part, full_cvalue)
    context_grad = lax.psum_scatter(
        context_part.astype(bf16), FS, scatter_dimension=0, tiled=True
    )
    context_grad = lax.all_gather(context_grad, FS, axis=0, tiled=True)
    context_grad = after(context_grad, grad_head1)
    grad_w_text = sum_rows_over_dp(dot_tn(text_columns, context_grad).astype(bf16))
    text_part = dot_nt(context_grad, w_text).astype(bf16)
    grad_text = lax.all_to_all(text_part, FS, split_axis=0, concat_axis=1, tiled=True)
    grad_text = grad_text[:CAP_TOK].astype(f32)

    grad_normed_one = reduce3(lambda dy, dx: row_block(normed_part, peer(dy, dx), TOK))
    grad_rows_in, grad_ln1_gain, grad_ln1_bias = pull_one(grad_normed_one)
    grad_tokens = grad_after_self + grad_rows_in
    grad_qkv_w = lax.all_to_all(grad_heads_w, FS, 0, 0, tiled=True)
    grad_qkv_w = jnp.concatenate(
        [
            jnp.concatenate(
                [
                    grad_qkv_w[SHARD * p : SHARD * (p + 1), SHARD * k : SHARD * (k + 1)]
                    for p in range(8)
                ],
                axis=1,
            )
            for k in range(3)
        ]
        + [jnp.zeros((512 - 3 * SHARD, D), bf16)],
        axis=0,
    )
    grad_qkv_w = sum_rows_over_dp(grad_qkv_w)
    grad_w_query, grad_w_key, grad_w_value = (
        grad_qkv_w[SHARD * k : SHARD * (k + 1)] for k in range(3)
    )
    norms = sum_everywhere(
        jnp.stack(
            [
                grad_ln1_gain,
                grad_ln1_bias,
                grad_ln2_gain,
                grad_ln2_bias,
                grad_ln3_gain,
                grad_ln3_bias,
            ]
        )
    )
    return (
        outputs[None],
        grad_tokens[None],
        grad_text[None],
        norms[0],
        norms[1],
        grad_w_query,
        grad_w_key,
        grad_w_value,
        grad_w_out,
        norms[2],
        norms[3],
        grad_c_query,
        grad_w_text,
        grad_c_key,
        grad_c_value,
        grad_c_out,
        norms[4],
        norms[5],
        grad_w_up,
        grad_w_down,
    )


def solution(mesh):
    split = Mesh(mesh.devices.reshape(2, 4, 2, 4, 2), ("xh", "z", "c", "y", "xl"))
    dp = ("xh", "z", "c")
    rows = P(dp, FS, None)
    per_row = P(dp, None)
    weight = P(FS, None)
    rep = P()
    in_specs = (
        rows, rows, per_row, per_row, per_row,
        rep, rep, weight, weight, weight, weight,
        rep, rep, weight, weight, weight, weight, weight,
        rep, rep, weight, weight, rows,
    )
    out_specs = (
        rows, rows, rows,
        rep, rep, weight, weight, weight, weight,
        rep, rep, weight, weight, weight, weight, weight,
        rep, rep, weight, weight,
    )
    return jax.shard_map(
        local, mesh=split, in_specs=in_specs, out_specs=out_specs, check_vma=False
    )
```

time: 982 us -> 901 us (0.918)
  waiting for transfers between devices: 392 us -> 258 us
  blocking collectives: 0 us -> 35.4 us
  Pallas kernels: 139 us -> 164 us
  starting transfers between devices: 188 us -> 168 us
  other arithmetic: 67.3 us -> 80.7 us
    psum x4 -> x0, waiting for transfers between devices: 166 us -> none  [the longest x1 67.5 us: local(): square = lax.psum(square, ('xh', 'z'))]
    all_gather x0 -> x3, blocking collectives: none -> 35.4 us  [sum_over_dp(): return lax.all_gather(part, 'z', axis=0, tiled=True)]
    ppermute x105 -> x101, waiting for transfers between devices: 207 us -> 236 us  [shift(): return lax.ppermute(x, axis, [(i, (i + by) % n) for i in range(n)])]
    ppermute x105 -> x101, starting transfers between devices: 164 us -> 144 us  [shift(): return lax.ppermute(x, axis, [(i, (i + by) % n) for i in range(n)])]
    all_gather x1, waiting for transfers between devices: 19 us -> 0.01 us  [local(): hidden_grad = lax.all_gather(hidden_grad, ('z', 'c'), axis=0)]
    all_gather x0 -> x2, waiting for transfers between devices: none -> 18.1 us  [the longest x1 18.1 us: local(): context = lax.all_gather(context_own, FS, axis=0, tiled=True)]
    pallas_call x1 -> x3, Pallas kernels: 22.6 us -> 39.5 us  [the longest x2 27.2 us: mlp(): pl.pallas_call(functools.partial(mlp_body, count, not before), in_specs=[...]
    unnamed x194 -> x228, local copies, waits for them, and re-layouts: 29.6 us -> 19.6 us
  transfers between devices with their start and end apart: 116 -> 115, of which waited for: 36 -> 36; matrix products, arithmetic and copies ran while one was open for 22% -> 26% of each run, Pallas kernels for 14% -> 18%
where the time goes in v2:
time: 901 us; the launch traced here: 890 us
  waiting for transfers between devices  258 us (29%)
  starting transfers between devices  168 us (19%)
  Pallas kernels  164 us (18%)
  local copies, waits for them, and re-layouts  86.2 us (10%)
  matrix products  81 us (9%)
  other arithmetic  80.7 us (9%)
  blocking collectives  35.4 us (4%)
  between operations  16.4 us (2%)
    ppermute x101, waiting for transfers between devices, shift(): return lax.ppermute(x, axis, [(i, (i + by) % n) for i in range(n)])  236 us
    ppermute x101, starting transfers between devices, shift(): return lax.ppermute(x, axis, [(i, (i + by) % n) for i in range(n)])  144 us
    pallas_call x2, Pallas kernels, self_backward(): pl.pallas_call(functools.partial(self_backward_body, head), grid=(ROW //...  37.3 us
    all_gather x3, blocking collectives, sum_over_dp(): return lax.all_gather(part, 'z', axis=0, tiled=True)  35.4 us
    dot_general x7, matrix products, dot_tn(): lax.dot_general(a, b, (((0,), (0,)), ((), ())), preferred_element_type=f32)  30 us
    dot_general x7, matrix products, dot_nn(): lax.dot_general(a, b, (((1,), (0,)), ((), ())), preferred_element_type=f32)  28.5 us
    pallas_call x2, Pallas kernels, mlp(): pl.pallas_call(functools.partial(mlp_body, count, not before), in_specs=[...  27.2 us
    pallas_call x2, Pallas kernels, self_forward(): pl.pallas_call(self_forward_body, grid=(ROW // TOK,), in_specs=[pl.BlockS...  24.3 us
  transfers between devices with their start and end apart: 115, of which 36 were waited for; matrix products, arithmetic and copies ran while one was open for 26% of the time, Pallas kernels for 18%

profile of v2, /device:TPU:1, one launch (start us, length us, event | category | flops | bytes accessed | tf_op | source)
XLA Modules:
  0.0 889.8 jit_solution(6836408388068457710)
XLA Ops:
  27.8 9.7 %collective-permute-done.1.refs_2_ = bf16[256,1152]{1,0:T(8,128)(2,1)} collective-permute-done((bf16[256,1152]{1,0:T(8,128)(2,1)S(1)}, bf16[256,1152]{1,0:T(8,128)(2,1)}, u32[]{:S(2)}, u32[]{:S(2)}) %collective-permute-start.1) | collective-permute-done | bytes 589856 | tf_op jit(solution)/shard_map/ppermute | solution.py:61
  52.3 13.9 %collective-permute-done.5.refs_6_ = bf16[256,1152]{1,0:T(8,128)(2,1)S(1)} collective-permute-done((bf16[256,1152]{1,0:T(8,128)(2,1)}, bf16[256,1152]{1,0:T(8,128)(2,1)S(1)}, u32[]{:S(2)}, u32[]{:S(2)}) %collective-permute-start.5) | collective-permute-done | bytes 589856 | tf_op jit(solution)/shard_map/ppermute | solution.py:61
  73.5 14.3 %collective-permute-done.29.refs_4_ = bf16[304,640]{1,0:T(8,128)(2,1)S(1)} collective-permute-done((bf16[304,640]{1,0:T(8,128)(2,1)}, bf16[304,640]{1,0:T(8,128)(2,1)S(1)}, u32[]{:S(2)}, u32[]{:S(2)}) %collective-permute-start.29) | collective-permute-done | bytes 389152 | tf_op jit(solution)/shard_map/ppermute | solution.py:61
  132.4 12.1 %shard_map.375 = (bf16[2048,72]{1,0:T(8,128)(2,1)}, f32[1,2048]{1,0:T(1,128)}) custom-call(s32[2048,1]{1,0:T(8,128)} %copy.182.seg_q.seg_k, s32[1,2048]{1,0:T(1,128)} %bitcast.152, bf16[2048,768]{1,0:T(8,128)(2,1)} %convolution_convert_fusion.1.q.kv, bf16[2048,768]{1,0:T(8,128)(2,1)} %convolution_convert_fusion.1.q.kv), custom_call_target="tpu_custom_call" | custom-call | tf_op jit(solution)/shard_map/pallas_call | solution.py:199
  155.7 9.1 %collective-permute-start.16 = (bf16[1152,1152]{1,0:T(8,128)(2,1)}, bf16[1152,1152]{1,0:T(8,128)(2,1)}, u32[]{:S(2)}, u32[]{:S(2)}) collective-permute-start(bf16[1152,1152]{1,0:T(8,128)(2,1)} %shard_map.377.m), channel_id=1, source_target_pairs={{0,8},{8,0},{1,9},{9,1},{2,10},{10,2},{3,11},{11,3},{4,12},{12,4},... | collective-permute-start | bytes 7962632 | tf_op jit(solution)/shard_map/ppermute | solution.py:61
  170.6 11.9 %collective-permute-done.18.refs_2_ = bf16[144,1792]{1,0:T(8,128)(2,1)} collective-permute-done((bf16[144,1792]{1,0:T(8,128)(2,1)S(1)}, bf16[144,1792]{1,0:T(8,128)(2,1)}, u32[]{:S(2)}, u32[]{:S(2)}) %collective-permute-start.18) | collective-permute-done | bytes 516128 | tf_op jit(solution)/shard_map/ppermute | solution.py:61
  188.8 12.1 %shard_map.376 = (bf16[2048,72]{1,0:T(8,128)(2,1)}, f32[1,2048]{1,0:T(1,128)}) custom-call(s32[2048,1]{1,0:T(8,128)} %copy.182.seg_q.seg_k, s32[1,2048]{1,0:T(1,128)} %bitcast.153, bf16[2048,768]{1,0:T(8,128)(2,1)} %convolution_convert_fusion.1.q.kv, bf16[2048,768]{1,0:T(8,128)(2,1)} %convolution_convert_fusion.1.q.kv), custom_call_target="tpu_custom_call" | custom-call | tf_op jit(solution)/shard_map/pallas_call | solution.py:199
  262.8 18.1 %all-gather.5.cloned.1.call-done = bf16[512,1152]{1,0:T(8,128)(2,1)} async-done(((bf16[64,1152]{1,0:T(8,128)(2,1)}), bf16[512,1152]{1,0:T(8,128)(2,1)}) %all-gather.5.cloned.1.call-update) | async-done | bytes 1179664 | tf_op jit(solution)/shard_map/all_gather | solution.py:599
  300.6 24.2 %collective-permute-done.37 = bf16[1216,640]{1,0:T(8,128)(2,1)S(1)} collective-permute-done((bf16[1216,640]{1,0:T(8,128)(2,1)S(1)}, bf16[1216,640]{1,0:T(8,128)(2,1)S(1)}, u32[]{:S(2)}, u32[]{:S(2)}) %collective-permute-start.37) | collective-permute-done | bytes 1556512 | tf_op jit(solution)/shard_map/ppermute | solution.py:61
  341.6 11.7 %shard_map.381 = bf16[256,1152]{1,0:T(8,128)(2,1)} custom-call(s32[256,1]{1,0:T(8,128)} %copy.185.cap_q, s32[1,512]{1,0:T(1,128)} %and_select_fusion.1.cap_t, bf16[256,1152]{1,0:T(8,128)(2,1)} %convolution_convert_fusion.14.q, bf16[512,1152]{1,0:T(8,128)(2,1)} %convolution_convert_fusion.10.k, bf16[512,1152]{1,0:T(8,128)(2,1)} %convolution_convert_fusion.9.v), custom_call_target="tpu_custom_call" | custom-call | tf_op jit(solution)/shard_map/pallas_call | solution.py:287
  358.5 17.9 %shard_map.383 = (f32[256,1152]{1,0:T(8,128)}, bf16[256,3840]{1,0:T(8,128)(2,1)}, bf16[256,3840]{1,0:T(8,128)(2,1)}, f32[256,1152]{1,0:T(8,128)}) custom-call(bf16[256,1152]{1,0:T(8,128)(2,1)} %add_convert_fusion.1.refs_0_.x0, bf16[256,1152]{1,0:T(8,128)(2,1)} %bitcast_convert_fusion.refs_1_.g0, bf16[2432,640]{1,0:T(8,128)(2,1)} %shard_map.382.refs_2_, ...), custom_call_target="tpu_custom_call" | custom-call | tf_op jit(solution)/shard_map/pallas_call | solution.py:385
  380.8 9.3 %shard_map.384 = (f32[256,1152]{1,0:T(8,128)}, bf16[256,1280]{1,0:T(8,128)(2,1)}, bf16[256,1280]{1,0:T(8,128)(2,1)}, f32[256,1152]{1,0:T(8,128)}) custom-call(bf16[256,1152]{1,0:T(8,128)(2,1)} %add_convert_fusion.1.refs_0_.x0, bf16[256,1152]{1,0:T(8,128)(2,1)} %bitcast_convert_fusion.refs_1_.g0, ...), custom_call_target="tpu_custom_call" | custom-call | tf_op jit(solution)/shard_map/pallas_call | solution.py:385
  406.5 12.3 %shard_map.385 = bf16[4,2432,640]{2,1,0:T(8,128)(2,1)} custom-call(bf16[256,1152]{1,0:T(8,128)(2,1)} %add_convert_fusion.1.refs_0_.x0, bf16[256,1152]{1,0:T(8,128)(2,1)} %collective-permute-done.42.x1, bf16[256,1152]{1,0:T(8,128)(2,1)} %bitcast_convert_fusion.refs_1_.g0, bf16[256,1152]{1,0:T(8,128)(2,1)} %collective-permute-done.43.g1, ...), custom_call_target="tpu_custom_call" | custom-call | tf_op jit(solution)/shard_map/pallas_call | solution.py:416
  424.5 15.1 %shard_map.386 = (bf16[256,1152]{1,0:T(8,128)(2,1)}, bf16[512,1152]{1,0:T(8,128)(2,1)}, bf16[512,1152]{1,0:T(8,128)(2,1)}) custom-call(s32[512,1]{1,0:T(8,128)} %fusion.58.cap_t, s32[1,256]{1,0:T(1,128)} %bitcast.159, bf16[256,1152]{1,0:T(8,128)(2,1)} %convolution_convert_fusion.14.q, bf16[512,1152]{1,0:T(8,128)(2,1)} %convolution_convert_fusion.10.k, ...), custom_call_target="tpu_custom_call" | custom-call | tf_op jit(solution)/shard_map/pallas_call | solution.py:315
  480.0 18.7 %shard_map.387 = bf16[2048,384]{1,0:T(8,128)(2,1)} custom-call(s32[2048,1]{1,0:T(8,128)} %copy.182.seg_q.seg_k, s32[1,2048]{1,0:T(1,128)} %bitcast.154, f32[1,2048]{1,0:T(1,128)} %get-tuple-element.105.total, bf16[2048,768]{1,0:T(8,128)(2,1)} %convolution_convert_fusion.1.q.kv, bf16[2048,768]{1,0:T(8,128)(2,1)} %convolution_convert_fusion.1.q.kv, ...), custom_call_target="tpu_custom_call" | custom-call | tf_op jit(solution)/shard_map/pallas_call | solution.py:250
  498.7 18.6 %shard_map.388 = bf16[2048,384]{1,0:T(8,128)(2,1)} custom-call(s32[2048,1]{1,0:T(8,128)} %copy.182.seg_q.seg_k, s32[1,2048]{1,0:T(1,128)} %bitcast.155, f32[1,2048]{1,0:T(1,128)} %get-tuple-element.106.total, bf16[2048,768]{1,0:T(8,128)(2,1)} %convolution_convert_fusion.1.q.kv, bf16[2048,768]{1,0:T(8,128)(2,1)} %convolution_convert_fusion.1.q.kv, ...), custom_call_target="tpu_custom_call" | custom-call | tf_op jit(solution)/shard_map/pallas_call | solution.py:250
  572.3 10.7 %collective-permute-done.76 = bf16[80,3200]{1,0:T(8,128)(2,1)S(1)} collective-permute-done((bf16[80,3200]{1,0:T(8,128)(2,1)S(1)}, bf16[80,3200]{1,0:T(8,128)(2,1)S(1)}, u32[]{:S(2)}, u32[]{:S(2)}) %collective-permute-start.76) | collective-permute-done | bytes 512032 | tf_op jit(solution)/shard_map/ppermute | solution.py:61
  633.5 10.8 %collective-permute-done.52 = bf16[256,1152]{1,0:T(8,128)(2,1)} collective-permute-done((bf16[256,1152]{1,0:T(8,128)(2,1)}, bf16[256,1152]{1,0:T(8,128)(2,1)}, u32[]{:S(2)}, u32[]{:S(2)}) %collective-permute-start.52) | collective-permute-done | bytes 589856 | tf_op jit(solution)/shard_map/ppermute | solution.py:61
  657.8 15.7 %collective-permute-done.81 = bf16[144,3200]{1,0:T(8,128)(2,1)} collective-permute-done((bf16[144,3200]{1,0:T(8,128)(2,1)}, bf16[144,3200]{1,0:T(8,128)(2,1)}, u32[]{:S(2)}, u32[]{:S(2)}) %collective-permute-start.81) | collective-permute-done | bytes 921632 | tf_op jit(solution)/shard_map/ppermute | solution.py:61
  681.1 38.6 %collective-permute-done.91 = bf16[2432,640]{1,0:T(8,128)(2,1)} collective-permute-done((bf16[2432,640]{1,0:T(8,128)(2,1)}, bf16[2432,640]{1,0:T(8,128)(2,1)}, u32[]{:S(2)}, u32[]{:S(2)}) %collective-permute-start.91) | collective-permute-done | bytes 3112992 | tf_op jit(solution)/shard_map/ppermute | solution.py:61
  779.7 13.8 %collective-permute-start.62 = (f32[6,1152]{1,0:T(8,128)S(1)}, f32[6,1152]{1,0:T(8,128)}, u32[]{:S(2)}, u32[]{:S(2)}) collective-permute-start(f32[6,1152]{1,0:T(8,128)S(1)} %add.770), channel_id=1, source_target_pairs={{0,8},{8,0},{1,9},{9,1},{2,10},{10,2},{3,11},{11,3},{4,12},{12,4},... | collective-permute-start | bytes 82952 | tf_op jit(solution)/shard_map/ppermute | solution.py:61
  803.2 14.2 %all_gather.23 = bf16[256,1152]{1,0:T(8,128)(2,1)S(1)} all-gather(bf16[64,1152]{1,0:T(8,128)(2,1)S(1)} %add.775), channel_id=1, replica_groups=mesh['xh'=2,'z'=4,'c'=2,'y'=4,'xl'=2] {'z'}, dimensions={0}, use_global_device_ids=true | all-gather | bytes 737280 | tf_op jit(solution)/shard_map/all_gather | solution.py:477
  831.5 11.2 %all_gather.24 = bf16[768,640]{1,0:T(8,128)(2,1)S(1)} all-gather(bf16[192,640]{1,0:T(8,128)(2,1)S(1)} %copy.199), channel_id=1, replica_groups=mesh['xh'=2,'z'=4,'c'=2,'y'=4,'xl'=2] {'z'}, dimensions={0}, use_global_device_ids=true | all-gather | bytes 1228800 | tf_op jit(solution)/shard_map/all_gather | solution.py:477
  858.2 10.0 %all_gather.25 = bf16[256,1152]{1,0:T(8,128)(2,1)S(1)} all-gather(bf16[64,1152]{1,0:T(8,128)(2,1)S(1)} %add.796), channel_id=1, replica_groups=mesh['xh'=2,'z'=4,'c'=2,'y'=4,'xl'=2] {'z'}, dimensions={0}, use_global_device_ids=true | all-gather | bytes 737280 | tf_op jit(solution)/shard_map/all_gather | solution.py:477
  (652 shorter events, 519.3 us)
Async XLA Ops:
  48.9 194.2 %reduce-scatter.8.cloned.1.call-start = ((), (), s32[]{:S(2)}) async-start(), calls=%async_computation.11 | async-start | bytes 1327104 | tf_op jit(solution)/shard_map/reduce_scatter | solution.py:596
  126.4 116.8 %collective-permute-start.34 = (bf16[2432,640]{1,0:T(8,128)(2,1)}, bf16[2432,640]{1,0:T(8,128)(2,1)}, u32[]{:S(2)}, u32[]{:S(2)}) collective-permute-start(bf16[2432,640]{1,0:T(8,128)(2,1)} %shard_map.382.refs_2_), channel_id=1, source_target_pairs={{0,16},{16,32},{32,48},{48,0},{1,17},{17,33},{33,49},{49,1},{2,18}... | collective-permute-start | bytes 9338888 | tf_op jit(solution)/shard_map/ppermute | solution.py:61
  155.7 90.1 %collective-permute-start.16 = (bf16[1152,1152]{1,0:T(8,128)(2,1)}, bf16[1152,1152]{1,0:T(8,128)(2,1)}, u32[]{:S(2)}, u32[]{:S(2)}) collective-permute-start(bf16[1152,1152]{1,0:T(8,128)(2,1)} %shard_map.377.m), channel_id=1, source_target_pairs={{0,8},{8,0},{1,9},{9,1},{2,10},{10,2},{3,11},{11,3},{4,12},{12,4},... | collective-permute-start | bytes 7962632 | tf_op jit(solution)/shard_map/ppermute | solution.py:61
  200.9 85.9 %collective-permute-start.36 = (bf16[2432,640]{1,0:T(8,128)(2,1)}, bf16[2432,640]{1,0:T(8,128)(2,1)}, u32[]{:S(2)}, u32[]{:S(2)}) collective-permute-start(bf16[2432,640]{1,0:T(8,128)(2,1)} %shard_map.382.refs_2_), channel_id=1, source_target_pairs={{0,48},{16,0},{32,16},{48,32},{1,49},{17,1},{33,17},{49,33},{2,50}... | collective-permute-start | bytes 9338888 | tf_op jit(solution)/shard_map/ppermute | solution.py:61
  239.7 87.1 %collective-permute-start.25 = (bf16[1152,1792]{1,0:T(8,128)(2,1)}, bf16[1152,1792]{1,0:T(8,128)(2,1)}, u32[]{:S(2)}, u32[]{:S(2)}) collective-permute-start(bf16[1152,1792]{1,0:T(8,128)(2,1)} %shard_map.379.m), channel_id=1, source_target_pairs={{0,8},{8,0},{1,9},{9,1},{2,10},{10,2},{3,11},{11,3},{4,12},{12,4},... | collective-permute-start | bytes 12386312 | tf_op jit(solution)/shard_map/ppermute | solution.py:61
  292.7 65.0 %collective-permute-start.39 = (bf16[2432,640]{1,0:T(8,128)(2,1)}, bf16[2432,640]{1,0:T(8,128)(2,1)}, u32[]{:S(2)}, u32[]{:S(2)}) collective-permute-start(bf16[2432,640]{1,0:T(8,128)(2,1)} %shard_map.382.refs_2_), channel_id=1, source_target_pairs={{0,8},{8,0},{1,9},{9,1},{2,10},{10,2},{3,11},{11,3},{4,12},{12,4},... | collective-permute-start | bytes 9338888 | tf_op jit(solution)/shard_map/ppermute | solution.py:61
  293.1 65.1 %collective-permute-start.40 = (bf16[2432,640]{1,0:T(8,128)(2,1)}, bf16[2432,640]{1,0:T(8,128)(2,1)}, u32[]{:S(2)}, u32[]{:S(2)}) collective-permute-start(bf16[2432,640]{1,0:T(8,128)(2,1)} %collective-permute-done.34.refs_3_), channel_id=1, source_target_pairs={{0,8},{8,0},{1,9},{9,1},{2,10},{10,2},{3,11},{11,3},{4,12},{12,4},... | collective-permute-start | bytes 9338888 | tf_op jit(solution)/shard_map/ppermute | solution.py:61
  324.7 81.7 %collective-permute-start.43 = (bf16[256,1152]{1,0:T(8,128)(2,1)}, bf16[256,1152]{1,0:T(8,128)(2,1)}, u32[]{:S(2)}, u32[]{:S(2)}) collective-permute-start(bf16[256,1152]{1,0:T(8,128)(2,1)} %bitcast_convert_fusion.refs_1_.g0), channel_id=1, source_target_pairs={{0,8},{8,0},{1,9},{9,1},{2,10},{10,2},{3,11},{11,3},{4,12},{12,4},... | collective-permute-start | bytes 1769480 | tf_op jit(solution)/shard_map/ppermute | solution.py:61
  402.4 72.5 %collective-permute-start.70 = (bf16[256,1152]{0,1:T(8,128)(2,1)}, bf16[256,1152]{0,1:T(8,128)(2,1)}, u32[]{:S(2)}, u32[]{:S(2)}) collective-permute-start(bf16[256,1152]{0,1:T(8,128)(2,1)} %bitcast.20), channel_id=1, source_target_pairs={{0,8},{8,0},{1,9},{9,1},{2,10},{10,2},{3,11},{11,3},{4,12},{12,4},... | collective-permute-start | bytes 1769480 | tf_op jit(solution)/shard_map/ppermute | solution.py:61
  406.4 64.2 %collective-permute-start.68 = (bf16[256,1152]{1,0:T(8,128)(2,1)}, bf16[256,1152]{1,0:T(8,128)(2,1)}, u32[]{:S(2)}, u32[]{:S(2)}) collective-permute-start(bf16[256,1152]{1,0:T(8,128)(2,1)} %add_convert_fusion.2), channel_id=1, source_target_pairs={{0,8},{8,0},{1,9},{9,1},{2,10},{10,2},{3,11},{11,3},{4,12},{12,4},... | collective-permute-start | bytes 1769480 | tf_op jit(solution)/shard_map/ppermute | solution.py:61
  453.6 155.2 %reduce-scatter.10.cloned.1.call-start = ((), (), s32[]{:S(2)}) async-start(), calls=%async_computation.13 | async-start | bytes 1327104 | tf_op jit(solution)/shard_map/reduce_scatter | solution.py:785
  453.7 147.5 %collective-permute-start.88 = (bf16[1216,640]{1,0:T(8,128)(2,1)}, bf16[1216,640]{1,0:T(8,128)(2,1)}, u32[]{:S(2)}, u32[]{:S(2)}) collective-permute-start(bf16[1216,640]{1,0:T(8,128)(2,1)} %get-tuple-element.268), channel_id=1, source_target_pairs={{0,48},{16,0},{32,16},{48,32},{1,49},{17,1},{33,17},{49,33},{2,50}... | collective-permute-start | bytes 4669448 | tf_op jit(solution)/shard_map/ppermute | solution.py:61
  470.7 133.2 %collective-permute-start.89 = (bf16[1216,640]{1,0:T(8,128)(2,1)}, bf16[1216,640]{1,0:T(8,128)(2,1)}, u32[]{:S(2)}, u32[]{:S(2)}) collective-permute-start(bf16[1216,640]{1,0:T(8,128)(2,1)} %get-tuple-element.267), channel_id=1, source_target_pairs={{0,16},{16,32},{32,48},{48,0},{1,17},{17,33},{33,49},{49,1},{2,18}... | collective-permute-start | bytes 4669448 | tf_op jit(solution)/shard_map/ppermute | solution.py:61
  470.7 71.5 %collective-permute-start.73 = (bf16[512,640]{1,0:T(8,128)(2,1)}, bf16[512,640]{1,0:T(8,128)(2,1)}, u32[]{:S(2)}, u32[]{:S(2)}) collective-permute-start(bf16[512,640]{1,0:T(8,128)(2,1)} %get-tuple-element.326), channel_id=1, source_target_pairs={{0,8},{8,0},{1,9},{9,1},{2,10},{10,2},{3,11},{11,3},{4,12},{12,4},... | collective-permute-start | bytes 1966088 | tf_op jit(solution)/shard_map/ppermute | solution.py:61
  474.9 74.2 %collective-permute-start.74 = (bf16[512,640]{1,0:T(8,128)(2,1)}, bf16[512,640]{1,0:T(8,128)(2,1)}, u32[]{:S(2)}, u32[]{:S(2)}) collective-permute-start(bf16[512,640]{1,0:T(8,128)(2,1)} %get-tuple-element.324), channel_id=1, source_target_pairs={{0,8},{8,0},{1,9},{9,1},{2,10},{10,2},{3,11},{11,3},{4,12},{12,4},... | collective-permute-start | bytes 1966088 | tf_op jit(solution)/shard_map/ppermute | solution.py:61
  537.5 139.3 %all-gather.7.cloned.1.call-start = ((), (), s32[]{:S(2)}) async-start(), calls=%async_computation.14 | async-start | bytes 1327104 | tf_op jit(solution)/shard_map/all_gather | solution.py:788
  608.8 184.7 %reduce-scatter.12.cloned.1.call-start = ((), (), s32[]{:S(2)}) async-start(), calls=%async_computation.15 | async-start | bytes 737280 | tf_op jit(solution)/shard_map/reduce_scatter | solution.py:475
  633.4 185.8 %reduce-scatter.16.cloned.1.call-start = ((), (), s32[]{:S(2)}) async-start(), calls=%async_computation.18 | async-start | bytes 1228800
  644.2 75.5 %collective-permute-start.91 = (bf16[2432,640]{1,0:T(8,128)(2,1)}, bf16[2432,640]{1,0:T(8,128)(2,1)}, u32[]{:S(2)}, u32[]{:S(2)}) collective-permute-start(bf16[2432,640]{1,0:T(8,128)(2,1)} %pad_maximum_fusion.2), channel_id=1, source_target_pairs={{0,16},{16,32},{32,48},{48,0},{1,17},{17,33},{33,49},{49,1},{2,18}... | collective-permute-start | bytes 9338888 | tf_op jit(solution)/shard_map/ppermute | solution.py:61
  644.2 76.5 %collective-permute-start.90 = (bf16[2432,640]{1,0:T(8,128)(2,1)}, bf16[2432,640]{1,0:T(8,128)(2,1)}, u32[]{:S(2)}, u32[]{:S(2)}) collective-permute-start(bf16[2432,640]{1,0:T(8,128)(2,1)} %pad_maximum_fusion.1), channel_id=1, source_target_pairs={{0,48},{16,0},{32,16},{48,32},{1,49},{17,1},{33,17},{49,33},{2,50}... | collective-permute-start | bytes 9338888 | tf_op jit(solution)/shard_map/ppermute | solution.py:61
  651.5 101.0 %collective-permute-start.54 = (f32[6,1152]{1,0:T(8,128)S(1)}, f32[6,1152]{1,0:T(8,128)S(1)}, u32[]{:S(2)}, u32[]{:S(2)}) collective-permute-start(f32[6,1152]{1,0:T(8,128)S(1)} %stack.29), channel_id=1, source_target_pairs={{0,2},{2,4},{4,6},{6,0},{1,3},{3,5},{5,7},{7,1},{8,10},{10,12},{12... | collective-permute-start | bytes 82952 | tf_op jit(solution)/shard_map/ppermute | solution.py:61
  657.8 96.1 %collective-permute-start.55 = (f32[6,1152]{1,0:T(8,128)S(1)}, f32[6,1152]{1,0:T(8,128)}, u32[]{:S(2)}, u32[]{:S(2)}) collective-permute-start(f32[6,1152]{1,0:T(8,128)S(1)} %stack.29), channel_id=1, source_target_pairs={{0,4},{2,6},{4,0},{6,2},{1,5},{3,7},{5,1},{7,3},{8,12},{10,14},{12... | collective-permute-start | bytes 82952 | tf_op jit(solution)/shard_map/ppermute | solution.py:61
  676.8 174.2 %reduce-scatter.14.cloned.1.call-start = ((), (), s32[]{:S(2)}) async-start(), calls=%async_computation.16 | async-start | bytes 737280 | tf_op jit(solution)/shard_map/reduce_scatter | solution.py:475
  744.4 132.6 %all-gather.9.cloned.1.call-start = ((), (), s32[]{:S(2)}) async-start(), calls=%async_computation.17 | async-start | bytes 3502080 | tf_op jit(solution)/shard_map/all_gather | solution.py:759
  (188 other events, 2976.9 us)
Sparse Core Ops, SparseCore 0:
  167.9 49.8 reduce-scatter.7
  243.3 37.5 all-gather.4
  467.1 34.9 reduce-scatter.9
  609.0 57.0 all-gather.6
  668.8 23.0 reduce-scatter.11
  694.8 28.7 reduce-scatter.15
  744.5 29.2 reduce-scatter.13
  798.1 28.6 all-gather.8

commit v3 on v2

v3 whole, which is shorter than its diff:
```python
import functools

import jax
import jax.numpy as jnp
from jax import lax
from jax.experimental import pallas as pl
from jax.experimental.pallas import tpu as pltpu
from jax.sharding import Mesh
from jax.sharding import PartitionSpec as P

HEADS = 16
HEAD = 72
D = 1152
FF = 4608
CAP_TOK = 60
TXT_OWN = 64
TXT = 8 * TXT_OWN
TOK = 256
ROW = 2048
CAP_LEN = 120
SEGS = 3
CAPS = 4
SHARD = 144
SLOT = 128
WIN = 640
STEP = 512

bf16 = jnp.bfloat16
f32 = jnp.float32
norm_eps = 1e-06
masked_score = -1e30
scale = HEAD ** (-0.5)
log2e = 1.4426950408889634
FS = ("y", "xl")
VMEM = 60 * 1024 * 1024


def dot_nn(a, b):
    return lax.dot_general(a, b, (((1,), (0,)), ((), ())), preferred_element_type=f32)


def dot_nt(a, b):
    return lax.dot_general(a, b, (((1,), (1,)), ((), ())), preferred_element_type=f32)


def dot_tn(a, b):
    return lax.dot_general(a, b, (((0,), (0,)), ((), ())), preferred_element_type=f32)


def params():
    return pltpu.CompilerParams(vmem_limit_bytes=VMEM)


def shift(x, axis, by):
    n = lax.axis_size(axis)
    return lax.ppermute(x, axis, [(i, (i + by) % n) for i in range(n)])


def halves(x):
    h = (x.shape[0] // 2 + 15) // 16 * 16
    return x[:h], x[h:]


def after(x, *others):
    return lax.optimization_barrier((x, *others))[0] if others else x


def gather_first(x):
    return shift(x, "xl", 1), shift(x, "y", -1), shift(x, "y", 1)


def gather_second(x01, x10):
    return shift(x01, "y", 1), shift(x10, "y", -1), shift(x10, "xl", 1)


def gather_third(x31, x11):
    return shift(halves(x11)[0], "y", -1), shift(halves(x31)[1], "y", 1)


NEAR = ((0, 0), (0, 1), (1, 0), (3, 0))
NEXT = ((3, 1), (2, 0), (1, 1))
LAST = (2, 1)


def reduce_first(chunk):
    lo, hi = halves(chunk(2, 1))
    return shift(lo, "y", 1), shift(hi, "y", -1), shift(chunk(2, 0), "y", 1)


def reduce_second(chunk, lo, hi):
    h = lo.shape[0]
    c11, c31 = chunk(1, 1), chunk(3, 1)
    c11 = jnp.concatenate([c11[:h] + lo, c11[h:]], axis=0)
    c31 = jnp.concatenate([c31[:h], c31[h:] + hi], axis=0)
    return shift(c11, "xl", 1), shift(c31, "y", -1)


def reduce_third(chunk, c20, c11, c31):
    return (
        shift(chunk(1, 0) + c20 + c11, "y", 1),
        shift(chunk(0, 1) + c31, "xl", 1),
        shift(chunk(3, 0), "y", -1),
    )


def reduce_last(chunk, *parts):
    return sum([p.astype(f32) for p in parts], chunk(0, 0).astype(f32))


def every_peer(x):
    copies = jnp.broadcast_to(x[None], (8, *x.shape)).reshape(8 * x.shape[0], x.shape[1])
    return lax.all_to_all(copies, FS, 0, 0, tiled=True)


def peers_sum(x):
    parts = lax.all_to_all(x, FS, 0, 0, tiled=True)
    return jnp.sum(parts.reshape(8, -1, x.shape[1]).astype(f32), axis=0)


def reduce_z(far, minus, plus):
    lo, hi = halves(far)
    lo, hi = shift(lo, "z", -1), shift(hi, "z", 1)
    h = lo.shape[0]
    return (
        jnp.concatenate([minus[:h] + lo, minus[h:]], axis=0),
        jnp.concatenate([plus[:h], plus[h:] + hi], axis=0),
    )


def peer(dy, dx):
    return ((lax.axis_index("y") + dy) % 4) * 2 + (lax.axis_index("xl") ^ dx)


def place(pieces, outs):
    arrays, index = [], {}

    def number(x):
        if id(x) not in index:
            index[id(x)] = len(arrays)
            arrays.append(x)
        return index[id(x)]

    block = sum(rows for _, _, rows, p, _ in pieces if p == NEAR[0])
    table, copies = [], []
    for source, first, rows, p, off in pieces:
        pair = source if isinstance(source, tuple) else (source, source)
        pair = tuple(number(x) for x in pair)
        for o, parts in enumerate(outs):
            for side, c0, cols, to in parts:
                copies.append((pair, side, first, rows, len(table), off, o, c0, cols, to))
        table.append(peer(*p))
    n_in, n_out = len(arrays), len(outs)
    widths = [sum(cols for _, _, cols, _ in parts) for parts in outs]

    def body(where, core, *refs):
        ins, targets, sem = refs[:n_in], refs[n_in : n_in + n_out], refs[-1]

        def run(this):
            started = []
            for k, (pair, side, first, rows, t, off, o, c0, cols, to) in enumerate(copies):
                src = ins[pair[0] if side == this else pair[1]]
                row = pl.multiple_of(where[t] * block + off, 16)
                one = pltpu.make_async_copy(
                    src.at[pl.ds(first, rows), pl.ds(c0, cols)],
                    targets[o].at[pl.ds(row, rows), pl.ds(to, cols)],
                    sem.at[k],
                )
                one.start()
                started.append(one)
            for one in started:
                one.wait()

        @pl.when(core[0] == 0)
        def _():
            run(0)

        @pl.when(core[0] != 0)
        def _():
            run(1)

    smem = pl.BlockSpec(memory_space=pltpu.SMEM)
    return pl.pallas_call(
        body,
        in_specs=[smem, smem] + [pl.BlockSpec(memory_space=pl.ANY)] * n_in,
        out_specs=[pl.BlockSpec(memory_space=pltpu.VMEM)] * n_out,
        out_shape=[jax.ShapeDtypeStruct((8 * block, w), bf16) for w in widths],
        scratch_shapes=[pltpu.SemaphoreType.DMA((len(copies),))],
        compiler_params=params(),
    )(jnp.stack(table).astype(jnp.int32), lax.axis_index("c").astype(jnp.int32)[None], *arrays)


def self_forward_body(seg_q, seg_k, q, kv, out, total):
    s = dot_nt(q[:, :SLOT], kv[:, SLOT : 2 * SLOT])
    s = jnp.where(seg_q[...] == seg_k[...], s, masked_score)
    top = jnp.max(s, axis=1, keepdims=True)
    p = jnp.exp2((s - top) * (scale * log2e))
    mass = jnp.sum(p, axis=1, keepdims=True)
    out[...] = (dot_nn(p.astype(bf16), kv[:, 2 * SLOT :]) / mass)[:, :HEAD].astype(bf16)
    log_total = top * (scale * log2e) + jnp.log2(mass)
    total[...] = jnp.transpose(jnp.broadcast_to(log_total, (TOK, SLOT)))[0:1, :]


def self_forward(head, seg_q, seg_k, qkv):
    return pl.pallas_call(
        self_forward_body,
        grid=(ROW // TOK,),
        in_specs=[
            pl.BlockSpec((TOK, 1), lambda i: (i, 0)),
            pl.BlockSpec((1, ROW), lambda i: (0, 0)),
            pl.BlockSpec((TOK, 3 * SLOT), lambda i: (i, head)),
            pl.BlockSpec((ROW, 3 * SLOT), lambda i: (0, head)),
        ],
        out_specs=[
            pl.BlockSpec((TOK, HEAD), lambda i: (i, 0)),
            pl.BlockSpec((1, TOK), lambda i: (0, i)),
        ],
        out_shape=[
            jax.ShapeDtypeStruct((ROW, HEAD), bf16),
            jax.ShapeDtypeStruct((1, ROW), f32),
        ],
        compiler_params=params(),
    )(seg_q, seg_k, qkv, qkv)


def self_backward_body(head, seg_k, seg_q, total, q, kv, g, grad, key_sum, value_sum, key_t):
    i = pl.program_id(0)

    @pl.when(i == 0)
    def _():
        key_sum[...] = jnp.zeros_like(key_sum)
        value_sum[...] = jnp.zeros_like(value_sum)
        key_t[...] = jnp.transpose(kv[:, SLOT : 2 * SLOT])

    rows = pl.ds(pl.multiple_of(i * TOK, TOK), TOK)
    q_h, k_h, v_h = q[:, :SLOT], kv[:, SLOT : 2 * SLOT], kv[:, 2 * SLOT :]
    g_both = g[...]
    g_h = jnp.concatenate(
        [g_both[:, HEAD * head : HEAD * (head + 1)], jnp.zeros((TOK, SLOT - HEAD), bf16)], axis=1
    )
    p = jnp.exp2(dot_nt(k_h, q_h) * (scale * log2e) - total[...])
    p = jnp.where(seg_k[...] == seg_q[...], p, 0.0)
    dp = dot_nt(v_h, g_h)
    ds = (p * (dp - jnp.sum(p * dp, axis=0, keepdims=True))).astype(bf16)
    value_sum[...] += dot_nn(p.astype(bf16), g_h)
    key_sum[...] += dot_nn(ds, q_h)
    grad[rows, :SLOT] = (jnp.transpose(dot_nn(key_t[...], ds)) * scale).astype(bf16)

    @pl.when(i == pl.num_programs(0) - 1)
    def _():
        grad[:, SLOT : 2 * SLOT] = (key_sum[...] * scale).astype(bf16)
        grad[:, 2 * SLOT :] = value_sum[...].astype(bf16)


def self_backward(head, seg_k, seg_q, total, qkv, g):
    return pl.pallas_call(
        functools.partial(self_backward_body, head),
        grid=(ROW // TOK,),
        in_specs=[
            pl.BlockSpec((ROW, 1), lambda i: (0, 0)),
            pl.BlockSpec((1, TOK), lambda i: (0, i)),
            pl.BlockSpec((1, TOK), lambda i: (0, i)),
            pl.BlockSpec((TOK, 3 * SLOT), lambda i: (i, head)),
            pl.BlockSpec((ROW, 3 * SLOT), lambda i: (0, head)),
            pl.BlockSpec((TOK, SHARD), lambda i: (i, 0)),
        ],
        out_specs=pl.BlockSpec((ROW, 3 * SLOT), lambda i: (0, 0)),
        out_shape=jax.ShapeDtypeStruct((ROW, 3 * SLOT), bf16),
        scratch_shapes=[
            pltpu.VMEM((ROW, SLOT), f32),
            pltpu.VMEM((ROW, SLOT), f32),
            pltpu.VMEM((SLOT, ROW), bf16),
        ],
        compiler_params=params(),
    )(seg_k, seg_q, total, qkv, qkv, g)


def cross_forward_body(cap_q, cap_t, q, k, v, out):
    allowed = cap_q[...] == cap_t[...]
    mixed = []
    for h in range(HEADS):
        a, b = HEAD * h, HEAD * (h + 1)
        s = dot_nt(q[:, a:b], k[:, a:b])
        s = jnp.where(allowed, s, masked_score)
        top = jnp.max(s, axis=1, keepdims=True)
        p = jnp.exp2((s - top) * (scale * log2e))
        mass = jnp.sum(p, axis=1, keepdims=True)
        mixed.append(dot_nn(p.astype(bf16), v[:, a:b]) / mass)
    out[...] = jnp.concatenate(mixed, axis=1).astype(bf16)


def cross_forward(cap_q, cap_t, q, k, v):
    return pl.pallas_call(
        cross_forward_body,
        out_shape=jax.ShapeDtypeStruct((TOK, D), bf16),
        compiler_params=params(),
    )(cap_q, cap_t, q, k, v)


def cross_backward_body(cap_t, cap_q, q, k, v, g, grad_q, grad_k, grad_v):
    allowed = cap_t[...] == cap_q[...]
    dq, dk, dv = [], [], []
    for h in range(HEADS):
        a, b = HEAD * h, HEAD * (h + 1)
        q_h, k_h, v_h, g_h = q[:, a:b], k[:, a:b], v[:, a:b], g[:, a:b]
        s = jnp.where(allowed, dot_nt(k_h, q_h), masked_score)
        top = jnp.max(s, axis=0, keepdims=True)
        p = jnp.exp2((s - top) * (scale * log2e))
        p = p / jnp.sum(p, axis=0, keepdims=True)
        dp = dot_nt(v_h, g_h)
        ds = (p * (dp - jnp.sum(p * dp, axis=0, keepdims=True))).astype(bf16)
        dv.append(dot_nn(p.astype(bf16), g_h))
        dk.append(dot_nn(ds, q_h) * scale)
        dq.append(dot_tn(ds, k_h) * scale)
    grad_q[...] = jnp.concatenate(dq, axis=1).astype(bf16)
    grad_k[...] = jnp.concatenate(dk, axis=1).astype(bf16)
    grad_v[...] = jnp.concatenate(dv, axis=1).astype(bf16)


def cross_backward(cap_t, cap_q, q, k, v, g):
    return pl.pallas_call(
        cross_backward_body,
        out_shape=[
            jax.ShapeDtypeStruct((TOK, D), bf16),
            jax.ShapeDtypeStruct((TXT, D), bf16),
            jax.ShapeDtypeStruct((TXT, D), bf16),
        ],
        compiler_params=params(),
    )(cap_t, cap_q, q, k, v, g)


def mlp_body(core, x, g, mine, other, out, act_out, pre_out, grad_x, up, down, sem):
    @pl.when(pl.program_id(0) == 0)
    def _():
        def fetch(first, second):
            one = pltpu.make_async_copy(first, up, sem.at[0])
            two = pltpu.make_async_copy(second, down, sem.at[1])
            one.start()
            two.start()
            one.wait()
            two.wait()

        @pl.when(core[0] == 0)
        def _():
            fetch(mine, other)

        @pl.when(core[0] != 0)
        def _():
            fetch(other, mine)

    pre = dot_nn(x[...], up[...])
    grad_act = dot_nt(g[...], down[...])
    cdf = 0.5 * (1.0 + lax.erf(pre * (0.5**0.5)))
    density = jnp.exp2(pre * pre * (-0.5 * log2e)) * 0.3989422804014327
    act = (pre * cdf).astype(bf16)
    grad_pre = (grad_act * (cdf + pre * density)).astype(bf16)
    act_out[...] = act
    pre_out[...] = grad_pre
    out[...] = dot_nn(act, down[...]).astype(out.dtype)
    grad_x[...] = dot_nt(grad_pre, up[...]).astype(grad_x.dtype)


def mlp(core, x, g, mine, other):
    n = x.shape[0]
    rows = pl.BlockSpec((TOK, D), lambda i: (i, 0))
    hbm = pl.BlockSpec(memory_space=pl.ANY)
    return pl.pallas_call(
        mlp_body,
        grid=(n // TOK,),
        in_specs=[pl.BlockSpec(memory_space=pltpu.SMEM), rows, rows, hbm, hbm],
        out_specs=[rows] * 4,
        out_shape=[jax.ShapeDtypeStruct((n, D), bf16)] * 4,
        scratch_shapes=[
            pltpu.VMEM((D, D), bf16),
            pltpu.VMEM((D, D), bf16),
            pltpu.SemaphoreType.DMA((2,)),
        ],
        compiler_params=params(),
    )(core, x, g, mine, other)


def mlp_grads_body(core, *refs):
    xs, pres, acts, gs = refs[0:3], refs[3:6], refs[6:9], refs[9:12]
    keep, send = refs[12:]
    up = sum(dot_tn(x[...], p[...]) for x, p in zip(xs, pres)).astype(bf16)
    down = sum(dot_tn(a[...], g[...]) for a, g in zip(acts, gs)).astype(bf16)
    first = core[0] == 0

    @pl.when(first)
    def _():
        keep[...] = up
        send[...] = down

    @pl.when(jnp.logical_not(first))
    def _():
        keep[...] = down
        send[...] = up


def mlp_grads(core, xs, pres, acts, gs):
    def whole(x):
        return pl.BlockSpec(x.shape, lambda k: (0, 0))

    def part(x):
        return pl.BlockSpec((x.shape[0], 384), lambda k: (0, k))

    out = pl.BlockSpec((D, 384), lambda k: (0, k))
    return pl.pallas_call(
        mlp_grads_body,
        grid=(3,),
        in_specs=[pl.BlockSpec(memory_space=pltpu.SMEM)]
        + [whole(x) for x in xs]
        + [part(x) for x in pres]
        + [whole(x) for x in acts]
        + [part(x) for x in gs],
        out_specs=[out, out],
        out_shape=[jax.ShapeDtypeStruct((D, D), bf16)] * 2,
        compiler_params=params(),
    )(core, *xs, *pres, *acts, *gs)


def sort_hidden_body(x, up, down):
    for f in range(8):
        lanes = slice(SHARD * f, SHARD * (f + 1))
        up[:, 4 * SHARD * f : 4 * SHARD * (f + 1)] = jnp.concatenate(
            [x[2 * z, :, lanes] for z in range(4)], axis=1
        ).astype(f32)
    for z in range(4):
        down[SHARD * z : SHARD * (z + 1), :] = x[2 * z + 1].astype(f32)


def sort_hidden(x):
    return pl.pallas_call(
        sort_hidden_body,
        out_shape=[
            jax.ShapeDtypeStruct((SHARD, FF), f32),
            jax.ShapeDtypeStruct((4 * SHARD, D), f32),
        ],
        compiler_params=params(),
    )(x)


def norm_layer(values, norm_gain, norm_shift):
    center = values - jnp.mean(values, axis=-1, keepdims=True)
    spread = jnp.mean(center * center, axis=-1, keepdims=True)
    return center * lax.rsqrt(spread + norm_eps) * norm_gain + norm_shift


def row_block(x, index, rows):
    return lax.dynamic_slice_in_dim(x, index * rows, rows, axis=0)


def core_window(x, core):
    return lax.dynamic_slice_in_dim(x, core * STEP, WIN, axis=1)


def both_cores(x):
    return jnp.concatenate([x, shift(x, "c", 1)], axis=0)


def window_grad(left, right):
    core = lax.axis_index("c")
    sent = shift(core_window(right, 1 - core), "c", 1)
    rights = jnp.concatenate([core_window(right, core), sent], axis=0)
    return dot_tn(both_cores(left), rights).astype(bf16)


def sum_over_dp(x):
    part = lax.psum_scatter(x, "z", scatter_dimension=0, tiled=True)
    part = part + shift(part, "xh", 1)
    return lax.all_gather(part, "z", axis=0, tiled=True)


def whole_columns(mine, count):
    other = shift(mine, "c", 1)
    first = lax.axis_index("c") == 0
    low = jnp.where(first, mine, other).astype(f32)
    high = jnp.where(first, other, mine).astype(f32)
    return [
        jnp.concatenate(
            [low[SHARD * k : SHARD * (k + 1)], high[SHARD * k : SHARD * (k + 1), 128:]], axis=1
        )
        for k in range(count)
    ]


def sum_rows_over_dp(x):
    core = lax.axis_index("c")
    rows = x.shape[0] // 2
    mine = row_block(x, core, rows) + shift(row_block(x, 1 - core, rows), "c", 1)
    mine = sum_over_dp(mine)
    other = shift(mine, "c", 1)
    first = core == 0
    low = jnp.where(first, mine, other)
    high = jnp.where(first, other, mine)
    return jnp.concatenate([low, high], axis=0).astype(f32)


def sum_everywhere(x):
    for axis in ("y", "xl", "z", "xh", "c"):
        n = lax.axis_size(axis)
        x = sum([shift(x, axis, k) for k in range(1, n)], x)
    return x


def local(
    tokens,
    text_states,
    seg_lengths,
    caption_of_segment,
    text_lengths,
    ln1_gain,
    ln1_bias,
    w_query,
    w_key,
    w_value,
    w_out,
    ln2_gain,
    ln2_bias,
    c_query,
    w_text,
    c_key,
    c_value,
    c_out,
    ln3_gain,
    ln3_bias,
    w_up,
    w_down,
    cotangent,
):
    core = lax.axis_index("c")
    first_core = core == 0
    core_index = core.astype(jnp.int32)[None]
    quarter = lax.axis_index("z")
    first_row = peer(0, 0) * TOK

    ends = jnp.cumsum(seg_lengths[0])
    positions = jnp.arange(ROW, dtype=jnp.int32)
    segment = jnp.sum((positions[:, None] >= ends[None, :]).astype(jnp.int32), axis=1)
    own_segment = lax.dynamic_slice_in_dim(segment, first_row, TOK)
    text_row = jnp.arange(TXT, dtype=jnp.int32)
    text_pos = text_row // TXT_OWN * CAP_TOK + text_row % TXT_OWN
    text_caption = text_pos // CAP_LEN
    live = jnp.sum(
        jnp.where(
            text_caption[:, None] == jnp.arange(CAPS, dtype=jnp.int32)[None, :],
            text_lengths[0][None, :],
            0,
        ),
        axis=1,
    )
    query_caption = jnp.sum(
        jnp.where(
            own_segment[:, None] == jnp.arange(SEGS, dtype=jnp.int32)[None, :],
            caption_of_segment[0][None, :],
            0,
        ),
        axis=1,
    )
    text_live = (text_row % TXT_OWN < CAP_TOK) & (text_pos % CAP_LEN < live)
    text_key = jnp.where(text_live, text_caption, -1)

    rows_in = tokens[0].astype(f32)
    normed_one, pull_one = jax.vjp(norm_layer, rows_in, ln1_gain, ln1_bias)
    normed_one = normed_one.astype(bf16)
    n01, n10, n30 = gather_first(normed_one)

    grad_out = cotangent[0]
    grad_mlp = grad_out.astype(bf16)
    mlp_minus, mlp_plus = shift(grad_mlp, "z", 1), shift(grad_mlp, "z", -1)

    text_own = jnp.pad(after(text_states[0], normed_one), ((0, TXT_OWN - CAP_TOK), (0, 0)))
    text_columns = lax.all_to_all(text_own, FS, split_axis=1, concat_axis=0, tiled=True)
    context_part = dot_nn(text_columns, w_text).astype(bf16)
    context_own = lax.psum_scatter(context_part, FS, scatter_dimension=0, tiled=True)
    context = lax.all_gather(context_own, FS, axis=0, tiled=True)

    packed = jnp.concatenate(
        [
            jnp.concatenate([w[:, SHARD * k : SHARD * (k + 1)] for k in range(8)], axis=0)
            for w in (w_query, w_key, w_value)
        ],
        axis=1,
    )
    heads_w = lax.all_to_all(after(packed, context_part), FS, 0, 0, tiled=True)

    n31, n20, n11 = gather_second(n01, n10)
    n21 = gather_third(n31, n11)
    lo = n21[0].shape[0]
    (normed_all,) = place(
        [(x, 0, TOK, p, 0) for x, p in zip((normed_one, n01, n10, n30), NEAR)]
        + [(x, 0, TOK, p, 0) for x, p in zip((n31, n20, n11), NEXT)]
        + [(n21[0], 0, lo, LAST, 0), (n21[1], 0, TOK - lo, LAST, lo)],
        [[(0, 0, D, 0)]],
    )
    far_lo = shift(halves(mlp_minus)[0], "z", 1)
    far_hi = shift(halves(mlp_plus)[1], "z", -1)
    mlp_far = jnp.concatenate([far_lo, far_hi], axis=0)
    mlp_near = jnp.concatenate([mlp_minus, mlp_plus], axis=0)

    blank = jnp.zeros((D, SLOT - HEAD), bf16)
    heads_w = jnp.concatenate(
        [
            part
            for h in range(2)
            for k in range(3)
            for part in (heads_w[:, SHARD * k + HEAD * h : SHARD * k + HEAD * (h + 1)], blank)
        ],
        axis=1,
    )

    pack = jnp.where(
        first_core,
        jnp.concatenate([w_out, c_key, c_out[:, :WIN]], axis=1),
        jnp.concatenate([c_query, c_value, c_out[:, STEP:]], axis=1),
    )
    pack = after(pack, normed_all)
    g01, g10, g30 = gather_first(pack)

    seg_col, seg_row = segment[:, None], segment[None, :]
    qkv = dot_nn(after(normed_all, context_own, mlp_far), heads_w).astype(bf16)
    head0, total0 = self_forward(0, seg_col, seg_row, qkv)
    g01, g10, g30, head0 = lax.optimization_barrier((g01, g10, g30, head0))
    g31, g20, g11 = gather_second(g01, g10)
    near_mine = jnp.concatenate([pack, g01, g10, g30], axis=0)
    near_other = shift(near_mine, "c", 1)
    head1, total1 = self_forward(1, seg_col, seg_row, after(qkv, head0))
    attended = lax.all_to_all(
        jnp.concatenate([head0, head1], axis=1), FS, split_axis=0, concat_axis=1, tiled=True
    )
    g31, g20, g11, attended = lax.optimization_barrier((g31, g20, g11, attended))
    g21 = gather_third(g31, g11)
    next_mine = jnp.concatenate([g31, g20, g11], axis=0)
    next_other = shift(next_mine, "c", 1)
    last_other = [shift(x, "c", 1) for x in g21]
    lo = g21[0].shape[0]
    square_pieces = (
        [((near_mine, near_other), SHARD * k, SHARD, p, 0) for k, p in enumerate(NEAR)]
        + [((next_mine, next_other), SHARD * k, SHARD, p, 0) for k, p in enumerate(NEXT)]
        + [
            ((g21[0], last_other[0]), 0, lo, LAST, 0),
            ((g21[1], last_other[1]), 0, SHARD - lo, LAST, lo),
        ]
    )
    full_out, full_cquery = place(square_pieces, [[(0, 0, D, 0)], [(1, 0, D, 0)]])
    after_self = rows_in + dot_nn(attended, full_out)

    up_own = jnp.concatenate(
        [
            lax.dynamic_slice(w_up, (0, 4 * SHARD * k + SHARD * quarter), (SHARD, SHARD))
            for k in range(8)
        ],
        axis=1,
    )
    hidden_own = jnp.where(first_core, up_own, row_block(w_down, quarter, SHARD))
    hidden_mine = every_peer(after(hidden_own, attended))
    hidden_other = shift(hidden_mine, "c", 1)

    full_ckey, full_cvalue, full_cout = place(
        square_pieces,
        [
            [(0, D, D, 0)],
            [(1, D, D, 0)],
            [(0, 2 * D, WIN, 0), (1, 2 * D + 128, STEP, WIN)],
        ],
    )
    normed_two, pull_two = jax.vjp(norm_layer, after_self, ln2_gain, ln2_bias)
    normed_two = normed_two.astype(bf16)
    cross_query = dot_nn(normed_two, full_cquery).astype(bf16)
    context = after(context, after_self)
    cross_key = dot_nn(context, full_ckey).astype(bf16)
    cross_value = dot_nn(context, full_cvalue).astype(bf16)
    cross_mixed = cross_forward(
        query_caption[:, None], text_key[None, :], cross_query, cross_key, cross_value
    )
    after_cross = after_self + dot_nn(cross_mixed, full_cout)

    normed_three, pull_three = jax.vjp(norm_layer, after_cross, ln3_gain, ln3_bias)
    normed_three = normed_three.astype(bf16)
    three_minus, three_plus = shift(normed_three, "z", 1), shift(normed_three, "z", -1)
    weights = (hidden_mine, hidden_other)
    out_own, act_own, pre_own, back_own = mlp(core_index, normed_three, grad_mlp, *weights)
    three_minus, three_plus, out_own = lax.optimization_barrier(
        (three_minus, three_plus, out_own)
    )
    three_far = jnp.concatenate(
        [shift(halves(three_minus)[0], "z", 1), shift(halves(three_plus)[1], "z", -1)], axis=0
    )
    three_near = jnp.concatenate([three_minus, three_plus], axis=0)
    out_near, act_near, pre_near, back_near = mlp(core_index, three_near, mlp_near, *weights)
    out_far, act_far, pre_far, back_far = mlp(
        core_index, after(three_far, out_near), mlp_far, *weights
    )
    back_minus, back_plus = reduce_z(back_far, back_near[:TOK], back_near[TOK:])
    keep, send = mlp_grads(
        core_index,
        (normed_three, three_near, after(three_far, back_minus, back_plus)),
        (pre_own, pre_near, pre_far),
        (act_own, act_near, act_far),
        (grad_mlp, mlp_near, mlp_far),
    )
    back_minus, back_plus = shift(back_minus, "z", -1), shift(back_plus, "z", 1)
    hidden_sum = keep + shift(send, "c", 1)
    grad_three = back_own.astype(f32) + back_minus.astype(f32) + back_plus.astype(f32)
    grad_cross_in, grad_ln3_gain, grad_ln3_bias = pull_three(grad_three)
    grad_after_cross = grad_out + grad_cross_in
    grad_cross_branch = grad_after_cross.astype(bf16)
    grad_cross_mixed = dot_nt(grad_cross_branch, full_cout).astype(bf16)

    out_minus, out_plus = reduce_z(
        after(out_far, grad_cross_mixed), out_near[:TOK], out_near[TOK:]
    )

    grad_cquery_rows, grad_key_part, grad_value_part = cross_backward(
        text_key[:, None],
        query_caption[None, :],
        cross_query,
        cross_key,
        cross_value,
        after(grad_cross_mixed, hidden_sum),
    )
    out_minus, out_plus = shift(out_minus, "z", -1), shift(out_plus, "z", 1)
    hidden_grad = peers_sum(hidden_sum).astype(bf16)
    grad_self_in, grad_ln2_gain, grad_ln2_bias = pull_two(
        dot_nt(after(grad_cquery_rows, out_minus, out_plus), full_cquery)
    )
    outputs = (
        after_cross
        + out_own.astype(f32)
        + out_minus.astype(f32)
        + out_plus.astype(f32)
    )
    grad_after_self = grad_after_cross + grad_self_in
    grad_self_branch = grad_after_self.astype(bf16)
    grad_attended = dot_nt(grad_self_branch, full_out).astype(bf16)
    grad_heads = lax.all_to_all(
        after(grad_attended, hidden_grad), FS, split_axis=1, concat_axis=0, tiled=True
    )
    hidden_grad = hidden_grad + shift(hidden_grad, "xh", 1)
    hidden_grad = lax.all_gather(hidden_grad, ("z", "c"), axis=0)

    square = jnp.concatenate(
        [
            window_grad(cross_mixed, grad_cross_branch),
            window_grad(normed_two, grad_cquery_rows),
            window_grad(attended, grad_self_branch),
            window_grad(context, grad_key_part),
            window_grad(context, grad_value_part),
        ],
        axis=1,
    )
    context_part = dot_nt(after(grad_key_part, grad_attended), full_ckey) + dot_nt(
        after(grad_value_part, grad_attended), full_cvalue
    )
    context_part = context_part.astype(bf16)
    grad_heads = after(grad_heads, square, context_part)
    context_grad = peers_sum(after(context_part, grad_heads)).astype(bf16)

    def square_chunk(dy, dx):
        return row_block(square, peer(dy, dx), SHARD)

    s_lo, s_hi, s20 = reduce_first(square_chunk)

    grad_head0 = self_backward(0, seg_col, seg_row, total0, qkv, grad_heads)
    s_lo, s_hi, s20, context_grad, grad_head0 = lax.optimization_barrier(
        (s_lo, s_hi, s20, context_grad, grad_head0)
    )
    context_grad = every_peer(context_grad)
    s11, s31 = reduce_second(square_chunk, s_lo, s_hi)
    grad_head1 = self_backward(1, seg_col, seg_row, total1, qkv, after(grad_heads, grad_head0))
    s11, s31, hidden_grad, context_grad, grad_head1 = lax.optimization_barrier(
        (s11, s31, hidden_grad, context_grad, grad_head1)
    )
    square_parts = reduce_third(square_chunk, s20, s11, s31)
    grad_qkv = jnp.concatenate([grad_head0, grad_head1], axis=1)
    normed_part = dot_nt(grad_qkv, heads_w).astype(bf16)

    def normed_chunk(dy, dx):
        return row_block(normed_part, peer(dy, dx), TOK)

    n_lo, n_hi, n20 = reduce_first(normed_chunk)
    grad_heads_w = dot_tn(normed_all, grad_qkv).astype(bf16)
    grad_heads_w = jnp.concatenate(
        [
            grad_heads_w[:, SLOT * (3 * h + k) : SLOT * (3 * h + k) + HEAD]
            for k in range(3)
            for h in range(2)
        ],
        axis=1,
    )
    grad_qkv_w = lax.all_to_all(grad_heads_w, FS, 0, 0, tiled=True)
    grad_w_text = dot_tn(text_columns, context_grad).astype(bf16)
    text_part = dot_nt(context_grad, w_text).astype(bf16)
    n_lo, n_hi, *square_parts = lax.optimization_barrier((n_lo, n_hi, *square_parts))
    n11, n31 = reduce_second(normed_chunk, n_lo, n_hi)
    square = reduce_last(square_chunk, *square_parts).astype(bf16)
    square = jnp.concatenate(
        [square[:, WIN * k : WIN * (k + 1)] for k in range(5)]
        + [jnp.zeros((768 - 5 * SHARD, WIN), bf16)],
        axis=0,
    )
    square = sum_over_dp(square)
    grad_c_out, grad_c_query, grad_w_out, grad_c_key, grad_c_value = whole_columns(square, 5)
    grad_w_text = sum_rows_over_dp(grad_w_text)
    grad_w_up, grad_w_down = sort_hidden(hidden_grad)

    n11, n31, grad_qkv_w = lax.optimization_barrier((n11, n31, grad_qkv_w))
    grad_normed_one = reduce_last(normed_chunk, *reduce_third(normed_chunk, n20, n11, n31))
    grad_qkv_w = jnp.concatenate(
        [
            jnp.concatenate(
                [
                    grad_qkv_w[SHARD * p : SHARD * (p + 1), SHARD * k : SHARD * (k + 1)]
                    for p in range(8)
                ],
                axis=1,
            )
            for k in range(3)
        ]
        + [jnp.zeros((512 - 3 * SHARD, D), bf16)],
        axis=0,
    )
    grad_qkv_w = sum_rows_over_dp(grad_qkv_w)
    grad_w_query, grad_w_key, grad_w_value = (
        grad_qkv_w[SHARD * k : SHARD * (k + 1)] for k in range(3)
    )
    grad_text = lax.all_to_all(
        after(text_part, grad_qkv_w), FS, split_axis=0, concat_axis=1, tiled=True
    )
    grad_text = grad_text[:CAP_TOK].astype(f32)
    grad_rows_in, grad_ln1_gain, grad_ln1_bias = pull_one(grad_normed_one)
    grad_tokens = grad_after_self + grad_rows_in
    norms = sum_everywhere(
        jnp.stack(
            [
                grad_ln1_gain,
                grad_ln1_bias,
                grad_ln2_gain,
                grad_ln2_bias,
                grad_ln3_gain,
                grad_ln3_bias,
            ]
        )
    )
    return (
        outputs[None],
        grad_tokens[None],
        grad_text[None],
        norms[0],
        norms[1],
        grad_w_query,
        grad_w_key,
        grad_w_value,
        grad_w_out,
        norms[2],
        norms[3],
        grad_c_query,
        grad_w_text,
        grad_c_key,
        grad_c_value,
        grad_c_out,
        norms[4],
        norms[5],
        grad_w_up,
        grad_w_down,
    )


def solution(mesh):
    split = Mesh(mesh.devices.reshape(2, 4, 2, 4, 2), ("xh", "z", "c", "y", "xl"))
    dp = ("xh", "z", "c")
    rows = P(dp, FS, None)
    per_row = P(dp, None)
    weight = P(FS, None)
    rep = P()
    in_specs = (
        rows, rows, per_row, per_row, per_row,
        rep, rep, weight, weight, weight, weight,
        rep, rep, weight, weight, weight, weight, weight,
        rep, rep, weight, weight, rows,
    )
    out_specs = (
        rows, rows, rows,
        rep, rep, weight, weight, weight, weight,
        rep, rep, weight, weight, weight, weight, weight,
        rep, rep, weight, weight,
    )
    return jax.shard_map(
        local, mesh=split, in_specs=in_specs, out_specs=out_specs, check_vma=False
    )
```

time: 901 us -> 824 us (0.915)
  waiting for transfers between devices: 258 us -> 159 us
  local copies, waits for them, and re-layouts: 86.2 us -> 120 us
    ppermute x101 -> x81, waiting for transfers between devices: 236 us -> 139 us  [shift(): return lax.ppermute(x, axis, [(i, (i + by) % n) for i in range(n)])]
    ppermute x101 -> x81, starting transfers between devices: 144 us -> 117 us  [shift(): return lax.ppermute(x, axis, [(i, (i + by) % n) for i in range(n)])]
    unnamed x228 -> x261, local copies, waits for them, and re-layouts: 19.6 us -> 39.5 us
    all_to_all x3 -> x7, starting transfers between devices: 10.6 us -> 29.8 us  [the longest x2 9.15 us: peers_sum(): parts = lax.all_to_all(x, FS, 0, 0, tiled=True)]
    all_to_all x3 -> x7, waiting for transfers between devices: 0.01 us -> 18.9 us  [the longest x2 9.41 us: peers_sum(): parts = lax.all_to_all(x, FS, 0, 0, tiled=True)]
    all_gather x1, waiting for transfers between devices: 18.1 us -> 0.02 us  [local(): context = lax.all_gather(context_own, FS, axis=0, tiled=True)]
    concatenate x2 -> x8, local copies, waits for them, and re-layouts: 1.56 us -> 15.2 us  [the longest x1 2.91 us: local(): grad_qkv = jnp.concatenate([grad_head0, grad_head1], axis=1)]
    slice x11 -> x12, local copies, waits for them, and re-layouts: 6.66 us -> 16.1 us  [halves(): return (x[:h], x[h:])]
  transfers between devices with their start and end apart: 115 -> 97, of which waited for: 36 -> 22; matrix products, arithmetic and copies ran while one was open for 26% -> 30% of each run, Pallas kernels for 18% -> 19%
where the time goes in v3:
time: 824 us; the launch traced here: 812 us
  Pallas kernels  162 us (20%)
  starting transfers between devices  160 us (19%)
  waiting for transfers between devices  159 us (19%)
  local copies, waits for them, and re-layouts  120 us (15%)
  other arithmetic  82.9 us (10%)
  matrix products  75.3 us (9%)
  blocking collectives  37.1 us (5%)
  between operations  16.3 us (2%)
    ppermute x81, waiting for transfers between devices, shift(): return lax.ppermute(x, axis, [(i, (i + by) % n) for i in range(n)])  139 us
    ppermute x81, starting transfers between devices, shift(): return lax.ppermute(x, axis, [(i, (i + by) % n) for i in range(n)])  117 us
    unnamed x261, local copies, waits for them, and re-layouts  39.5 us
    pallas_call x2, Pallas kernels, self_backward(): pl.pallas_call(functools.partial(self_backward_body, head), grid=(ROW //...  37.2 us
    all_gather x3, blocking collectives, sum_over_dp(): return lax.all_gather(part, 'z', axis=0, tiled=True)  37.1 us
    dot_general x7, matrix products, dot_nn(): lax.dot_general(a, b, (((1,), (0,)), ((), ())), preferred_element_type=f32)  29.3 us
    pallas_call x3, Pallas kernels, mlp(): pl.pallas_call(mlp_body, grid=(n // TOK,), in_specs=[pl.BlockSpec(memory_...  28.3 us
    pallas_call x3, Pallas kernels, place(): pl.pallas_call(body, in_specs=[smem, smem] + [pl.BlockSpec(memory_space=p...  27.1 us
  transfers between devices with their start and end apart: 97, of which 22 were waited for; matrix products, arithmetic and copies ran while one was open for 30% of the time, Pallas kernels for 19%

profile of v3, /device:TPU:1, one launch (start us, length us, event | category | flops | bytes accessed | tf_op | source)
XLA Modules:
  0.0 812.0 jit_solution(18177095662870002024)
XLA Ops:
  72.8 27.7 %collective-permute-done.5.refs_6_ = bf16[256,1152]{1,0:T(8,128)(2,1)S(1)} collective-permute-done((bf16[256,1152]{1,0:T(8,128)(2,1)}, bf16[256,1152]{1,0:T(8,128)(2,1)S(1)}, u32[]{:S(2)}, u32[]{:S(2)}) %collective-permute-start.5) | collective-permute-done | bytes 589856 | tf_op jit(solution)/shard_map/ppermute | solution.py:56
  123.5 8.8 %convolution_convert_fusion.1.q.kv = bf16[2048,768]{1,0:T(8,128)(2,1)} fusion(bf16[2048,1152]{1,0:T(8,128)(2,1)} %shard_map.374, bf16[1152,768]{1,0:T(8,128)(2,1)} %concatenate.149), kind=kOutput, calls=%fused_computation.1 | convolution fusion | flops 3625451520 | bytes 9633792 | tf_op jit(solution)/shard_map/dot_general | solution.py:39
  132.3 12.1 %shard_map.375 = (bf16[2048,72]{1,0:T(8,128)(2,1)}, f32[1,2048]{1,0:T(1,128)}) custom-call(s32[2048,1]{1,0:T(8,128)} %copy.182.seg_q.seg_k, s32[1,2048]{1,0:T(1,128)} %bitcast.143, bf16[2048,768]{1,0:T(8,128)(2,1)} %convolution_convert_fusion.1.q.kv, bf16[2048,768]{1,0:T(8,128)(2,1)} %convolution_convert_fusion.1.q.kv), custom_call_target="tpu_custom_call" | custom-call | tf_op jit(solution)/shard_map/pallas_call | solution.py:204
  145.8 12.1 %shard_map.376 = (bf16[2048,72]{1,0:T(8,128)(2,1)}, f32[1,2048]{1,0:T(1,128)}) custom-call(s32[2048,1]{1,0:T(8,128)} %copy.182.seg_q.seg_k, s32[1,2048]{1,0:T(1,128)} %bitcast.144, bf16[2048,768]{1,0:T(8,128)(2,1)} %convolution_convert_fusion.1.q.kv, bf16[2048,768]{1,0:T(8,128)(2,1)} %convolution_convert_fusion.1.q.kv), custom_call_target="tpu_custom_call" | custom-call | tf_op jit(solution)/shard_map/pallas_call | solution.py:204
  176.1 15.6 %collective-permute-done.15 = bf16[144,2944]{1,0:T(8,128)(2,1)S(1)} collective-permute-done((bf16[144,2944]{1,0:T(8,128)(2,1)S(1)}, bf16[144,2944]{1,0:T(8,128)(2,1)S(1)}, u32[]{:S(2)}, u32[]{:S(2)}) %collective-permute-start.15) | collective-permute-done | bytes 847904 | tf_op jit(solution)/shard_map/ppermute | solution.py:56
  213.2 34.4 %collective-permute-done.20.refs_4_ = bf16[80,2944]{1,0:T(8,128)(2,1)S(1)} collective-permute-done((bf16[80,2944]{1,0:T(8,128)(2,1)}, bf16[80,2944]{1,0:T(8,128)(2,1)S(1)}, u32[]{:S(2)}, u32[]{:S(2)}) %collective-permute-start.20) | collective-permute-done | bytes 471072 | tf_op jit(solution)/shard_map/ppermute | solution.py:56
  250.6 8.3 %all-to-all-done.3 = bf16[8,144,1152]{2,1,0:T(8,128)(2,1)} async-done(((bf16[8,144,1152]{2,1,0:T(8,128)(2,1)}), bf16[8,144,1152]{2,1,0:T(8,128)(2,1)}, u32[]{:S(2)}, u32[]{:S(2)}) %all-to-all-start.3) | async-done | bytes 2654240 | tf_op jit(solution)/shard_map/all_to_all | solution.py:112
  270.4 15.9 %shard_map.378 = (bf16[1152,1152]{1,0:T(8,128)(2,1)}, bf16[1152,1152]{1,0:T(8,128)(2,1)}, bf16[1152,1152]{1,0:T(8,128)(2,1)}) custom-call(s32[9]{0:T(128)} %stack.28.where, s32[1]{0:T(128)} %bitcast.9.core, bf16[576,2944]{1,0:T(8,128)(2,1)} %constant_dynamic-update-slice_fusion.26.refs_0_, bf16[576,2944]{1,0:T(8,128)(2,1)} %collective-permute-done.18.refs_1_, ...), custom_call_target="tpu_custom_call" | custom-call | tf_op jit(solution)/shard_map/pallas_call | solution.py:182
  298.5 11.7 %shard_map.379 = bf16[256,1152]{1,0:T(8,128)(2,1)} custom-call(s32[256,1]{1,0:T(8,128)} %copy.185.cap_q, s32[1,512]{1,0:T(1,128)} %and_select_fusion.1.cap_t, bf16[256,1152]{1,0:T(8,128)(2,1)} %convolution_convert_fusion.14.q, bf16[512,1152]{1,0:T(8,128)(2,1)} %convolution_convert_fusion.10.k, bf16[512,1152]{1,0:T(8,128)(2,1)} %convolution_convert_fusion.9.v), custom_call_target="tpu_custom_call" | custom-call | tf_op jit(solution)/shard_map/pallas_call | solution.py:292
  321.5 8.2 %shard_map.380 = (bf16[256,1152]{1,0:T(8,128)(2,1)}, bf16[256,1152]{1,0:T(8,128)(2,1)}, bf16[256,1152]{1,0:T(8,128)(2,1)}, bf16[256,1152]{1,0:T(8,128)(2,1)}) custom-call(s32[1]{0:T(128)} %bitcast.9.core, bf16[256,1152]{1,0:T(8,128)(2,1)} %copy-done.9, bf16[256,1152]{1,0:T(8,128)(2,1)} %copy-done.8, bf16[1152,1152]{1,0:T(8,128)(2,1)} %bitcast.27.mine, ...), custom_call_target="tpu_custom_call" | custom-call | tf_op jit(solution)/shard_map/pallas_call | solution.py:366
  340.6 11.9 %shard_map.381 = (bf16[512,1152]{1,0:T(8,128)(2,1)}, bf16[512,1152]{1,0:T(8,128)(2,1)}, bf16[512,1152]{1,0:T(8,128)(2,1)}, bf16[512,1152]{1,0:T(8,128)(2,1)}) custom-call(s32[1]{0:T(128)} %bitcast.9.core, bf16[512,1152]{1,0:T(8,128)(2,1)} %constant_dynamic-update-slice_fusion.33.x.refs_1_, bf16[512,1152]{1,0:T(8,128)(2,1)} %constant_dynamic-update-slice_fusion.35.g.refs_10_, ...), custom_call_target="tpu_custom_call" | custom-call | tf_op jit(solution)/shard_map/pallas_call | solution.py:366
  354.3 8.2 %shard_map.382 = (bf16[256,1152]{1,0:T(8,128)(2,1)}, bf16[256,1152]{1,0:T(8,128)(2,1)}, bf16[256,1152]{1,0:T(8,128)(2,1)}, bf16[256,1152]{1,0:T(8,128)(2,1)}) custom-call(s32[1]{0:T(128)} %bitcast.9.core, bf16[256,1152]{1,0:T(8,128)(2,1)} %copy-done.14, bf16[256,1152]{1,0:T(8,128)(2,1)} %copy-done.13, bf16[1152,1152]{1,0:T(8,128)(2,1)} %bitcast.27.mine, ...), custom_call_target="tpu_custom_call" | custom-call | tf_op jit(solution)/shard_map/pallas_call | solution.py:366
  380.7 12.9 %shard_map.383 = (bf16[1152,1152]{1,0:T(8,128)(2,1)}, bf16[1152,1152]{1,0:T(8,128)(2,1)}) custom-call(s32[1]{0:T(128)} %bitcast.9.core, bf16[256,1152]{1,0:T(8,128)(2,1)} %copy-done.9, bf16[512,1152]{1,0:T(8,128)(2,1)} %constant_dynamic-update-slice_fusion.33.x.refs_1_, bf16[256,1152]{1,0:T(8,128)(2,1)} %copy-done.14, ...), custom_call_target="tpu_custom_call" | custom-call | tf_op jit(solution)/shard_map/pallas_call | solution.py:407
  427.8 15.3 %shard_map.384 = (bf16[256,1152]{1,0:T(8,128)(2,1)}, bf16[512,1152]{1,0:T(8,128)(2,1)}, bf16[512,1152]{1,0:T(8,128)(2,1)}) custom-call(s32[512,1]{1,0:T(8,128)} %fusion.46.cap_t, s32[1,256]{1,0:T(1,128)} %bitcast.150, bf16[256,1152]{1,0:T(8,128)(2,1)} %convolution_convert_fusion.14.q, bf16[512,1152]{1,0:T(8,128)(2,1)} %convolution_convert_fusion.10.k, ...), custom_call_target="tpu_custom_call" | custom-call | tf_op jit(solution)/shard_map/pallas_call | solution.py:320
  476.3 9.4 %all-to-all-done.4 = bf16[8,144,1152]{2,1,0:T(8,128)(2,1)} async-done(((bf16[8,144,1152]{2,1,0:T(8,128)(2,1)}), bf16[8,144,1152]{2,1,0:T(8,128)(2,1)}, u32[]{:S(2)}, u32[]{:S(2)}) %all-to-all-start.4) | async-done | bytes 2654240 | tf_op jit(solution)/shard_map/all_to_all | solution.py:116
  520.5 18.7 %shard_map.385 = bf16[2048,384]{1,0:T(8,128)(2,1)} custom-call(s32[2048,1]{1,0:T(8,128)} %copy.182.seg_q.seg_k, s32[1,2048]{1,0:T(1,128)} %bitcast.145, f32[1,2048]{1,0:T(1,128)} %get-tuple-element.148.total, bf16[2048,768]{1,0:T(8,128)(2,1)} %convolution_convert_fusion.1.q.kv, bf16[2048,768]{1,0:T(8,128)(2,1)} %convolution_convert_fusion.1.q.kv, ...), custom_call_target="tpu_custom_call" | custom-call | tf_op jit(solution)/shard_map/pallas_call | solution.py:255
  541.3 6.4 collective-permute-done.47
  567.4 18.6 %shard_map.386 = bf16[2048,384]{1,0:T(8,128)(2,1)} custom-call(s32[2048,1]{1,0:T(8,128)} %copy.182.seg_q.seg_k, s32[1,2048]{1,0:T(1,128)} %bitcast.146, f32[1,2048]{1,0:T(1,128)} %get-tuple-element.153.total, bf16[2048,768]{1,0:T(8,128)(2,1)} %convolution_convert_fusion.1.q.kv, bf16[2048,768]{1,0:T(8,128)(2,1)} %convolution_convert_fusion.1.q.kv, ...), custom_call_target="tpu_custom_call" | custom-call | tf_op jit(solution)/shard_map/pallas_call | solution.py:255
  593.2 6.3 convolution_convert_fusion
  642.8 7.2 collective-permute-done.55
  689.1 9.7 %collective-permute-done.61 = bf16[256,1152]{1,0:T(8,128)(2,1)S(1)} collective-permute-done((bf16[256,1152]{1,0:T(8,128)(2,1)}, bf16[256,1152]{1,0:T(8,128)(2,1)S(1)}, u32[]{:S(2)}, u32[]{:S(2)}) %collective-permute-start.61) | collective-permute-done | bytes 589856 | tf_op jit(solution)/shard_map/ppermute | solution.py:56
  718.0 13.5 %all_gather.23 = bf16[256,1152]{1,0:T(8,128)(2,1)S(1)} all-gather(bf16[64,1152]{1,0:T(8,128)(2,1)S(1)} %add.702), channel_id=1, replica_groups=mesh['xh'=2,'z'=4,'c'=2,'y'=4,'xl'=2] {'z'}, dimensions={0}, use_global_device_ids=true | all-gather | bytes 737280 | tf_op jit(solution)/shard_map/all_gather | solution.py:470
  754.6 10.4 %all_gather.21 = bf16[256,1152]{1,0:T(8,128)(2,1)S(1)} all-gather(bf16[64,1152]{1,0:T(8,128)(2,1)S(1)} %add.686), channel_id=1, replica_groups=mesh['xh'=2,'z'=4,'c'=2,'y'=4,'xl'=2] {'z'}, dimensions={0}, use_global_device_ids=true | all-gather | bytes 737280 | tf_op jit(solution)/shard_map/all_gather | solution.py:470
  770.4 13.2 %all_gather.22 = bf16[768,640]{1,0:T(8,128)(2,1)S(1)} all-gather(bf16[192,640]{1,0:T(8,128)(2,1)S(1)} %copy.199), channel_id=1, replica_groups=mesh['xh'=2,'z'=4,'c'=2,'y'=4,'xl'=2] {'z'}, dimensions={0}, use_global_device_ids=true | all-gather | bytes 1228800 | tf_op jit(solution)/shard_map/all_gather | solution.py:470
  (632 shorter events, 479.1 us)
Async XLA Ops:
  12.3 50.1 %collective-permute-start.1 = (bf16[256,1152]{1,0:T(8,128)(2,1)}, bf16[256,1152]{1,0:T(8,128)(2,1)}, u32[]{:S(2)}, u32[]{:S(2)}) collective-permute-start(bf16[256,1152]{1,0:T(8,128)(2,1)} %fusion.20.refs_0_), channel_id=1, source_target_pairs={{0,6},{2,0},{4,2},{6,4},{1,7},{3,1},{5,3},{7,5},{8,14},{10,8},{12,... | collective-permute-start | bytes 1769480 | tf_op jit(solution)/shard_map/ppermute | solution.py:56
  15.9 48.0 %collective-permute-start = (bf16[256,1152]{1,0:T(8,128)(2,1)}, bf16[256,1152]{1,0:T(8,128)(2,1)}, u32[]{:S(2)}, u32[]{:S(2)}) collective-permute-start(bf16[256,1152]{1,0:T(8,128)(2,1)} %fusion.20.refs_0_), channel_id=1, source_target_pairs={{0,1},{1,0},{2,3},{3,2},{4,5},{5,4},{6,7},{7,6},{8,9},{9,8},{10,11... | collective-permute-start | bytes 1769480 | tf_op jit(solution)/shard_map/ppermute | solution.py:56
  17.1 95.1 %collective-permute-start.2 = (bf16[256,1152]{1,0:T(8,128)(2,1)}, bf16[256,1152]{1,0:T(8,128)(2,1)}, u32[]{:S(2)}, u32[]{:S(2)}) collective-permute-start(bf16[256,1152]{1,0:T(8,128)(2,1)} %fusion.20.refs_0_), channel_id=1, source_target_pairs={{0,2},{2,4},{4,6},{6,0},{1,3},{3,5},{5,7},{7,1},{8,10},{10,12},{12... | collective-permute-start | bytes 1769480 | tf_op jit(solution)/shard_map/ppermute | solution.py:56
  26.3 97.2 %reduce-scatter.7.cloned.1.call-start = ((), (), s32[]{:S(2)}) async-start(), calls=%async_computation.14 | async-start | bytes 1327104 | tf_op jit(solution)/shard_map/reduce_scatter | solution.py:574
  46.3 59.2 %all-to-all-start.1 = ((bf16[8,144,432]{2,1,0:T(8,128)(2,1)}), bf16[8,144,432]{2,1,0:T(8,128)(2,1)S(1)}, u32[]{:S(2)}, u32[]{:S(2)}) async-start(bf16[8,144,432]{2,1,0:T(8,128)(2,1)} %bitcast.133), calls=%async_computation.2 | async-start | bytes 2359296 | tf_op jit(solution)/shard_map/all_to_all | solution.py:584
  69.3 42.8 %collective-permute-start.4 = (bf16[256,1152]{1,0:T(8,128)(2,1)}, bf16[256,1152]{1,0:T(8,128)(2,1)}, u32[]{:S(2)}, u32[]{:S(2)}) collective-permute-start(bf16[256,1152]{1,0:T(8,128)(2,1)} %collective-permute-done.1.refs_2_), channel_id=1, source_target_pairs={{0,6},{2,0},{4,2},{6,4},{1,7},{3,1},{5,3},{7,5},{8,14},{10,8},{12,... | collective-permute-start | bytes 1769480 | tf_op jit(solution)/shard_map/ppermute | solution.py:56
  144.5 47.3 %collective-permute-start.16 = (bf16[144,2944]{1,0:T(8,128)(2,1)}, bf16[144,2944]{1,0:T(8,128)(2,1)}, u32[]{:S(2)}, u32[]{:S(2)}) collective-permute-start(bf16[144,2944]{1,0:T(8,128)(2,1)} %collective-permute-done.9), channel_id=1, source_target_pairs={{0,6},{2,0},{4,2},{6,4},{1,7},{3,1},{5,3},{7,5},{8,14},{10,8},{12,... | collective-permute-start | bytes 2543624 | tf_op jit(solution)/shard_map/ppermute | solution.py:56
  144.6 47.2 %collective-permute-start.17 = (bf16[144,2944]{1,0:T(8,128)(2,1)}, bf16[144,2944]{1,0:T(8,128)(2,1)}, u32[]{:S(2)}, u32[]{:S(2)}) collective-permute-start(bf16[144,2944]{1,0:T(8,128)(2,1)} %collective-permute-done.9), channel_id=1, source_target_pairs={{0,1},{1,0},{2,3},{3,2},{4,5},{5,4},{6,7},{7,6},{8,9},{9,8},{10,11... | collective-permute-start | bytes 2543624 | tf_op jit(solution)/shard_map/ppermute | solution.py:56
  171.9 88.6 %collective-permute-start.18 = (bf16[576,2944]{1,0:T(8,128)(2,1)}, bf16[576,2944]{1,0:T(8,128)(2,1)}, u32[]{:S(2)}, u32[]{:S(2)}) collective-permute-start(bf16[576,2944]{1,0:T(8,128)(2,1)} %constant_dynamic-update-slice_fusion.26.refs_0_), channel_id=1, source_target_pairs={{0,8},{8,0},{1,9},{9,1},{2,10},{10,2},{3,11},{11,3},{4,12},{12,4},... | collective-permute-start | bytes 10174472 | tf_op jit(solution)/shard_map/ppermute | solution.py:56
  197.1 63.4 %collective-permute-start.19 = (bf16[432,2944]{1,0:T(8,128)(2,1)}, bf16[432,2944]{1,0:T(8,128)(2,1)}, u32[]{:S(2)}, u32[]{:S(2)}) collective-permute-start(bf16[432,2944]{1,0:T(8,128)(2,1)} %constant_dynamic-update-slice_fusion.30.refs_2_), channel_id=1, source_target_pairs={{0,8},{8,0},{1,9},{9,1},{2,10},{10,2},{3,11},{11,3},{4,12},{12,4},... | collective-permute-start | bytes 7630856 | tf_op jit(solution)/shard_map/ppermute | solution.py:56
  202.1 56.8 %all-to-all-start.3 = ((bf16[8,144,1152]{2,1,0:T(8,128)(2,1)}), bf16[8,144,1152]{2,1,0:T(8,128)(2,1)}, u32[]{:S(2)}, u32[]{:S(2)}) async-start(bf16[8,144,1152]{2,1,0:T(8,128)(2,1)} %broadcast_in_dim.125), calls=%async_computation.4 | async-start | bytes 5308416 | tf_op jit(solution)/shard_map/all_to_all | solution.py:112
  206.5 63.5 %all-gather.4.cloned.1.call-start = ((), (), s32[]{:S(2)}) async-start(), calls=%async_computation.15 | async-start | bytes 1327104 | tf_op jit(solution)/shard_map/all_gather | solution.py:575
  258.9 62.6 %collective-permute-start.26 = (bf16[1152,1152]{1,0:T(8,128)(2,1)}, bf16[1152,1152]{1,0:T(8,128)(2,1)}, u32[]{:S(2)}, u32[]{:S(2)}) collective-permute-start(bf16[1152,1152]{1,0:T(8,128)(2,1)} %bitcast.27.mine), channel_id=1, source_target_pairs={{0,8},{8,0},{1,9},{9,1},{2,10},{10,2},{3,11},{11,3},{4,12},{12,4},... | collective-permute-start | bytes 7962632 | tf_op jit(solution)/shard_map/ppermute | solution.py:56
  377.3 40.1 %collective-permute-start.44 = (bf16[512,1152]{1,0:T(8,128)(2,1)}, bf16[512,1152]{1,0:T(8,128)(2,1)}, u32[]{:S(2)}, u32[]{:S(2)}) collective-permute-start(bf16[512,1152]{1,0:T(8,128)(2,1)} %all-gather.4.cloned.1.call-done), channel_id=1, source_target_pairs={{0,8},{8,0},{1,9},{9,1},{2,10},{10,2},{3,11},{11,3},{4,12},{12,4},... | collective-permute-start | bytes 3538952 | tf_op jit(solution)/shard_map/ppermute | solution.py:56
  419.1 50.2 %collective-permute-start.42 = (bf16[256,1152]{0,1:T(8,128)(2,1)}, bf16[256,1152]{0,1:T(8,128)(2,1)}, u32[]{:S(2)}, u32[]{:S(2)}) collective-permute-start(bf16[256,1152]{0,1:T(8,128)(2,1)} %bitcast.22), channel_id=1, source_target_pairs={{0,8},{8,0},{1,9},{9,1},{2,10},{10,2},{3,11},{11,3},{4,12},{12,4},... | collective-permute-start | bytes 1769480 | tf_op jit(solution)/shard_map/ppermute | solution.py:56
  421.2 43.8 %collective-permute-start.40 = (bf16[256,1152]{1,0:T(8,128)(2,1)}, bf16[256,1152]{1,0:T(8,128)(2,1)}, u32[]{:S(2)}, u32[]{:S(2)}) collective-permute-start(bf16[256,1152]{1,0:T(8,128)(2,1)} %add_convert_fusion.2), channel_id=1, source_target_pairs={{0,8},{8,0},{1,9},{9,1},{2,10},{10,2},{3,11},{11,3},{4,12},{12,4},... | collective-permute-start | bytes 1769480 | tf_op jit(solution)/shard_map/ppermute | solution.py:56
  493.2 97.1 %all-gather.6.cloned.1.call-start = ((), (), s32[]{:S(2)}) async-start(), calls=%async_computation.18 | async-start | bytes 2985984 | tf_op jit(solution)/shard_map/all_gather | solution.py:739
  502.5 45.2 %collective-permute-start.49 = (bf16[144,3200]{1,0:T(8,128)(2,1)}, bf16[144,3200]{1,0:T(8,128)(2,1)}, u32[]{:S(2)}, u32[]{:S(2)}) collective-permute-start(bf16[144,3200]{1,0:T(8,128)(2,1)} %constant_dynamic-slice_fusion.12), channel_id=1, source_target_pairs={{0,2},{2,4},{4,6},{6,0},{1,3},{3,5},{5,7},{7,1},{8,10},{10,12},{12... | collective-permute-start | bytes 2764808 | tf_op jit(solution)/shard_map/ppermute | solution.py:56
  608.6 41.5 %collective-permute-start.56 = (bf16[144,3200]{1,0:T(8,128)(2,1)}, bf16[144,3200]{1,0:T(8,128)(2,1)}, u32[]{:S(2)}, u32[]{:S(2)}) collective-permute-start(bf16[144,3200]{1,0:T(8,128)(2,1)} %get-tuple-element.317), channel_id=1, source_target_pairs={{0,2},{2,4},{4,6},{6,0},{1,3},{3,5},{5,7},{7,1},{8,10},{10,12},{12... | collective-permute-start | bytes 2764808 | tf_op jit(solution)/shard_map/ppermute | solution.py:56
  609.8 40.3 %collective-permute-start.57 = (bf16[144,3200]{1,0:T(8,128)(2,1)}, bf16[144,3200]{1,0:T(8,128)(2,1)}, u32[]{:S(2)}, u32[]{:S(2)}) collective-permute-start(bf16[144,3200]{1,0:T(8,128)(2,1)} %get-tuple-element.316), channel_id=1, source_target_pairs={{0,1},{1,0},{2,3},{3,2},{4,5},{5,4},{6,7},{7,6},{8,9},{9,8},{10,11... | collective-permute-start | bytes 2764808 | tf_op jit(solution)/shard_map/ppermute | solution.py:56
  610.1 39.9 %collective-permute-start.58 = (bf16[144,3200]{1,0:T(8,128)(2,1)}, bf16[144,3200]{1,0:T(8,128)(2,1)}, u32[]{:S(2)}, u32[]{:S(2)}) collective-permute-start(bf16[144,3200]{1,0:T(8,128)(2,1)} %get-tuple-element.315), channel_id=1, source_target_pairs={{0,6},{2,0},{4,2},{6,4},{1,7},{3,1},{5,3},{7,5},{8,14},{10,8},{12,... | collective-permute-start | bytes 2764808 | tf_op jit(solution)/shard_map/ppermute | solution.py:56
  627.8 81.7 %reduce-scatter.11.cloned.1.call-start = ((), (), s32[]{:S(2)}) async-start(), calls=%async_computation.17 | async-start | bytes 737280 | tf_op jit(solution)/shard_map/reduce_scatter | solution.py:468
  642.7 103.7 %reduce-scatter.9.cloned.1.call-start = ((), (), s32[]{:S(2)}) async-start(), calls=%async_computation.16 | async-start | bytes 737280 | tf_op jit(solution)/shard_map/reduce_scatter | solution.py:468
  689.1 60.5 %reduce-scatter.13.cloned.1.call-start = ((), (), s32[]{:S(2)}) async-start(), calls=%async_computation.19 | async-start | bytes 1228800
  (182 other events, 2313.5 us)
Sparse Core Ops, SparseCore 0:
  41.6 57.9 reduce-scatter.6
  209.0 53.1 all-gather.3
  509.0 27.2 all-gather.5
  642.8 17.4 reduce-scatter.10
  689.2 16.5 reduce-scatter.8
  712.2 23.6 reduce-scatter.12

commit v4 on v3

--- a/solution.py
+++ b/solution.py
@@ -107,14 +107,17 @@
     return sum([p.astype(f32) for p in parts], chunk(0, 0).astype(f32))
 
 
-def every_peer(x):
+def every_peer(x, axes=FS):
     copies = jnp.broadcast_to(x[None], (8, *x.shape)).reshape(8 * x.shape[0], x.shape[1])
-    return lax.all_to_all(copies, FS, 0, 0, tiled=True)
-
-
-def peers_sum(x):
-    parts = lax.all_to_all(x, FS, 0, 0, tiled=True)
-    return jnp.sum(parts.reshape(8, -1, x.shape[1]).astype(f32), axis=0)
+    return lax.all_to_all(copies, axes, 0, 0, tiled=True)
+
+
+def peers_parts(x, axes=FS):
+    return lax.all_to_all(x, axes, 0, 0, tiled=True)
+
+
+def sum_parts(parts):
+    return jnp.sum(parts.reshape(8, -1, parts.shape[1]).astype(f32), axis=0)
 
 
 def reduce_z(far, minus, plus):
@@ -131,62 +134,37 @@
     return ((lax.axis_index("y") + dy) % 4) * 2 + (lax.axis_index("xl") ^ dx)
 
 
-def place(pieces, outs):
-    arrays, index = [], {}
-
-    def number(x):
-        if id(x) not in index:
-            index[id(x)] = len(arrays)
-            arrays.append(x)
-        return index[id(x)]
-
-    block = sum(rows for _, _, rows, p, _ in pieces if p == NEAR[0])
-    table, copies = [], []
-    for source, first, rows, p, off in pieces:
-        pair = source if isinstance(source, tuple) else (source, source)
-        pair = tuple(number(x) for x in pair)
-        for o, parts in enumerate(outs):
-            for side, c0, cols, to in parts:
-                copies.append((pair, side, first, rows, len(table), off, o, c0, cols, to))
-        table.append(peer(*p))
-    n_in, n_out = len(arrays), len(outs)
-    widths = [sum(cols for _, _, cols, _ in parts) for parts in outs]
-
-    def body(where, core, *refs):
-        ins, targets, sem = refs[:n_in], refs[n_in : n_in + n_out], refs[-1]
-
-        def run(this):
-            started = []
-            for k, (pair, side, first, rows, t, off, o, c0, cols, to) in enumerate(copies):
-                src = ins[pair[0] if side == this else pair[1]]
-                row = pl.multiple_of(where[t] * block + off, 16)
-                one = pltpu.make_async_copy(
-                    src.at[pl.ds(first, rows), pl.ds(c0, cols)],
-                    targets[o].at[pl.ds(row, rows), pl.ds(to, cols)],
-                    sem.at[k],
-                )
-                one.start()
-                started.append(one)
-            for one in started:
-                one.wait()
-
-        @pl.when(core[0] == 0)
-        def _():
-            run(0)
-
-        @pl.when(core[0] != 0)
-        def _():
-            run(1)
-
-    smem = pl.BlockSpec(memory_space=pltpu.SMEM)
+def place(own, first, second, third):
+    lo = third[0].shape[0]
+    rows, cols = own.shape
+    pieces = [(x, p, 0) for x, p in zip((own, *first), NEAR)]
+    pieces += [(x, p, 0) for x, p in zip(second, NEXT)]
+    pieces += [(third[0], LAST, 0), (third[1], LAST, lo)]
+    count = len(pieces)
+
+    def body(where, *refs):
+        ins, out, sem = refs[:count], refs[count], refs[-1]
+        started = []
+        for k, (x, _, off) in enumerate(pieces):
+            row = pl.multiple_of(where[k] * rows + off, 16)
+            one = pltpu.make_async_copy(ins[k], out.at[pl.ds(row, x.shape[0])], sem.at[k])
+            one.start()
+            started.append(one)
+        for one in started:
+            one.wait()
+
     return pl.pallas_call(
         body,
-        in_specs=[smem, smem] + [pl.BlockSpec(memory_space=pl.ANY)] * n_in,
-        out_specs=[pl.BlockSpec(memory_space=pltpu.VMEM)] * n_out,
-        out_shape=[jax.ShapeDtypeStruct((8 * block, w), bf16) for w in widths],
-        scratch_shapes=[pltpu.SemaphoreType.DMA((len(copies),))],
+        in_specs=[pl.BlockSpec(memory_space=pltpu.SMEM)]
+        + [pl.BlockSpec(memory_space=pl.ANY)] * count,
+        out_specs=pl.BlockSpec(memory_space=pltpu.VMEM),
+        out_shape=jax.ShapeDtypeStruct((8 * rows, cols), own.dtype),
+        scratch_shapes=[pltpu.SemaphoreType.DMA((count,))],
         compiler_params=params(),
-    )(jnp.stack(table).astype(jnp.int32), lax.axis_index("c").astype(jnp.int32)[None], *arrays)
+    )(
+        jnp.stack([peer(*p) for _, p, _ in pieces]).astype(jnp.int32),
+        *[x for x, _, _ in pieces],
+    )
 
 
 def self_forward_body(seg_q, seg_k, q, kv, out, total):
@@ -564,39 +542,29 @@
     normed_one = normed_one.astype(bf16)
     n01, n10, n30 = gather_first(normed_one)
 
+    packed = jnp.concatenate(
+        [
+            jnp.concatenate([w[:, SHARD * k : SHARD * (k + 1)] for k in range(8)], axis=0)
+            for w in (w_query, w_key, w_value)
+        ],
+        axis=1,
+    )
+    heads_w = peers_parts(packed)
+    n01, n10, heads_w = lax.optimization_barrier((n01, n10, heads_w))
+    n31, n20, n11 = gather_second(n01, n10)
+
     grad_out = cotangent[0]
     grad_mlp = grad_out.astype(bf16)
     mlp_minus, mlp_plus = shift(grad_mlp, "z", 1), shift(grad_mlp, "z", -1)
 
-    text_own = jnp.pad(after(text_states[0], normed_one), ((0, TXT_OWN - CAP_TOK), (0, 0)))
+    text_own = jnp.pad(after(text_states[0], heads_w), ((0, TXT_OWN - CAP_TOK), (0, 0)))
     text_columns = lax.all_to_all(text_own, FS, split_axis=1, concat_axis=0, tiled=True)
     context_part = dot_nn(text_columns, w_text).astype(bf16)
     context_own = lax.psum_scatter(context_part, FS, scatter_dimension=0, tiled=True)
     context = lax.all_gather(context_own, FS, axis=0, tiled=True)
 
-    packed = jnp.concatenate(
-        [
-            jnp.concatenate([w[:, SHARD * k : SHARD * (k + 1)] for k in range(8)], axis=0)
-            for w in (w_query, w_key, w_value)
-        ],
-        axis=1,
-    )
-    heads_w = lax.all_to_all(after(packed, context_part), FS, 0, 0, tiled=True)
-
-    n31, n20, n11 = gather_second(n01, n10)
+    n31, n11, context_part = lax.optimization_barrier((n31, n11, context_part))
     n21 = gather_third(n31, n11)
-    lo = n21[0].shape[0]
-    (normed_all,) = place(
-        [(x, 0, TOK, p, 0) for x, p in zip((normed_one, n01, n10, n30), NEAR)]
-        + [(x, 0, TOK, p, 0) for x, p in zip((n31, n20, n11), NEXT)]
-        + [(n21[0], 0, lo, LAST, 0), (n21[1], 0, TOK - lo, LAST, lo)],
-        [[(0, 0, D, 0)]],
-    )
-    far_lo = shift(halves(mlp_minus)[0], "z", 1)
-    far_hi = shift(halves(mlp_plus)[1], "z", -1)
-    mlp_far = jnp.concatenate([far_lo, far_hi], axis=0)
-    mlp_near = jnp.concatenate([mlp_minus, mlp_plus], axis=0)
-
     blank = jnp.zeros((D, SLOT - HEAD), bf16)
     heads_w = jnp.concatenate(
         [
@@ -607,11 +575,17 @@
         ],
         axis=1,
     )
-
+    normed_all = place(normed_one, (n01, n10, n30), (n31, n20, n11), n21)
+    mlp_far = jnp.concatenate(
+        [shift(halves(mlp_minus)[0], "z", 1), shift(halves(mlp_plus)[1], "z", -1)], axis=0
+    )
+    mlp_near = jnp.concatenate([mlp_minus, mlp_plus], axis=0)
+
+    first_mine = every_peer(after(jnp.where(first_core, w_out, c_query), context_part))
     pack = jnp.where(
         first_core,
-        jnp.concatenate([w_out, c_key, c_out[:, :WIN]], axis=1),
-        jnp.concatenate([c_query, c_value, c_out[:, STEP:]], axis=1),
+        jnp.concatenate([c_key, c_out[:, :WIN]], axis=1),
+        jnp.concatenate([c_value, c_out[:, STEP:]], axis=1),
     )
     pack = after(pack, normed_all)
     g01, g10, g30 = gather_first(pack)
@@ -619,30 +593,23 @@
     seg_col, seg_row = segment[:, None], segment[None, :]
     qkv = dot_nn(after(normed_all, context_own, mlp_far), heads_w).astype(bf16)
     head0, total0 = self_forward(0, seg_col, seg_row, qkv)
-    g01, g10, g30, head0 = lax.optimization_barrier((g01, g10, g30, head0))
+    g01, g10, g30, first_mine, head0 = lax.optimization_barrier(
+        (g01, g10, g30, first_mine, head0)
+    )
+    first_other = shift(first_mine, "c", 1)
     g31, g20, g11 = gather_second(g01, g10)
-    near_mine = jnp.concatenate([pack, g01, g10, g30], axis=0)
-    near_other = shift(near_mine, "c", 1)
     head1, total1 = self_forward(1, seg_col, seg_row, after(qkv, head0))
     attended = lax.all_to_all(
         jnp.concatenate([head0, head1], axis=1), FS, split_axis=0, concat_axis=1, tiled=True
     )
-    g31, g20, g11, attended = lax.optimization_barrier((g31, g20, g11, attended))
-    g21 = gather_third(g31, g11)
-    next_mine = jnp.concatenate([g31, g20, g11], axis=0)
-    next_other = shift(next_mine, "c", 1)
-    last_other = [shift(x, "c", 1) for x in g21]
-    lo = g21[0].shape[0]
-    square_pieces = (
-        [((near_mine, near_other), SHARD * k, SHARD, p, 0) for k, p in enumerate(NEAR)]
-        + [((next_mine, next_other), SHARD * k, SHARD, p, 0) for k, p in enumerate(NEXT)]
-        + [
-            ((g21[0], last_other[0]), 0, lo, LAST, 0),
-            ((g21[1], last_other[1]), 0, SHARD - lo, LAST, lo),
-        ]
-    )
-    full_out, full_cquery = place(square_pieces, [[(0, 0, D, 0)], [(1, 0, D, 0)]])
+    g31, g20, g11, first_other, attended = lax.optimization_barrier(
+        (g31, g20, g11, first_other, attended)
+    )
+    square_mine = place(pack, (g01, g10, g30), (g31, g20, g11), gather_third(g31, g11))
+    square_other = shift(square_mine, "c", 1)
+    full_out = jnp.where(first_core, first_mine, first_other)
     after_self = rows_in + dot_nn(attended, full_out)
+    full_cquery = jnp.where(first_core, first_other, first_mine)
 
     up_own = jnp.concatenate(
         [
@@ -655,20 +622,21 @@
     hidden_mine = every_peer(after(hidden_own, attended))
     hidden_other = shift(hidden_mine, "c", 1)
 
-    full_ckey, full_cvalue, full_cout = place(
-        square_pieces,
-        [
-            [(0, D, D, 0)],
-            [(1, D, D, 0)],
-            [(0, 2 * D, WIN, 0), (1, 2 * D + 128, STEP, WIN)],
-        ],
-    )
     normed_two, pull_two = jax.vjp(norm_layer, after_self, ln2_gain, ln2_bias)
     normed_two = normed_two.astype(bf16)
     cross_query = dot_nn(normed_two, full_cquery).astype(bf16)
-    context = after(context, after_self)
-    cross_key = dot_nn(context, full_ckey).astype(bf16)
-    cross_value = dot_nn(context, full_cvalue).astype(bf16)
+    context = after(context, after_self, hidden_mine)
+    kv_mine = dot_nn(context, square_mine[:, :D]).astype(bf16)
+    kv_other = dot_nn(context, square_other[:, :D]).astype(bf16)
+    cross_key = jnp.where(first_core, kv_mine, kv_other)
+    cross_value = jnp.where(first_core, kv_other, kv_mine)
+    full_cout = jnp.concatenate(
+        [
+            jnp.where(first_core, square_mine[:, D:], square_other[:, D:]),
+            jnp.where(first_core, square_other[:, D + 128 :], square_mine[:, D + 128 :]),
+        ],
+        axis=1,
+    )
     cross_mixed = cross_forward(
         query_caption[:, None], text_key[None, :], cross_query, cross_key, cross_value
     )
@@ -706,10 +674,7 @@
     grad_cross_branch = grad_after_cross.astype(bf16)
     grad_cross_mixed = dot_nt(grad_cross_branch, full_cout).astype(bf16)
 
-    out_minus, out_plus = reduce_z(
-        after(out_far, grad_cross_mixed), out_near[:TOK], out_near[TOK:]
-    )
-
+    hidden_parts = peers_parts(hidden_sum)
     grad_cquery_rows, grad_key_part, grad_value_part = cross_backward(
         text_key[:, None],
         query_caption[None, :],
@@ -718,58 +683,55 @@
         cross_value,
         after(grad_cross_mixed, hidden_sum),
     )
-    out_minus, out_plus = shift(out_minus, "z", -1), shift(out_plus, "z", 1)
-    hidden_grad = peers_sum(hidden_sum).astype(bf16)
-    grad_self_in, grad_ln2_gain, grad_ln2_bias = pull_two(
-        dot_nt(after(grad_cquery_rows, out_minus, out_plus), full_cquery)
-    )
-    outputs = (
-        after_cross
-        + out_own.astype(f32)
-        + out_minus.astype(f32)
-        + out_plus.astype(f32)
-    )
-    grad_after_self = grad_after_cross + grad_self_in
-    grad_self_branch = grad_after_self.astype(bf16)
-    grad_attended = dot_nt(grad_self_branch, full_out).astype(bf16)
-    grad_heads = lax.all_to_all(
-        after(grad_attended, hidden_grad), FS, split_axis=1, concat_axis=0, tiled=True
-    )
-    hidden_grad = hidden_grad + shift(hidden_grad, "xh", 1)
-    hidden_grad = lax.all_gather(hidden_grad, ("z", "c"), axis=0)
-
     square = jnp.concatenate(
         [
             window_grad(cross_mixed, grad_cross_branch),
             window_grad(normed_two, grad_cquery_rows),
-            window_grad(attended, grad_self_branch),
             window_grad(context, grad_key_part),
             window_grad(context, grad_value_part),
         ],
         axis=1,
     )
-    context_part = dot_nt(after(grad_key_part, grad_attended), full_ckey) + dot_nt(
-        after(grad_value_part, grad_attended), full_cvalue
-    )
-    context_part = context_part.astype(bf16)
-    grad_heads = after(grad_heads, square, context_part)
-    context_grad = peers_sum(after(context_part, grad_heads)).astype(bf16)
 
     def square_chunk(dy, dx):
         return row_block(square, peer(dy, dx), SHARD)
 
+    grad_cquery_rows, square, hidden_parts = lax.optimization_barrier(
+        (grad_cquery_rows, square, hidden_parts)
+    )
     s_lo, s_hi, s20 = reduce_first(square_chunk)
+    grad_self_in, grad_ln2_gain, grad_ln2_bias = pull_two(dot_nt(grad_cquery_rows, full_cquery))
+    grad_after_self = grad_after_cross + grad_self_in
+    grad_self_branch = grad_after_self.astype(bf16)
+    grad_attended = dot_nt(grad_self_branch, full_out).astype(bf16)
+    grad_heads = lax.all_to_all(grad_attended, FS, split_axis=1, concat_axis=0, tiled=True)
+
+    hidden_grad = sum_parts(hidden_parts).astype(bf16)
+    hidden_grad = hidden_grad + shift(hidden_grad, "xh", 1)
+    hidden_grad = lax.all_gather(hidden_grad, ("z", "c"), axis=0)
+    out_window = window_grad(attended, grad_self_branch)
+    grad_m = jnp.where(first_core, grad_key_part, grad_value_part)
+    grad_o = jnp.where(first_core, grad_value_part, grad_key_part)
+    grad_m, grad_o, grad_attended = lax.optimization_barrier((grad_m, grad_o, grad_attended))
+    context_part = dot_nt(grad_m, square_mine[:, :D]) + dot_nt(grad_o, square_other[:, :D])
+    grad_heads, out_window, context_part = lax.optimization_barrier(
+        (grad_heads, out_window, context_part.astype(bf16))
+    )
+    context_parts = peers_parts(context_part)
 
     grad_head0 = self_backward(0, seg_col, seg_row, total0, qkv, grad_heads)
-    s_lo, s_hi, s20, context_grad, grad_head0 = lax.optimization_barrier(
-        (s_lo, s_hi, s20, context_grad, grad_head0)
-    )
-    context_grad = every_peer(context_grad)
+    s_lo, s_hi, s20, context_parts, grad_head0 = lax.optimization_barrier(
+        (s_lo, s_hi, s20, context_parts, grad_head0)
+    )
+    out_parts = peers_parts(after(out_window, context_parts))
     s11, s31 = reduce_second(square_chunk, s_lo, s_hi)
+    out_minus, out_plus = reduce_z(after(out_far, grad_head0), out_near[:TOK], out_near[TOK:])
     grad_head1 = self_backward(1, seg_col, seg_row, total1, qkv, after(grad_heads, grad_head0))
-    s11, s31, hidden_grad, context_grad, grad_head1 = lax.optimization_barrier(
-        (s11, s31, hidden_grad, context_grad, grad_head1)
-    )
+    s11, s31, hidden_grad, out_parts, out_minus, out_plus, grad_head1 = lax.optimization_barrier(
+        (s11, s31, hidden_grad, out_parts, out_minus, out_plus, grad_head1)
+    )
+    context_grad = sum_parts(context_parts).astype(bf16)
+    context_grad = every_peer(after(context_grad, out_parts))
     square_parts = reduce_third(square_chunk, s20, s11, s31)
     grad_qkv = jnp.concatenate([grad_head0, grad_head1], axis=1)
     normed_part = dot_nt(grad_qkv, heads_w).astype(bf16)
@@ -778,7 +740,7 @@
         return row_block(normed_part, peer(dy, dx), TOK)
 
     n_lo, n_hi, n20 = reduce_first(normed_chunk)
-    grad_heads_w = dot_tn(normed_all, grad_qkv).astype(bf16)
+    grad_heads_w = dot_tn(normed_all, after(grad_qkv, normed_part)).astype(bf16)
     grad_heads_w = jnp.concatenate(
         [
             grad_heads_w[:, SLOT * (3 * h + k) : SLOT * (3 * h + k) + HEAD]
@@ -787,21 +749,25 @@
         ],
         axis=1,
     )
-    grad_qkv_w = lax.all_to_all(grad_heads_w, FS, 0, 0, tiled=True)
+    grad_qkv_w = peers_parts(after(grad_heads_w, context_grad))
+    n_lo, n_hi, *square_parts = lax.optimization_barrier((n_lo, n_hi, *square_parts))
+    n11, n31 = reduce_second(normed_chunk, n_lo, n_hi)
+    out_minus, out_plus = shift(out_minus, "z", -1), shift(out_plus, "z", 1)
+    square = reduce_last(square_chunk, *square_parts).astype(bf16)
+    square = jnp.concatenate(
+        [square[:, WIN * k : WIN * (k + 1)] for k in range(4)]
+        + [sum_parts(out_parts).astype(bf16), jnp.zeros((768 - 5 * SHARD, WIN), bf16)],
+        axis=0,
+    )
+    square = sum_over_dp(square)
+    grad_c_out, grad_c_query, grad_c_key, grad_c_value, grad_w_out = whole_columns(square, 5)
     grad_w_text = dot_tn(text_columns, context_grad).astype(bf16)
     text_part = dot_nt(context_grad, w_text).astype(bf16)
-    n_lo, n_hi, *square_parts = lax.optimization_barrier((n_lo, n_hi, *square_parts))
-    n11, n31 = reduce_second(normed_chunk, n_lo, n_hi)
-    square = reduce_last(square_chunk, *square_parts).astype(bf16)
-    square = jnp.concatenate(
-        [square[:, WIN * k : WIN * (k + 1)] for k in range(5)]
-        + [jnp.zeros((768 - 5 * SHARD, WIN), bf16)],
-        axis=0,
-    )
-    square = sum_over_dp(square)
-    grad_c_out, grad_c_query, grad_w_out, grad_c_key, grad_c_value = whole_columns(square, 5)
     grad_w_text = sum_rows_over_dp(grad_w_text)
     grad_w_up, grad_w_down = sort_hidden(hidden_grad)
+    outputs = (
+        after_cross + out_own.astype(f32) + out_minus.astype(f32) + out_plus.astype(f32)
+    )
 
     n11, n31, grad_qkv_w = lax.optimization_barrier((n11, n31, grad_qkv_w))
     grad_normed_one = reduce_last(normed_chunk, *reduce_third(normed_chunk, n20, n11, n31))
@@ -819,12 +785,20 @@
         + [jnp.zeros((512 - 3 * SHARD, D), bf16)],
         axis=0,
     )
-    grad_qkv_w = sum_rows_over_dp(grad_qkv_w)
+    half = row_block(grad_qkv_w, core, 256) + shift(
+        row_block(grad_qkv_w, 1 - core, 256), "c", 1
+    )
+    half = sum_parts(peers_parts(half, ("xh", "z"))).astype(bf16)
+    half = every_peer(half, ("xh", "z"))
+    other_half = shift(half, "c", 1)
+    grad_qkv_w = jnp.concatenate(
+        [jnp.where(first_core, half, other_half), jnp.where(first_core, other_half, half)], axis=0
+    ).astype(f32)
     grad_w_query, grad_w_key, grad_w_value = (
         grad_qkv_w[SHARD * k : SHARD * (k + 1)] for k in range(3)
     )
     grad_text = lax.all_to_all(
-        after(text_part, grad_qkv_w), FS, split_axis=0, concat_axis=1, tiled=True
+        after(text_part, half), FS, split_axis=0, concat_axis=1, tiled=True
     )
     grad_text = grad_text[:CAP_TOK].astype(f32)
     grad_rows_in, grad_ln1_gain, grad_ln1_bias = pull_one(grad_normed_one)

time: 824 us -> 864 us (1.049)
  starting transfers between devices: 160 us -> 186 us
  waiting for transfers between devices: 159 us -> 185 us
  Pallas kernels: 162 us -> 145 us
  blocking collectives: 37.1 us -> 26.1 us
  other arithmetic: 82.9 us -> 92.9 us
    all_to_all x8 -> x12, waiting for transfers between devices: 18.9 us -> 68 us  [the longest x4 39.6 us: every_peer(): return lax.all_to_all(copies, axes, 0, 0, tiled=True)]
    ppermute x81 -> x78, waiting for transfers between devices: 139 us -> 102 us  [shift(): return lax.ppermute(x, axis, [(i, (i + by) % n) for i in range(n)])]
    all_to_all x8 -> x12, starting transfers between devices: 34.8 us -> 53.3 us  [the longest x6 27 us: peers_parts(): return lax.all_to_all(x, axes, 0, 0, tiled=True)]
    pallas_call x3 -> x2, Pallas kernels: 27.1 us -> 10 us  [place(): pl.pallas_call(body, in_specs=[pl.BlockSpec(memory_space=pltpu.SMEM)] + [...]
    all_gather x3 -> x2, blocking collectives: 37.1 us -> 26.1 us  [sum_over_dp(): return lax.all_gather(part, 'z', axis=0, tiled=True)]
    ppermute x81 -> x78, starting transfers between devices: 117 us -> 122 us  [shift(): return lax.ppermute(x, axis, [(i, (i + by) % n) for i in range(n)])]
    unnamed x261 -> x240, local copies, waits for them, and re-layouts: 39.5 us -> 42 us
  transfers between devices with their start and end apart: 97 -> 97, of which waited for: 22 -> 17; matrix products, arithmetic and copies ran while one was open for 30% -> 30% of each run, Pallas kernels for 19% -> 15%
where the time goes in v4:
time: 864 us; the launch traced here: 851 us
  starting transfers between devices  186 us (22%)
  waiting for transfers between devices  185 us (21%)
  Pallas kernels  145 us (17%)
  local copies, waits for them, and re-layouts  123 us (14%)
  other arithmetic  92.9 us (11%)
  matrix products  76.9 us (9%)
  blocking collectives  26.1 us (3%)
  between operations  16.1 us (2%)
    ppermute x78, starting transfers between devices, shift(): return lax.ppermute(x, axis, [(i, (i + by) % n) for i in range(n)])  122 us
    ppermute x78, waiting for transfers between devices, shift(): return lax.ppermute(x, axis, [(i, (i + by) % n) for i in range(n)])  102 us
    unnamed x240, local copies, waits for them, and re-layouts  42 us
    all_to_all x4, waiting for transfers between devices, every_peer(): return lax.all_to_all(copies, axes, 0, 0, tiled=True)  39.6 us
    pallas_call x2, Pallas kernels, self_backward(): pl.pallas_call(functools.partial(self_backward_body, head), grid=(ROW //...  37.1 us
    pallas_call x3, Pallas kernels, mlp(): pl.pallas_call(mlp_body, grid=(n // TOK,), in_specs=[pl.BlockSpec(memory_...  28.3 us
    all_to_all x6, waiting for transfers between devices, peers_parts(): return lax.all_to_all(x, axes, 0, 0, tiled=True)  28.1 us
    dot_general x7, matrix products, dot_nn(): lax.dot_general(a, b, (((1,), (0,)), ((), ())), preferred_element_type=f32)  27.7 us
  transfers between devices with their start and end apart: 97, of which 17 were waited for; matrix products, arithmetic and copies ran while one was open for 30% of the time, Pallas kernels for 15%

profile of v4, /device:TPU:1, one launch (start us, length us, event | category | flops | bytes accessed | tf_op | source)
XLA Modules:
  0.0 850.7 jit_solution(9256552963272528138)
XLA Ops:
  31.3 20.7 %collective-permute-done.refs_1_ = bf16[256,1152]{1,0:T(8,128)(2,1)} collective-permute-done((bf16[256,1152]{1,0:T(8,128)(2,1)}, bf16[256,1152]{1,0:T(8,128)(2,1)}, u32[]{:S(2)}, u32[]{:S(2)}) %collective-permute-start) | collective-permute-done | bytes 589856 | tf_op jit(solution)/shard_map/ppermute | solution.py:56
  60.3 7.9 all-to-all-done.1
  102.9 42.8 %collective-permute-done.4.refs_6_ = bf16[256,1152]{1,0:T(8,128)(2,1)} collective-permute-done((bf16[256,1152]{1,0:T(8,128)(2,1)}, bf16[256,1152]{1,0:T(8,128)(2,1)}, u32[]{:S(2)}, u32[]{:S(2)}) %collective-permute-start.4) | collective-permute-done | bytes 589856 | tf_op jit(solution)/shard_map/ppermute | solution.py:56
  176.3 8.8 %convolution_convert_fusion.1.q.kv = bf16[2048,768]{1,0:T(8,128)(2,1)} fusion(bf16[2048,1152]{1,0:T(8,128)(2,1)} %shard_map.374, bf16[1152,768]{1,0:T(8,128)(2,1)} %concatenate.146), kind=kOutput, calls=%fused_computation.2 | convolution fusion | flops 3625451520 | bytes 9633792 | tf_op jit(solution)/shard_map/dot_general | solution.py:39
  185.1 12.1 %shard_map.375 = (bf16[2048,72]{1,0:T(8,128)(2,1)}, f32[1,2048]{1,0:T(1,128)}) custom-call(s32[2048,1]{1,0:T(8,128)} %copy.165.seg_q.seg_k, s32[1,2048]{1,0:T(1,128)} %bitcast.153, bf16[2048,768]{1,0:T(8,128)(2,1)} %convolution_convert_fusion.1.q.kv, bf16[2048,768]{1,0:T(8,128)(2,1)} %convolution_convert_fusion.1.q.kv), custom_call_target="tpu_custom_call" | custom-call | tf_op jit(solution)/shard_map/pallas_call | solution.py:182
  200.6 12.1 %shard_map.376 = (bf16[2048,72]{1,0:T(8,128)(2,1)}, f32[1,2048]{1,0:T(1,128)}) custom-call(s32[2048,1]{1,0:T(8,128)} %copy.165.seg_q.seg_k, s32[1,2048]{1,0:T(1,128)} %bitcast.154, bf16[2048,768]{1,0:T(8,128)(2,1)} %convolution_convert_fusion.1.q.kv, bf16[2048,768]{1,0:T(8,128)(2,1)} %convolution_convert_fusion.1.q.kv), custom_call_target="tpu_custom_call" | custom-call | tf_op jit(solution)/shard_map/pallas_call | solution.py:182
  230.5 10.0 %collective-permute-done.15.refs_4_ = bf16[144,1792]{1,0:T(8,128)(2,1)S(1)} collective-permute-done((bf16[144,1792]{1,0:T(8,128)(2,1)}, bf16[144,1792]{1,0:T(8,128)(2,1)S(1)}, u32[]{:S(2)}, u32[]{:S(2)}) %collective-permute-start.15) | collective-permute-done | bytes 516128 | tf_op jit(solution)/shard_map/ppermute | solution.py:56
  242.2 7.0 collective-permute-done.20.refs_8_
  275.8 39.6 %all-to-all-done.4 = bf16[8,144,1152]{2,1,0:T(8,128)(2,1)} async-done(((bf16[8,144,1152]{2,1,0:T(8,128)(2,1)}), bf16[8,144,1152]{2,1,0:T(8,128)(2,1)}, u32[]{:S(2)}, u32[]{:S(2)}) %all-to-all-start.4) | async-done | bytes 2654240 | tf_op jit(solution)/shard_map/all_to_all | solution.py:112
  315.4 10.2 %collective-permute-start.24 = (bf16[1152,1152]{1,0:T(8,128)(2,1)}, bf16[1152,1152]{1,0:T(8,128)(2,1)}, u32[]{:S(2)}, u32[]{:S(2)}) collective-permute-start(bf16[1152,1152]{1,0:T(8,128)(2,1)} %bitcast.27.mine), channel_id=1, source_target_pairs={{0,8},{8,0},{1,9},{9,1},{2,10},{10,2},{3,11},{11,3},{4,12},{12,4},... | collective-permute-start | bytes 7962632 | tf_op jit(solution)/shard_map/ppermute | solution.py:56
  334.8 11.7 %shard_map.378 = bf16[256,1152]{1,0:T(8,128)(2,1)} custom-call(s32[256,1]{1,0:T(8,128)} %copy.168.cap_q, s32[1,512]{1,0:T(1,128)} %and_select_fusion.1.cap_t, bf16[256,1152]{1,0:T(8,128)(2,1)} %convolution_convert_fusion.13.q, bf16[512,1152]{1,0:T(8,128)(2,1)} %get-tuple-element.332.k, bf16[512,1152]{1,0:T(8,128)(2,1)} %get-tuple-element.331.v), custom_call_target="tpu_custom_call" | custom-call | tf_op jit(solution)/shard_map/pallas_call | solution.py:270
  360.3 8.2 shard_map.379
  379.3 11.9 %shard_map.380 = (bf16[512,1152]{1,0:T(8,128)(2,1)}, bf16[512,1152]{1,0:T(8,128)(2,1)}, bf16[512,1152]{1,0:T(8,128)(2,1)}, bf16[512,1152]{1,0:T(8,128)(2,1)}) custom-call(s32[1]{0:T(128)} %bitcast.28.core, bf16[512,1152]{1,0:T(8,128)(2,1)} %constant_dynamic-update-slice_fusion.26.x.refs_1_, ...), custom_call_target="tpu_custom_call" | custom-call | tf_op jit(solution)/shard_map/pallas_call | solution.py:344
  393.0 8.2 shard_map.381
  422.1 12.8 %shard_map.382 = (bf16[1152,1152]{1,0:T(8,128)(2,1)}, bf16[1152,1152]{1,0:T(8,128)(2,1)}) custom-call(s32[1]{0:T(128)} %bitcast.28.core, bf16[256,1152]{1,0:T(8,128)(2,1)} %copy-done.12, bf16[512,1152]{1,0:T(8,128)(2,1)} %constant_dynamic-update-slice_fusion.26.x.refs_1_, bf16[256,1152]{1,0:T(8,128)(2,1)} %copy-done.16, ...), custom_call_target="tpu_custom_call" | custom-call | tf_op jit(solution)/shard_map/pallas_call | solution.py:385
  451.0 15.3 %shard_map.383 = (bf16[256,1152]{1,0:T(8,128)(2,1)}, bf16[512,1152]{1,0:T(8,128)(2,1)}, bf16[512,1152]{1,0:T(8,128)(2,1)}) custom-call(s32[512,1]{1,0:T(8,128)} %fusion.50.cap_t, s32[1,256]{1,0:T(1,128)} %bitcast.160, bf16[256,1152]{1,0:T(8,128)(2,1)} %convolution_convert_fusion.13.q, bf16[512,1152]{1,0:T(8,128)(2,1)} %get-tuple-element.332.k, ...), custom_call_target="tpu_custom_call" | custom-call | tf_op jit(solution)/shard_map/pallas_call | solution.py:298
  491.3 17.8 %all-to-all-done.5 = bf16[8,144,1152]{2,1,0:T(8,128)(2,1)} async-done(((bf16[8,144,1152]{2,1,0:T(8,128)(2,1)}), bf16[8,144,1152]{2,1,0:T(8,128)(2,1)}, u32[]{:S(2)}, u32[]{:S(2)}) %all-to-all-start.5) | async-done | bytes 2654240 | tf_op jit(solution)/shard_map/all_to_all | solution.py:116
  559.1 18.6 %shard_map.384 = bf16[2048,384]{1,0:T(8,128)(2,1)} custom-call(s32[2048,1]{1,0:T(8,128)} %copy.165.seg_q.seg_k, s32[1,2048]{1,0:T(1,128)} %bitcast.155, f32[1,2048]{1,0:T(1,128)} %get-tuple-element.155.total, bf16[2048,768]{1,0:T(8,128)(2,1)} %convolution_convert_fusion.1.q.kv, bf16[2048,768]{1,0:T(8,128)(2,1)} %convolution_convert_fusion.1.q.kv, ...), custom_call_target="tpu_custom_call" | custom-call | tf_op jit(solution)/shard_map/pallas_call | solution.py:233
  595.0 18.5 %shard_map.385 = bf16[2048,384]{1,0:T(8,128)(2,1)} custom-call(s32[2048,1]{1,0:T(8,128)} %copy.165.seg_q.seg_k, s32[1,2048]{1,0:T(1,128)} %bitcast.156, f32[1,2048]{1,0:T(1,128)} %get-tuple-element.166.total, bf16[2048,768]{1,0:T(8,128)(2,1)} %convolution_convert_fusion.1.q.kv, bf16[2048,768]{1,0:T(8,128)(2,1)} %convolution_convert_fusion.1.q.kv, ...), custom_call_target="tpu_custom_call" | custom-call | tf_op jit(solution)/shard_map/pallas_call | solution.py:233
  638.5 7.6 convolution_convert_fusion.2
  673.9 7.7 collective-permute-start.75
  704.4 10.3 %all-to-all-done.10 = bf16[8,144,432]{2,1,0:T(8,128)(2,1)S(1)} async-done(((bf16[8,144,432]{2,1,0:T(8,128)(2,1)}), bf16[8,144,432]{2,1,0:T(8,128)(2,1)S(1)}, u32[]{:S(2)}, u32[]{:S(2)}) %all-to-all-start.10) | async-done | bytes 995360 | tf_op jit(solution)/shard_map/all_to_all | solution.py:116
  779.2 11.7 %all_gather.19 = bf16[256,1152]{1,0:T(8,128)(2,1)} all-gather(bf16[64,1152]{1,0:T(8,128)(2,1)S(1)} %add.671), channel_id=1, replica_groups=mesh['xh'=2,'z'=4,'c'=2,'y'=4,'xl'=2] {'z'}, dimensions={0}, use_global_device_ids=true | all-gather | bytes 737280 | tf_op jit(solution)/shard_map/all_gather | solution.py:448
  806.7 14.3 %all_gather.18 = bf16[768,640]{1,0:T(8,128)(2,1)S(1)} all-gather(bf16[192,640]{1,0:T(8,128)(2,1)S(1)} %copy.181), channel_id=1, replica_groups=mesh['xh'=2,'z'=4,'c'=2,'y'=4,'xl'=2] {'z'}, dimensions={0}, use_global_device_ids=true | all-gather | bytes 1228800 | tf_op jit(solution)/shard_map/all_gather | solution.py:448
  (611 shorter events, 488.5 us)
Async XLA Ops:
  58.8 117.5 %reduce-scatter.6.cloned.1.call-start = ((), (), s32[]{:S(2)}) async-start(), calls=%async_computation.17 | async-start | bytes 1327104 | tf_op jit(solution)/shard_map/reduce_scatter | solution.py:563
  58.9 102.3 %collective-permute-start.2 = (bf16[256,1152]{1,0:T(8,128)(2,1)}, bf16[256,1152]{1,0:T(8,128)(2,1)}, u32[]{:S(2)}, u32[]{:S(2)}) collective-permute-start(bf16[256,1152]{1,0:T(8,128)(2,1)} %fusion.21.refs_0_), channel_id=1, source_target_pairs={{0,2},{2,4},{4,6},{6,0},{1,3},{3,5},{5,7},{7,1},{8,10},{10,12},{12... | collective-permute-start | bytes 1769480 | tf_op jit(solution)/shard_map/ppermute | solution.py:56
  83.5 113.8 %all-to-all-start.2 = ((bf16[8,144,1152]{2,1,0:T(8,128)(2,1)}), bf16[8,144,1152]{2,1,0:T(8,128)(2,1)}, u32[]{:S(2)}, u32[]{:S(2)}) async-start(bf16[8,144,1152]{2,1,0:T(8,128)(2,1)} %broadcast_in_dim.70), calls=%async_computation.2 | async-start | bytes 5308416 | tf_op jit(solution)/shard_map/all_to_all | solution.py:112
  88.0 57.6 %collective-permute-start.4 = (bf16[256,1152]{1,0:T(8,128)(2,1)}, bf16[256,1152]{1,0:T(8,128)(2,1)}, u32[]{:S(2)}, u32[]{:S(2)}) collective-permute-start(bf16[256,1152]{1,0:T(8,128)(2,1)} %collective-permute-done.1.refs_2_), channel_id=1, source_target_pairs={{0,1},{1,0},{2,3},{3,2},{4,5},{5,4},{6,7},{7,6},{8,9},{9,8},{10,11... | collective-permute-start | bytes 1769480 | tf_op jit(solution)/shard_map/ppermute | solution.py:56
  93.5 60.7 %collective-permute-start.3 = (bf16[256,1152]{1,0:T(8,128)(2,1)}, bf16[256,1152]{1,0:T(8,128)(2,1)}, u32[]{:S(2)}, u32[]{:S(2)}) collective-permute-start(bf16[256,1152]{1,0:T(8,128)(2,1)} %collective-permute-done.refs_1_), channel_id=1, source_target_pairs={{0,2},{2,4},{4,6},{6,0},{1,3},{3,5},{5,7},{7,1},{8,10},{10,12},{12... | collective-permute-start | bytes 1769480 | tf_op jit(solution)/shard_map/ppermute | solution.py:56
  98.5 58.2 %collective-permute-start.12 = (bf16[128,1152]{1,0:T(8,128)(2,1)}, bf16[128,1152]{1,0:T(8,128)(2,1)}, u32[]{:S(2)}, u32[]{:S(2)}) collective-permute-start(bf16[128,1152]{1,0:T(8,128)(2,1)} %slice.511), channel_id=1, source_target_pairs={{0,16},{16,32},{32,48},{48,0},{1,17},{17,33},{33,49},{49,1},{2,18}... | collective-permute-start | bytes 884744 | tf_op jit(solution)/shard_map/ppermute | solution.py:56
  100.2 59.3 %collective-permute-start.14 = (bf16[128,1152]{1,0:T(8,128)(2,1)}, bf16[128,1152]{1,0:T(8,128)(2,1)}, u32[]{:S(2)}, u32[]{:S(2)}) collective-permute-start(bf16[128,1152]{1,0:T(8,128)(2,1)} %slice.512), channel_id=1, source_target_pairs={{0,48},{16,0},{32,16},{48,32},{1,49},{17,1},{33,17},{49,33},{2,50}... | collective-permute-start | bytes 884744 | tf_op jit(solution)/shard_map/ppermute | solution.py:56
  197.3 43.2 %collective-permute-start.18 = (bf16[1152,1152]{1,0:T(8,128)(2,1)}, bf16[1152,1152]{1,0:T(8,128)(2,1)}, u32[]{:S(2)}, u32[]{:S(2)}) collective-permute-start(bf16[1152,1152]{1,0:T(8,128)(2,1)} %bitcast.14), channel_id=1, source_target_pairs={{0,8},{8,0},{1,9},{9,1},{2,10},{10,2},{3,11},{11,3},{4,12},{12,4},... | collective-permute-start | bytes 7962632 | tf_op jit(solution)/shard_map/ppermute | solution.py:56
  255.5 74.2 %collective-permute-start.21 = (bf16[1152,1792]{1,0:T(8,128)(2,1)}, bf16[1152,1792]{1,0:T(8,128)(2,1)}, u32[]{:S(2)}, u32[]{:S(2)}) collective-permute-start(bf16[1152,1792]{1,0:T(8,128)(2,1)} %shard_map.377), channel_id=1, source_target_pairs={{0,8},{8,0},{1,9},{9,1},{2,10},{10,2},{3,11},{11,3},{4,12},{12,4},... | collective-permute-start | bytes 12386312 | tf_op jit(solution)/shard_map/ppermute | solution.py:56
  261.1 54.3 %all-to-all-start.4 = ((bf16[8,144,1152]{2,1,0:T(8,128)(2,1)}), bf16[8,144,1152]{2,1,0:T(8,128)(2,1)}, u32[]{:S(2)}, u32[]{:S(2)}) async-start(bf16[8,144,1152]{2,1,0:T(8,128)(2,1)} %broadcast_in_dim.134), calls=%async_computation.5 | async-start | bytes 5308416 | tf_op jit(solution)/shard_map/all_to_all | solution.py:112
  265.5 60.1 %all-gather.4.cloned.1.call-start = ((), (), s32[]{:S(2)}) async-start(), calls=%async_computation.18 | async-start | bytes 1327104 | tf_op jit(solution)/shard_map/all_gather | solution.py:564
  315.4 44.8 %collective-permute-start.24 = (bf16[1152,1152]{1,0:T(8,128)(2,1)}, bf16[1152,1152]{1,0:T(8,128)(2,1)}, u32[]{:S(2)}, u32[]{:S(2)}) collective-permute-start(bf16[1152,1152]{1,0:T(8,128)(2,1)} %bitcast.27.mine), channel_id=1, source_target_pairs={{0,8},{8,0},{1,9},{9,1},{2,10},{10,2},{3,11},{11,3},{4,12},{12,4},... | collective-permute-start | bytes 7962632 | tf_op jit(solution)/shard_map/ppermute | solution.py:56
  418.6 60.8 %collective-permute-start.34 = (bf16[256,1152]{1,0:T(8,128)(2,1)}, bf16[256,1152]{1,0:T(8,128)(2,1)}, u32[]{:S(2)}, u32[]{:S(2)}) collective-permute-start(bf16[256,1152]{1,0:T(8,128)(2,1)} %copy-done.48), channel_id=1, source_target_pairs={{0,8},{8,0},{1,9},{9,1},{2,10},{10,2},{3,11},{11,3},{4,12},{12,4},... | collective-permute-start | bytes 1769480 | tf_op jit(solution)/shard_map/ppermute | solution.py:56
  422.1 118.1 %collective-permute-start.42 = (bf16[256,1152]{0,1:T(8,128)(2,1)}, bf16[256,1152]{0,1:T(8,128)(2,1)}, u32[]{:S(2)}, u32[]{:S(2)}) collective-permute-start(bf16[256,1152]{0,1:T(8,128)(2,1)} %bitcast.22), channel_id=1, source_target_pairs={{0,8},{8,0},{1,9},{9,1},{2,10},{10,2},{3,11},{11,3},{4,12},{12,4},... | collective-permute-start | bytes 1769480 | tf_op jit(solution)/shard_map/ppermute | solution.py:56
  471.7 37.5 %all-to-all-start.5 = ((bf16[8,144,1152]{2,1,0:T(8,128)(2,1)}), bf16[8,144,1152]{2,1,0:T(8,128)(2,1)}, u32[]{:S(2)}, u32[]{:S(2)}) async-start(bf16[8,144,1152]{2,1,0:T(8,128)(2,1)} %bitcast.131), calls=%async_computation.6 | async-start | bytes 5308416 | tf_op jit(solution)/shard_map/all_to_all | solution.py:116
  524.2 95.2 %all-gather.6.cloned.1.call-start = ((), (), s32[]{:S(2)}) async-start(), calls=%async_computation.20 | async-start | bytes 2985984 | tf_op jit(solution)/shard_map/all_gather | solution.py:711
  526.3 51.4 %collective-permute-start.41 = (bf16[144,2560]{1,0:T(8,128)(2,1)}, bf16[144,2560]{1,0:T(8,128)(2,1)}, u32[]{:S(2)}, u32[]{:S(2)}) collective-permute-start(bf16[144,2560]{1,0:T(8,128)(2,1)} %constant_dynamic-slice_fusion.13), channel_id=1, source_target_pairs={{0,2},{2,4},{4,6},{6,0},{1,3},{3,5},{5,7},{7,1},{8,10},{10,12},{12... | collective-permute-start | bytes 2211848 | tf_op jit(solution)/shard_map/ppermute | solution.py:56
  581.1 38.3 %all-to-all-start.8 = ((bf16[8,144,640]{2,1,0:T(8,128)(2,1)}), bf16[8,144,640]{2,1,0:T(8,128)(2,1)}, u32[]{:S(2)}, u32[]{:S(2)}) async-start(bf16[8,144,640]{2,1,0:T(8,128)(2,1)} %bitcast.147), calls=%async_computation.9 | async-start | bytes 2949120 | tf_op jit(solution)/shard_map/all_to_all | solution.py:116
  623.4 48.1 %collective-permute-start.54 = (bf16[144,2560]{1,0:T(8,128)(2,1)}, bf16[144,2560]{1,0:T(8,128)(2,1)}, u32[]{:S(2)}, u32[]{:S(2)}) collective-permute-start(bf16[144,2560]{1,0:T(8,128)(2,1)} %get-tuple-element.315), channel_id=1, source_target_pairs={{0,2},{2,4},{4,6},{6,0},{1,3},{3,5},{5,7},{7,1},{8,10},{10,12},{12... | collective-permute-start | bytes 2211848 | tf_op jit(solution)/shard_map/ppermute | solution.py:56
  623.4 48.1 %collective-permute-start.55 = (bf16[144,2560]{1,0:T(8,128)(2,1)}, bf16[144,2560]{1,0:T(8,128)(2,1)}, u32[]{:S(2)}, u32[]{:S(2)}) collective-permute-start(bf16[144,2560]{1,0:T(8,128)(2,1)} %get-tuple-element.314), channel_id=1, source_target_pairs={{0,1},{1,0},{2,3},{3,2},{4,5},{5,4},{6,7},{7,6},{8,9},{9,8},{10,11... | collective-permute-start | bytes 2211848 | tf_op jit(solution)/shard_map/ppermute | solution.py:56
  625.4 46.2 %collective-permute-start.56 = (bf16[144,2560]{1,0:T(8,128)(2,1)}, bf16[144,2560]{1,0:T(8,128)(2,1)}, u32[]{:S(2)}, u32[]{:S(2)}) collective-permute-start(bf16[144,2560]{1,0:T(8,128)(2,1)} %get-tuple-element.313), channel_id=1, source_target_pairs={{0,6},{2,0},{4,2},{6,4},{1,7},{3,1},{5,3},{7,5},{8,14},{10,8},{12,... | collective-permute-start | bytes 2211848 | tf_op jit(solution)/shard_map/ppermute | solution.py:56
  638.5 126.3 %reduce-scatter.8.cloned.1.call-start = ((), (), s32[]{:S(2)}) async-start(), calls=%async_computation.19 | async-start | bytes 737280 | tf_op jit(solution)/shard_map/reduce_scatter | solution.py:446
  671.4 44.7 %collective-permute-start.51 = (bf16[256,1152]{1,0:T(8,128)(2,1)}, bf16[256,1152]{1,0:T(8,128)(2,1)}, u32[]{:S(2)}, u32[]{:S(2)}) collective-permute-start(bf16[256,1152]{1,0:T(8,128)(2,1)} %constant_dynamic-slice_fusion.10), channel_id=1, source_target_pairs={{0,2},{2,4},{4,6},{6,0},{1,3},{3,5},{5,7},{7,1},{8,10},{10,12},{12... | collective-permute-start | bytes 1769480 | tf_op jit(solution)/shard_map/ppermute | solution.py:56
  698.1 77.4 %reduce-scatter.10.cloned.1.call-start = ((), (), s32[]{:S(2)}) async-start(), calls=%async_computation.21 | async-start | bytes 1228800
  (174 other events, 1889.3 us)
Sparse Core Ops, SparseCore 0:
  70.2 48.9 reduce-scatter.5
  268.0 53.1 all-gather.3
  544.8 24.8 all-gather.5
  688.5 19.5 reduce-scatter.7
  710.9 23.2 reduce-scatter.9

commit v5 on v4

--- a/solution.py
+++ b/solution.py
@@ -108,7 +108,8 @@
 
 
 def every_peer(x, axes=FS):
-    copies = jnp.broadcast_to(x[None], (8, *x.shape)).reshape(8 * x.shape[0], x.shape[1])
+    n = lax.axis_size(axes)
+    copies = jnp.broadcast_to(x[None], (n, *x.shape)).reshape(n * x.shape[0], x.shape[1])
     return lax.all_to_all(copies, axes, 0, 0, tiled=True)
 
 
@@ -165,6 +166,39 @@
         jnp.stack([peer(*p) for _, p, _ in pieces]).astype(jnp.int32),
         *[x for x, _, _ in pieces],
     )
+
+
+def pack_heads_body(wq, wk, wv, out):
+    for p in range(8):
+        rows = slice(SHARD * p, SHARD * (p + 1))
+        out[rows, :] = jnp.concatenate([w[:, rows] for w in (wq, wk, wv)], axis=1)
+
+
+def pack_heads(*weights):
+    return pl.pallas_call(
+        pack_heads_body,
+        out_shape=jax.ShapeDtypeStruct((D, 3 * SHARD), bf16),
+        compiler_params=params(),
+    )(*weights)
+
+
+def spread_heads_body(x, out):
+    blank = jnp.zeros((D, SLOT - HEAD), bf16)
+    for h in range(2):
+        for k in range(3):
+            first = SHARD * k + HEAD * h
+            slot = SLOT * (3 * h + k)
+            out[:, slot : slot + SLOT] = jnp.concatenate(
+                [x[:, first : first + HEAD], blank], axis=1
+            )
+
+
+def spread_heads(x):
+    return pl.pallas_call(
+        spread_heads_body,
+        out_shape=jax.ShapeDtypeStruct((D, 6 * SLOT), bf16),
+        compiler_params=params(),
+    )(x)
 
 
 def self_forward_body(seg_q, seg_k, q, kv, out, total):
@@ -445,7 +479,7 @@
 def sum_over_dp(x):
     part = lax.psum_scatter(x, "z", scatter_dimension=0, tiled=True)
     part = part + shift(part, "xh", 1)
-    return lax.all_gather(part, "z", axis=0, tiled=True)
+    return every_peer(part, "z")
 
 
 def whole_columns(mine, count):
@@ -542,46 +576,27 @@
     normed_one = normed_one.astype(bf16)
     n01, n10, n30 = gather_first(normed_one)
 
-    packed = jnp.concatenate(
-        [
-            jnp.concatenate([w[:, SHARD * k : SHARD * (k + 1)] for k in range(8)], axis=0)
-            for w in (w_query, w_key, w_value)
-        ],
-        axis=1,
-    )
-    heads_w = peers_parts(packed)
-    n01, n10, heads_w = lax.optimization_barrier((n01, n10, heads_w))
+    heads_w = peers_parts(pack_heads(after(w_query, normed_one), w_key, w_value))
+    n01, n10, n30 = lax.optimization_barrier((n01, n10, n30))
     n31, n20, n11 = gather_second(n01, n10)
+    n31, n20, n11, heads_w = lax.optimization_barrier((n31, n20, n11, heads_w))
+    n21 = gather_third(n31, n11)
+
+    text_own = jnp.pad(after(text_states[0], n11), ((0, TXT_OWN - CAP_TOK), (0, 0)))
+    text_columns = lax.all_to_all(text_own, FS, split_axis=1, concat_axis=0, tiled=True)
+    heads_w = spread_heads(heads_w)
+    normed_all = place(
+        after(normed_one, text_columns), (n01, n10, n30), (n31, n20, n11), n21
+    )
+    context_part = dot_nn(after(text_columns, normed_all), w_text).astype(bf16)
+    context_own = lax.psum_scatter(context_part, FS, scatter_dimension=0, tiled=True)
 
     grad_out = cotangent[0]
     grad_mlp = grad_out.astype(bf16)
-    mlp_minus, mlp_plus = shift(grad_mlp, "z", 1), shift(grad_mlp, "z", -1)
-
-    text_own = jnp.pad(after(text_states[0], heads_w), ((0, TXT_OWN - CAP_TOK), (0, 0)))
-    text_columns = lax.all_to_all(text_own, FS, split_axis=1, concat_axis=0, tiled=True)
-    context_part = dot_nn(text_columns, w_text).astype(bf16)
-    context_own = lax.psum_scatter(context_part, FS, scatter_dimension=0, tiled=True)
-    context = lax.all_gather(context_own, FS, axis=0, tiled=True)
-
-    n31, n11, context_part = lax.optimization_barrier((n31, n11, context_part))
-    n21 = gather_third(n31, n11)
-    blank = jnp.zeros((D, SLOT - HEAD), bf16)
-    heads_w = jnp.concatenate(
-        [
-            part
-            for h in range(2)
-            for k in range(3)
-            for part in (heads_w[:, SHARD * k + HEAD * h : SHARD * k + HEAD * (h + 1)], blank)
-        ],
-        axis=1,
-    )
-    normed_all = place(normed_one, (n01, n10, n30), (n31, n20, n11), n21)
-    mlp_far = jnp.concatenate(
-        [shift(halves(mlp_minus)[0], "z", 1), shift(halves(mlp_plus)[1], "z", -1)], axis=0
-    )
-    mlp_near = jnp.concatenate([mlp_minus, mlp_plus], axis=0)
-
-    first_mine = every_peer(after(jnp.where(first_core, w_out, c_query), context_part))
+    grad_sent = after(grad_mlp, normed_all)
+    mlp_minus, mlp_plus = shift(grad_sent, "z", 1), shift(grad_sent, "z", -1)
+
+    first_mine = every_peer(after(jnp.where(first_core, w_out, c_query), normed_all))
     pack = jnp.where(
         first_core,
         jnp.concatenate([c_key, c_out[:, :WIN]], axis=1),
@@ -591,20 +606,26 @@
     g01, g10, g30 = gather_first(pack)
 
     seg_col, seg_row = segment[:, None], segment[None, :]
-    qkv = dot_nn(after(normed_all, context_own, mlp_far), heads_w).astype(bf16)
+    qkv = dot_nn(after(normed_all, context_part), heads_w).astype(bf16)
     head0, total0 = self_forward(0, seg_col, seg_row, qkv)
-    g01, g10, g30, first_mine, head0 = lax.optimization_barrier(
-        (g01, g10, g30, first_mine, head0)
-    )
-    first_other = shift(first_mine, "c", 1)
+    g01, g10, g30, mlp_minus, mlp_plus, head0 = lax.optimization_barrier(
+        (g01, g10, g30, mlp_minus, mlp_plus, head0)
+    )
     g31, g20, g11 = gather_second(g01, g10)
     head1, total1 = self_forward(1, seg_col, seg_row, after(qkv, head0))
+    g31, g20, g11, first_mine, head1 = lax.optimization_barrier(
+        (g31, g20, g11, first_mine, head1)
+    )
+    first_other = shift(first_mine, "c", 1)
     attended = lax.all_to_all(
         jnp.concatenate([head0, head1], axis=1), FS, split_axis=0, concat_axis=1, tiled=True
     )
-    g31, g20, g11, first_other, attended = lax.optimization_barrier(
-        (g31, g20, g11, first_other, attended)
-    )
+    mlp_far = jnp.concatenate(
+        [shift(halves(mlp_minus)[0], "z", 1), shift(halves(mlp_plus)[1], "z", -1)], axis=0
+    )
+    mlp_near = jnp.concatenate([mlp_minus, mlp_plus], axis=0)
+    attended, context_own = lax.optimization_barrier((attended, context_own))
+    context = every_peer(context_own)
     square_mine = place(pack, (g01, g10, g30), (g31, g20, g11), gather_third(g31, g11))
     square_other = shift(square_mine, "c", 1)
     full_out = jnp.where(first_core, first_mine, first_other)
@@ -619,13 +640,12 @@
         axis=1,
     )
     hidden_own = jnp.where(first_core, up_own, row_block(w_down, quarter, SHARD))
-    hidden_mine = every_peer(after(hidden_own, attended))
-    hidden_other = shift(hidden_mine, "c", 1)
+    hidden_mine = every_peer(after(hidden_own, context))
 
     normed_two, pull_two = jax.vjp(norm_layer, after_self, ln2_gain, ln2_bias)
     normed_two = normed_two.astype(bf16)
     cross_query = dot_nn(normed_two, full_cquery).astype(bf16)
-    context = after(context, after_self, hidden_mine)
+    context = after(context, cross_query)
     kv_mine = dot_nn(context, square_mine[:, :D]).astype(bf16)
     kv_other = dot_nn(context, square_other[:, :D]).astype(bf16)
     cross_key = jnp.where(first_core, kv_mine, kv_other)
@@ -638,14 +658,19 @@
         axis=1,
     )
     cross_mixed = cross_forward(
-        query_caption[:, None], text_key[None, :], cross_query, cross_key, cross_value
+        query_caption[:, None],
+        text_key[None, :],
+        after(cross_query, mlp_far),
+        cross_key,
+        cross_value,
     )
     after_cross = after_self + dot_nn(cross_mixed, full_cout)
 
     normed_three, pull_three = jax.vjp(norm_layer, after_cross, ln3_gain, ln3_bias)
     normed_three = normed_three.astype(bf16)
     three_minus, three_plus = shift(normed_three, "z", 1), shift(normed_three, "z", -1)
-    weights = (hidden_mine, hidden_other)
+    hidden_mine = after(hidden_mine, cross_mixed)
+    weights = (hidden_mine, shift(hidden_mine, "c", 1))
     out_own, act_own, pre_own, back_own = mlp(core_index, normed_three, grad_mlp, *weights)
     three_minus, three_plus, out_own = lax.optimization_barrier(
         (three_minus, three_plus, out_own)
@@ -674,7 +699,6 @@
     grad_cross_branch = grad_after_cross.astype(bf16)
     grad_cross_mixed = dot_nt(grad_cross_branch, full_cout).astype(bf16)
 
-    hidden_parts = peers_parts(hidden_sum)
     grad_cquery_rows, grad_key_part, grad_value_part = cross_backward(
         text_key[:, None],
         query_caption[None, :],
@@ -683,56 +707,52 @@
         cross_value,
         after(grad_cross_mixed, hidden_sum),
     )
-    square = jnp.concatenate(
-        [
-            window_grad(cross_mixed, grad_cross_branch),
-            window_grad(normed_two, grad_cquery_rows),
-            window_grad(context, grad_key_part),
-            window_grad(context, grad_value_part),
-        ],
-        axis=1,
-    )
-
-    def square_chunk(dy, dx):
-        return row_block(square, peer(dy, dx), SHARD)
-
-    grad_cquery_rows, square, hidden_parts = lax.optimization_barrier(
-        (grad_cquery_rows, square, hidden_parts)
-    )
-    s_lo, s_hi, s20 = reduce_first(square_chunk)
     grad_self_in, grad_ln2_gain, grad_ln2_bias = pull_two(dot_nt(grad_cquery_rows, full_cquery))
     grad_after_self = grad_after_cross + grad_self_in
     grad_self_branch = grad_after_self.astype(bf16)
     grad_attended = dot_nt(grad_self_branch, full_out).astype(bf16)
     grad_heads = lax.all_to_all(grad_attended, FS, split_axis=1, concat_axis=0, tiled=True)
 
-    hidden_grad = sum_parts(hidden_parts).astype(bf16)
-    hidden_grad = hidden_grad + shift(hidden_grad, "xh", 1)
-    hidden_grad = lax.all_gather(hidden_grad, ("z", "c"), axis=0)
-    out_window = window_grad(attended, grad_self_branch)
-    grad_m = jnp.where(first_core, grad_key_part, grad_value_part)
-    grad_o = jnp.where(first_core, grad_value_part, grad_key_part)
-    grad_m, grad_o, grad_attended = lax.optimization_barrier((grad_m, grad_o, grad_attended))
+    key_rows, value_rows, query_rows, _ = lax.optimization_barrier(
+        (grad_key_part, grad_value_part, grad_cquery_rows, grad_attended)
+    )
+    square = jnp.concatenate(
+        [
+            window_grad(cross_mixed, grad_cross_branch),
+            window_grad(normed_two, query_rows),
+            window_grad(context, key_rows),
+            window_grad(context, value_rows),
+            window_grad(attended, grad_self_branch),
+        ],
+        axis=1,
+    )
+
+    def square_chunk(dy, dx):
+        return row_block(square, peer(dy, dx), SHARD)
+
+    grad_heads, square = lax.optimization_barrier((grad_heads, square))
+    s_lo, s_hi, s20 = reduce_first(square_chunk)
+    hidden_parts = peers_parts(after(hidden_sum, grad_heads))
+    grad_m = jnp.where(first_core, key_rows, value_rows)
+    grad_o = jnp.where(first_core, value_rows, key_rows)
     context_part = dot_nt(grad_m, square_mine[:, :D]) + dot_nt(grad_o, square_other[:, :D])
-    grad_heads, out_window, context_part = lax.optimization_barrier(
-        (grad_heads, out_window, context_part.astype(bf16))
-    )
-    context_parts = peers_parts(context_part)
-
-    grad_head0 = self_backward(0, seg_col, seg_row, total0, qkv, grad_heads)
-    s_lo, s_hi, s20, context_parts, grad_head0 = lax.optimization_barrier(
-        (s_lo, s_hi, s20, context_parts, grad_head0)
-    )
-    out_parts = peers_parts(after(out_window, context_parts))
+    context_part = context_part.astype(bf16)
+    context_grad = lax.psum_scatter(context_part, FS, scatter_dimension=0, tiled=True)
+
+    grad_head0 = self_backward(
+        0, seg_col, seg_row, total0, qkv, after(grad_heads, context_part)
+    )
+    s_lo, s_hi, s20, grad_head0 = lax.optimization_barrier((s_lo, s_hi, s20, grad_head0))
     s11, s31 = reduce_second(square_chunk, s_lo, s_hi)
     out_minus, out_plus = reduce_z(after(out_far, grad_head0), out_near[:TOK], out_near[TOK:])
     grad_head1 = self_backward(1, seg_col, seg_row, total1, qkv, after(grad_heads, grad_head0))
-    s11, s31, hidden_grad, out_parts, out_minus, out_plus, grad_head1 = lax.optimization_barrier(
-        (s11, s31, hidden_grad, out_parts, out_minus, out_plus, grad_head1)
-    )
-    context_grad = sum_parts(context_parts).astype(bf16)
-    context_grad = every_peer(after(context_grad, out_parts))
+    s11, s31, hidden_parts, context_grad, out_minus, out_plus, grad_head1 = (
+        lax.optimization_barrier(
+            (s11, s31, hidden_parts, context_grad, out_minus, out_plus, grad_head1)
+        )
+    )
     square_parts = reduce_third(square_chunk, s20, s11, s31)
+    context_grad = every_peer(context_grad)
     grad_qkv = jnp.concatenate([grad_head0, grad_head1], axis=1)
     normed_part = dot_nt(grad_qkv, heads_w).astype(bf16)
 
@@ -740,7 +760,12 @@
         return row_block(normed_part, peer(dy, dx), TOK)
 
     n_lo, n_hi, n20 = reduce_first(normed_chunk)
-    grad_heads_w = dot_tn(normed_all, after(grad_qkv, normed_part)).astype(bf16)
+    hidden_grad = sum_parts(hidden_parts).astype(bf16)
+    hidden_grad = hidden_grad + shift(hidden_grad, "xh", 1)
+    hidden_all = lax.all_gather(hidden_grad, ("z", "c"), axis=0)
+    grad_heads_w = dot_tn(
+        normed_all, after(grad_qkv, normed_part, hidden_grad, context_grad)
+    ).astype(bf16)
     grad_heads_w = jnp.concatenate(
         [
             grad_heads_w[:, SLOT * (3 * h + k) : SLOT * (3 * h + k) + HEAD]
@@ -749,28 +774,33 @@
         ],
         axis=1,
     )
-    grad_qkv_w = peers_parts(after(grad_heads_w, context_grad))
-    n_lo, n_hi, *square_parts = lax.optimization_barrier((n_lo, n_hi, *square_parts))
+    n_lo, n_hi, grad_heads_w, *square_parts = lax.optimization_barrier(
+        (n_lo, n_hi, grad_heads_w, *square_parts)
+    )
+    grad_qkv_w = peers_parts(grad_heads_w)
     n11, n31 = reduce_second(normed_chunk, n_lo, n_hi)
-    out_minus, out_plus = shift(out_minus, "z", -1), shift(out_plus, "z", 1)
+    grad_w_text = dot_tn(text_columns, context_grad).astype(bf16)
+    text_part = dot_nt(context_grad, w_text).astype(bf16)
     square = reduce_last(square_chunk, *square_parts).astype(bf16)
     square = jnp.concatenate(
-        [square[:, WIN * k : WIN * (k + 1)] for k in range(4)]
-        + [sum_parts(out_parts).astype(bf16), jnp.zeros((768 - 5 * SHARD, WIN), bf16)],
+        [square[:, WIN * k : WIN * (k + 1)] for k in range(5)]
+        + [jnp.zeros((768 - 5 * SHARD, WIN), bf16)],
         axis=0,
     )
+    n11, n31, n20, grad_qkv_w, grad_w_text, square = lax.optimization_barrier(
+        (n11, n31, n20, grad_qkv_w, grad_w_text, square)
+    )
+    normed_sums = reduce_third(normed_chunk, n20, n11, n31)
+    out_minus, out_plus = shift(out_minus, "z", -1), shift(out_plus, "z", 1)
+    outputs = (
+        after_cross + out_own.astype(f32) + out_minus.astype(f32) + out_plus.astype(f32)
+    )
+    grad_w_text = sum_rows_over_dp(grad_w_text)
     square = sum_over_dp(square)
     grad_c_out, grad_c_query, grad_c_key, grad_c_value, grad_w_out = whole_columns(square, 5)
-    grad_w_text = dot_tn(text_columns, context_grad).astype(bf16)
-    text_part = dot_nt(context_grad, w_text).astype(bf16)
-    grad_w_text = sum_rows_over_dp(grad_w_text)
-    grad_w_up, grad_w_down = sort_hidden(hidden_grad)
-    outputs = (
-        after_cross + out_own.astype(f32) + out_minus.astype(f32) + out_plus.astype(f32)
-    )
-
-    n11, n31, grad_qkv_w = lax.optimization_barrier((n11, n31, grad_qkv_w))
-    grad_normed_one = reduce_last(normed_chunk, *reduce_third(normed_chunk, n20, n11, n31))
+    grad_w_up, grad_w_down = sort_hidden(hidden_all)
+
+    grad_normed_one = reduce_last(normed_chunk, *normed_sums)
     grad_qkv_w = jnp.concatenate(
         [
             jnp.concatenate(

time: 864 us -> 768 us (0.89)
  waiting for transfers between devices: 185 us -> 135 us
  blocking collectives: 26.1 us -> 0 us
  starting transfers between devices: 186 us -> 172 us
  local copies, waits for them, and re-layouts: 123 us -> 111 us
    all_gather x2 -> x0, blocking collectives: 26.1 us -> none  [sum_over_dp(): return lax.all_gather(part, 'z', axis=0, tiled=True)]
    all_to_all x4 -> x7, waiting for transfers between devices: 39.6 us -> 17.4 us  [every_peer(): return lax.all_to_all(copies, axes, 0, 0, tiled=True)]
    unnamed x240 -> x239, local copies, waits for them, and re-layouts: 42 us -> 25.6 us
    ppermute x78, starting transfers between devices: 122 us -> 109 us  [shift(): return lax.ppermute(x, axis, [(i, (i + by) % n) for i in range(n)])]
    all_to_all x6 -> x4, waiting for transfers between devices: 28.1 us -> 16.7 us  [peers_parts(): return lax.all_to_all(x, axes, 0, 0, tiled=True)]
    all_to_all x4 -> x7, starting transfers between devices: 18.6 us -> 29.8 us  [every_peer(): return lax.all_to_all(copies, axes, 0, 0, tiled=True)]
    all_to_all x6 -> x4, starting transfers between devices: 27 us -> 16.6 us  [peers_parts(): return lax.all_to_all(x, axes, 0, 0, tiled=True)]
  transfers between devices with their start and end apart: 97 -> 98, of which waited for: 17 -> 33; matrix products, arithmetic and copies ran while one was open for 30% -> 31% of each run, Pallas kernels for 15% -> 18%
where the time goes in v5:
time: 768 us; the launch traced here: 758 us
  starting transfers between devices  172 us (22%)
  Pallas kernels  151 us (20%)
  waiting for transfers between devices  135 us (18%)
  local copies, waits for them, and re-layouts  111 us (14%)
  other arithmetic  87.4 us (11%)
  matrix products  84.7 us (11%)
  between operations  15.6 us (2%)
    ppermute x78, starting transfers between devices, shift(): return lax.ppermute(x, axis, [(i, (i + by) % n) for i in range(n)])  109 us
    ppermute x78, waiting for transfers between devices, shift(): return lax.ppermute(x, axis, [(i, (i + by) % n) for i in range(n)])  101 us
    pallas_call x2, Pallas kernels, self_backward(): pl.pallas_call(functools.partial(self_backward_body, head), grid=(ROW //...  37.2 us
    dot_general x7, matrix products, dot_tn(): lax.dot_general(a, b, (((0,), (0,)), ((), ())), preferred_element_type=f32)  29.9 us
    all_to_all x7, starting transfers between devices, every_peer(): return lax.all_to_all(copies, axes, 0, 0, tiled=True)  29.8 us
    pallas_call x3, Pallas kernels, mlp(): pl.pallas_call(mlp_body, grid=(n // TOK,), in_specs=[pl.BlockSpec(memory_...  28.6 us
    dot_general x7, matrix products, dot_nn(): lax.dot_general(a, b, (((1,), (0,)), ((), ())), preferred_element_type=f32)  27.4 us
    dot_general x7, matrix products, dot_nt(): lax.dot_general(a, b, (((1,), (1,)), ((), ())), preferred_element_type=f32)  27.4 us
  transfers between devices with their start and end apart: 98, of which 33 were waited for; matrix products, arithmetic and copies ran while one was open for 31% of the time, Pallas kernels for 18%

profile of v5, /device:TPU:1, one launch (start us, length us, event | category | flops | bytes accessed | tf_op | source)
XLA Modules:
  0.0 757.6 jit_solution(526876428632439087)
XLA Ops:
  34.7 5.8 all-to-all-done
  40.6 11.5 %collective-permute-done.4.refs_5_ = bf16[256,1152]{1,0:T(8,128)(2,1)} collective-permute-done((bf16[256,1152]{1,0:T(8,128)(2,1)}, bf16[256,1152]{1,0:T(8,128)(2,1)}, u32[]{:S(2)}, u32[]{:S(2)}) %collective-permute-start.4) | collective-permute-done | bytes 589856 | tf_op jit(solution)/shard_map/ppermute | solution.py:56
  102.8 8.9 %convolution_convert_fusion.1.q.kv = bf16[2048,768]{1,0:T(8,128)(2,1)} fusion(bf16[2048,1152]{1,0:T(8,128)(2,1)} %shard_map.375, bf16[1152,768]{1,0:T(8,128)(2,1)} %shard_map.376), kind=kOutput, calls=%fused_computation.1 | convolution fusion | flops 3625451520 | bytes 9633792 | tf_op jit(solution)/shard_map/dot_general | solution.py:39
  111.7 12.1 %shard_map.377 = (bf16[2048,72]{1,0:T(8,128)(2,1)}, f32[1,2048]{1,0:T(1,128)}) custom-call(s32[2048,1]{1,0:T(8,128)} %copy.157.seg_q.seg_k, s32[1,2048]{1,0:T(1,128)} %bitcast.149, bf16[2048,768]{1,0:T(8,128)(2,1)} %convolution_convert_fusion.1.q.kv, bf16[2048,768]{1,0:T(8,128)(2,1)} %convolution_convert_fusion.1.q.kv), custom_call_target="tpu_custom_call" | custom-call | tf_op jit(solution)/shard_map/pallas_call | solution.py:216
  123.8 10.7 %collective-permute-done.10.refs_3_ = bf16[144,1792]{1,0:T(8,128)(2,1)} collective-permute-done((bf16[144,1792]{1,0:T(8,128)(2,1)S(1)}, bf16[144,1792]{1,0:T(8,128)(2,1)}, u32[]{:S(2)}, u32[]{:S(2)}) %collective-permute-start.10) | collective-permute-done | bytes 516128 | tf_op jit(solution)/shard_map/ppermute | solution.py:56
  134.5 6.7 collective-permute-done.8.refs_1_
  144.0 12.2 %shard_map.378 = (bf16[2048,72]{1,0:T(8,128)(2,1)}, f32[1,2048]{1,0:T(1,128)}) custom-call(s32[2048,1]{1,0:T(8,128)} %copy.157.seg_q.seg_k, s32[1,2048]{1,0:T(1,128)} %bitcast.150, bf16[2048,768]{1,0:T(8,128)(2,1)} %convolution_convert_fusion.1.q.kv, bf16[2048,768]{1,0:T(8,128)(2,1)} %convolution_convert_fusion.1.q.kv), custom_call_target="tpu_custom_call" | custom-call | tf_op jit(solution)/shard_map/pallas_call | solution.py:216
  159.8 6.4 collective-permute-start.16
  234.4 11.9 %shard_map.380 = bf16[256,1152]{1,0:T(8,128)(2,1)} custom-call(s32[256,1]{1,0:T(8,128)} %copy.160.cap_q, s32[1,512]{1,0:T(1,128)} %and_select_fusion.1.cap_t, bf16[256,1152]{1,0:T(8,128)(2,1)} %convolution_convert_fusion.13.q, bf16[512,1152]{1,0:T(8,128)(2,1)} %get-tuple-element.312.k, bf16[512,1152]{1,0:T(8,128)(2,1)} %get-tuple-element.311.v), custom_call_target="tpu_custom_call" | custom-call | tf_op jit(solution)/shard_map/pallas_call | solution.py:304
  265.5 8.2 %shard_map.381 = (bf16[256,1152]{1,0:T(8,128)(2,1)}, bf16[256,1152]{1,0:T(8,128)(2,1)}, bf16[256,1152]{1,0:T(8,128)(2,1)}, bf16[256,1152]{1,0:T(8,128)(2,1)}) custom-call(s32[1]{0:T(128)} %bitcast.29.core, bf16[256,1152]{1,0:T(8,128)(2,1)} %copy-done.14, bf16[256,1152]{1,0:T(8,128)(2,1)} %copy-done.13, bf16[1152,1152]{1,0:T(8,128)(2,1)} %bitcast.30.mine, ...), custom_call_target="tpu_custom_call" | custom-call | tf_op jit(solution)/shard_map/pallas_call | solution.py:378
  285.8 12.3 %shard_map.382 = (bf16[512,1152]{1,0:T(8,128)(2,1)}, bf16[512,1152]{1,0:T(8,128)(2,1)}, bf16[512,1152]{1,0:T(8,128)(2,1)}, bf16[512,1152]{1,0:T(8,128)(2,1)}) custom-call(s32[1]{0:T(128)} %bitcast.29.core, bf16[512,1152]{1,0:T(8,128)(2,1)} %copy-done.11, bf16[512,1152]{1,0:T(8,128)(2,1)} %constant_dynamic-update-slice_fusion.4.g.refs_10_, ...), custom_call_target="tpu_custom_call" | custom-call | tf_op jit(solution)/shard_map/pallas_call | solution.py:378
  300.9 8.2 %shard_map.383 = (bf16[256,1152]{1,0:T(8,128)(2,1)}, bf16[256,1152]{1,0:T(8,128)(2,1)}, bf16[256,1152]{1,0:T(8,128)(2,1)}, bf16[256,1152]{1,0:T(8,128)(2,1)}) custom-call(s32[1]{0:T(128)} %bitcast.29.core, bf16[256,1152]{1,0:T(8,128)(2,1)} %copy-done.22, bf16[256,1152]{1,0:T(8,128)(2,1)} %copy-done.21, bf16[1152,1152]{1,0:T(8,128)(2,1)} %bitcast.30.mine, ...), custom_call_target="tpu_custom_call" | custom-call | tf_op jit(solution)/shard_map/pallas_call | solution.py:378
  311.8 5.9 collective-permute-done.27
  329.1 12.8 %shard_map.384 = (bf16[1152,1152]{1,0:T(8,128)(2,1)}, bf16[1152,1152]{1,0:T(8,128)(2,1)}) custom-call(s32[1]{0:T(128)} %bitcast.29.core, bf16[256,1152]{1,0:T(8,128)(2,1)} %copy-done.14, bf16[512,1152]{1,0:T(8,128)(2,1)} %copy-done.11, bf16[256,1152]{1,0:T(8,128)(2,1)} %copy-done.22, bf16[256,1152]{1,0:T(8,128)(2,1)} %get-tuple-element.161.refs_3_, ...), custom_call_target="tpu_custom_call" | custom-call | tf_op jit(solution)/shard_map/pallas_call | solution.py:419
  357.7 15.3 %shard_map.385 = (bf16[256,1152]{1,0:T(8,128)(2,1)}, bf16[512,1152]{1,0:T(8,128)(2,1)}, bf16[512,1152]{1,0:T(8,128)(2,1)}) custom-call(s32[512,1]{1,0:T(8,128)} %fusion.59.cap_t, s32[1,256]{1,0:T(1,128)} %bitcast.156, bf16[256,1152]{1,0:T(8,128)(2,1)} %convolution_convert_fusion.13.q, bf16[512,1152]{1,0:T(8,128)(2,1)} %get-tuple-element.312.k, ...), custom_call_target="tpu_custom_call" | custom-call | tf_op jit(solution)/shard_map/pallas_call | solution.py:332
  394.3 5.5 fusion.7
  438.2 18.6 %shard_map.386 = bf16[2048,384]{1,0:T(8,128)(2,1)} custom-call(s32[2048,1]{1,0:T(8,128)} %copy.157.seg_q.seg_k, s32[1,2048]{1,0:T(1,128)} %bitcast.151, f32[1,2048]{1,0:T(1,128)} %get-tuple-element.177.total, bf16[2048,768]{1,0:T(8,128)(2,1)} %convolution_convert_fusion.1.q.kv, bf16[2048,768]{1,0:T(8,128)(2,1)} %convolution_convert_fusion.1.q.kv, ...), custom_call_target="tpu_custom_call" | custom-call | tf_op jit(solution)/shard_map/pallas_call | solution.py:267
  456.9 15.6 %collective-permute-done.41 = bf16[80,3200]{1,0:T(8,128)(2,1)} collective-permute-done((bf16[80,3200]{1,0:T(8,128)(2,1)}, bf16[80,3200]{1,0:T(8,128)(2,1)}, u32[]{:S(2)}, u32[]{:S(2)}) %collective-permute-start.41) | collective-permute-done | bytes 512032 | tf_op jit(solution)/shard_map/ppermute | solution.py:56
  486.2 18.6 %shard_map.387 = bf16[2048,384]{1,0:T(8,128)(2,1)} custom-call(s32[2048,1]{1,0:T(8,128)} %copy.157.seg_q.seg_k, s32[1,2048]{1,0:T(1,128)} %bitcast.152, f32[1,2048]{1,0:T(1,128)} %get-tuple-element.186.total, bf16[2048,768]{1,0:T(8,128)(2,1)} %convolution_convert_fusion.1.q.kv, bf16[2048,768]{1,0:T(8,128)(2,1)} %convolution_convert_fusion.1.q.kv, ...), custom_call_target="tpu_custom_call" | custom-call | tf_op jit(solution)/shard_map/pallas_call | solution.py:267
  529.7 6.2 convolution_convert_fusion
  547.3 10.2 %all-to-all-done.8 = bf16[8,64,1152]{2,1,0:T(8,128)(2,1)} async-done(((bf16[8,64,1152]{2,1,0:T(8,128)(2,1)}), bf16[8,64,1152]{2,1,0:T(8,128)(2,1)}, u32[]{:S(2)}, u32[]{:S(2)}) %all-to-all-start.8) | async-done | bytes 1179680 | tf_op jit(solution)/shard_map/all_to_all | solution.py:113
  557.6 7.6 %convolution_convert_fusion.2 = bf16[1152,768]{0,1:T(8,128)(2,1)S(1)} fusion(bf16[2048,1152]{1,0:T(8,128)(2,1)} %shard_map.375, bf16[2048,768]{1,0:T(8,128)(2,1)} %constant_dynamic-update-slice_fusion.10), kind=kOutput, calls=%fused_computation.2 | convolution fusion | flops 3624763392 | bytes 9633792 | tf_op jit(solution)/shard_map/dot_general | solution.py:47
  589.8 10.8 %all-to-all-done.9 = bf16[8,144,432]{2,1,0:T(8,128)(2,1)} async-done(((bf16[8,144,432]{2,1,0:T(8,128)(2,1)}), bf16[8,144,432]{2,1,0:T(8,128)(2,1)}, u32[]{:S(2)}, u32[]{:S(2)}) %all-to-all-start.9) | async-done | bytes 995360 | tf_op jit(solution)/shard_map/all_to_all | solution.py:117
  690.5 5.6 collective-permute-start.71
  (605 shorter events, 494.3 us)
Async XLA Ops:
  83.2 76.7 %all-to-all-start.2 = ((bf16[8,144,1152]{2,1,0:T(8,128)(2,1)}), bf16[8,144,1152]{2,1,0:T(8,128)(2,1)}, u32[]{:S(2)}, u32[]{:S(2)}) async-start(bf16[8,144,1152]{2,1,0:T(8,128)(2,1)} %broadcast_in_dim.76), calls=%async_computation.2 | async-start | bytes 5308416 | tf_op jit(solution)/shard_map/all_to_all | solution.py:113
  87.7 98.6 %reduce-scatter.7.cloned.1.call-start = ((), (), s32[]{:S(2)}) async-start(), calls=%async_computation.19 | async-start | bytes 1327104 | tf_op jit(solution)/shard_map/reduce_scatter | solution.py:592
  92.8 48.5 %collective-permute-start.11 = (bf16[256,1152]{1,0:T(8,128)(2,1)S(1)}, bf16[256,1152]{1,0:T(8,128)(2,1)S(1)}, u32[]{:S(2)}, u32[]{:S(2)}) collective-permute-start(bf16[256,1152]{1,0:T(8,128)(2,1)S(1)} %bitcast_convert_fusion.g.refs_9_), channel_id=1, source_target_pairs={{0,16},{16,32},{32,48},{48,0},{1,17},{17,33},{33,49},{49,1},{2,18}... | collective-permute-start | bytes 1769480 | tf_op jit(solution)/shard_map/ppermute | solution.py:56
  94.4 46.9 %collective-permute-start.12 = (bf16[256,1152]{1,0:T(8,128)(2,1)S(1)}, bf16[256,1152]{1,0:T(8,128)(2,1)}, u32[]{:S(2)}, u32[]{:S(2)}) collective-permute-start(bf16[256,1152]{1,0:T(8,128)(2,1)S(1)} %bitcast_convert_fusion.g.refs_9_), channel_id=1, source_target_pairs={{0,48},{16,0},{32,16},{48,32},{1,49},{17,1},{33,17},{49,33},{2,50}... | collective-permute-start | bytes 1769480 | tf_op jit(solution)/shard_map/ppermute | solution.py:56
  96.5 38.0 %collective-permute-start.10 = (bf16[144,1792]{1,0:T(8,128)(2,1)S(1)}, bf16[144,1792]{1,0:T(8,128)(2,1)}, u32[]{:S(2)}, u32[]{:S(2)}) collective-permute-start(bf16[144,1792]{1,0:T(8,128)(2,1)S(1)} %copy-done.29), channel_id=1, source_target_pairs={{0,2},{2,4},{4,6},{6,0},{1,3},{3,5},{5,7},{7,1},{8,10},{10,12},{12... | collective-permute-start | bytes 1548296 | tf_op jit(solution)/shard_map/ppermute | solution.py:56
  97.8 43.4 %collective-permute-start.8 = (bf16[144,1792]{1,0:T(8,128)(2,1)S(1)}, bf16[144,1792]{1,0:T(8,128)(2,1)}, u32[]{:S(2)}, u32[]{:S(2)}) collective-permute-start(bf16[144,1792]{1,0:T(8,128)(2,1)S(1)} %copy-done.29), channel_id=1, source_target_pairs={{0,1},{1,0},{2,3},{3,2},{4,5},{5,4},{6,7},{7,6},{8,9},{9,8},{10,11... | collective-permute-start | bytes 1548296 | tf_op jit(solution)/shard_map/ppermute | solution.py:56
  99.0 42.2 %collective-permute-start.9 = (bf16[144,1792]{1,0:T(8,128)(2,1)S(1)}, bf16[144,1792]{1,0:T(8,128)(2,1)}, u32[]{:S(2)}, u32[]{:S(2)}) collective-permute-start(bf16[144,1792]{1,0:T(8,128)(2,1)S(1)} %copy-done.29), channel_id=1, source_target_pairs={{0,6},{2,0},{4,2},{6,4},{1,7},{3,1},{5,3},{7,5},{8,14},{10,8},{12,... | collective-permute-start | bytes 1548296 | tf_op jit(solution)/shard_map/ppermute | solution.py:56
  159.8 57.0 %collective-permute-start.16 = (bf16[1152,1152]{1,0:T(8,128)(2,1)}, bf16[1152,1152]{1,0:T(8,128)(2,1)}, u32[]{:S(2)}, u32[]{:S(2)}) collective-permute-start(bf16[1152,1152]{1,0:T(8,128)(2,1)} %bitcast.20), channel_id=1, source_target_pairs={{0,8},{8,0},{1,9},{9,1},{2,10},{10,2},{3,11},{11,3},{4,12},{12,4},... | collective-permute-start | bytes 7962632 | tf_op jit(solution)/shard_map/ppermute | solution.py:56
  181.3 47.6 %collective-permute-start.21 = (bf16[1152,1792]{1,0:T(8,128)(2,1)}, bf16[1152,1792]{1,0:T(8,128)(2,1)}, u32[]{:S(2)}, u32[]{:S(2)}) collective-permute-start(bf16[1152,1792]{1,0:T(8,128)(2,1)} %shard_map.379), channel_id=1, source_target_pairs={{0,8},{8,0},{1,9},{9,1},{2,10},{10,2},{3,11},{11,3},{4,12},{12,4},... | collective-permute-start | bytes 12386312 | tf_op jit(solution)/shard_map/ppermute | solution.py:56
  212.4 35.6 %all-to-all-start.5 = ((bf16[8,144,1152]{2,1,0:T(8,128)(2,1)}), bf16[8,144,1152]{2,1,0:T(8,128)(2,1)}, u32[]{:S(2)}, u32[]{:S(2)}) async-start(bf16[8,144,1152]{2,1,0:T(8,128)(2,1)} %broadcast_in_dim.150), calls=%async_computation.6 | async-start | bytes 5308416 | tf_op jit(solution)/shard_map/all_to_all | solution.py:113
  325.9 90.9 %collective-permute-start.39 = (bf16[256,1152]{0,1:T(8,128)(2,1)}, bf16[256,1152]{0,1:T(8,128)(2,1)}, u32[]{:S(2)}, u32[]{:S(2)}) collective-permute-start(bf16[256,1152]{0,1:T(8,128)(2,1)} %bitcast.144), channel_id=1, source_target_pairs={{0,8},{8,0},{1,9},{9,1},{2,10},{10,2},{3,11},{11,3},{4,12},{12,4},... | collective-permute-start | bytes 1769480 | tf_op jit(solution)/shard_map/ppermute | solution.py:56
  329.1 71.7 %collective-permute-start.34 = (bf16[256,1152]{1,0:T(8,128)(2,1)}, bf16[256,1152]{1,0:T(8,128)(2,1)}, u32[]{:S(2)}, u32[]{:S(2)}) collective-permute-start(bf16[256,1152]{1,0:T(8,128)(2,1)} %copy-done.61), channel_id=1, source_target_pairs={{0,8},{8,0},{1,9},{9,1},{2,10},{10,2},{3,11},{11,3},{4,12},{12,4},... | collective-permute-start | bytes 1769480 | tf_op jit(solution)/shard_map/ppermute | solution.py:56
  394.3 112.9 %reduce-scatter.9.cloned.1.call-start = ((), (), s32[]{:S(2)}) async-start(), calls=%async_computation.20 | async-start | bytes 1327104 | tf_op jit(solution)/shard_map/reduce_scatter | solution.py:740
  424.8 47.7 %collective-permute-start.43 = (bf16[144,3200]{1,0:T(8,128)(2,1)}, bf16[144,3200]{1,0:T(8,128)(2,1)}, u32[]{:S(2)}, u32[]{:S(2)}) collective-permute-start(bf16[144,3200]{1,0:T(8,128)(2,1)} %constant_dynamic-slice_fusion.11), channel_id=1, source_target_pairs={{0,2},{2,4},{4,6},{6,0},{1,3},{3,5},{5,7},{7,1},{8,10},{10,12},{12... | collective-permute-start | bytes 2764808 | tf_op jit(solution)/shard_map/ppermute | solution.py:56
  426.4 46.1 %collective-permute-start.41 = (bf16[80,3200]{1,0:T(8,128)(2,1)}, bf16[80,3200]{1,0:T(8,128)(2,1)}, u32[]{:S(2)}, u32[]{:S(2)}) collective-permute-start(bf16[80,3200]{1,0:T(8,128)(2,1)} %get-tuple-element.299), channel_id=1, source_target_pairs={{0,2},{2,4},{4,6},{6,0},{1,3},{3,5},{5,7},{7,1},{8,10},{10,12},{12... | collective-permute-start | bytes 1536008 | tf_op jit(solution)/shard_map/ppermute | solution.py:56
  433.8 76.8 %all-to-all-start.7 = ((bf16[8,144,1152]{2,1,0:T(8,128)(2,1)}), bf16[8,144,1152]{2,1,0:T(8,128)(2,1)}, u32[]{:S(2)}, u32[]{:S(2)}) async-start(bf16[8,144,1152]{2,1,0:T(8,128)(2,1)} %bitcast.130), calls=%async_computation.8 | async-start | bytes 5308416 | tf_op jit(solution)/shard_map/all_to_all | solution.py:117
  514.9 50.7 %collective-permute-start.53 = (bf16[144,3200]{1,0:T(8,128)(2,1)}, bf16[144,3200]{1,0:T(8,128)(2,1)}, u32[]{:S(2)}, u32[]{:S(2)}) collective-permute-start(bf16[144,3200]{1,0:T(8,128)(2,1)} %get-tuple-element.297), channel_id=1, source_target_pairs={{0,2},{2,4},{4,6},{6,0},{1,3},{3,5},{5,7},{7,1},{8,10},{10,12},{12... | collective-permute-start | bytes 2764808 | tf_op jit(solution)/shard_map/ppermute | solution.py:56
  516.1 49.5 %collective-permute-start.54 = (bf16[144,3200]{1,0:T(8,128)(2,1)}, bf16[144,3200]{1,0:T(8,128)(2,1)}, u32[]{:S(2)}, u32[]{:S(2)}) collective-permute-start(bf16[144,3200]{1,0:T(8,128)(2,1)} %get-tuple-element.296), channel_id=1, source_target_pairs={{0,1},{1,0},{2,3},{3,2},{4,5},{5,4},{6,7},{7,6},{8,9},{9,8},{10,11... | collective-permute-start | bytes 2764808 | tf_op jit(solution)/shard_map/ppermute | solution.py:56
  516.4 49.9 %collective-permute-start.55 = (bf16[144,3200]{1,0:T(8,128)(2,1)}, bf16[144,3200]{1,0:T(8,128)(2,1)}, u32[]{:S(2)}, u32[]{:S(2)}) collective-permute-start(bf16[144,3200]{1,0:T(8,128)(2,1)} %get-tuple-element.295), channel_id=1, source_target_pairs={{0,6},{2,0},{4,2},{6,4},{1,7},{3,1},{5,3},{7,5},{8,14},{10,8},{12,... | collective-permute-start | bytes 2764808 | tf_op jit(solution)/shard_map/ppermute | solution.py:56
  522.4 35.1 %all-to-all-start.8 = ((bf16[8,64,1152]{2,1,0:T(8,128)(2,1)}), bf16[8,64,1152]{2,1,0:T(8,128)(2,1)}, u32[]{:S(2)}, u32[]{:S(2)}) async-start(bf16[8,64,1152]{2,1,0:T(8,128)(2,1)} %broadcast_in_dim.157), calls=%async_computation.10 | async-start | bytes 2359296 | tf_op jit(solution)/shard_map/all_to_all | solution.py:113
  582.5 103.2 %reduce-scatter.11.cloned.1.call-start = ((), (), s32[]{:S(2)}) async-start(), calls=%async_computation.21 | async-start | bytes 737280 | tf_op jit(solution)/shard_map/reduce_scatter | solution.py:480
  610.7 87.1 %reduce-scatter.13.cloned.1.call-start = ((), (), s32[]{:S(2)}) async-start(), calls=%async_computation.23 | async-start | bytes 1228800
  633.2 33.9 %collective-permute-start.48 = (bf16[256,1152]{1,0:T(8,128)(2,1)}, bf16[256,1152]{1,0:T(8,128)(2,1)}, u32[]{:S(2)}, u32[]{:S(2)}) collective-permute-start(bf16[256,1152]{1,0:T(8,128)(2,1)} %get-tuple-element.188), channel_id=1, source_target_pairs={{0,48},{16,0},{32,16},{48,32},{1,49},{17,1},{33,17},{49,33},{2,50}... | collective-permute-start | bytes 1769480 | tf_op jit(solution)/shard_map/ppermute | solution.py:56
  640.7 98.9 %all-gather.3.cloned.1.call-start = ((), (), s32[]{:S(2)}) async-start(), calls=%async_computation.22 | async-start | bytes 2985984 | tf_op jit(solution)/shard_map/all_gather | solution.py:765
  (185 other events, 1892.7 us)
Sparse Core Ops, SparseCore 0:
  102.9 54.9 reduce-scatter.6
  433.9 54.3 reduce-scatter.8
  610.8 15.7 reduce-scatter.10
  629.4 34.5 reduce-scatter.12
  665.6 27.5 all-gather.2

commit v6 on v5

v6 whole, which is shorter than its diff:
```python
import functools

import jax
import jax.numpy as jnp
from jax import lax
from jax.experimental import pallas as pl
from jax.experimental.pallas import tpu as pltpu
from jax.sharding import Mesh
from jax.sharding import PartitionSpec as P

HEADS = 16
HEAD = 72
D = 1152
FF = 4608
CAP_TOK = 60
TXT_OWN = 64
TXT = 8 * TXT_OWN
TOK = 256
ROW = 2048
CAP_LEN = 120
SEGS = 3
CAPS = 4
SHARD = 144
SLOT = 128
WIN = 640
STEP = 512

bf16 = jnp.bfloat16
f32 = jnp.float32
norm_eps = 1e-06
masked_score = -1e30
scale = HEAD ** (-0.5)
log2e = 1.4426950408889634
FS = ("y", "xl")
VMEM = 60 * 1024 * 1024


def dot_nn(a, b):
    return lax.dot_general(a, b, (((1,), (0,)), ((), ())), preferred_element_type=f32)


def dot_nt(a, b):
    return lax.dot_general(a, b, (((1,), (1,)), ((), ())), preferred_element_type=f32)


def dot_tn(a, b):
    return lax.dot_general(a, b, (((0,), (0,)), ((), ())), preferred_element_type=f32)


def params():
    return pltpu.CompilerParams(vmem_limit_bytes=VMEM)


def shift(x, axis, by):
    n = lax.axis_size(axis)
    return lax.ppermute(x, axis, [(i, (i + by) % n) for i in range(n)])


def halves(x):
    h = (x.shape[0] // 2 + 15) // 16 * 16
    return x[:h], x[h:]


def after(x, *others):
    return lax.optimization_barrier((x, *others))[0]


def gather_first(x):
    return shift(x, "xl", 1), shift(x, "y", -1), shift(x, "y", 1)


def gather_second(x01, x10):
    return shift(x01, "y", 1), shift(x10, "y", -1), shift(x10, "xl", 1)


def gather_third(x31, x11):
    return shift(halves(x11)[0], "y", -1), shift(halves(x31)[1], "y", 1)


NEAR = ((0, 0), (0, 1), (1, 0), (3, 0))
NEXT = ((3, 1), (2, 0), (1, 1))
LAST = (2, 1)


def reduce_first(chunk):
    lo, hi = halves(chunk(2, 1))
    return shift(lo, "y", 1), shift(hi, "y", -1), shift(chunk(2, 0), "y", 1)


def reduce_second(chunk, lo, hi):
    h = lo.shape[0]
    c11, c31 = chunk(1, 1), chunk(3, 1)
    c11 = jnp.concatenate([c11[:h] + lo, c11[h:]], axis=0)
    c31 = jnp.concatenate([c31[:h], c31[h:] + hi], axis=0)
    return shift(c11, "xl", 1), shift(c31, "y", -1)


def reduce_third(chunk, c20, c11, c31):
    return (
        shift(chunk(1, 0) + c20 + c11, "y", 1),
        shift(chunk(0, 1) + c31, "xl", 1),
        shift(chunk(3, 0), "y", -1),
    )


def reduce_last(chunk, *parts):
    return sum([p.astype(f32) for p in parts], chunk(0, 0).astype(f32))


def every_peer(x, axes=FS):
    n = lax.axis_size(axes)
    copies = jnp.broadcast_to(x[None], (n, *x.shape)).reshape(n * x.shape[0], x.shape[1])
    return lax.all_to_all(copies, axes, 0, 0, tiled=True)


def peers_parts(x, axes=FS):
    return lax.all_to_all(x, axes, 0, 0, tiled=True)


def sum_parts(parts):
    return jnp.sum(parts.reshape(8, -1, parts.shape[1]).astype(f32), axis=0)


def reduce_z(far, minus, plus):
    lo, hi = halves(far)
    lo, hi = shift(lo, "z", -1), shift(hi, "z", 1)
    h = lo.shape[0]
    return (
        jnp.concatenate([minus[:h] + lo, minus[h:]], axis=0),
        jnp.concatenate([plus[:h], plus[h:] + hi], axis=0),
    )


def peer(dy, dx):
    return ((lax.axis_index("y") + dy) % 4) * 2 + (lax.axis_index("xl") ^ dx)


def place_rows(own, first, second, third, gain, bias):
    lo = third[0].shape[0]
    rows, cols = own.shape
    pieces = [(x, p, 0) for x, p in zip((own, *first), NEAR)]
    pieces += [(x, p, 0) for x, p in zip(second, NEXT)]
    pieces += [(third[0], LAST, 0), (third[1], LAST, lo)]
    count = len(pieces)

    def body(where, gain, bias, *refs):
        ins, plain, normed, sem = refs[:count], refs[count], refs[count + 1], refs[-1]
        started = []
        for k, (x, _, off) in enumerate(pieces):
            row = pl.multiple_of(where[k] * rows + off, 16)
            one = pltpu.make_async_copy(ins[k], plain.at[pl.ds(row, x.shape[0])], sem.at[k])
            one.start()
            started.append(one)
        for one in started:
            one.wait()

        def step(i, carry):
            part = pl.ds(pl.multiple_of(i * rows, rows), rows)
            normed[part, :] = (plain[part, :].astype(f32) * gain[...] + bias[...]).astype(bf16)
            return carry

        lax.fori_loop(0, 8, step, 0)

    vmem = pl.BlockSpec(memory_space=pltpu.VMEM)
    return pl.pallas_call(
        body,
        in_specs=[pl.BlockSpec(memory_space=pltpu.SMEM), vmem, vmem]
        + [pl.BlockSpec(memory_space=pl.ANY)] * count,
        out_specs=[vmem, vmem],
        out_shape=[jax.ShapeDtypeStruct((8 * rows, cols), bf16)] * 2,
        scratch_shapes=[pltpu.SemaphoreType.DMA((count,))],
        compiler_params=params(),
    )(
        jnp.stack([peer(*p) for _, p, _ in pieces]).astype(jnp.int32),
        gain,
        bias,
        *[x for x, _, _ in pieces],
    )


def pack_heads_body(wq, wk, wv, out):
    for p in range(8):
        rows = slice(SHARD * p, SHARD * (p + 1))
        out[rows, :] = jnp.concatenate([w[:, rows] for w in (wq, wk, wv)], axis=1)


def pack_heads(*weights):
    return pl.pallas_call(
        pack_heads_body,
        out_shape=jax.ShapeDtypeStruct((D, 3 * SHARD), bf16),
        compiler_params=params(),
    )(*weights)


def spread_heads_body(x, out):
    blank = jnp.zeros((D, SLOT - HEAD), bf16)
    for h in range(2):
        for k in range(3):
            first = SHARD * k + HEAD * h
            slot = SLOT * (3 * h + k)
            out[:, slot : slot + SLOT] = jnp.concatenate(
                [x[:, first : first + HEAD], blank], axis=1
            )


def spread_heads(x):
    return pl.pallas_call(
        spread_heads_body,
        out_shape=jax.ShapeDtypeStruct((D, 6 * SLOT), bf16),
        compiler_params=params(),
    )(x)


def self_forward_body(seg_q, seg_k, q, kv, out, total):
    s = dot_nt(q[:, :SLOT], kv[:, SLOT : 2 * SLOT])
    s = jnp.where(seg_q[...] == seg_k[...], s, masked_score)
    top = jnp.max(s, axis=1, keepdims=True)
    p = jnp.exp2((s - top) * (scale * log2e))
    mass = jnp.sum(p, axis=1, keepdims=True)
    out[...] = (dot_nn(p.astype(bf16), kv[:, 2 * SLOT :]) / mass)[:, :HEAD].astype(bf16)
    log_total = top * (scale * log2e) + jnp.log2(mass)
    total[...] = jnp.transpose(jnp.broadcast_to(log_total, (TOK, SLOT)))[0:1, :]


def self_forward(head, seg_q, seg_k, qkv):
    return pl.pallas_call(
        self_forward_body,
        grid=(ROW // TOK,),
        in_specs=[
            pl.BlockSpec((TOK, 1), lambda i: (i, 0)),
            pl.BlockSpec((1, ROW), lambda i: (0, 0)),
            pl.BlockSpec((TOK, 3 * SLOT), lambda i: (i, head)),
            pl.BlockSpec((ROW, 3 * SLOT), lambda i: (0, head)),
        ],
        out_specs=[
            pl.BlockSpec((TOK, HEAD), lambda i: (i, 0)),
            pl.BlockSpec((1, TOK), lambda i: (0, i)),
        ],
        out_shape=[
            jax.ShapeDtypeStruct((ROW, HEAD), bf16),
            jax.ShapeDtypeStruct((1, ROW), f32),
        ],
        compiler_params=params(),
    )(seg_q, seg_k, qkv, qkv)


def self_backward_body(head, seg_k, seg_q, total, q, kv, g, *refs):
    grad, key_sum, value_sum, key_t = refs[-4:]
    i = pl.program_id(0)

    @pl.when(i == 0)
    def _():
        key_sum[...] = jnp.zeros_like(key_sum)
        value_sum[...] = jnp.zeros_like(value_sum)
        key_t[...] = jnp.transpose(kv[:, SLOT : 2 * SLOT])

    rows = pl.ds(pl.multiple_of(i * TOK, TOK), TOK)
    q_h, k_h, v_h = q[:, :SLOT], kv[:, SLOT : 2 * SLOT], kv[:, 2 * SLOT :]
    g_both = g[...]
    g_h = jnp.concatenate(
        [g_both[:, HEAD * head : HEAD * (head + 1)], jnp.zeros((TOK, SLOT - HEAD), bf16)], axis=1
    )
    p = jnp.exp2(dot_nt(k_h, q_h) * (scale * log2e) - total[...])
    p = jnp.where(seg_k[...] == seg_q[...], p, 0.0)
    dp = dot_nt(v_h, g_h)
    ds = (p * (dp - jnp.sum(p * dp, axis=0, keepdims=True))).astype(bf16)
    value_sum[...] += dot_nn(p.astype(bf16), g_h)
    key_sum[...] += dot_nn(ds, q_h)
    grad[rows, :SLOT] = (jnp.transpose(dot_nn(key_t[...], ds)) * scale).astype(bf16)

    @pl.when(i == pl.num_programs(0) - 1)
    def _():
        grad[:, SLOT : 2 * SLOT] = (key_sum[...] * scale).astype(bf16)
        grad[:, 2 * SLOT :] = value_sum[...].astype(bf16)


def self_backward(head, seg_k, seg_q, total, qkv, g, before=()):
    return pl.pallas_call(
        functools.partial(self_backward_body, head),
        grid=(ROW // TOK,),
        in_specs=[
            pl.BlockSpec((ROW, 1), lambda i: (0, 0)),
            pl.BlockSpec((1, TOK), lambda i: (0, i)),
            pl.BlockSpec((1, TOK), lambda i: (0, i)),
            pl.BlockSpec((TOK, 3 * SLOT), lambda i: (i, head)),
            pl.BlockSpec((ROW, 3 * SLOT), lambda i: (0, head)),
            pl.BlockSpec((TOK, SHARD), lambda i: (i, 0)),
        ]
        + [pl.BlockSpec(memory_space=pl.ANY)] * len(before),
        out_specs=pl.BlockSpec((ROW, 3 * SLOT), lambda i: (0, head)),
        out_shape=jax.ShapeDtypeStruct((ROW, 6 * SLOT), bf16),
        input_output_aliases={6: 0} if before else {},
        scratch_shapes=[
            pltpu.VMEM((ROW, SLOT), f32),
            pltpu.VMEM((ROW, SLOT), f32),
            pltpu.VMEM((SLOT, ROW), bf16),
        ],
        compiler_params=params(),
    )(seg_k, seg_q, total, qkv, qkv, g, *before)


def cross_forward_body(cap_q, cap_t, q, k, v, out):
    allowed = cap_q[...] == cap_t[...]
    mixed = []
    for h in range(HEADS):
        a, b = HEAD * h, HEAD * (h + 1)
        s = dot_nt(q[:, a:b], k[:, a:b])
        s = jnp.where(allowed, s, masked_score)
        top = jnp.max(s, axis=1, keepdims=True)
        p = jnp.exp2((s - top) * (scale * log2e))
        mass = jnp.sum(p, axis=1, keepdims=True)
        mixed.append(dot_nn(p.astype(bf16), v[:, a:b]) / mass)
    out[...] = jnp.concatenate(mixed, axis=1).astype(bf16)


def cross_forward(cap_q, cap_t, q, k, v):
    return pl.pallas_call(
        cross_forward_body,
        out_shape=jax.ShapeDtypeStruct((TOK, D), bf16),
        compiler_params=params(),
    )(cap_q, cap_t, q, k, v)


def cross_backward_body(cap_t, cap_q, q, k, v, g, grad_q, grad_kv):
    allowed = cap_t[...] == cap_q[...]
    dq, dk, dv = [], [], []
    for h in range(HEADS):
        a, b = HEAD * h, HEAD * (h + 1)
        q_h, k_h, v_h, g_h = q[:, a:b], k[:, a:b], v[:, a:b], g[:, a:b]
        s = jnp.where(allowed, dot_nt(k_h, q_h), masked_score)
        top = jnp.max(s, axis=0, keepdims=True)
        p = jnp.exp2((s - top) * (scale * log2e))
        p = p / jnp.sum(p, axis=0, keepdims=True)
        dp = dot_nt(v_h, g_h)
        ds = (p * (dp - jnp.sum(p * dp, axis=0, keepdims=True))).astype(bf16)
        dv.append(dot_nn(p.astype(bf16), g_h))
        dk.append(dot_nn(ds, q_h) * scale)
        dq.append(dot_tn(ds, k_h) * scale)
    grad_q[...] = jnp.concatenate(dq, axis=1).astype(bf16)
    grad_kv[:, :D] = jnp.concatenate(dk, axis=1).astype(bf16)
    grad_kv[:, D:] = jnp.concatenate(dv, axis=1).astype(bf16)


def cross_backward(cap_t, cap_q, q, k, v, g):
    return pl.pallas_call(
        cross_backward_body,
        out_shape=[
            jax.ShapeDtypeStruct((TOK, D), bf16),
            jax.ShapeDtypeStruct((TXT, 2 * D), bf16),
        ],
        compiler_params=params(),
    )(cap_t, cap_q, q, k, v, g)


def fetch_pair(core, mine, other, first, second, sem):
    def run(a, b):
        one = pltpu.make_async_copy(a, first, sem.at[0])
        two = pltpu.make_async_copy(b, second, sem.at[1])
        one.start()
        two.start()
        one.wait()
        two.wait()

    @pl.when(core[0] == 0)
    def _():
        run(mine, other)

    @pl.when(core[0] != 0)
    def _():
        run(other, mine)


def fetch_windows(core, mine, other, whole, sem):
    def run(a, b):
        one = pltpu.make_async_copy(a, whole.at[:, pl.ds(0, WIN)], sem.at[0])
        two = pltpu.make_async_copy(
            b.at[:, pl.ds(128, STEP)], whole.at[:, pl.ds(WIN, STEP)], sem.at[1]
        )
        one.start()
        two.start()
        one.wait()
        two.wait()

    @pl.when(core[0] == 0)
    def _():
        run(mine, other)

    @pl.when(core[0] != 0)
    def _():
        run(other, mine)


def mlp_body(parts, count, core, *refs):
    xs, gs = refs[: parts * count], refs[parts * count : 2 * parts * count]
    mine, other = refs[2 * parts * count : 2 * parts * count + 2]
    outs = refs[2 * parts * count + 2 : -3]
    up, down, sem = refs[-3:]
    fetch_pair(core, mine, other, up, down, sem)
    for k in range(count):
        x = jnp.concatenate([r[...] for r in xs[parts * k : parts * (k + 1)]], axis=0)
        g = jnp.concatenate([r[...] for r in gs[parts * k : parts * (k + 1)]], axis=0)
        out, act_out, pre_out, grad_x = outs[4 * k : 4 * (k + 1)]
        pre = dot_nn(x, up[...])
        grad_act = dot_nt(g, down[...])
        cdf = 0.5 * (1.0 + lax.erf(pre * (0.5**0.5)))
        density = jnp.exp2(pre * pre * (-0.5 * log2e)) * 0.3989422804014327
        act = (pre * cdf).astype(bf16)
        grad_pre = (grad_act * (cdf + pre * density)).astype(bf16)
        act_out[...] = act
        pre_out[...] = grad_pre
        out[...] = dot_nn(act, down[...]).astype(out.dtype)
        grad_x[...] = dot_nt(grad_pre, up[...]).astype(grad_x.dtype)


def mlp(core, xs, gs, mine, other):
    parts = TOK // xs[0].shape[0]
    count = len(xs) // parts
    vmem = pl.BlockSpec(memory_space=pltpu.VMEM)
    hbm = pl.BlockSpec(memory_space=pl.ANY)
    return pl.pallas_call(
        functools.partial(mlp_body, parts, count),
        in_specs=[pl.BlockSpec(memory_space=pltpu.SMEM)]
        + [vmem] * (2 * parts * count)
        + [hbm, hbm],
        out_specs=[vmem] * (4 * count),
        out_shape=[jax.ShapeDtypeStruct((TOK, D), bf16)] * (4 * count),
        scratch_shapes=[
            pltpu.VMEM((D, D), bf16),
            pltpu.VMEM((D, D), bf16),
            pltpu.SemaphoreType.DMA((2,)),
        ],
        compiler_params=params(),
    )(core, *xs, *gs, mine, other)


def mlp_grads_body(core, *refs):
    xs, pres, acts, gs = refs[0:4], refs[4:8], refs[8:12], refs[12:16]
    keep, send = refs[16:]
    up = sum(dot_tn(x[...], p[...]) for x, p in zip(xs, pres)).astype(bf16)
    down = sum(dot_tn(a[...], g[...]) for a, g in zip(acts, gs)).astype(bf16)
    first = core[0] == 0

    @pl.when(first)
    def _():
        keep[...] = up
        send[...] = down

    @pl.when(jnp.logical_not(first))
    def _():
        keep[...] = down
        send[...] = up


def mlp_grads(core, xs, pres, acts, gs):
    def whole(x):
        return pl.BlockSpec(x.shape, lambda k: (0, 0))

    def part(x):
        return pl.BlockSpec((x.shape[0], 384), lambda k: (0, k))

    out = pl.BlockSpec((D, 384), lambda k: (0, k))
    return pl.pallas_call(
        mlp_grads_body,
        grid=(3,),
        in_specs=[pl.BlockSpec(memory_space=pltpu.SMEM)]
        + [whole(x) for x in xs]
        + [part(x) for x in pres]
        + [whole(x) for x in acts]
        + [part(x) for x in gs],
        out_specs=[out, out],
        out_shape=[jax.ShapeDtypeStruct((D, D), bf16)] * 2,
        compiler_params=params(),
    )(core, *xs, *pres, *acts, *gs)


def sort_hidden_body(core, mine, other, up, down):
    def run(ups, downs):
        for f in range(8):
            lanes = slice(SHARD * f, SHARD * (f + 1))
            up[:, 4 * SHARD * f : 4 * SHARD * (f + 1)] = jnp.concatenate(
                [ups[SHARD * z : SHARD * (z + 1), lanes] for z in range(4)], axis=1
            ).astype(f32)
        down[...] = downs[...].astype(f32)

    @pl.when(core[0] == 0)
    def _():
        run(mine, other)

    @pl.when(core[0] != 0)
    def _():
        run(other, mine)


def sort_hidden(core, mine, other):
    vmem = pl.BlockSpec(memory_space=pltpu.VMEM)
    return pl.pallas_call(
        sort_hidden_body,
        in_specs=[pl.BlockSpec(memory_space=pltpu.SMEM), vmem, vmem],
        out_specs=[vmem, vmem],
        out_shape=[
            jax.ShapeDtypeStruct((SHARD, FF), f32),
            jax.ShapeDtypeStruct((4 * SHARD, D), f32),
        ],
        compiler_params=params(),
    )(core, mine, other)


def normalize(x):
    center = x - jnp.mean(x, axis=-1, keepdims=True)
    inverse = lax.rsqrt(jnp.mean(center * center, axis=-1, keepdims=True) + norm_eps)
    return center * inverse, inverse


def norm_back(x, g, gain):
    plain, inverse = normalize(x)
    scaled = g * gain
    mixed = jnp.mean(scaled * plain, axis=-1, keepdims=True)
    grad = inverse * (scaled - jnp.mean(scaled, axis=-1, keepdims=True) - plain * mixed)
    sums = [jnp.sum(g * plain, axis=0, keepdims=True), jnp.sum(g, axis=0, keepdims=True)]
    return grad, sums


def call(body, ins, outs, scratch):
    spaces = {"vmem": pltpu.VMEM, "hbm": pl.ANY, "smem": pltpu.SMEM}
    return pl.pallas_call(
        body,
        in_specs=[pl.BlockSpec(memory_space=spaces[where]) for _, where in ins],
        out_specs=[pl.BlockSpec(memory_space=pltpu.VMEM)] * len(outs),
        out_shape=[jax.ShapeDtypeStruct(*o) for o in outs],
        scratch_shapes=scratch,
        compiler_params=params(),
    )(*[x for x, _ in ins])


def square_scratch(count):
    return [pltpu.VMEM((D, D), bf16)] * count + [pltpu.SemaphoreType.DMA((2,))]


def after_self_body(core, x, mixed, gain, bias, mine, other, total, normed, query, w1, w2, sem):
    fetch_pair(core, mine, other, w1, w2, sem)
    rows = x[...].astype(f32) + dot_nn(mixed[...], w1[...])
    total[...] = rows
    low = (normalize(rows)[0] * gain[...] + bias[...]).astype(bf16)
    normed[...] = low
    query[...] = dot_nn(low, w2[...]).astype(bf16)


def text_keys_body(core, context, mine, other, key, value, w1, w2, sem):
    fetch_pair(core, mine, other, w1, w2, sem)
    key[...] = dot_nn(context[...], w1[...]).astype(bf16)
    value[...] = dot_nn(context[...], w2[...]).astype(bf16)


def after_cross_body(core, x, mixed, gain, bias, mine, other, total, normed, w, sem):
    fetch_windows(core, mine, other, w, sem)
    rows = x[...] + dot_nn(mixed[...], w[...])
    total[...] = rows
    normed[...] = (normalize(rows)[0] * gain[...] + bias[...]).astype(bf16)


def third_back_body(core, x, g0, g1, g2, cot, gain, mine, other, grad, low, mixed, sums, w, sem):
    fetch_windows(core, mine, other, w, sem)
    g = g0[...].astype(f32) + g1[...].astype(f32) + g2[...].astype(f32)
    back, both = norm_back(x[...], g, gain[...])
    total = cot[...] + back
    grad[...] = total
    low[...] = total.astype(bf16)
    mixed[...] = dot_nt(total.astype(bf16), w[...]).astype(bf16)
    sums[...] = jnp.concatenate(both + [jnp.zeros((6, D), f32)], axis=0)


def second_back_body(core, x, gq, before, gain, mine, other, grad, low, mixed, sums, w1, w2, sem):
    fetch_pair(core, mine, other, w1, w2, sem)
    back, both = norm_back(x[...], dot_nt(gq[...], w2[...]), gain[...])
    total = before[...] + back
    grad[...] = total
    low[...] = total.astype(bf16)
    mixed[...] = dot_nt(total.astype(bf16), w1[...]).astype(bf16)
    sums[...] = jnp.concatenate(both + [jnp.zeros((6, D), f32)], axis=0)


def first_back_body(x, parts, before, gain, grad):
    g = parts[:TOK, :].astype(f32)
    for k in range(1, 8):
        g = g + parts[TOK * k : TOK * (k + 1), :].astype(f32)
    grad[...] = before[...] + norm_back(x[...].astype(f32), g, gain[...])[0]


def text_back_body(
    core, kv, cols, text, w_text, mine, other, part, grad_text, grad_kv, w1, w2, sem
):
    fetch_pair(core, mine, other, w1, w2, sem)
    low = (dot_nt(kv[:, :D], w1[...]) + dot_nt(kv[:, D:], w2[...])).astype(bf16)
    part[...] = dot_nt(low, w_text[...]).astype(bf16)
    grad_text[...] = dot_tn(text[...], low).astype(bf16)
    grad_kv[...] = dot_tn(cols[...], kv[...]).astype(bf16)


def first_part_body(g, w, plain, part, sums):
    rows = dot_nt(g[...], w[...])
    part[...] = rows.astype(bf16)
    both = [
        jnp.sum(rows * plain[...].astype(f32), axis=0, keepdims=True),
        jnp.sum(rows, axis=0, keepdims=True),
        jnp.zeros((6, D), f32),
    ]
    both = jnp.concatenate(both, axis=0)

    @pl.when(pl.program_id(0) == 0)
    def _():
        sums[...] = both

    @pl.when(pl.program_id(0) != 0)
    def _():
        sums[...] += both


def first_part(g, w, plain):
    return pl.pallas_call(
        first_part_body,
        grid=(ROW // TOK,),
        in_specs=[
            pl.BlockSpec((TOK, 6 * SLOT), lambda i: (i, 0)),
            pl.BlockSpec((D, 6 * SLOT), lambda i: (0, 0)),
            pl.BlockSpec((TOK, D), lambda i: (i, 0)),
        ],
        out_specs=[
            pl.BlockSpec((TOK, D), lambda i: (i, 0)),
            pl.BlockSpec((8, D), lambda i: (0, 0)),
        ],
        out_shape=[jax.ShapeDtypeStruct((ROW, D), bf16), jax.ShapeDtypeStruct((8, D), f32)],
        compiler_params=params(),
    )(g, w, plain)


def heads_grad_body(x, g, out):
    grad = dot_tn(x[...], g[...]).astype(bf16)
    out[...] = jnp.concatenate(
        [
            grad[:, SLOT * (3 * h + k) : SLOT * (3 * h + k) + HEAD]
            for k in range(3)
            for h in range(2)
        ],
        axis=1,
    )


def heads_grad(x, g):
    return pl.pallas_call(
        heads_grad_body,
        grid=(3,),
        in_specs=[
            pl.BlockSpec((ROW, 384), lambda i: (0, i)),
            pl.BlockSpec((ROW, 6 * SLOT), lambda i: (0, 0)),
        ],
        out_specs=pl.BlockSpec((384, 3 * SHARD), lambda i: (i, 0)),
        out_shape=jax.ShapeDtypeStruct((D, 3 * SHARD), bf16),
        compiler_params=params(),
    )(x, g)


def unpack_heads_body(x, out):
    for k in range(3):
        out[SHARD * k : SHARD * (k + 1), :] = jnp.concatenate(
            [x[SHARD * p : SHARD * (p + 1), SHARD * k : SHARD * (k + 1)] for p in range(8)], axis=1
        )


def unpack_heads(x):
    return pl.pallas_call(
        unpack_heads_body,
        out_shape=jax.ShapeDtypeStruct((3 * SHARD, D), bf16),
        compiler_params=params(),
    )(x)


def row_block(x, index, rows):
    return lax.dynamic_slice_in_dim(x, index * rows, rows, axis=0)


def core_window(x, core):
    return lax.dynamic_slice_in_dim(x, core * STEP, WIN, axis=1)


def both_cores(x):
    return jnp.concatenate([x, shift(x, "c", 1)], axis=0)


def window_grad(left, right):
    core = lax.axis_index("c")
    sent = shift(core_window(right, 1 - core), "c", 1)
    rights = jnp.concatenate([core_window(right, core), sent], axis=0)
    return dot_tn(both_cores(left), rights).astype(bf16)


def scatter_over_dp(x):
    part = lax.psum_scatter(x, "z", scatter_dimension=0, tiled=True)
    return part + shift(part, "xh", 1)


def whole_columns(mine, count):
    other = shift(mine, "c", 1)
    first = lax.axis_index("c") == 0
    low = jnp.where(first, mine, other).astype(f32)
    high = jnp.where(first, other, mine).astype(f32)
    return [
        jnp.concatenate(
            [low[SHARD * k : SHARD * (k + 1)], high[SHARD * k : SHARD * (k + 1), 128:]], axis=1
        )
        for k in range(count)
    ]


def sum_everywhere(x):
    for axis in ("y", "xl", "z", "xh", "c"):
        n = lax.axis_size(axis)
        x = sum([shift(x, axis, k) for k in range(1, n)], x)
    return x


def local(
    tokens,
    text_states,
    seg_lengths,
    caption_of_segment,
    text_lengths,
    ln1_gain,
    ln1_bias,
    w_query,
    w_key,
    w_value,
    w_out,
    ln2_gain,
    ln2_bias,
    c_query,
    w_text,
    c_key,
    c_value,
    c_out,
    ln3_gain,
    ln3_bias,
    w_up,
    w_down,
    cotangent,
):
    core = lax.axis_index("c")
    first_core = core == 0
    core_index = core.astype(jnp.int32)[None]
    quarter = lax.axis_index("z")
    first_row = peer(0, 0) * TOK

    ends = jnp.cumsum(seg_lengths[0])
    positions = jnp.arange(ROW, dtype=jnp.int32)
    segment = jnp.sum((positions[:, None] >= ends[None, :]).astype(jnp.int32), axis=1)
    own_segment = lax.dynamic_slice_in_dim(segment, first_row, TOK)
    text_row = jnp.arange(TXT, dtype=jnp.int32)
    text_pos = text_row // TXT_OWN * CAP_TOK + text_row % TXT_OWN
    text_caption = text_pos // CAP_LEN
    live = jnp.sum(
        jnp.where(
            text_caption[:, None] == jnp.arange(CAPS, dtype=jnp.int32)[None, :],
            text_lengths[0][None, :],
            0,
        ),
        axis=1,
    )
    query_caption = jnp.sum(
        jnp.where(
            own_segment[:, None] == jnp.arange(SEGS, dtype=jnp.int32)[None, :],
            caption_of_segment[0][None, :],
            0,
        ),
        axis=1,
    )
    text_live = (text_row % TXT_OWN < CAP_TOK) & (text_pos % CAP_LEN < live)
    text_key = jnp.where(text_live, text_caption, -1)

    def row(x):
        return x[None, :]

    first_mine = lax.all_gather(jnp.where(first_core, w_out, c_query), FS, axis=0, tiled=True)

    rows_in = tokens[0]
    plain = normalize(rows_in.astype(f32))[0].astype(bf16)
    n01, n10, n30 = gather_first(plain)

    heads_w = peers_parts(pack_heads(after(w_query, plain), w_key, w_value))
    n01, n10, n30 = lax.optimization_barrier((n01, n10, n30))
    n31, n20, n11 = gather_second(n01, n10)
    n31, n20, n11, heads_w = lax.optimization_barrier((n31, n20, n11, heads_w))
    n21 = gather_third(n31, n11)

    text_own = jnp.pad(after(text_states[0], n11), ((0, TXT_OWN - CAP_TOK), (0, 0)))
    text_columns = lax.all_to_all(text_own, FS, split_axis=1, concat_axis=0, tiled=True)
    heads_w = spread_heads(heads_w)
    plain_all, normed_all = place_rows(
        after(plain, text_columns),
        (n01, n10, n30),
        (n31, n20, n11),
        n21,
        row(ln1_gain),
        row(ln1_bias),
    )

    second_pack = jnp.where(first_core, c_key, c_value)
    second_pack, first_mine, normed_all = lax.optimization_barrier(
        (second_pack, first_mine, normed_all)
    )
    second_mine = lax.all_gather(second_pack, FS, axis=0, tiled=True)

    seg_col, seg_row = segment[:, None], segment[None, :]
    qkv = dot_nn(normed_all, heads_w).astype(bf16)
    context_part = dot_nn(after(text_columns, qkv), w_text).astype(bf16)
    context_parts = peers_parts(context_part)
    grad_out = cotangent[0]
    grad_mlp = grad_out.astype(bf16)
    grad_sent = after(grad_mlp, qkv)
    mlp_minus, mlp_plus = shift(grad_sent, "z", 1), shift(grad_sent, "z", -1)
    head0, total0 = self_forward(0, seg_col, seg_row, qkv)
    mlp_minus, mlp_plus, context_parts, head0 = lax.optimization_barrier(
        (mlp_minus, mlp_plus, context_parts, head0)
    )
    context = every_peer(sum_parts(context_parts).astype(bf16))
    mlp_far = (
        shift(halves(mlp_minus)[0], "z", 1),
        shift(halves(mlp_plus)[1], "z", -1),
    )
    head1, total1 = self_forward(1, seg_col, seg_row, after(qkv, head0))
    head1, context, *mlp_far = lax.optimization_barrier((head1, context, *mlp_far))
    first_other = shift(first_mine, "c", 1)
    attended = lax.all_to_all(
        jnp.concatenate([head0, head1], axis=1), FS, split_axis=0, concat_axis=1, tiled=True
    )

    up_own = jnp.concatenate(
        [
            lax.dynamic_slice(w_up, (0, 4 * SHARD * k + SHARD * quarter), (SHARD, SHARD))
            for k in range(8)
        ],
        axis=1,
    )
    hidden_own = jnp.where(first_core, up_own, row_block(w_down, quarter, SHARD))
    hidden_mine = every_peer(after(hidden_own, attended))

    after_self, normed_two, cross_query = call(
        after_self_body,
        [
            (core_index, "smem"), (rows_in, "vmem"), (attended, "vmem"),
            (row(ln2_gain), "vmem"), (row(ln2_bias), "vmem"),
            (first_mine, "hbm"), (first_other, "hbm"),
        ],
        [((TOK, D), f32), ((TOK, D), bf16), ((TOK, D), bf16)],
        square_scratch(2),
    )
    second_mine = after(second_mine, cross_query)
    second_other = shift(second_mine, "c", 1)
    third_pack = after(jnp.where(first_core, c_out[:, :WIN], c_out[:, STEP:]), second_mine)
    third_mine = lax.all_gather(third_pack, FS, axis=0, tiled=True)
    cross_key, cross_value = call(
        text_keys_body,
        [
            (core_index, "smem"), (after(context, cross_query), "vmem"),
            (second_mine, "hbm"), (second_other, "hbm"),
        ],
        [((TXT, D), bf16), ((TXT, D), bf16)],
        square_scratch(2),
    )
    cross_mixed = cross_forward(
        query_caption[:, None], text_key[None, :], cross_query, cross_key, cross_value
    )
    third_mine, hidden_mine, cross_mixed = lax.optimization_barrier(
        (third_mine, hidden_mine, cross_mixed)
    )
    third_other = shift(third_mine, "c", 1)
    weights = (hidden_mine, shift(hidden_mine, "c", 1))
    after_cross, normed_three = call(
        after_cross_body,
        [
            (core_index, "smem"), (after_self, "vmem"), (cross_mixed, "vmem"),
            (row(ln3_gain), "vmem"), (row(ln3_bias), "vmem"),
            (third_mine, "hbm"), (third_other, "hbm"),
        ],
        [((TOK, D), f32), ((TOK, D), bf16)],
        square_scratch(1),
    )

    three_minus, three_plus = shift(normed_three, "z", 1), shift(normed_three, "z", -1)
    out_own, act_own, pre_own, back_own = mlp(core_index, (normed_three,), (grad_mlp,), *weights)
    three_minus, three_plus, out_own = lax.optimization_barrier(
        (three_minus, three_plus, out_own)
    )
    three_far = (
        shift(halves(three_minus)[0], "z", 1),
        shift(halves(three_plus)[1], "z", -1),
    )
    near = mlp(core_index, (three_minus, three_plus), (mlp_minus, mlp_plus), *weights)
    out_m, act_m, pre_m, back_m, out_p, act_p, pre_p, back_p = near
    *three_far, out_m = lax.optimization_barrier((*three_far, out_m))
    out_far, act_far, pre_far, back_far = mlp(core_index, three_far, mlp_far, *weights)
    back_minus, back_plus = reduce_z(back_far, back_m, back_p)
    keep, send = mlp_grads(
        core_index,
        (
            normed_three,
            three_minus,
            three_plus,
            after(jnp.concatenate(three_far, axis=0), back_minus, back_plus),
        ),
        (pre_own, pre_m, pre_p, pre_far),
        (act_own, act_m, act_p, act_far),
        (grad_mlp, mlp_minus, mlp_plus, jnp.concatenate(mlp_far, axis=0)),
    )
    back_minus, back_plus = shift(back_minus, "z", -1), shift(back_plus, "z", 1)
    hidden_sum = keep + shift(send, "c", 1)
    grad_after_cross, grad_cross_branch, grad_cross_mixed, sums_three = call(
        third_back_body,
        [
            (core_index, "smem"), (after_cross, "vmem"), (back_own, "vmem"),
            (back_minus, "vmem"), (back_plus, "vmem"), (grad_out, "vmem"),
            (row(ln3_gain), "vmem"), (third_mine, "hbm"), (third_other, "hbm"),
        ],
        [((TOK, D), f32), ((TOK, D), bf16), ((TOK, D), bf16), ((8, D), f32)],
        square_scratch(1),
    )

    grad_cquery_rows, grad_kv = cross_backward(
        text_key[:, None],
        query_caption[None, :],
        cross_query,
        cross_key,
        cross_value,
        after(grad_cross_mixed, hidden_sum),
    )
    kv_own = lax.psum_scatter(grad_kv, FS, scatter_dimension=0, tiled=True)
    grad_after_self, grad_self_branch, grad_attended, sums_two = call(
        second_back_body,
        [
            (core_index, "smem"), (after_self, "vmem"), (grad_cquery_rows, "vmem"),
            (grad_after_cross, "vmem"), (row(ln2_gain), "vmem"),
            (first_mine, "hbm"), (first_other, "hbm"),
        ],
        [((TOK, D), f32), ((TOK, D), bf16), ((TOK, D), bf16), ((8, D), f32)],
        square_scratch(2),
    )
    grad_heads = lax.all_to_all(grad_attended, FS, split_axis=1, concat_axis=0, tiled=True)

    query_rows = after(grad_cquery_rows, grad_attended)
    square = jnp.concatenate(
        [
            window_grad(cross_mixed, grad_cross_branch),
            window_grad(normed_two, query_rows),
            window_grad(attended, grad_self_branch),
        ],
        axis=1,
    )

    def square_chunk(dy, dx):
        return row_block(square, peer(dy, dx), SHARD)

    grad_heads, square = lax.optimization_barrier((grad_heads, square))
    s_lo, s_hi, s20 = reduce_first(square_chunk)
    hidden_parts = peers_parts(after(hidden_sum, grad_heads))

    grad_qkv = self_backward(0, seg_col, seg_row, total0, qkv, grad_heads)
    s_lo, s_hi, s20, kv_own, grad_qkv = lax.optimization_barrier(
        (s_lo, s_hi, s20, kv_own, grad_qkv)
    )
    kv_all = lax.all_gather(kv_own, FS, axis=0, tiled=True)
    s11, s31 = reduce_second(square_chunk, s_lo, s_hi)
    out_minus, out_plus = reduce_z(after(out_far, grad_qkv), out_m, out_p)
    grad_qkv = self_backward(1, seg_col, seg_row, total1, qkv, grad_heads, (grad_qkv,))
    s11, s31, hidden_parts, out_minus, out_plus, grad_qkv = lax.optimization_barrier(
        (s11, s31, hidden_parts, out_minus, out_plus, grad_qkv)
    )
    square_parts = reduce_third(square_chunk, s20, s11, s31)
    heads_own = heads_grad(normed_all, grad_qkv)
    heads_part = peers_parts(heads_own)
    normed_part, sums_one = first_part(after(grad_qkv, heads_own), heads_w, plain_all)
    normed_parts = peers_parts(after(normed_part, heads_part))
    norms = sum_everywhere(
        jnp.concatenate([sums_one[:2], sums_two[:2], sums_three[:2], jnp.zeros((2, D), f32)])
    )
    square = reduce_last(square_chunk, *square_parts).astype(bf16)
    square = jnp.concatenate(
        [square[:, WIN * k : WIN * (k + 1)] for k in range(3)]
        + [jnp.zeros((512 - 3 * SHARD, WIN), bf16)],
        axis=0,
    )
    out_minus, out_plus = shift(out_minus, "z", -1), shift(out_plus, "z", 1)
    outputs = (
        after_cross + out_own.astype(f32) + out_minus.astype(f32) + out_plus.astype(f32)
    )
    hidden_grad = sum_parts(after(hidden_parts, normed_part)).astype(bf16)
    hidden_grad = hidden_grad + shift(hidden_grad, "xh", 1)
    square = scatter_over_dp(square)
    normed_parts, norms, hidden_grad, square = lax.optimization_barrier(
        (normed_parts, norms, hidden_grad, square)
    )
    square = every_peer(square, "z")
    hidden_grad = every_peer(hidden_grad, "z")
    grad_w_up, grad_w_down = sort_hidden(core_index, hidden_grad, shift(hidden_grad, "c", 1))

    own_columns = lax.dynamic_slice_in_dim(context, peer(0, 0) * SHARD, SHARD, axis=1)
    text_part, grad_w_text, grad_w_kv = call(
        text_back_body,
        [
            (core_index, "smem"), (after(kv_all, normed_part), "vmem"), (own_columns, "vmem"),
            (text_columns, "vmem"), (w_text, "vmem"),
            (second_mine, "hbm"), (second_other, "hbm"),
        ],
        [((TXT, TXT), bf16), ((TXT, D), bf16), ((SHARD, 2 * D), bf16)],
        square_scratch(2),
    )

    grad_c_out, grad_c_query, grad_w_out = whole_columns(square, 3)
    heads_rows = unpack_heads(heads_part)

    def half(which):
        kv = jnp.where(which == 0, grad_w_kv[:, :D], grad_w_kv[:, D:])
        return jnp.concatenate(
            [
                row_block(grad_w_text, which, 256),
                row_block(heads_rows, which, 216),
                kv,
                jnp.zeros((640 - 616, D), bf16),
            ],
            axis=0,
        )

    mine = scatter_over_dp(half(core) + shift(half(1 - core), "c", 1))
    mine = every_peer(after(mine, normed_parts), "z")
    other = shift(mine, "c", 1)
    low = jnp.where(first_core, mine, other).astype(f32)
    high = jnp.where(first_core, other, mine).astype(f32)
    grad_w_text = jnp.concatenate([low[:256], high[:256]], axis=0)
    grad_w_query = low[256:400]
    grad_w_key = jnp.concatenate([low[400:472], high[256:328]], axis=0)
    grad_w_value = high[328:472]
    grad_c_key, grad_c_value = low[472:616], high[472:616]

    grad_tokens = call(
        first_back_body,
        [
            (rows_in, "vmem"), (normed_parts, "vmem"), (grad_after_self, "vmem"),
            (row(ln1_gain), "vmem"),
        ],
        [((TOK, D), f32)],
        [],
    )[0]
    grad_text = lax.all_to_all(
        after(text_part, normed_parts), FS, split_axis=0, concat_axis=1, tiled=True
    )
    grad_text = grad_text[:CAP_TOK].astype(f32)
    return (
        outputs[None],
        grad_tokens[None],
        grad_text[None],
        norms[0],
        norms[1],
        grad_w_query,
        grad_w_key,
        grad_w_value,
        grad_w_out,
        norms[2],
        norms[3],
        grad_c_query,
        grad_w_text,
        grad_c_key,
        grad_c_value,
        grad_c_out,
        norms[4],
        norms[5],
        grad_w_up,
        grad_w_down,
    )


def solution(mesh):
    split = Mesh(mesh.devices.reshape(2, 4, 2, 4, 2), ("xh", "z", "c", "y", "xl"))
    dp = ("xh", "z", "c")
    rows = P(dp, FS, None)
    per_row = P(dp, None)
    weight = P(FS, None)
    rep = P()
    in_specs = (
        rows, rows, per_row, per_row, per_row,
        rep, rep, weight, weight, weight, weight,
        rep, rep, weight, weight, weight, weight, weight,
        rep, rep, weight, weight, rows,
    )
    out_specs = (
        rows, rows, rows,
        rep, rep, weight, weight, weight, weight,
        rep, rep, weight, weight, weight, weight, weight,
        rep, rep, weight, weight,
    )
    return jax.shard_map(
        local, mesh=split, in_specs=in_specs, out_specs=out_specs, check_vma=False
    )
```

time: 768 us -> 792 us (1.031)
  waiting for transfers between devices: 135 us -> 229 us
  Pallas kernels: 151 us -> 221 us
  matrix products: 84.7 us -> 18.1 us
  local copies, waits for them, and re-layouts: 111 us -> 60.4 us
  other arithmetic: 87.4 us -> 55.4 us
  blocking collectives: 0 us -> 11.1 us
    pallas_call x6 -> x15, Pallas kernels: 43.8 us -> 114 us  [the longest x7 51.4 us: call(): pl.pallas_call(body, in_specs=[pl.BlockSpec(memory_space=spaces[where]) f...]
    all_to_all x7 -> x4, waiting for transfers between devices: 17.4 us -> 47.1 us  [every_peer(): return lax.all_to_all(copies, axes, 0, 0, tiled=True)]
    dot_general x7 -> x0, matrix products: 27.4 us -> none  [dot_nt(): lax.dot_general(a, b, (((1,), (1,)), ((), ())), preferred_element_type=f32)]
    dot_general x7 -> x3, matrix products: 29.9 us -> 7.26 us  [dot_tn(): lax.dot_general(a, b, (((0,), (0,)), ((), ())), preferred_element_type=f32)]
    all_to_all x4 -> x5, waiting for transfers between devices: 16.7 us -> 39.2 us  [peers_parts(): return lax.all_to_all(x, axes, 0, 0, tiled=True)]
    unnamed x239 -> x117, local copies, waits for them, and re-layouts: 25.6 us -> 7.79 us
    dot_general x7 -> x2, matrix products: 27.4 us -> 10.8 us  [dot_nn(): lax.dot_general(a, b, (((1,), (0,)), ((), ())), preferred_element_type=f32)]
    all_to_all x7 -> x4, starting transfers between devices: 29.8 us -> 15.1 us  [every_peer(): return lax.all_to_all(copies, axes, 0, 0, tiled=True)]
  transfers between devices with their start and end apart: 98 -> 79, of which waited for: 33 -> 29; matrix products, arithmetic and copies ran while one was open for 31% -> 15% of each run, Pallas kernels for 18% -> 24%
where the time goes in v6:
time: 792 us; the launch traced here: 780 us
  waiting for transfers between devices  229 us (29%)
  Pallas kernels  221 us (28%)
  starting transfers between devices  170 us (21%)
  local copies, waits for them, and re-layouts  60.4 us (8%)
  other arithmetic  55.4 us (7%)
  matrix products  18.1 us (2%)
  between operations  15.4 us (2%)
  blocking collectives  11.1 us (1%)
    ppermute x59, starting transfers between devices, shift(): return lax.ppermute(x, axis, [(i, (i + by) % n) for i in range(n)])  113 us
    ppermute x59, waiting for transfers between devices, shift(): return lax.ppermute(x, axis, [(i, (i + by) % n) for i in range(n)])  110 us
    pallas_call x7, Pallas kernels, call(): pl.pallas_call(body, in_specs=[pl.BlockSpec(memory_space=spaces[where]) f...  51.4 us
    all_to_all x4, waiting for transfers between devices, every_peer(): return lax.all_to_all(copies, axes, 0, 0, tiled=True)  47.1 us
    all_to_all x5, waiting for transfers between devices, peers_parts(): return lax.all_to_all(x, axes, 0, 0, tiled=True)  39.2 us
    pallas_call x2, Pallas kernels, self_backward(): pl.pallas_call(functools.partial(self_backward_body, head), grid=(ROW //...  37.2 us
    pallas_call x3, Pallas kernels, mlp(): pl.pallas_call(functools.partial(mlp_body, parts, count), in_specs=[pl.Bl...  28.3 us
    pallas_call x2, Pallas kernels, self_forward(): pl.pallas_call(self_forward_body, grid=(ROW // TOK,), in_specs=[pl.BlockS...  24.3 us
  transfers between devices with their start and end apart: 79, of which 29 were waited for; matrix products, arithmetic and copies ran while one was open for 15% of the time, Pallas kernels for 24%

profile of v6, /device:TPU:1, one launch (start us, length us, event | category | flops | bytes accessed | tf_op | source)
XLA Modules:
  0.0 780.0 jit_solution(17719120430577169095)
XLA Ops:
  34.1 19.5 %all-to-all-done = bf16[8,144,432]{2,1,0:T(8,128)(2,1)S(1)} async-done(((bf16[8,144,432]{2,1,0:T(8,128)(2,1)}), bf16[8,144,432]{2,1,0:T(8,128)(2,1)S(1)}, u32[]{:S(2)}, u32[]{:S(2)}) %all-to-all-start) | async-done | bytes 995360 | tf_op jit(solution)/shard_map/all_to_all | solution.py:117
  53.6 22.7 %collective-permute-done.5.refs_6_ = bf16[256,1152]{1,0:T(8,128)(2,1)S(1)} collective-permute-done((bf16[256,1152]{1,0:T(8,128)(2,1)S(1)}, bf16[256,1152]{1,0:T(8,128)(2,1)S(1)}, u32[]{:S(2)}, u32[]{:S(2)}) %collective-permute-start.5) | collective-permute-done | bytes 589856 | tf_op jit(solution)/shard_map/ppermute | solution.py:56
  89.8 10.2 %all-to-all-done.1 = bf16[64,8,512]{2,0,1:T(8,128)(2,1)S(1)} async-done(((bf16[64,8,512]{2,0,1:T(8,128)(2,1)}), bf16[64,8,512]{2,0,1:T(8,128)(2,1)S(1)}, u32[]{:S(2)}, u32[]{:S(2)}) %all-to-all-start.1) | async-done | bytes 524320 | tf_op jit(solution)/shard_map/all_to_all | solution.py:794
  116.7 9.0 %convolution_convert_fusion.q.kv = bf16[2048,768]{1,0:T(8,128)(2,1)} fusion(bf16[2048,1152]{1,0:T(8,128)(2,1)} %get-tuple-element.143.x, bf16[1152,768]{1,0:T(8,128)(2,1)} %shard_map.376.w), kind=kOutput, calls=%fused_computation.1 | convolution fusion | flops 3625451520 | bytes 9633792 | tf_op jit(solution)/shard_map/dot_general | solution.py:39
  143.3 12.1 %shard_map.377 = (bf16[2048,72]{1,0:T(8,128)(2,1)}, f32[1,2048]{1,0:T(1,128)}) custom-call(s32[2048,1]{1,0:T(8,128)} %copy.149.seg_q.seg_k, s32[1,2048]{1,0:T(1,128)} %bitcast.104, bf16[2048,768]{1,0:T(8,128)(2,1)} %convolution_convert_fusion.q.kv, bf16[2048,768]{1,0:T(8,128)(2,1)} %convolution_convert_fusion.q.kv), custom_call_target="tpu_custom_call" | custom-call | tf_op jit(solution)/shard_map/pallas_call | solution.py:226
  175.7 12.1 %shard_map.378 = (bf16[2048,72]{1,0:T(8,128)(2,1)}, f32[1,2048]{1,0:T(1,128)}) custom-call(s32[2048,1]{1,0:T(8,128)} %copy.149.seg_q.seg_k, s32[1,2048]{1,0:T(1,128)} %bitcast.105, bf16[2048,768]{1,0:T(8,128)(2,1)} %convolution_convert_fusion.q.kv, bf16[2048,768]{1,0:T(8,128)(2,1)} %convolution_convert_fusion.q.kv), custom_call_target="tpu_custom_call" | custom-call | tf_op jit(solution)/shard_map/pallas_call | solution.py:226
  236.5 8.3 %shard_map.380 = (bf16[512,1152]{1,0:T(8,128)(2,1)}, bf16[512,1152]{1,0:T(8,128)(2,1)}) custom-call(s32[1]{0:T(128)} %bitcast.core, bf16[512,1152]{1,0:T(8,128)(2,1)} %bitcast.24.context, bf16[1152,1152]{1,0:T(8,128)(2,1)} %all-gather.7.cloned.1.call-done.mine, bf16[1152,1152]{1,0:T(8,128)(2,1)} %collective-permute-done.13.other), custom_call_target="tpu_custom_call" | custom-call | tf_op jit(solution)/shard_map/pallas_call | solution.py:525
  244.9 11.7 %shard_map.381.mixed = bf16[256,1152]{1,0:T(8,128)(2,1)} custom-call(s32[256,1]{1,0:T(8,128)} %copy.153.cap_q, s32[1,512]{1,0:T(1,128)} %and_select_fusion.1.cap_t, bf16[256,1152]{1,0:T(8,128)(2,1)} %get-tuple-element.158.q, bf16[512,1152]{1,0:T(8,128)(2,1)} %get-tuple-element.164.k, bf16[512,1152]{1,0:T(8,128)(2,1)} %get-tuple-element.165.v), custom_call_target="tpu_custom_call" | custom-call | tf_op jit(solution)/shard_map/pallas_call | solution.py:317
  256.6 36.1 %all-to-all-done.5 = bf16[8,144,1152]{2,1,0:T(8,128)(2,1)S(1)} async-done(((bf16[8,144,1152]{2,1,0:T(8,128)(2,1)}), bf16[8,144,1152]{2,1,0:T(8,128)(2,1)S(1)}, u32[]{:S(2)}, u32[]{:S(2)}) %all-to-all-start.5) | async-done | bytes 2654240 | tf_op jit(solution)/shard_map/all_to_all | solution.py:113
  312.1 8.2 %shard_map.383 = (bf16[256,1152]{1,0:T(8,128)(2,1)}, bf16[256,1152]{1,0:T(8,128)(2,1)}, bf16[256,1152]{1,0:T(8,128)(2,1)}, bf16[256,1152]{1,0:T(8,128)(2,1)}) custom-call(s32[1]{0:T(128)} %bitcast.core, bf16[256,1152]{1,0:T(8,128)(2,1)} %get-tuple-element.169.refs_0_, bf16[256,1152]{1,0:T(8,128)(2,1)} %copy-done.3, bf16[1152,1152]{1,0:T(8,128)(2,1)} %bitcast.74, ...), custom_call_target="tpu_custom_call" | custom-call | tf_op jit(solution)/shard_map/pallas_call | solution.py:420
  329.6 11.9 %shard_map.384 = (bf16[256,1152]{1,0:T(8,128)(2,1)}, bf16[256,1152]{1,0:T(8,128)(2,1)}, bf16[256,1152]{1,0:T(8,128)(2,1)}, bf16[256,1152]{1,0:T(8,128)(2,1)}, bf...) custom-call(s32[1]{0:T(128)} %bitcast.core, ...), custom_call_target="tpu_custom_call" | custom-call | tf_op jit(solution)/shard_map/pallas_call | solution.py:420
  361.8 13.0 %shard_map.387 = (bf16[1152,1152]{1,0:T(8,128)(2,1)}, bf16[1152,1152]{1,0:T(8,128)(2,1)}) custom-call(s32[1]{0:T(128)} %bitcast.core, bf16[256,1152]{1,0:T(8,128)(2,1)} %get-tuple-element.169.refs_0_, bf16[256,1152]{1,0:T(8,128)(2,1)} %copy-done.6, bf16[256,1152]{1,0:T(8,128)(2,1)} %collective-permute-done.16.refs_1_.refs_2_, ...), custom_call_target="tpu_custom_call" | custom-call | tf_op jit(solution)/shard_map/pallas_call | solution.py:462
  381.5 12.2 %collective-permute-done.23.g2 = bf16[256,1152]{1,0:T(8,128)(2,1)S(1)} collective-permute-done((bf16[256,1152]{1,0:T(8,128)(2,1)S(1)}, bf16[256,1152]{1,0:T(8,128)(2,1)S(1)}, u32[]{:S(2)}, u32[]{:S(2)}) %collective-permute-start.23) | collective-permute-done | bytes 589856 | tf_op jit(solution)/shard_map/ppermute | solution.py:56
  405.4 15.3 %shard_map.388 = (bf16[256,1152]{1,0:T(8,128)(2,1)}, bf16[512,2304]{1,0:T(8,128)(2,1)}) custom-call(s32[512,1]{1,0:T(8,128)} %fusion.26.cap_t, s32[1,256]{1,0:T(1,128)} %bitcast.111, bf16[256,1152]{1,0:T(8,128)(2,1)} %get-tuple-element.158.q, bf16[512,1152]{1,0:T(8,128)(2,1)} %get-tuple-element.164.k, bf16[512,1152]{1,0:T(8,128)(2,1)} %get-tuple-element.165.v, ...), custom_call_target="tpu_custom_call" | custom-call | tf_op jit(solution)/shard_map/pallas_call | solution.py:345
  449.9 10.3 %all-to-all-done.6 = bf16[256,8,144]{0,2,1:T(8,128)(2,1)S(1)} async-done(((bf16[256,8,144]{0,2,1:T(8,128)(2,1)}), bf16[256,8,144]{0,2,1:T(8,128)(2,1)S(1)}, u32[]{:S(2)}, u32[]{:S(2)}) %all-to-all-start.6) | async-done | bytes 589856 | tf_op jit(solution)/shard_map/all_to_all | solution.py:945
  469.7 18.7 %shard_map.390.refs_0_ = bf16[2048,768]{1,0:T(8,128)(2,1)} custom-call(s32[2048,1]{1,0:T(8,128)} %copy.149.seg_q.seg_k, s32[1,2048]{1,0:T(1,128)} %bitcast.106, f32[1,2048]{1,0:T(1,128)} %get-tuple-element.206.total, bf16[2048,768]{1,0:T(8,128)(2,1)} %convolution_convert_fusion.q.kv, bf16[2048,768]{1,0:T(8,128)(2,1)} %convolution_convert_fusion.q.kv, ...), custom_call_target="tpu_custom_call" | custom-call | tf_op jit(solution)/shard_map/pallas_call | solution.py:278
  493.5 18.6 %shard_map.391.g = bf16[2048,768]{1,0:T(8,128)(2,1)} custom-call(s32[2048,1]{1,0:T(8,128)} %copy.149.seg_q.seg_k, s32[1,2048]{1,0:T(1,128)} %bitcast.107, f32[1,2048]{1,0:T(1,128)} %get-tuple-element.216.total, bf16[2048,768]{1,0:T(8,128)(2,1)} %convolution_convert_fusion.q.kv, ...), custom_call_target="tpu_custom_call", output_to_operand_aliasing={{}: (6, {})} | custom-call | tf_op jit(solution)/shard_map/pallas_call | solution.py:278
  523.8 14.4 %all-to-all-done.7 = bf16[8,144,1152]{2,1,0:T(8,128)(2,1)S(1)} async-done(((bf16[8,144,1152]{2,1,0:T(8,128)(2,1)}), bf16[8,144,1152]{2,1,0:T(8,128)(2,1)S(1)}, u32[]{:S(2)}, u32[]{:S(2)}) %all-to-all-start.7) | async-done | bytes 2654240 | tf_op jit(solution)/shard_map/all_to_all | solution.py:117
  538.2 21.6 %collective-permute-done.34 = bf16[144,1920]{1,0:T(8,128)(2,1)} collective-permute-done((bf16[144,1920]{1,0:T(8,128)(2,1)}, bf16[144,1920]{1,0:T(8,128)(2,1)}, u32[]{:S(2)}, u32[]{:S(2)}) %collective-permute-start.34) | collective-permute-done | bytes 552992 | tf_op jit(solution)/shard_map/ppermute | solution.py:56
  581.0 10.7 %shard_map.393 = (bf16[2048,1152]{1,0:T(8,128)(2,1)}, f32[8,1152]{1,0:T(8,128)}) custom-call(bf16[2048,768]{1,0:T(8,128)(2,1)} %shard_map.391.g, bf16[1152,768]{1,0:T(8,128)(2,1)} %shard_map.376.w, bf16[2048,1152]{1,0:T(8,128)(2,1)} %get-tuple-element.221.plain), custom_call_target="tpu_custom_call" | custom-call | tf_op jit(solution)/shard_map/pallas_call | solution.py:619
  602.0 11.0 %shard_map.395 = (bf16[512,512]{1,0:T(8,128)(2,1)}, bf16[512,1152]{1,0:T(8,128)(2,1)}, bf16[144,2304]{1,0:T(8,128)(2,1)}) custom-call(s32[1]{0:T(128)} %bitcast.core, bf16[512,2304]{1,0:T(8,128)(2,1)} %all-gather.11.cloned.1.call-done.kv, bf16[512,144]{1,0:T(8,128)(2,1)} %constant_dynamic-slice_fusion.6.cols, bf16[512,512]{1,0:T(8,128)(2,1)} %bitcast.97, ...), custom_call_target="tpu_custom_call" | custom-call | tf_op jit(solution)/shard_map/pallas_call | solution.py:525
  639.0 10.2 %collective-permute-done.40 = f32[8,1152]{1,0:T(8,128)S(1)} collective-permute-done((f32[8,1152]{1,0:T(8,128)S(1)}, f32[8,1152]{1,0:T(8,128)S(1)}, u32[]{:S(2)}, u32[]{:S(2)}) %collective-permute-start.40) | collective-permute-done | bytes 36896 | tf_op jit(solution)/shard_map/ppermute | solution.py:56
  683.0 9.1 %all-to-all-done.10 = bf16[8,64,512]{2,1,0:T(8,128)(2,1)S(1)} async-done(((bf16[8,64,512]{2,1,0:T(8,128)(2,1)}), bf16[8,64,512]{2,1,0:T(8,128)(2,1)S(1)}, u32[]{:S(2)}, u32[]{:S(2)}) %all-to-all-start.10) | async-done | bytes 524320 | tf_op jit(solution)/shard_map/all_to_all | solution.py:1050
  692.2 11.1 %all_to_all.176 = bf16[4,128,640]{2,1,0:T(8,128)(2,1)S(1)} all-to-all(bf16[4,128,640]{2,1,0:T(8,128)(2,1)S(1)} %broadcast_in_dim.143), channel_id=1, replica_groups=mesh['xh'=2,'z'=4,'c'=2,'y'=4,'xl'=2] {'z'}, dimensions={0} | all-to-all | bytes 1310720 | tf_op jit(solution)/shard_map/all_to_all | solution.py:113
  (410 shorter events, 426.6 us)
Async XLA Ops:
  7.2 106.2 %all-gather.5.cloned.1.call-start = ((), (), s32[]{:S(2)}) async-start(), calls=%async_computation.17 | async-start | bytes 2985984 | tf_op jit(solution)/shard_map/all_gather | solution.py:781
  17.4 36.2 %all-to-all-start = ((bf16[8,144,432]{2,1,0:T(8,128)(2,1)}), bf16[8,144,432]{2,1,0:T(8,128)(2,1)S(1)}, u32[]{:S(2)}, u32[]{:S(2)}) async-start(bf16[8,144,432]{2,1,0:T(8,128)(2,1)} %bitcast.88), calls=%async_computation | async-start | bytes 2359296 | tf_op jit(solution)/shard_map/all_to_all | solution.py:117
  31.6 44.7 %collective-permute-start.5 = (bf16[256,1152]{1,0:T(8,128)(2,1)S(1)}, bf16[256,1152]{1,0:T(8,128)(2,1)S(1)}, u32[]{:S(2)}, u32[]{:S(2)}) collective-permute-start(bf16[256,1152]{1,0:T(8,128)(2,1)S(1)} %collective-permute-done.1.refs_2_), channel_id=1, source_target_pairs={{0,1},{1,0},{2,3},{3,2},{4,5},{5,4},{6,7},{7,6},{8,9},{9,8},{10,11... | collective-permute-start | bytes 1769480 | tf_op jit(solution)/shard_map/ppermute | solution.py:56
  31.6 44.7 %collective-permute-start.3 = (bf16[256,1152]{1,0:T(8,128)(2,1)S(1)}, bf16[256,1152]{1,0:T(8,128)(2,1)S(1)}, u32[]{:S(2)}, u32[]{:S(2)}) collective-permute-start(bf16[256,1152]{1,0:T(8,128)(2,1)S(1)} %collective-permute-done.refs_1_), channel_id=1, source_target_pairs={{0,2},{2,4},{4,6},{6,0},{1,3},{3,5},{5,7},{7,1},{8,10},{10,12},{12... | collective-permute-start | bytes 1769480 | tf_op jit(solution)/shard_map/ppermute | solution.py:56
  85.2 134.9 %all-gather.7.cloned.1.call-start = ((), (), s32[]{:S(2)}) async-start(), calls=%async_computation.18 | async-start | bytes 2985984 | tf_op jit(solution)/shard_map/all_gather | solution.py:809
  127.5 33.1 %all-to-all-start.2 = ((bf16[8,64,1152]{2,1,0:T(8,128)(2,1)}), bf16[8,64,1152]{2,1,0:T(8,128)(2,1)}, u32[]{:S(2)}, u32[]{:S(2)}) async-start(bf16[8,64,1152]{2,1,0:T(8,128)(2,1)} %bitcast.101), calls=%async_computation.2 | async-start | bytes 2359296 | tf_op jit(solution)/shard_map/all_to_all | solution.py:117
  131.8 81.3 %collective-permute-start.12 = (bf16[1152,1152]{1,0:T(8,128)(2,1)S(1)}, bf16[1152,1152]{1,0:T(8,128)(2,1)}, u32[]{:S(2)}, u32[]{:S(2)}) collective-permute-start(bf16[1152,1152]{1,0:T(8,128)(2,1)S(1)} %copy-done.2), channel_id=1, source_target_pairs={{0,8},{8,0},{1,9},{9,1},{2,10},{10,2},{3,11},{11,3},{4,12},{12,4},... | collective-permute-start | bytes 7962632 | tf_op jit(solution)/shard_map/ppermute | solution.py:56
  163.2 32.8 %all-to-all-start.3 = ((bf16[8,64,1152]{2,1,0:T(8,128)(2,1)}), bf16[8,64,1152]{2,1,0:T(8,128)(2,1)}, u32[]{:S(2)}, u32[]{:S(2)}) async-start(bf16[8,64,1152]{2,1,0:T(8,128)(2,1)} %broadcast_in_dim.124), calls=%async_computation.3 | async-start | bytes 2359296 | tf_op jit(solution)/shard_map/all_to_all | solution.py:113
  204.3 90.4 %all-gather.9.cloned.1.call-start = ((), (), s32[]{:S(2)}) async-start(), calls=%async_computation.19 | async-start | bytes 1658880 | tf_op jit(solution)/shard_map/all_gather | solution.py:858
  229.9 62.8 %all-to-all-start.5 = ((bf16[8,144,1152]{2,1,0:T(8,128)(2,1)}), bf16[8,144,1152]{2,1,0:T(8,128)(2,1)S(1)}, u32[]{:S(2)}, u32[]{:S(2)}) async-start(bf16[8,144,1152]{2,1,0:T(8,128)(2,1)} %broadcast_in_dim.127), calls=%async_computation.5 | async-start | bytes 5308416 | tf_op jit(solution)/shard_map/all_to_all | solution.py:113
  233.6 258.9 %reduce-scatter.6.cloned.1.call-start = ((), (), s32[]{:S(2)}) async-start(), calls=%async_computation.20 | async-start | bytes 2654208 | tf_op jit(solution)/shard_map/reduce_scatter | solution.py:934
  463.3 29.2 %collective-permute-start.33 = (bf16[144,1920]{1,0:T(8,128)(2,1)}, bf16[144,1920]{1,0:T(8,128)(2,1)}, u32[]{:S(2)}, u32[]{:S(2)}) collective-permute-start(bf16[144,1920]{1,0:T(8,128)(2,1)} %constant_dynamic-slice_fusion.8), channel_id=1, source_target_pairs={{0,2},{2,4},{4,6},{6,0},{1,3},{3,5},{5,7},{7,1},{8,10},{10,12},{12... | collective-permute-start | bytes 1658888 | tf_op jit(solution)/shard_map/ppermute | solution.py:56
  488.4 49.8 %all-to-all-start.7 = ((bf16[8,144,1152]{2,1,0:T(8,128)(2,1)}), bf16[8,144,1152]{2,1,0:T(8,128)(2,1)S(1)}, u32[]{:S(2)}, u32[]{:S(2)}) async-start(bf16[8,144,1152]{2,1,0:T(8,128)(2,1)} %bitcast.79), calls=%async_computation.8 | async-start | bytes 5308416 | tf_op jit(solution)/shard_map/all_to_all | solution.py:117
  492.1 109.8 %all-gather.11.cloned.1.call-start = ((), (), s32[]{:S(2)}) async-start(), calls=%async_computation.21 | async-start | bytes 2654208 | tf_op jit(solution)/shard_map/all_gather | solution.py:968
  520.7 39.1 %collective-permute-start.34 = (bf16[144,1920]{1,0:T(8,128)(2,1)}, bf16[144,1920]{1,0:T(8,128)(2,1)}, u32[]{:S(2)}, u32[]{:S(2)}) collective-permute-start(bf16[144,1920]{1,0:T(8,128)(2,1)} %pad_maximum_fusion.13), channel_id=1, source_target_pairs={{0,1},{1,0},{2,3},{3,2},{4,5},{5,4},{6,7},{7,6},{8,9},{9,8},{10,11... | collective-permute-start | bytes 1658888 | tf_op jit(solution)/shard_map/ppermute | solution.py:56
  577.1 48.1 %collective-permute-start.50 = (bf16[144,1920]{1,0:T(8,128)(2,1)}, bf16[144,1920]{1,0:T(8,128)(2,1)}, u32[]{:S(2)}, u32[]{:S(2)}) collective-permute-start(bf16[144,1920]{1,0:T(8,128)(2,1)} %get-tuple-element.312), channel_id=1, source_target_pairs={{0,2},{2,4},{4,6},{6,0},{1,3},{3,5},{5,7},{7,1},{8,10},{10,12},{12... | collective-permute-start | bytes 1658888 | tf_op jit(solution)/shard_map/ppermute | solution.py:56
  578.3 46.8 %collective-permute-start.51 = (bf16[144,1920]{1,0:T(8,128)(2,1)}, bf16[144,1920]{1,0:T(8,128)(2,1)}, u32[]{:S(2)}, u32[]{:S(2)}) collective-permute-start(bf16[144,1920]{1,0:T(8,128)(2,1)} %get-tuple-element.314), channel_id=1, source_target_pairs={{0,1},{1,0},{2,3},{3,2},{4,5},{5,4},{6,7},{7,6},{8,9},{9,8},{10,11... | collective-permute-start | bytes 1658888 | tf_op jit(solution)/shard_map/ppermute | solution.py:56
  579.5 45.7 %collective-permute-start.52 = (bf16[144,1920]{1,0:T(8,128)(2,1)}, bf16[144,1920]{1,0:T(8,128)(2,1)}, u32[]{:S(2)}, u32[]{:S(2)}) collective-permute-start(bf16[144,1920]{1,0:T(8,128)(2,1)} %get-tuple-element.313), channel_id=1, source_target_pairs={{0,6},{2,0},{4,2},{6,4},{1,7},{3,1},{5,3},{7,5},{8,14},{10,8},{12,... | collective-permute-start | bytes 1658888 | tf_op jit(solution)/shard_map/ppermute | solution.py:56
  594.7 82.1 %all-to-all-start.9 = ((bf16[8,256,1152]{2,1,0:T(8,128)(2,1)}), bf16[8,256,1152]{2,1,0:T(8,128)(2,1)}, u32[]{:S(2)}, u32[]{:S(2)}) async-start(bf16[8,256,1152]{2,1,0:T(8,128)(2,1)} %bitcast.87), calls=%async_computation.10 | async-start | bytes 9437184 | tf_op jit(solution)/shard_map/all_to_all | solution.py:117
  599.3 62.9 %reduce-scatter.10.cloned.1.call-start = ((), (), s32[]{:S(2)}) async-start(), calls=%async_computation.23 | async-start | bytes 819200
  628.1 82.5 %reduce-scatter.8.cloned.1.call-start = ((), (), s32[]{:S(2)}) async-start(), calls=%async_computation.22 | async-start | bytes 1843200 | tf_op jit(solution)/shard_map/reduce_scatter | solution.py:697
  708.0 27.8 %collective-permute-start.38 = (bf16[256,1152]{1,0:T(8,128)(2,1)}, bf16[256,1152]{1,0:T(8,128)(2,1)}, u32[]{:S(2)}, u32[]{:S(2)}) collective-permute-start(bf16[256,1152]{1,0:T(8,128)(2,1)} %pad_maximum_fusion.11), channel_id=1, source_target_pairs={{0,48},{16,0},{32,16},{48,32},{1,49},{17,1},{33,17},{49,33},{2,50}... | collective-permute-start | bytes 1769480 | tf_op jit(solution)/shard_map/ppermute | solution.py:56
  724.1 32.8 %all-to-all-start.11 = ((bf16[4,160,1152]{2,1,0:T(8,128)(2,1)}), bf16[4,160,1152]{2,1,0:T(8,128)(2,1)S(1)}, u32[]{:S(2)}, u32[]{:S(2)}) async-start(bf16[4,160,1152]{2,1,0:T(8,128)(2,1)} %broadcast_in_dim.142), calls=%async_computation.13 | async-start | bytes 2949120 | tf_op jit(solution)/shard_map/all_to_all | solution.py:113
  727.7 29.3 %collective-permute-start.57 = (bf16[512,640]{1,0:T(8,128)(2,1)S(1)}, bf16[512,640]{1,0:T(8,128)(2,1)}, u32[]{:S(2)}, u32[]{:S(2)}) collective-permute-start(bf16[512,640]{1,0:T(8,128)(2,1)S(1)} %bitcast.91), channel_id=1, source_target_pairs={{0,8},{8,0},{1,9},{9,1},{2,10},{10,2},{3,11},{11,3},{4,12},{12,4},... | collective-permute-start | bytes 1966088 | tf_op jit(solution)/shard_map/ppermute | solution.py:56
  (113 other events, 1422.1 us)
Sparse Core Ops, SparseCore 0:
  10.3 98.6 all-gather.4
  113.6 91.5 all-gather.6
  227.2 67.3 all-gather.8
  420.9 61.8 reduce-scatter.5
  494.3 89.1 all-gather.10
  628.2 20.2 reduce-scatter.9
  651.6 24.9 reduce-scatter.7

commit v7 on v6

--- a/solution.py
+++ b/solution.py
@@ -121,6 +121,29 @@
     return jnp.sum(parts.reshape(8, -1, parts.shape[1]).astype(f32), axis=0)
 
 
+def neighbours(x):
+    return x, shift(x, "z", 1), shift(x, "z", 2), shift(x, "z", -1)
+
+
+def in_order(*around):
+    rows, cols = around[0].shape
+
+    def body(where, *refs):
+        ins, out = refs[:4], refs[4]
+        for k in range(4):
+            row = pl.multiple_of(lax.rem(where[0] + 4 - k, 4) * rows, 16)
+            out[pl.ds(row, rows), :] = ins[k][...]
+
+    vmem = pl.BlockSpec(memory_space=pltpu.VMEM)
+    return pl.pallas_call(
+        body,
+        in_specs=[pl.BlockSpec(memory_space=pltpu.SMEM)] + [vmem] * 4,
+        out_specs=vmem,
+        out_shape=jax.ShapeDtypeStruct((4 * rows, cols), bf16),
+        compiler_params=params(),
+    )(lax.axis_index("z").astype(jnp.int32)[None], *around)
+
+
 def reduce_z(far, minus, plus):
     lo, hi = halves(far)
     lo, hi = shift(lo, "z", -1), shift(hi, "z", 1)
@@ -176,6 +199,35 @@
         bias,
         *[x for x, _, _ in pieces],
     )
+
+
+QUARTER = 768
+
+
+def place_quarters(*quarters):
+    def body(where, own, minus, plus, far_lo, far_hi, out, sem):
+        started = []
+        half = far_lo.shape[0]
+        for k, (ref, turn, row) in enumerate(
+            ((own, 0, 0), (minus, 3, 0), (plus, 1, 0), (far_lo, 2, 0), (far_hi, 2, half))
+        ):
+            column = pl.multiple_of(lax.rem(where[0] + turn, 4) * QUARTER, 128)
+            one = pltpu.make_async_copy(
+                ref, out.at[pl.ds(row, ref.shape[0]), pl.ds(column, QUARTER)], sem.at[k]
+            )
+            one.start()
+            started.append(one)
+        for one in started:
+            one.wait()
+
+    return pl.pallas_call(
+        body,
+        in_specs=[pl.BlockSpec(memory_space=pltpu.SMEM)] + [pl.BlockSpec(memory_space=pl.ANY)] * 5,
+        out_specs=pl.BlockSpec(memory_space=pltpu.VMEM),
+        out_shape=jax.ShapeDtypeStruct((D, 4 * QUARTER), bf16),
+        scratch_shapes=[pltpu.SemaphoreType.DMA((5,))],
+        compiler_params=params(),
+    )(lax.axis_index("z").astype(jnp.int32)[None], *quarters)
 
 
 def pack_heads_body(wq, wk, wv, out):
@@ -352,10 +404,11 @@
     )(cap_t, cap_q, q, k, v, g)
 
 
-def fetch_pair(core, mine, other, first, second, sem):
+def fetch_pair(core, mine, other, first, second, sem, column=0):
     def run(a, b):
-        one = pltpu.make_async_copy(a, first, sem.at[0])
-        two = pltpu.make_async_copy(b, second, sem.at[1])
+        columns = pl.ds(column, D)
+        one = pltpu.make_async_copy(a.at[:, columns], first, sem.at[0])
+        two = pltpu.make_async_copy(b.at[:, columns], second, sem.at[1])
         one.start()
         two.start()
         one.wait()
@@ -372,9 +425,11 @@
 
 def fetch_windows(core, mine, other, whole, sem):
     def run(a, b):
-        one = pltpu.make_async_copy(a, whole.at[:, pl.ds(0, WIN)], sem.at[0])
+        one = pltpu.make_async_copy(
+            a.at[:, pl.ds(2 * D, WIN)], whole.at[:, pl.ds(0, WIN)], sem.at[0]
+        )
         two = pltpu.make_async_copy(
-            b.at[:, pl.ds(128, STEP)], whole.at[:, pl.ds(WIN, STEP)], sem.at[1]
+            b.at[:, pl.ds(2 * D + 128, STEP)], whole.at[:, pl.ds(WIN, STEP)], sem.at[1]
         )
         one.start()
         two.start()
@@ -433,42 +488,30 @@
     )(core, *xs, *gs, mine, other)
 
 
-def mlp_grads_body(core, *refs):
-    xs, pres, acts, gs = refs[0:4], refs[4:8], refs[8:12], refs[12:16]
-    keep, send = refs[16:]
-    up = sum(dot_tn(x[...], p[...]) for x, p in zip(xs, pres)).astype(bf16)
-    down = sum(dot_tn(a[...], g[...]) for a, g in zip(acts, gs)).astype(bf16)
-    first = core[0] == 0
-
-    @pl.when(first)
+def mlp_grad_body(which, core, *refs):
+    out = refs[16]
+
+    def run(xs, gs):
+        out[...] = sum(dot_tn(x[...], g[...]) for x, g in zip(xs, gs)).astype(bf16)
+
+    @pl.when(core[0] == which)
     def _():
-        keep[...] = up
-        send[...] = down
-
-    @pl.when(jnp.logical_not(first))
+        run(refs[:4], refs[4:8])
+
+    @pl.when(core[0] != which)
     def _():
-        keep[...] = down
-        send[...] = up
-
-
-def mlp_grads(core, xs, pres, acts, gs):
-    def whole(x):
-        return pl.BlockSpec(x.shape, lambda k: (0, 0))
-
-    def part(x):
-        return pl.BlockSpec((x.shape[0], 384), lambda k: (0, k))
-
-    out = pl.BlockSpec((D, 384), lambda k: (0, k))
-    return pl.pallas_call(
-        mlp_grads_body,
+        run(refs[8:12], refs[12:16])
+
+
+def mlp_grad(which, core, xs, pres, acts, gs):
+    whole = [pl.BlockSpec((TOK, D), lambda k: (0, 0))] * 4
+    part = [pl.BlockSpec((TOK, 384), lambda k: (0, k))] * 4
+    return pl.pallas_call(
+        functools.partial(mlp_grad_body, which),
         grid=(3,),
-        in_specs=[pl.BlockSpec(memory_space=pltpu.SMEM)]
-        + [whole(x) for x in xs]
-        + [part(x) for x in pres]
-        + [whole(x) for x in acts]
-        + [part(x) for x in gs],
-        out_specs=[out, out],
-        out_shape=[jax.ShapeDtypeStruct((D, D), bf16)] * 2,
+        in_specs=[pl.BlockSpec(memory_space=pltpu.SMEM)] + whole + part + whole + part,
+        out_specs=pl.BlockSpec((D, 384), lambda k: (0, k)),
+        out_shape=jax.ShapeDtypeStruct((D, D), bf16),
         compiler_params=params(),
     )(core, *xs, *pres, *acts, *gs)
 
@@ -546,7 +589,7 @@
 
 
 def text_keys_body(core, context, mine, other, key, value, w1, w2, sem):
-    fetch_pair(core, mine, other, w1, w2, sem)
+    fetch_pair(core, mine, other, w1, w2, sem, D)
     key[...] = dot_nn(context[...], w1[...]).astype(bf16)
     value[...] = dot_nn(context[...], w2[...]).astype(bf16)
 
@@ -589,7 +632,7 @@
 def text_back_body(
     core, kv, cols, text, w_text, mine, other, part, grad_text, grad_kv, w1, w2, sem
 ):
-    fetch_pair(core, mine, other, w1, w2, sem)
+    fetch_pair(core, mine, other, w1, w2, sem, D)
     low = (dot_nt(kv[:, :D], w1[...]) + dot_nt(kv[:, D:], w2[...])).astype(bf16)
     part[...] = dot_nt(low, w_text[...]).astype(bf16)
     grad_text[...] = dot_tn(text[...], low).astype(bf16)
@@ -696,19 +739,6 @@
 def scatter_over_dp(x):
     part = lax.psum_scatter(x, "z", scatter_dimension=0, tiled=True)
     return part + shift(part, "xh", 1)
-
-
-def whole_columns(mine, count):
-    other = shift(mine, "c", 1)
-    first = lax.axis_index("c") == 0
-    low = jnp.where(first, mine, other).astype(f32)
-    high = jnp.where(first, other, mine).astype(f32)
-    return [
-        jnp.concatenate(
-            [low[SHARD * k : SHARD * (k + 1)], high[SHARD * k : SHARD * (k + 1), 128:]], axis=1
-        )
-        for k in range(count)
-    ]
 
 
 def sum_everywhere(x):
@@ -778,7 +808,14 @@
     def row(x):
         return x[None, :]
 
-    first_mine = lax.all_gather(jnp.where(first_core, w_out, c_query), FS, axis=0, tiled=True)
+    gap = jnp.zeros((SHARD, 128), bf16)
+    square_pack = jnp.where(
+        first_core,
+        jnp.concatenate([w_out, c_key, c_out[:, :WIN], gap], axis=1),
+        jnp.concatenate([c_query, c_value, c_out[:, STEP:], gap], axis=1),
+    )
+    square_pack = lax.dynamic_slice_in_dim(square_pack, quarter * QUARTER, QUARTER, axis=1)
+    quarter_own = lax.all_gather(square_pack, FS, axis=0, tiled=True)
 
     rows_in = tokens[0]
     plain = normalize(rows_in.astype(f32))[0].astype(bf16)
@@ -787,50 +824,24 @@
     heads_w = peers_parts(pack_heads(after(w_query, plain), w_key, w_value))
     n01, n10, n30 = lax.optimization_barrier((n01, n10, n30))
     n31, n20, n11 = gather_second(n01, n10)
-    n31, n20, n11, heads_w = lax.optimization_barrier((n31, n20, n11, heads_w))
+
+    text_own = jnp.pad(after(text_states[0], heads_w), ((0, TXT_OWN - CAP_TOK), (0, 0)))
+    text_columns = lax.all_to_all(text_own, FS, split_axis=1, concat_axis=0, tiled=True)
+    n31, n20, n11, text_columns = lax.optimization_barrier((n31, n20, n11, text_columns))
     n21 = gather_third(n31, n11)
-
-    text_own = jnp.pad(after(text_states[0], n11), ((0, TXT_OWN - CAP_TOK), (0, 0)))
-    text_columns = lax.all_to_all(text_own, FS, split_axis=1, concat_axis=0, tiled=True)
     heads_w = spread_heads(heads_w)
+    context_part = dot_nn(text_columns, w_text).astype(bf16)
+    context_own = lax.psum_scatter(context_part, FS, scatter_dimension=0, tiled=True)
     plain_all, normed_all = place_rows(
-        after(plain, text_columns),
+        after(plain, context_part),
         (n01, n10, n30),
         (n31, n20, n11),
         n21,
         row(ln1_gain),
         row(ln1_bias),
     )
-
-    second_pack = jnp.where(first_core, c_key, c_value)
-    second_pack, first_mine, normed_all = lax.optimization_barrier(
-        (second_pack, first_mine, normed_all)
-    )
-    second_mine = lax.all_gather(second_pack, FS, axis=0, tiled=True)
-
-    seg_col, seg_row = segment[:, None], segment[None, :]
-    qkv = dot_nn(normed_all, heads_w).astype(bf16)
-    context_part = dot_nn(after(text_columns, qkv), w_text).astype(bf16)
-    context_parts = peers_parts(context_part)
-    grad_out = cotangent[0]
-    grad_mlp = grad_out.astype(bf16)
-    grad_sent = after(grad_mlp, qkv)
-    mlp_minus, mlp_plus = shift(grad_sent, "z", 1), shift(grad_sent, "z", -1)
-    head0, total0 = self_forward(0, seg_col, seg_row, qkv)
-    mlp_minus, mlp_plus, context_parts, head0 = lax.optimization_barrier(
-        (mlp_minus, mlp_plus, context_parts, head0)
-    )
-    context = every_peer(sum_parts(context_parts).astype(bf16))
-    mlp_far = (
-        shift(halves(mlp_minus)[0], "z", 1),
-        shift(halves(mlp_plus)[1], "z", -1),
-    )
-    head1, total1 = self_forward(1, seg_col, seg_row, after(qkv, head0))
-    head1, context, *mlp_far = lax.optimization_barrier((head1, context, *mlp_far))
-    first_other = shift(first_mine, "c", 1)
-    attended = lax.all_to_all(
-        jnp.concatenate([head0, head1], axis=1), FS, split_axis=0, concat_axis=1, tiled=True
-    )
+    quarter_own, normed_all = lax.optimization_barrier((quarter_own, normed_all))
+    quarter_minus, quarter_plus = shift(quarter_own, "z", 1), shift(quarter_own, "z", -1)
 
     up_own = jnp.concatenate(
         [
@@ -840,6 +851,29 @@
         axis=1,
     )
     hidden_own = jnp.where(first_core, up_own, row_block(w_down, quarter, SHARD))
+
+    seg_col, seg_row = segment[:, None], segment[None, :]
+    qkv = dot_nn(normed_all, heads_w).astype(bf16)
+    head0, total0 = self_forward(0, seg_col, seg_row, qkv)
+    head1, total1 = self_forward(1, seg_col, seg_row, after(qkv, head0))
+    quarter_minus, quarter_plus, context_own, head1 = lax.optimization_barrier(
+        (quarter_minus, quarter_plus, context_own, head1)
+    )
+    context = lax.all_gather(context_own, FS, axis=0, tiled=True)
+    quarter_far = (
+        shift(halves(quarter_minus)[0], "z", 1),
+        shift(halves(quarter_plus)[1], "z", -1),
+    )
+    attended = lax.all_to_all(
+        jnp.concatenate([head0, head1], axis=1), FS, split_axis=0, concat_axis=1, tiled=True
+    )
+    attended, *quarter_far = lax.optimization_barrier((attended, *quarter_far))
+    square_mine = place_quarters(quarter_own, quarter_minus, quarter_plus, *quarter_far)
+    square_other = shift(square_mine, "c", 1)
+    grad_out = cotangent[0]
+    grad_mlp = grad_out.astype(bf16)
+    grad_sent = after(grad_mlp, square_mine)
+    mlp_minus, mlp_plus = shift(grad_sent, "z", 1), shift(grad_sent, "z", -1)
     hidden_mine = every_peer(after(hidden_own, attended))
 
     after_self, normed_two, cross_query = call(
@@ -847,20 +881,16 @@
         [
             (core_index, "smem"), (rows_in, "vmem"), (attended, "vmem"),
             (row(ln2_gain), "vmem"), (row(ln2_bias), "vmem"),
-            (first_mine, "hbm"), (first_other, "hbm"),
+            (square_mine, "hbm"), (square_other, "hbm"),
         ],
         [((TOK, D), f32), ((TOK, D), bf16), ((TOK, D), bf16)],
         square_scratch(2),
     )
-    second_mine = after(second_mine, cross_query)
-    second_other = shift(second_mine, "c", 1)
-    third_pack = after(jnp.where(first_core, c_out[:, :WIN], c_out[:, STEP:]), second_mine)
-    third_mine = lax.all_gather(third_pack, FS, axis=0, tiled=True)
     cross_key, cross_value = call(
         text_keys_body,
         [
-            (core_index, "smem"), (after(context, cross_query), "vmem"),
-            (second_mine, "hbm"), (second_other, "hbm"),
+            (core_index, "smem"), (after(context, cross_query, mlp_minus, mlp_plus), "vmem"),
+            (square_mine, "hbm"), (square_other, "hbm"),
         ],
         [((TXT, D), bf16), ((TXT, D), bf16)],
         square_scratch(2),
@@ -868,20 +898,23 @@
     cross_mixed = cross_forward(
         query_caption[:, None], text_key[None, :], cross_query, cross_key, cross_value
     )
-    third_mine, hidden_mine, cross_mixed = lax.optimization_barrier(
-        (third_mine, hidden_mine, cross_mixed)
-    )
-    third_other = shift(third_mine, "c", 1)
+    hidden_mine = after(hidden_mine, cross_mixed)
     weights = (hidden_mine, shift(hidden_mine, "c", 1))
     after_cross, normed_three = call(
         after_cross_body,
         [
             (core_index, "smem"), (after_self, "vmem"), (cross_mixed, "vmem"),
             (row(ln3_gain), "vmem"), (row(ln3_bias), "vmem"),
-            (third_mine, "hbm"), (third_other, "hbm"),
+            (square_mine, "hbm"), (square_other, "hbm"),
         ],
         [((TOK, D), f32), ((TOK, D), bf16)],
         square_scratch(1),
+    )
+
+    mlp_sent = lax.optimization_barrier((mlp_minus, mlp_plus, cross_query))
+    mlp_far = (
+        shift(halves(mlp_sent[0])[0], "z", 1),
+        shift(halves(mlp_sent[1])[1], "z", -1),
     )
 
     three_minus, three_plus = shift(normed_three, "z", 1), shift(normed_three, "z", -1)
@@ -898,26 +931,24 @@
     *three_far, out_m = lax.optimization_barrier((*three_far, out_m))
     out_far, act_far, pre_far, back_far = mlp(core_index, three_far, mlp_far, *weights)
     back_minus, back_plus = reduce_z(back_far, back_m, back_p)
-    keep, send = mlp_grads(
-        core_index,
-        (
-            normed_three,
-            three_minus,
-            three_plus,
-            after(jnp.concatenate(three_far, axis=0), back_minus, back_plus),
-        ),
-        (pre_own, pre_m, pre_p, pre_far),
-        (act_own, act_m, act_p, act_far),
-        (grad_mlp, mlp_minus, mlp_plus, jnp.concatenate(mlp_far, axis=0)),
-    )
+    three_parts = (normed_three, three_minus, three_plus, jnp.concatenate(three_far, axis=0))
+    pre_parts = (pre_own, pre_m, pre_p, pre_far)
+    act_parts = (act_own, act_m, act_p, act_far)
+    mlp_parts = (grad_mlp, mlp_minus, mlp_plus, jnp.concatenate(mlp_far, axis=0))
+    send = mlp_grad(1, core_index, three_parts, pre_parts, act_parts, mlp_parts)
+    back_minus, back_plus, send = lax.optimization_barrier((back_minus, back_plus, send))
     back_minus, back_plus = shift(back_minus, "z", -1), shift(back_plus, "z", 1)
+    keep = mlp_grad(
+        0, core_index, three_parts, pre_parts, act_parts, (after(grad_mlp, send), *mlp_parts[1:])
+    )
+    back_minus, back_plus, keep = lax.optimization_barrier((back_minus, back_plus, keep))
     hidden_sum = keep + shift(send, "c", 1)
     grad_after_cross, grad_cross_branch, grad_cross_mixed, sums_three = call(
         third_back_body,
         [
             (core_index, "smem"), (after_cross, "vmem"), (back_own, "vmem"),
             (back_minus, "vmem"), (back_plus, "vmem"), (grad_out, "vmem"),
-            (row(ln3_gain), "vmem"), (third_mine, "hbm"), (third_other, "hbm"),
+            (row(ln3_gain), "vmem"), (square_mine, "hbm"), (square_other, "hbm"),
         ],
         [((TOK, D), f32), ((TOK, D), bf16), ((TOK, D), bf16), ((8, D), f32)],
         square_scratch(1),
@@ -929,7 +960,7 @@
         cross_query,
         cross_key,
         cross_value,
-        after(grad_cross_mixed, hidden_sum),
+        grad_cross_mixed,
     )
     kv_own = lax.psum_scatter(grad_kv, FS, scatter_dimension=0, tiled=True)
     grad_after_self, grad_self_branch, grad_attended, sums_two = call(
@@ -937,18 +968,17 @@
         [
             (core_index, "smem"), (after_self, "vmem"), (grad_cquery_rows, "vmem"),
             (grad_after_cross, "vmem"), (row(ln2_gain), "vmem"),
-            (first_mine, "hbm"), (first_other, "hbm"),
+            (square_mine, "hbm"), (square_other, "hbm"),
         ],
         [((TOK, D), f32), ((TOK, D), bf16), ((TOK, D), bf16), ((8, D), f32)],
         square_scratch(2),
     )
     grad_heads = lax.all_to_all(grad_attended, FS, split_axis=1, concat_axis=0, tiled=True)
 
-    query_rows = after(grad_cquery_rows, grad_attended)
     square = jnp.concatenate(
         [
-            window_grad(cross_mixed, grad_cross_branch),
-            window_grad(normed_two, query_rows),
+            window_grad(cross_mixed, after(grad_cross_branch, grad_attended)),
+            window_grad(normed_two, after(grad_cquery_rows, grad_attended)),
             window_grad(attended, grad_self_branch),
         ],
         axis=1,
@@ -958,47 +988,30 @@
         return row_block(square, peer(dy, dx), SHARD)
 
     grad_heads, square = lax.optimization_barrier((grad_heads, square))
+    hidden_parts = peers_parts(after(hidden_sum, grad_heads))
+    grad_qkv = self_backward(0, seg_col, seg_row, total0, qkv, grad_heads)
+    kv_own, grad_qkv, square = lax.optimization_barrier((kv_own, grad_qkv, square))
     s_lo, s_hi, s20 = reduce_first(square_chunk)
-    hidden_parts = peers_parts(after(hidden_sum, grad_heads))
-
-    grad_qkv = self_backward(0, seg_col, seg_row, total0, qkv, grad_heads)
-    s_lo, s_hi, s20, kv_own, grad_qkv = lax.optimization_barrier(
-        (s_lo, s_hi, s20, kv_own, grad_qkv)
-    )
     kv_all = lax.all_gather(kv_own, FS, axis=0, tiled=True)
+    out_minus, out_plus = reduce_z(after(out_far, kv_own), out_m, out_p)
+    grad_qkv = self_backward(
+        1, seg_col, seg_row, total1, qkv, after(grad_heads, kv_own), (grad_qkv,)
+    )
+    s_lo, s_hi, out_minus, out_plus, grad_qkv = lax.optimization_barrier(
+        (s_lo, s_hi, out_minus, out_plus, grad_qkv)
+    )
     s11, s31 = reduce_second(square_chunk, s_lo, s_hi)
-    out_minus, out_plus = reduce_z(after(out_far, grad_qkv), out_m, out_p)
-    grad_qkv = self_backward(1, seg_col, seg_row, total1, qkv, grad_heads, (grad_qkv,))
-    s11, s31, hidden_parts, out_minus, out_plus, grad_qkv = lax.optimization_barrier(
-        (s11, s31, hidden_parts, out_minus, out_plus, grad_qkv)
-    )
-    square_parts = reduce_third(square_chunk, s20, s11, s31)
     heads_own = heads_grad(normed_all, grad_qkv)
+    heads_own, hidden_parts = lax.optimization_barrier((heads_own, hidden_parts))
     heads_part = peers_parts(heads_own)
     normed_part, sums_one = first_part(after(grad_qkv, heads_own), heads_w, plain_all)
     normed_parts = peers_parts(after(normed_part, heads_part))
-    norms = sum_everywhere(
-        jnp.concatenate([sums_one[:2], sums_two[:2], sums_three[:2], jnp.zeros((2, D), f32)])
-    )
+    s11, s31, normed_part = lax.optimization_barrier((s11, s31, normed_part))
+    square_parts = reduce_third(square_chunk, s20, s11, s31)
     square = reduce_last(square_chunk, *square_parts).astype(bf16)
-    square = jnp.concatenate(
-        [square[:, WIN * k : WIN * (k + 1)] for k in range(3)]
-        + [jnp.zeros((512 - 3 * SHARD, WIN), bf16)],
-        axis=0,
-    )
-    out_minus, out_plus = shift(out_minus, "z", -1), shift(out_plus, "z", 1)
-    outputs = (
-        after_cross + out_own.astype(f32) + out_minus.astype(f32) + out_plus.astype(f32)
-    )
     hidden_grad = sum_parts(after(hidden_parts, normed_part)).astype(bf16)
     hidden_grad = hidden_grad + shift(hidden_grad, "xh", 1)
-    square = scatter_over_dp(square)
-    normed_parts, norms, hidden_grad, square = lax.optimization_barrier(
-        (normed_parts, norms, hidden_grad, square)
-    )
-    square = every_peer(square, "z")
-    hidden_grad = every_peer(hidden_grad, "z")
-    grad_w_up, grad_w_down = sort_hidden(core_index, hidden_grad, shift(hidden_grad, "c", 1))
+    hidden_z = neighbours(hidden_grad)
 
     own_columns = lax.dynamic_slice_in_dim(context, peer(0, 0) * SHARD, SHARD, axis=1)
     text_part, grad_w_text, grad_w_kv = call(
@@ -1006,37 +1019,69 @@
         [
             (core_index, "smem"), (after(kv_all, normed_part), "vmem"), (own_columns, "vmem"),
             (text_columns, "vmem"), (w_text, "vmem"),
-            (second_mine, "hbm"), (second_other, "hbm"),
+            (square_mine, "hbm"), (square_other, "hbm"),
         ],
         [((TXT, TXT), bf16), ((TXT, D), bf16), ((SHARD, 2 * D), bf16)],
         square_scratch(2),
     )
 
-    grad_c_out, grad_c_query, grad_w_out = whole_columns(square, 3)
     heads_rows = unpack_heads(heads_part)
+    early = row_block(heads_rows, core, 216) + shift(row_block(heads_rows, 1 - core, 216), "c", 1)
+    early = jnp.concatenate([early, jnp.zeros((256 - 216, D), bf16)], axis=0)
+    rest = jnp.zeros((256 - SHARD, WIN), bf16)
+    square = jnp.concatenate(
+        [early] + [
+            jnp.concatenate([square[:, WIN * k : WIN * (k + 1)], rest], axis=0) for k in range(3)
+        ],
+        axis=1,
+    )
+    early = scatter_over_dp(square)
 
     def half(which):
         kv = jnp.where(which == 0, grad_w_kv[:, :D], grad_w_kv[:, D:])
         return jnp.concatenate(
+            [row_block(grad_w_text, which, 256), kv, jnp.zeros((512 - 400, D), bf16)], axis=0
+        )
+
+    late = half(core) + shift(half(1 - core), "c", 1)
+    late = scatter_over_dp(late)
+    normed_parts, early, late, *hidden_z = lax.optimization_barrier(
+        (normed_parts, early, late, *hidden_z)
+    )
+    early = in_order(*neighbours(early))
+    late = in_order(*neighbours(late))
+    hidden_grad = in_order(*hidden_z)
+    grad_w_up, grad_w_down = sort_hidden(core_index, hidden_grad, shift(hidden_grad, "c", 1))
+    sums_one = after(sums_one, normed_parts)
+    norms = sum_everywhere(
+        jnp.concatenate([sums_one[:2], sums_two[:2], sums_three[:2], jnp.zeros((2, D), f32)])
+    )
+    other = shift(early, "c", 1)
+    low = jnp.where(first_core, early, other).astype(f32)
+    high = jnp.where(first_core, other, early).astype(f32)
+    grad_w_query = low[:144, :D]
+    grad_w_key = jnp.concatenate([low[144:216, :D], high[:72, :D]], axis=0)
+    grad_w_value = high[72:216, :D]
+    grad_c_out, grad_c_query, grad_w_out = (
+        jnp.concatenate(
             [
-                row_block(grad_w_text, which, 256),
-                row_block(heads_rows, which, 216),
-                kv,
-                jnp.zeros((640 - 616, D), bf16),
+                low[:SHARD, D + WIN * k : D + WIN * (k + 1)],
+                high[:SHARD, D + WIN * k + 128 : D + WIN * (k + 1)],
             ],
-            axis=0,
+            axis=1,
         )
-
-    mine = scatter_over_dp(half(core) + shift(half(1 - core), "c", 1))
-    mine = every_peer(after(mine, normed_parts), "z")
-    other = shift(mine, "c", 1)
-    low = jnp.where(first_core, mine, other).astype(f32)
-    high = jnp.where(first_core, other, mine).astype(f32)
+        for k in range(3)
+    )
+
+    other = shift(late, "c", 1)
+    low = jnp.where(first_core, late, other).astype(f32)
+    high = jnp.where(first_core, other, late).astype(f32)
     grad_w_text = jnp.concatenate([low[:256], high[:256]], axis=0)
-    grad_w_query = low[256:400]
-    grad_w_key = jnp.concatenate([low[400:472], high[256:328]], axis=0)
-    grad_w_value = high[328:472]
-    grad_c_key, grad_c_value = low[472:616], high[472:616]
+    grad_c_key, grad_c_value = low[256:400], high[256:400]
+    out_minus, out_plus = shift(out_minus, "z", -1), shift(out_plus, "z", 1)
+    outputs = (
+        after_cross + out_own.astype(f32) + out_minus.astype(f32) + out_plus.astype(f32)
+    )
 
     grad_tokens = call(
         first_back_body,

time: 792 us -> 784 us (0.990)
  starting transfers between devices: 170 us -> 140 us
  Pallas kernels: 221 us -> 240 us
  waiting for transfers between devices: 229 us -> 245 us
    ppermute x59 -> x71, waiting for transfers between devices: 110 us -> 174 us  [shift(): return lax.ppermute(x, axis, [(i, (i + by) % n) for i in range(n)])]
    all_to_all x4 -> x1, waiting for transfers between devices: 47.1 us -> 0.01 us  [every_peer(): return lax.all_to_all(copies, axes, 0, 0, tiled=True)]
    all_gather x3 -> x2, waiting for transfers between devices: 2.05 us -> 37 us  [the longest x1 37 us: local(): context = lax.all_gather(context_own, FS, axis=0, tiled=True)]
    all_to_all x5 -> x4, waiting for transfers between devices: 39.2 us -> 16.5 us  [peers_parts(): return lax.all_to_all(x, axes, 0, 0, tiled=True)]
    pallas_call x1 -> x6, Pallas kernels: 13 us -> 30.9 us  [the longest x2 17.4 us: mlp_grad(): pl.pallas_call(functools.partial(mlp_grad_body, which), grid=(3,), in_spe...]
    all_to_all x4 -> x1, starting transfers between devices: 15.1 us -> 3.63 us  [every_peer(): return lax.all_to_all(copies, axes, 0, 0, tiled=True)]
    all_to_all x1, waiting for transfers between devices: 9.08 us -> 0.01 us  [local(): lax.all_to_all(after(text_part, normed_parts), FS, split_axis=0, concat_a...]
    ppermute x59 -> x71, starting transfers between devices: 113 us -> 106 us  [shift(): return lax.ppermute(x, axis, [(i, (i + by) % n) for i in range(n)])]
  transfers between devices with their start and end apart: 79 -> 86, of which waited for: 29 -> 32; matrix products, arithmetic and copies ran while one was open for 15% -> 14% of each run, Pallas kernels for 24% -> 26%
where the time goes in v7:
time: 784 us; the launch traced here: 775 us
  waiting for transfers between devices  245 us (31%)
  Pallas kernels  240 us (31%)
  starting transfers between devices  140 us (18%)
  local copies, waits for them, and re-layouts  56.1 us (7%)
  other arithmetic  48.7 us (6%)
  matrix products  19.1 us (2%)
  between operations  15.6 us (2%)
  blocking collectives  11.1 us (1%)
    ppermute x71, waiting for transfers between devices, shift(): return lax.ppermute(x, axis, [(i, (i + by) % n) for i in range(n)])  174 us
    ppermute x71, starting transfers between devices, shift(): return lax.ppermute(x, axis, [(i, (i + by) % n) for i in range(n)])  106 us
    pallas_call x7, Pallas kernels, call(): pl.pallas_call(body, in_specs=[pl.BlockSpec(memory_space=spaces[where]) f...  51.4 us
    pallas_call x2, Pallas kernels, self_backward(): pl.pallas_call(functools.partial(self_backward_body, head), grid=(ROW //...  37.4 us
    all_gather x1, waiting for transfers between devices, local(): context = lax.all_gather(context_own, FS, axis=0, tiled=True)  37 us
    pallas_call x3, Pallas kernels, mlp(): pl.pallas_call(functools.partial(mlp_body, parts, count), in_specs=[pl.Bl...  28.7 us
    pallas_call x2, Pallas kernels, self_forward(): pl.pallas_call(self_forward_body, grid=(ROW // TOK,), in_specs=[pl.BlockS...  24.3 us
    all_to_all x4, starting transfers between devices, peers_parts(): return lax.all_to_all(x, axes, 0, 0, tiled=True)  18.6 us
  transfers between devices with their start and end apart: 86, of which 32 were waited for; matrix products, arithmetic and copies ran while one was open for 14% of the time, Pallas kernels for 26%

profile of v7, /device:TPU:1, one launch (start us, length us, event | category | flops | bytes accessed | tf_op | source)
XLA Modules:
  0.0 775.0 jit_solution(7590721255876844726)
XLA Ops:
  24.0 45.3 %collective-permute-done.refs_1_ = bf16[256,1152]{1,0:T(8,128)(2,1)S(1)} collective-permute-done((bf16[256,1152]{1,0:T(8,128)(2,1)S(1)}, bf16[256,1152]{1,0:T(8,128)(2,1)S(1)}, u32[]{:S(2)}, u32[]{:S(2)}) %collective-permute-start) | collective-permute-done | bytes 589856 | tf_op jit(solution)/shard_map/ppermute | solution.py:56
  78.5 8.1 %collective-permute-done.3.refs_4_ = bf16[256,1152]{1,0:T(8,128)(2,1)S(1)} collective-permute-done((bf16[256,1152]{1,0:T(8,128)(2,1)S(1)}, bf16[256,1152]{1,0:T(8,128)(2,1)S(1)}, u32[]{:S(2)}, u32[]{:S(2)}) %collective-permute-start.3) | collective-permute-done | bytes 589856 | tf_op jit(solution)/shard_map/ppermute | solution.py:56
  127.2 8.8 %convolution_convert_fusion.q.kv = bf16[2048,768]{1,0:T(8,128)(2,1)} fusion(bf16[2048,1152]{1,0:T(8,128)(2,1)} %get-tuple-element.149.x, bf16[1152,768]{1,0:T(8,128)(2,1)} %shard_map.376.w), kind=kOutput, calls=%fused_computation.5 | convolution fusion | flops 3625451520 | bytes 9633792 | tf_op jit(solution)/shard_map/dot_general | solution.py:39
  136.0 12.1 %shard_map.377 = (bf16[2048,72]{1,0:T(8,128)(2,1)}, f32[1,2048]{1,0:T(1,128)}) custom-call(s32[2048,1]{1,0:T(8,128)} %copy.114.seg_q.seg_k, s32[1,2048]{1,0:T(1,128)} %bitcast.88, bf16[2048,768]{1,0:T(8,128)(2,1)} %convolution_convert_fusion.q.kv, bf16[2048,768]{1,0:T(8,128)(2,1)} %convolution_convert_fusion.q.kv), custom_call_target="tpu_custom_call" | custom-call | tf_op jit(solution)/shard_map/pallas_call | solution.py:278
  148.2 12.2 %shard_map.378 = (bf16[2048,72]{1,0:T(8,128)(2,1)}, f32[1,2048]{1,0:T(1,128)}) custom-call(s32[2048,1]{1,0:T(8,128)} %copy.114.seg_q.seg_k, s32[1,2048]{1,0:T(1,128)} %bitcast.89, bf16[2048,768]{1,0:T(8,128)(2,1)} %convolution_convert_fusion.q.kv, bf16[2048,768]{1,0:T(8,128)(2,1)} %convolution_convert_fusion.q.kv), custom_call_target="tpu_custom_call" | custom-call | tf_op jit(solution)/shard_map/pallas_call | solution.py:278
  167.7 11.1 %all_to_all.128 = bf16[8,256,144]{1,2,0:T(8,128)(2,1)} all-to-all(bf16[8,256,144]{1,2,0:T(8,128)(2,1)S(1)} %copy.116), channel_id=1, replica_groups=mesh['xh'=2,'z'=4,'c'=2,'y'=4,'xl'=2] {'y','xl'}, dimensions={0} | all-to-all | bytes 1179648 | tf_op jit(solution)/shard_map/all_to_all | solution.py:867
  221.2 37.0 %all-gather.6.cloned.1.call-done.context = bf16[512,1152]{1,0:T(8,128)(2,1)} async-done(((bf16[64,1152]{1,0:T(8,128)(2,1)}), bf16[512,1152]{1,0:T(8,128)(2,1)}) %all-gather.6.cloned.1.call-update) | async-done | bytes 1179664 | tf_op jit(solution)/shard_map/all_gather | solution.py:862
  258.2 8.4 %shard_map.381 = (bf16[512,1152]{1,0:T(8,128)(2,1)}, bf16[512,1152]{1,0:T(8,128)(2,1)}) custom-call(s32[1]{0:T(128)} %bitcast.core, bf16[512,1152]{1,0:T(8,128)(2,1)} %all-gather.6.cloned.1.call-done.context, bf16[1152,3072]{1,0:T(8,128)(2,1)} %shard_map.379.mine, bf16[1152,3072]{1,0:T(8,128)(2,1)} %collective-permute-done.12.other), custom_call_target="tpu_custom_call" | custom-call | tf_op jit(solution)/shard_map/pallas_call | solution.py:568
  266.6 11.7 %shard_map.382.mixed = bf16[256,1152]{1,0:T(8,128)(2,1)} custom-call(s32[256,1]{1,0:T(8,128)} %copy.118.cap_q, s32[1,512]{1,0:T(1,128)} %and_select_fusion.1.cap_t, bf16[256,1152]{1,0:T(8,128)(2,1)} %get-tuple-element.161.q, bf16[512,1152]{1,0:T(8,128)(2,1)} %get-tuple-element.165.k, bf16[512,1152]{1,0:T(8,128)(2,1)} %get-tuple-element.166.v), custom_call_target="tpu_custom_call" | custom-call | tf_op jit(solution)/shard_map/pallas_call | solution.py:369
  294.6 8.2 %shard_map.384 = (bf16[256,1152]{1,0:T(8,128)(2,1)}, bf16[256,1152]{1,0:T(8,128)(2,1)}, bf16[256,1152]{1,0:T(8,128)(2,1)}, bf16[256,1152]{1,0:T(8,128)(2,1)}) custom-call(s32[1]{0:T(128)} %bitcast.core, bf16[256,1152]{1,0:T(8,128)(2,1)} %get-tuple-element.168.refs_0_, bf16[256,1152]{1,0:T(8,128)(2,1)} %copy-done.3, bf16[1152,1152]{1,0:T(8,128)(2,1)} %bitcast.63, ...), custom_call_target="tpu_custom_call" | custom-call | tf_op jit(solution)/shard_map/pallas_call | solution.py:475
  308.8 12.3 %shard_map.385 = (bf16[256,1152]{1,0:T(8,128)(2,1)}, bf16[256,1152]{1,0:T(8,128)(2,1)}, bf16[256,1152]{1,0:T(8,128)(2,1)}, bf16[256,1152]{1,0:T(8,128)(2,1)}, bf...) custom-call(s32[1]{0:T(128)} %bitcast.core, ...), custom_call_target="tpu_custom_call" | custom-call | tf_op jit(solution)/shard_map/pallas_call | solution.py:475
  322.0 8.2 %shard_map.386 = (bf16[256,1152]{1,0:T(8,128)(2,1)}, bf16[256,1152]{1,0:T(8,128)(2,1)}, bf16[256,1152]{1,0:T(8,128)(2,1)}, bf16[256,1152]{1,0:T(8,128)(2,1)}) custom-call(s32[1]{0:T(128)} %bitcast.core, bf16[128,1152]{1,0:T(8,128)(2,1)} %copy-done.25, bf16[128,1152]{1,0:T(8,128)(2,1)} %copy-done.26, bf16[128,1152]{1,0:T(8,128)(2,1)} %copy-done.23, ...), custom_call_target="tpu_custom_call" | custom-call | tf_op jit(solution)/shard_map/pallas_call | solution.py:475
  335.9 8.8 %shard_map.387 = bf16[1152,1152]{1,0:T(8,128)(2,1)} custom-call(s32[1]{0:T(128)} %bitcast.core, bf16[256,1152]{1,0:T(8,128)(2,1)} %get-tuple-element.168.refs_0_, bf16[256,1152]{1,0:T(8,128)(2,1)} %copy-done.4, bf16[256,1152]{1,0:T(8,128)(2,1)} %collective-permute-done.16.refs_1_.refs_2_, bf16[256,1152]{1,0:T(8,128)(2,1)} %copy-done.12, ...), custom_call_target="tpu_custom_call" | custom-call | tf_op jit(solution)/shard_map/pallas_call | solution.py:509
  348.9 8.7 %shard_map.388 = bf16[1152,1152]{1,0:T(8,128)(2,1)} custom-call(s32[1]{0:T(128)} %bitcast.core, bf16[256,1152]{1,0:T(8,128)(2,1)} %get-tuple-element.168.refs_0_, bf16[256,1152]{1,0:T(8,128)(2,1)} %copy-done.4, bf16[256,1152]{1,0:T(8,128)(2,1)} %collective-permute-done.16.refs_1_.refs_2_, bf16[256,1152]{1,0:T(8,128)(2,1)} %copy-done.12, ...), custom_call_target="tpu_custom_call" | custom-call | tf_op jit(solution)/shard_map/pallas_call | solution.py:509
  368.7 15.3 %shard_map.390 = (bf16[256,1152]{1,0:T(8,128)(2,1)}, bf16[512,2304]{1,0:T(8,128)(2,1)}) custom-call(s32[512,1]{1,0:T(8,128)} %fusion.35.cap_t, s32[1,256]{1,0:T(1,128)} %bitcast.95, bf16[256,1152]{1,0:T(8,128)(2,1)} %get-tuple-element.161.q, bf16[512,1152]{1,0:T(8,128)(2,1)} %get-tuple-element.165.k, bf16[512,1152]{1,0:T(8,128)(2,1)} %get-tuple-element.166.v, ...), custom_call_target="tpu_custom_call" | custom-call | tf_op jit(solution)/shard_map/pallas_call | solution.py:397
  415.1 8.1 %all-to-all-done.4 = bf16[256,8,144]{0,2,1:T(8,128)(2,1)S(1)} async-done(((bf16[256,8,144]{0,2,1:T(8,128)(2,1)}), bf16[256,8,144]{0,2,1:T(8,128)(2,1)S(1)}, u32[]{:S(2)}, u32[]{:S(2)}) %all-to-all-start.4) | async-done | bytes 589856 | tf_op jit(solution)/shard_map/all_to_all | solution.py:976
  424.5 18.8 %shard_map.392.refs_0_ = bf16[2048,768]{1,0:T(8,128)(2,1)} custom-call(s32[2048,1]{1,0:T(8,128)} %copy.114.seg_q.seg_k, s32[1,2048]{1,0:T(1,128)} %bitcast.90, f32[1,2048]{1,0:T(1,128)} %get-tuple-element.200.total, bf16[2048,768]{1,0:T(8,128)(2,1)} %convolution_convert_fusion.q.kv, bf16[2048,768]{1,0:T(8,128)(2,1)} %convolution_convert_fusion.q.kv, ...), custom_call_target="tpu_custom_call" | custom-call | tf_op jit(solution)/shard_map/pallas_call | solution.py:330
  458.7 18.6 %shard_map.393.g = bf16[2048,768]{1,0:T(8,128)(2,1)} custom-call(s32[2048,1]{1,0:T(8,128)} %copy.114.seg_q.seg_k, s32[1,2048]{1,0:T(1,128)} %bitcast.91, f32[1,2048]{1,0:T(1,128)} %get-tuple-element.217.total, bf16[2048,768]{1,0:T(8,128)(2,1)} %convolution_convert_fusion.q.kv, ...), custom_call_target="tpu_custom_call", output_to_operand_aliasing={{}: (6, {})} | custom-call | tf_op jit(solution)/shard_map/pallas_call | solution.py:330
  489.6 9.8 %collective-permute-start.41 = (bf16[144,1920]{1,0:T(8,128)(2,1)S(1)}, bf16[144,1920]{1,0:T(8,128)(2,1)}, u32[]{:S(2)}, u32[]{:S(2)}) collective-permute-start(bf16[144,1920]{1,0:T(8,128)(2,1)S(1)} %pad_maximum_fusion.11), channel_id=1, source_target_pairs={{0,1},{1,0},{2,3},{3,2},{4,5},{5,4},{6,7},{7,6},{8,9},{9,8},{10,11... | collective-permute-start | bytes 1658888 | tf_op jit(solution)/shard_map/ppermute | solution.py:56
  516.1 10.8 %shard_map.395 = (bf16[2048,1152]{1,0:T(8,128)(2,1)}, f32[8,1152]{1,0:T(8,128)}) custom-call(bf16[2048,768]{1,0:T(8,128)(2,1)} %shard_map.393.g, bf16[1152,768]{1,0:T(8,128)(2,1)} %shard_map.376.w, bf16[2048,1152]{1,0:T(8,128)(2,1)} %get-tuple-element.227.plain), custom_call_target="tpu_custom_call" | custom-call | tf_op jit(solution)/shard_map/pallas_call | solution.py:662
  533.9 16.5 %all-to-all-done.6 = bf16[8,144,432]{2,1,0:T(8,128)(2,1)} async-done(((bf16[8,144,432]{2,1,0:T(8,128)(2,1)}), bf16[8,144,432]{2,1,0:T(8,128)(2,1)}, u32[]{:S(2)}, u32[]{:S(2)}) %all-to-all-start.6) | async-done | bytes 995360 | tf_op jit(solution)/shard_map/all_to_all | solution.py:117
  570.9 11.0 %shard_map.397 = (bf16[512,512]{1,0:T(8,128)(2,1)}, bf16[512,1152]{1,0:T(8,128)(2,1)}, bf16[144,2304]{1,0:T(8,128)(2,1)}) custom-call(s32[1]{0:T(128)} %bitcast.core, bf16[512,2304]{1,0:T(8,128)(2,1)} %all-gather.8.cloned.1.call-done.kv, bf16[512,144]{1,0:T(8,128)(2,1)} %constant_dynamic-slice_fusion.4.cols, bf16[512,512]{1,0:T(8,128)(2,1)} %bitcast.82, ...), custom_call_target="tpu_custom_call" | custom-call | tf_op jit(solution)/shard_map/pallas_call | solution.py:568
  597.7 55.0 %collective-permute-done.49 = bf16[144,1152]{1,0:T(8,128)(2,1)S(1)} collective-permute-done((bf16[144,1152]{1,0:T(8,128)(2,1)S(1)}, bf16[144,1152]{1,0:T(8,128)(2,1)S(1)}, u32[]{:S(2)}, u32[]{:S(2)}) %collective-permute-start.49) | collective-permute-done | bytes 331808 | tf_op jit(solution)/shard_map/ppermute | solution.py:56
  716.9 11.1 %collective-permute-done.63.refs_2_ = bf16[64,3072]{1,0:T(8,128)(2,1)S(1)} collective-permute-done((bf16[64,3072]{1,0:T(8,128)(2,1)S(1)}, bf16[64,3072]{1,0:T(8,128)(2,1)S(1)}, u32[]{:S(2)}, u32[]{:S(2)}) %collective-permute-start.63) | collective-permute-done | bytes 393248 | tf_op jit(solution)/shard_map/ppermute | solution.py:56
  (438 shorter events, 383.6 us)
Async XLA Ops:
  7.2 112.0 %all-gather.4.cloned.1.call-start = ((), (), s32[]{:S(2)}) async-start(), calls=%async_computation.13 | async-start | bytes 1990656 | tf_op jit(solution)/shard_map/all_gather | solution.py:818
  14.2 58.5 %all-to-all-start = ((bf16[8,144,432]{2,1,0:T(8,128)(2,1)}), bf16[8,144,432]{2,1,0:T(8,128)(2,1)S(1)}, u32[]{:S(2)}, u32[]{:S(2)}) async-start(bf16[8,144,432]{2,1,0:T(8,128)(2,1)} %bitcast.74), calls=%async_computation | async-start | bytes 2359296 | tf_op jit(solution)/shard_map/all_to_all | solution.py:117
  20.1 49.2 %collective-permute-start = (bf16[256,1152]{1,0:T(8,128)(2,1)S(1)}, bf16[256,1152]{1,0:T(8,128)(2,1)S(1)}, u32[]{:S(2)}, u32[]{:S(2)}) collective-permute-start(bf16[256,1152]{1,0:T(8,128)(2,1)S(1)} %fusion.12.refs_0_), channel_id=1, source_target_pairs={{0,1},{1,0},{2,3},{3,2},{4,5},{5,4},{6,7},{7,6},{8,9},{9,8},{10,11... | collective-permute-start | bytes 1769480 | tf_op jit(solution)/shard_map/ppermute | solution.py:56
  21.6 47.7 %collective-permute-start.1 = (bf16[256,1152]{1,0:T(8,128)(2,1)S(1)}, bf16[256,1152]{1,0:T(8,128)(2,1)}, u32[]{:S(2)}, u32[]{:S(2)}) collective-permute-start(bf16[256,1152]{1,0:T(8,128)(2,1)S(1)} %fusion.12.refs_0_), channel_id=1, source_target_pairs={{0,6},{2,0},{4,2},{6,4},{1,7},{3,1},{5,3},{7,5},{8,14},{10,8},{12,... | collective-permute-start | bytes 1769480 | tf_op jit(solution)/shard_map/ppermute | solution.py:56
  24.0 45.3 %collective-permute-start.2 = (bf16[256,1152]{1,0:T(8,128)(2,1)S(1)}, bf16[256,1152]{1,0:T(8,128)(2,1)}, u32[]{:S(2)}, u32[]{:S(2)}) collective-permute-start(bf16[256,1152]{1,0:T(8,128)(2,1)S(1)} %fusion.12.refs_0_), channel_id=1, source_target_pairs={{0,2},{2,4},{4,6},{6,0},{1,3},{3,5},{5,7},{7,1},{8,10},{10,12},{12... | collective-permute-start | bytes 1769480 | tf_op jit(solution)/shard_map/ppermute | solution.py:56
  78.5 81.9 %reduce-scatter.5.cloned.1.call-start = ((), (), s32[]{:S(2)}) async-start(), calls=%async_computation.14 | async-start | bytes 1327104 | tf_op jit(solution)/shard_map/reduce_scatter | solution.py:834
  119.2 41.2 %collective-permute-start.8 = (bf16[1152,768]{1,0:T(8,128)(2,1)}, bf16[1152,768]{1,0:T(8,128)(2,1)S(1)}, u32[]{:S(2)}, u32[]{:S(2)}) collective-permute-start(bf16[1152,768]{1,0:T(8,128)(2,1)} %all-gather.4.cloned.1.call-done.own), channel_id=1, source_target_pairs={{0,16},{16,32},{32,48},{48,0},{1,17},{17,33},{33,49},{49,1},{2,18}... | collective-permute-start | bytes 5308424 | tf_op jit(solution)/shard_map/ppermute | solution.py:56
  122.2 38.7 %collective-permute-start.9 = (bf16[1152,768]{1,0:T(8,128)(2,1)}, bf16[1152,768]{1,0:T(8,128)(2,1)}, u32[]{:S(2)}, u32[]{:S(2)}) collective-permute-start(bf16[1152,768]{1,0:T(8,128)(2,1)} %all-gather.4.cloned.1.call-done.own), channel_id=1, source_target_pairs={{0,48},{16,0},{32,16},{48,32},{1,49},{17,1},{33,17},{49,33},{2,50}... | collective-permute-start | bytes 5308424 | tf_op jit(solution)/shard_map/ppermute | solution.py:56
  198.8 79.5 %all-to-all-start.3 = ((bf16[8,144,1152]{2,1,0:T(8,128)(2,1)}), bf16[8,144,1152]{2,1,0:T(8,128)(2,1)S(1)}, u32[]{:S(2)}, u32[]{:S(2)}) async-start(bf16[8,144,1152]{2,1,0:T(8,128)(2,1)} %broadcast_in_dim.121), calls=%async_computation.4 | async-start | bytes 5308416 | tf_op jit(solution)/shard_map/all_to_all | solution.py:113
  202.5 55.7 %all-gather.6.cloned.1.call-start = ((), (), s32[]{:S(2)}) async-start(), calls=%async_computation.15 | async-start | bytes 1327104 | tf_op jit(solution)/shard_map/all_gather | solution.py:862
  203.2 247.8 %reduce-scatter.7.cloned.1.call-start = ((), (), s32[]{:S(2)}) async-start(), calls=%async_computation.16 | async-start | bytes 2654208 | tf_op jit(solution)/shard_map/reduce_scatter | solution.py:965
  384.1 59.2 %collective-permute-start.38 = (bf16[1152,1152]{1,0:T(8,128)(2,1)}, bf16[1152,1152]{1,0:T(8,128)(2,1)}, u32[]{:S(2)}, u32[]{:S(2)}) collective-permute-start(bf16[1152,1152]{1,0:T(8,128)(2,1)} %shard_map.387), channel_id=1, source_target_pairs={{0,8},{8,0},{1,9},{9,1},{2,10},{10,2},{3,11},{11,3},{4,12},{12,4},... | collective-permute-start | bytes 7962632 | tf_op jit(solution)/shard_map/ppermute | solution.py:56
  447.2 64.5 %all-to-all-start.5 = ((bf16[8,144,1152]{2,1,0:T(8,128)(2,1)}), bf16[8,144,1152]{2,1,0:T(8,128)(2,1)S(1)}, u32[]{:S(2)}, u32[]{:S(2)}) async-start(bf16[8,144,1152]{2,1,0:T(8,128)(2,1)} %bitcast.68), calls=%async_computation.7 | async-start | bytes 5308416 | tf_op jit(solution)/shard_map/all_to_all | solution.py:117
  451.0 119.9 %all-gather.8.cloned.1.call-start = ((), (), s32[]{:S(2)}) async-start(), calls=%async_computation.18 | async-start | bytes 2654208 | tf_op jit(solution)/shard_map/all_gather | solution.py:995
  489.6 37.3 %collective-permute-start.41 = (bf16[144,1920]{1,0:T(8,128)(2,1)S(1)}, bf16[144,1920]{1,0:T(8,128)(2,1)}, u32[]{:S(2)}, u32[]{:S(2)}) collective-permute-start(bf16[144,1920]{1,0:T(8,128)(2,1)S(1)} %pad_maximum_fusion.11), channel_id=1, source_target_pairs={{0,1},{1,0},{2,3},{3,2},{4,5},{5,4},{6,7},{7,6},{8,9},{9,8},{10,11... | collective-permute-start | bytes 1658888 | tf_op jit(solution)/shard_map/ppermute | solution.py:56
  511.7 38.7 %all-to-all-start.6 = ((bf16[8,144,432]{2,1,0:T(8,128)(2,1)}), bf16[8,144,432]{2,1,0:T(8,128)(2,1)}, u32[]{:S(2)}, u32[]{:S(2)}) async-start(bf16[8,144,432]{2,1,0:T(8,128)(2,1)} %bitcast.72), calls=%async_computation.8 | async-start | bytes 2359296 | tf_op jit(solution)/shard_map/all_to_all | solution.py:117
  516.0 81.2 %reduce-scatter.9.cloned.1.call-start = ((), (), s32[]{:S(2)}) async-start(), calls=%async_computation.17 | async-start | bytes 1966080 | tf_op jit(solution)/shard_map/reduce_scatter | solution.py:740
  586.6 83.4 %all-to-all-start.7 = ((bf16[8,256,1152]{2,1,0:T(8,128)(2,1)}), bf16[8,256,1152]{2,1,0:T(8,128)(2,1)}, u32[]{:S(2)}, u32[]{:S(2)}) async-start(bf16[8,256,1152]{2,1,0:T(8,128)(2,1)} %bitcast.73), calls=%async_computation.9 | async-start | bytes 9437184 | tf_op jit(solution)/shard_map/all_to_all | solution.py:117
  591.2 64.4 %reduce-scatter.11.cloned.1.call-start = ((), (), s32[]{:S(2)}) async-start(), calls=%async_computation.19 | async-start | bytes 1474560 | tf_op jit(solution)/shard_map/reduce_scatter | solution.py:740
  594.7 58.1 %collective-permute-start.49 = (bf16[144,1152]{1,0:T(8,128)(2,1)S(1)}, bf16[144,1152]{1,0:T(8,128)(2,1)S(1)}, u32[]{:S(2)}, u32[]{:S(2)}) collective-permute-start(bf16[144,1152]{1,0:T(8,128)(2,1)S(1)} %reduce_sum.68), channel_id=1, source_target_pairs={{0,64},{64,0},{1,65},{65,1},{2,66},{66,2},{3,67},{67,3},{4,68},{68... | collective-permute-start | bytes 995336 | tf_op jit(solution)/shard_map/ppermute | solution.py:56
  597.2 63.9 %collective-permute-start.46 = (bf16[64,3072]{1,0:T(8,128)(2,1)}, bf16[64,3072]{1,0:T(8,128)(2,1)S(1)}, u32[]{:S(2)}, u32[]{:S(2)}) collective-permute-start(bf16[64,3072]{1,0:T(8,128)(2,1)} %reduce-scatter.9.cloned.1.call-done), channel_id=1, source_target_pairs={{0,64},{64,0},{1,65},{65,1},{2,66},{66,2},{3,67},{67,3},{4,68},{68... | collective-permute-start | bytes 1179656 | tf_op jit(solution)/shard_map/ppermute | solution.py:56
  693.9 45.8 %collective-permute-start.37 = (bf16[256,1152]{1,0:T(8,128)(2,1)S(1)}, bf16[256,1152]{1,0:T(8,128)(2,1)}, u32[]{:S(2)}, u32[]{:S(2)}) collective-permute-start(bf16[256,1152]{1,0:T(8,128)(2,1)S(1)} %copy-done.33), channel_id=1, source_target_pairs={{0,16},{16,32},{32,48},{48,0},{1,17},{17,33},{33,49},{49,1},{2,18}... | collective-permute-start | bytes 1769480 | tf_op jit(solution)/shard_map/ppermute | solution.py:56
  693.9 46.0 %collective-permute-start.36 = (bf16[256,1152]{1,0:T(8,128)(2,1)S(1)}, bf16[256,1152]{1,0:T(8,128)(2,1)}, u32[]{:S(2)}, u32[]{:S(2)}) collective-permute-start(bf16[256,1152]{1,0:T(8,128)(2,1)S(1)} %copy-done.32), channel_id=1, source_target_pairs={{0,48},{16,0},{32,16},{48,32},{1,49},{17,1},{33,17},{49,33},{2,50}... | collective-permute-start | bytes 1769480 | tf_op jit(solution)/shard_map/ppermute | solution.py:56
  707.6 43.4 %collective-permute-start.70 = (bf16[576,1152]{1,0:T(8,128)(2,1)}, bf16[576,1152]{1,0:T(8,128)(2,1)}, u32[]{:S(2)}, u32[]{:S(2)}) collective-permute-start(bf16[576,1152]{1,0:T(8,128)(2,1)} %shard_map.401.mine), channel_id=1, source_target_pairs={{0,8},{8,0},{1,9},{9,1},{2,10},{10,2},{3,11},{11,3},{4,12},{12,4},... | collective-permute-start | bytes 3981320 | tf_op jit(solution)/shard_map/ppermute | solution.py:56
  (125 other events, 1625.0 us)
Sparse Core Ops, SparseCore 0:
  10.6 78.1 all-gather.3
  103.4 38.1 reduce-scatter.4
  205.0 53.1 all-gather.5
  384.2 63.3 reduce-scatter.6
  453.2 99.4 all-gather.7
  569.1 23.9 reduce-scatter.8
  596.1 23.5 reduce-scatter.10

commit v8 on v7

--- a/solution.py
+++ b/solution.py
@@ -22,6 +22,7 @@
 CAPS = 4
 SHARD = 144
 SLOT = 128
+SPLIT = 1
 WIN = 640
 STEP = 512
 
@@ -622,10 +623,16 @@
     sums[...] = jnp.concatenate(both + [jnp.zeros((6, D), f32)], axis=0)
 
 
-def first_back_body(x, parts, before, gain, grad):
-    g = parts[:TOK, :].astype(f32)
-    for k in range(1, 8):
-        g = g + parts[TOK * k : TOK * (k + 1), :].astype(f32)
+def first_back_body(x, *refs):
+    before, gain, grad = refs[SPLIT:]
+    size = TOK // SPLIT
+    sums = []
+    for parts in refs[:SPLIT]:
+        g = parts[:size, :].astype(f32)
+        for k in range(1, 8):
+            g = g + parts[size * k : size * (k + 1), :].astype(f32)
+        sums.append(g)
+    g = jnp.concatenate(sums, axis=0)
     grad[...] = before[...] + norm_back(x[...].astype(f32), g, gain[...])[0]
 
 
@@ -639,9 +646,12 @@
     grad_kv[...] = dot_tn(cols[...], kv[...]).astype(bf16)
 
 
-def first_part_body(g, w, plain, part, sums):
+def first_part_body(g, w, plain, *refs):
     rows = dot_nt(g[...], w[...])
-    part[...] = rows.astype(bf16)
+    sums = refs[-1]
+    size = TOK // SPLIT
+    for k in range(SPLIT):
+        refs[k][...] = rows[size * k : size * (k + 1)].astype(bf16)
     both = [
         jnp.sum(rows * plain[...].astype(f32), axis=0, keepdims=True),
         jnp.sum(rows, axis=0, keepdims=True),
@@ -668,10 +678,11 @@
             pl.BlockSpec((TOK, D), lambda i: (i, 0)),
         ],
         out_specs=[
-            pl.BlockSpec((TOK, D), lambda i: (i, 0)),
+            *[pl.BlockSpec((TOK // SPLIT, D), lambda i: (i, 0))] * SPLIT,
             pl.BlockSpec((8, D), lambda i: (0, 0)),
         ],
-        out_shape=[jax.ShapeDtypeStruct((ROW, D), bf16), jax.ShapeDtypeStruct((8, D), f32)],
+        out_shape=[jax.ShapeDtypeStruct((ROW // SPLIT, D), bf16)] * SPLIT
+        + [jax.ShapeDtypeStruct((8, D), f32)],
         compiler_params=params(),
     )(g, w, plain)
 
@@ -736,13 +747,8 @@
     return dot_tn(both_cores(left), rights).astype(bf16)
 
 
-def scatter_over_dp(x):
-    part = lax.psum_scatter(x, "z", scatter_dimension=0, tiled=True)
-    return part + shift(part, "xh", 1)
-
-
-def sum_everywhere(x):
-    for axis in ("y", "xl", "z", "xh", "c"):
+def sum_over(x, *axes):
+    for axis in axes:
         n = lax.axis_size(axis)
         x = sum([shift(x, axis, k) for k in range(1, n)], x)
     return x
@@ -821,8 +827,9 @@
     plain = normalize(rows_in.astype(f32))[0].astype(bf16)
     n01, n10, n30 = gather_first(plain)
 
-    heads_w = peers_parts(pack_heads(after(w_query, plain), w_key, w_value))
-    n01, n10, n30 = lax.optimization_barrier((n01, n10, n30))
+    heads_pack = pack_heads(after(w_query, plain), w_key, w_value)
+    n01, n10, n30, heads_pack = lax.optimization_barrier((n01, n10, n30, heads_pack))
+    heads_w = peers_parts(heads_pack)
     n31, n20, n11 = gather_second(n01, n10)
 
     text_own = jnp.pad(after(text_states[0], heads_w), ((0, TXT_OWN - CAP_TOK), (0, 0)))
@@ -856,10 +863,9 @@
     qkv = dot_nn(normed_all, heads_w).astype(bf16)
     head0, total0 = self_forward(0, seg_col, seg_row, qkv)
     head1, total1 = self_forward(1, seg_col, seg_row, after(qkv, head0))
-    quarter_minus, quarter_plus, context_own, head1 = lax.optimization_barrier(
-        (quarter_minus, quarter_plus, context_own, head1)
-    )
-    context = lax.all_gather(context_own, FS, axis=0, tiled=True)
+    quarter_minus, quarter_plus, head1 = lax.optimization_barrier(
+        (quarter_minus, quarter_plus, head1)
+    )
     quarter_far = (
         shift(halves(quarter_minus)[0], "z", 1),
         shift(halves(quarter_plus)[1], "z", -1),
@@ -867,14 +873,17 @@
     attended = lax.all_to_all(
         jnp.concatenate([head0, head1], axis=1), FS, split_axis=0, concat_axis=1, tiled=True
     )
-    attended, *quarter_far = lax.optimization_barrier((attended, *quarter_far))
+    attended, context_own, *quarter_far = lax.optimization_barrier(
+        (attended, context_own, *quarter_far)
+    )
+    context = every_peer(context_own)
     square_mine = place_quarters(quarter_own, quarter_minus, quarter_plus, *quarter_far)
     square_other = shift(square_mine, "c", 1)
     grad_out = cotangent[0]
     grad_mlp = grad_out.astype(bf16)
     grad_sent = after(grad_mlp, square_mine)
     mlp_minus, mlp_plus = shift(grad_sent, "z", 1), shift(grad_sent, "z", -1)
-    hidden_mine = every_peer(after(hidden_own, attended))
+    hidden_mine = every_peer(after(hidden_own, context))
 
     after_self, normed_two, cross_query = call(
         after_self_body,
@@ -943,12 +952,17 @@
     )
     back_minus, back_plus, keep = lax.optimization_barrier((back_minus, back_plus, keep))
     hidden_sum = keep + shift(send, "c", 1)
+
+    def hidden_chunk(dy, dx):
+        return row_block(hidden_sum, peer(dy, dx), SHARD)
+
+    h_lo, h_hi, h20 = reduce_first(hidden_chunk)
     grad_after_cross, grad_cross_branch, grad_cross_mixed, sums_three = call(
         third_back_body,
         [
             (core_index, "smem"), (after_cross, "vmem"), (back_own, "vmem"),
             (back_minus, "vmem"), (back_plus, "vmem"), (grad_out, "vmem"),
-            (row(ln3_gain), "vmem"), (square_mine, "hbm"), (square_other, "hbm"),
+            (after(row(ln3_gain), hidden_sum), "vmem"), (square_mine, "hbm"), (square_other, "hbm"),
         ],
         [((TOK, D), f32), ((TOK, D), bf16), ((TOK, D), bf16), ((8, D), f32)],
         square_scratch(1),
@@ -960,19 +974,21 @@
         cross_query,
         cross_key,
         cross_value,
-        grad_cross_mixed,
-    )
+        after(grad_cross_mixed, h_lo, h_hi),
+    )
+    h11, h31 = reduce_second(hidden_chunk, h_lo, h_hi)
     kv_own = lax.psum_scatter(grad_kv, FS, scatter_dimension=0, tiled=True)
     grad_after_self, grad_self_branch, grad_attended, sums_two = call(
         second_back_body,
         [
-            (core_index, "smem"), (after_self, "vmem"), (grad_cquery_rows, "vmem"),
+            (core_index, "smem"), (after_self, "vmem"), (after(grad_cquery_rows, h11, h31, h20), "vmem"),
             (grad_after_cross, "vmem"), (row(ln2_gain), "vmem"),
             (square_mine, "hbm"), (square_other, "hbm"),
         ],
         [((TOK, D), f32), ((TOK, D), bf16), ((TOK, D), bf16), ((8, D), f32)],
         square_scratch(2),
     )
+    hidden_parts = reduce_third(hidden_chunk, h20, h11, h31)
     grad_heads = lax.all_to_all(grad_attended, FS, split_axis=1, concat_axis=0, tiled=True)
 
     square = jnp.concatenate(
@@ -987,55 +1003,46 @@
     def square_chunk(dy, dx):
         return row_block(square, peer(dy, dx), SHARD)
 
-    grad_heads, square = lax.optimization_barrier((grad_heads, square))
-    hidden_parts = peers_parts(after(hidden_sum, grad_heads))
+    grad_heads, square, *hidden_parts = lax.optimization_barrier(
+        (grad_heads, square, *hidden_parts)
+    )
+    hidden_grad = reduce_last(hidden_chunk, *hidden_parts).astype(bf16)
     grad_qkv = self_backward(0, seg_col, seg_row, total0, qkv, grad_heads)
     kv_own, grad_qkv, square = lax.optimization_barrier((kv_own, grad_qkv, square))
     s_lo, s_hi, s20 = reduce_first(square_chunk)
-    kv_all = lax.all_gather(kv_own, FS, axis=0, tiled=True)
+    kv_all = every_peer(kv_own)
+    hidden_grad = after(hidden_grad, kv_own)
+    hidden_grad = hidden_grad + shift(hidden_grad, "xh", 1)
     out_minus, out_plus = reduce_z(after(out_far, kv_own), out_m, out_p)
     grad_qkv = self_backward(
         1, seg_col, seg_row, total1, qkv, after(grad_heads, kv_own), (grad_qkv,)
     )
-    s_lo, s_hi, out_minus, out_plus, grad_qkv = lax.optimization_barrier(
-        (s_lo, s_hi, out_minus, out_plus, grad_qkv)
-    )
-    s11, s31 = reduce_second(square_chunk, s_lo, s_hi)
+    s_lo, s_hi, out_minus, out_plus, hidden_grad, grad_qkv = lax.optimization_barrier(
+        (s_lo, s_hi, out_minus, out_plus, hidden_grad, grad_qkv)
+    )
     heads_own = heads_grad(normed_all, grad_qkv)
-    heads_own, hidden_parts = lax.optimization_barrier((heads_own, hidden_parts))
+    heads_own, kv_all = lax.optimization_barrier((heads_own, kv_all))
     heads_part = peers_parts(heads_own)
-    normed_part, sums_one = first_part(after(grad_qkv, heads_own), heads_w, plain_all)
-    normed_parts = peers_parts(after(normed_part, heads_part))
-    s11, s31, normed_part = lax.optimization_barrier((s11, s31, normed_part))
-    square_parts = reduce_third(square_chunk, s20, s11, s31)
-    square = reduce_last(square_chunk, *square_parts).astype(bf16)
-    hidden_grad = sum_parts(after(hidden_parts, normed_part)).astype(bf16)
-    hidden_grad = hidden_grad + shift(hidden_grad, "xh", 1)
-    hidden_z = neighbours(hidden_grad)
-
+    part, sums_one = first_part(after(grad_qkv, heads_own), heads_w, plain_all)
+    part, heads_part = lax.optimization_barrier((part, heads_part))
+    sent = peers_parts(part)
+
+    s11, s31 = reduce_second(square_chunk, after(s_lo, part), s_hi)
+    hidden_z = neighbours(after(hidden_grad, part))
+    heads_rows = unpack_heads(heads_part)
+    early = row_block(heads_rows, core, 216) + shift(row_block(heads_rows, 1 - core, 216), "c", 1)
+    early = jnp.concatenate([early, jnp.zeros((256 - 216, D), bf16)], axis=0)
     own_columns = lax.dynamic_slice_in_dim(context, peer(0, 0) * SHARD, SHARD, axis=1)
     text_part, grad_w_text, grad_w_kv = call(
         text_back_body,
         [
-            (core_index, "smem"), (after(kv_all, normed_part), "vmem"), (own_columns, "vmem"),
+            (core_index, "smem"), (after(kv_all, part), "vmem"), (own_columns, "vmem"),
             (text_columns, "vmem"), (w_text, "vmem"),
             (square_mine, "hbm"), (square_other, "hbm"),
         ],
         [((TXT, TXT), bf16), ((TXT, D), bf16), ((SHARD, 2 * D), bf16)],
         square_scratch(2),
     )
-
-    heads_rows = unpack_heads(heads_part)
-    early = row_block(heads_rows, core, 216) + shift(row_block(heads_rows, 1 - core, 216), "c", 1)
-    early = jnp.concatenate([early, jnp.zeros((256 - 216, D), bf16)], axis=0)
-    rest = jnp.zeros((256 - SHARD, WIN), bf16)
-    square = jnp.concatenate(
-        [early] + [
-            jnp.concatenate([square[:, WIN * k : WIN * (k + 1)], rest], axis=0) for k in range(3)
-        ],
-        axis=1,
-    )
-    early = scatter_over_dp(square)
 
     def half(which):
         kv = jnp.where(which == 0, grad_w_kv[:, :D], grad_w_kv[:, D:])
@@ -1044,40 +1051,47 @@
         )
 
     late = half(core) + shift(half(1 - core), "c", 1)
-    late = scatter_over_dp(late)
-    normed_parts, early, late, *hidden_z = lax.optimization_barrier(
-        (normed_parts, early, late, *hidden_z)
-    )
+    early = lax.psum_scatter(early, "z", scatter_dimension=0, tiled=True)
+    square_parts = reduce_third(square_chunk, s20, s11, s31)
+    square = reduce_last(square_chunk, *square_parts).astype(bf16)
+    square = jnp.concatenate(
+        [square[:, WIN * k : WIN * (k + 1)] for k in range(3)]
+        + [jnp.zeros((512 - 3 * SHARD, WIN), bf16)],
+        axis=0,
+    )
+    late = jnp.concatenate([late, square], axis=1)
+    late = lax.psum_scatter(late, "z", scatter_dimension=0, tiled=True)
+    part, early, late, *hidden_z = lax.optimization_barrier((sent, early, late, *hidden_z))
+    early = early + shift(early, "xh", 1)
+    norms = jnp.concatenate([sums_one[:2], sums_two[:2], sums_three[:2], jnp.zeros((2, D), f32)])
+    norms = sum_over(after(norms, part), "z", "c")
+
+    norms = sum_over(norms, "y", "xl", "xh")
+    late = late + shift(late, "xh", 1)
     early = in_order(*neighbours(early))
     late = in_order(*neighbours(late))
     hidden_grad = in_order(*hidden_z)
     grad_w_up, grad_w_down = sort_hidden(core_index, hidden_grad, shift(hidden_grad, "c", 1))
-    sums_one = after(sums_one, normed_parts)
-    norms = sum_everywhere(
-        jnp.concatenate([sums_one[:2], sums_two[:2], sums_three[:2], jnp.zeros((2, D), f32)])
-    )
-    other = shift(early, "c", 1)
-    low = jnp.where(first_core, early, other).astype(f32)
-    high = jnp.where(first_core, other, early).astype(f32)
-    grad_w_query = low[:144, :D]
-    grad_w_key = jnp.concatenate([low[144:216, :D], high[:72, :D]], axis=0)
-    grad_w_value = high[72:216, :D]
+
+    def by_core(x):
+        other = shift(x, "c", 1)
+        low, high = jnp.where(first_core, x, other), jnp.where(first_core, other, x)
+        return low.astype(f32), high.astype(f32)
+
+    low, high = by_core(early)
+    grad_w_query = low[:144]
+    grad_w_key = jnp.concatenate([low[144:216], high[:72]], axis=0)
+    grad_w_value = high[72:216]
+    low, high = by_core(late)
+    grad_w_text = jnp.concatenate([low[:256, :D], high[:256, :D]], axis=0)
+    grad_c_key, grad_c_value = low[256:400, :D], high[256:400, :D]
     grad_c_out, grad_c_query, grad_w_out = (
         jnp.concatenate(
-            [
-                low[:SHARD, D + WIN * k : D + WIN * (k + 1)],
-                high[:SHARD, D + WIN * k + 128 : D + WIN * (k + 1)],
-            ],
+            [low[SHARD * k : SHARD * (k + 1), D:], high[SHARD * k : SHARD * (k + 1), D + 128 :]],
             axis=1,
         )
         for k in range(3)
     )
-
-    other = shift(late, "c", 1)
-    low = jnp.where(first_core, late, other).astype(f32)
-    high = jnp.where(first_core, other, late).astype(f32)
-    grad_w_text = jnp.concatenate([low[:256], high[:256]], axis=0)
-    grad_c_key, grad_c_value = low[256:400], high[256:400]
     out_minus, out_plus = shift(out_minus, "z", -1), shift(out_plus, "z", 1)
     outputs = (
         after_cross + out_own.astype(f32) + out_minus.astype(f32) + out_plus.astype(f32)
@@ -1086,14 +1100,14 @@
     grad_tokens = call(
         first_back_body,
         [
-            (rows_in, "vmem"), (normed_parts, "vmem"), (grad_after_self, "vmem"),
+            (rows_in, "vmem"), (part, "vmem"), (grad_after_self, "vmem"),
             (row(ln1_gain), "vmem"),
         ],
         [((TOK, D), f32)],
         [],
     )[0]
     grad_text = lax.all_to_all(
-        after(text_part, normed_parts), FS, split_axis=0, concat_axis=1, tiled=True
+        after(text_part, part), FS, split_axis=0, concat_axis=1, tiled=True
     )
     grad_text = grad_text[:CAP_TOK].astype(f32)
     return (

time: 784 us -> 766 us (0.977)
  waiting for transfers between devices: 245 us -> 196 us
  starting transfers between devices: 140 us -> 173 us
  blocking collectives: 11.1 us -> 0 us
  local copies, waits for them, and re-layouts: 56.1 us -> 65.2 us
    ppermute x71 -> x79, waiting for transfers between devices: 174 us -> 124 us  [shift(): return lax.ppermute(x, axis, [(i, (i + by) % n) for i in range(n)])]
    all_gather x2 -> x0, waiting for transfers between devices: 37 us -> none  [the longest x1 37 us: local(): context = lax.all_gather(context_own, FS, axis=0, tiled=True)]
    ppermute x71 -> x79, starting transfers between devices: 106 us -> 133 us  [shift(): return lax.ppermute(x, axis, [(i, (i + by) % n) for i in range(n)])]
    reduce_scatter x2, waiting for transfers between devices: 0.01 us -> 16 us  [the longest x1 16 us: local(): late = lax.psum_scatter(late, 'z', scatter_dimension=0, tiled=True)]
    all_to_all x1 -> x3, waiting for transfers between devices: 0.01 us -> 14.3 us  [every_peer(): return lax.all_to_all(copies, axes, 0, 0, tiled=True)]
    all_to_all x1 -> x0, blocking collectives: 11.1 us -> none  [local(): lax.all_to_all(jnp.concatenate([head0, head1], axis=1), FS, split_axis=0,...]
    all_to_all x4 -> x3, waiting for transfers between devices: 16.5 us -> 24.9 us  [peers_parts(): return lax.all_to_all(x, axes, 0, 0, tiled=True)]
    all_to_all x1 -> x3, starting transfers between devices: 3.63 us -> 11.8 us  [every_peer(): return lax.all_to_all(copies, axes, 0, 0, tiled=True)]
  transfers between devices with their start and end apart: 86 -> 94, of which waited for: 32 -> 34; matrix products, arithmetic and copies ran while one was open for 14% -> 14% of each run, Pallas kernels for 26% -> 28%
where the time goes in v8:
time: 766 us; the launch traced here: 757 us
  Pallas kernels  239 us (31%)
  waiting for transfers between devices  196 us (26%)
  starting transfers between devices  173 us (23%)
  local copies, waits for them, and re-layouts  65.2 us (9%)
  other arithmetic  49.4 us (6%)
  matrix products  18.9 us (2%)
  between operations  15.4 us (2%)
    ppermute x79, starting transfers between devices, shift(): return lax.ppermute(x, axis, [(i, (i + by) % n) for i in range(n)])  133 us
    ppermute x79, waiting for transfers between devices, shift(): return lax.ppermute(x, axis, [(i, (i + by) % n) for i in range(n)])  124 us
    pallas_call x7, Pallas kernels, call(): pl.pallas_call(body, in_specs=[pl.BlockSpec(memory_space=spaces[where]) f...  51.5 us
    pallas_call x2, Pallas kernels, self_backward(): pl.pallas_call(functools.partial(self_backward_body, head), grid=(ROW //...  37.2 us
    pallas_call x3, Pallas kernels, mlp(): pl.pallas_call(functools.partial(mlp_body, parts, count), in_specs=[pl.Bl...  28.7 us
    all_to_all x3, waiting for transfers between devices, peers_parts(): return lax.all_to_all(x, axes, 0, 0, tiled=True)  24.9 us
    pallas_call x2, Pallas kernels, self_forward(): pl.pallas_call(self_forward_body, grid=(ROW // TOK,), in_specs=[pl.BlockS...  24.3 us
    pallas_call x2, Pallas kernels, mlp_grad(): pl.pallas_call(functools.partial(mlp_grad_body, which), grid=(3,), in_spe...  17.4 us
  transfers between devices with their start and end apart: 94, of which 34 were waited for; matrix products, arithmetic and copies ran while one was open for 14% of the time, Pallas kernels for 28%

profile of v8, /device:TPU:1, one launch (start us, length us, event | category | flops | bytes accessed | tf_op | source)
XLA Modules:
  0.0 757.0 jit_solution(7045245913230803093)
XLA Ops:
  18.8 9.6 %collective-permute-done.refs_1_ = bf16[256,1152]{1,0:T(8,128)(2,1)S(1)} collective-permute-done((bf16[256,1152]{1,0:T(8,128)(2,1)S(1)}, bf16[256,1152]{1,0:T(8,128)(2,1)S(1)}, u32[]{:S(2)}, u32[]{:S(2)}) %collective-permute-start) | collective-permute-done | bytes 589856 | tf_op jit(solution)/shard_map/ppermute | solution.py:57
  41.1 24.9 %all-to-all-done = bf16[8,144,432]{2,1,0:T(8,128)(2,1)S(1)} async-done(((bf16[8,144,432]{2,1,0:T(8,128)(2,1)}), bf16[8,144,432]{2,1,0:T(8,128)(2,1)S(1)}, u32[]{:S(2)}, u32[]{:S(2)}) %all-to-all-start) | async-done | bytes 995360 | tf_op jit(solution)/shard_map/all_to_all | solution.py:118
  73.9 10.6 %collective-permute-done.5.refs_6_ = bf16[256,1152]{1,0:T(8,128)(2,1)S(1)} collective-permute-done((bf16[256,1152]{1,0:T(8,128)(2,1)}, bf16[256,1152]{1,0:T(8,128)(2,1)S(1)}, u32[]{:S(2)}, u32[]{:S(2)}) %collective-permute-start.5) | collective-permute-done | bytes 589856 | tf_op jit(solution)/shard_map/ppermute | solution.py:57
  84.4 8.3 %all-to-all-done.1 = bf16[64,8,512]{2,0,1:T(8,128)(2,1)S(1)} async-done(((bf16[64,8,512]{2,0,1:T(8,128)(2,1)}), bf16[64,8,512]{2,0,1:T(8,128)(2,1)S(1)}, u32[]{:S(2)}, u32[]{:S(2)}) %all-to-all-start.1) | async-done | bytes 524320 | tf_op jit(solution)/shard_map/all_to_all | solution.py:836
  117.6 8.8 %convolution_convert_fusion.q.kv = bf16[2048,768]{1,0:T(8,128)(2,1)} fusion(bf16[2048,1152]{1,0:T(8,128)(2,1)} %get-tuple-element.157.x, bf16[1152,768]{1,0:T(8,128)(2,1)} %shard_map.376.w), kind=kOutput, calls=%fused_computation.1 | convolution fusion | flops 3625451520 | bytes 9633792 | tf_op jit(solution)/shard_map/dot_general | solution.py:40
  126.5 12.1 %shard_map.377 = (bf16[2048,72]{1,0:T(8,128)(2,1)}, f32[1,2048]{1,0:T(1,128)}) custom-call(s32[2048,1]{1,0:T(8,128)} %copy.114.seg_q.seg_k, s32[1,2048]{1,0:T(1,128)} %bitcast.87, bf16[2048,768]{1,0:T(8,128)(2,1)} %convolution_convert_fusion.q.kv, bf16[2048,768]{1,0:T(8,128)(2,1)} %convolution_convert_fusion.q.kv), custom_call_target="tpu_custom_call" | custom-call | tf_op jit(solution)/shard_map/pallas_call | solution.py:279
  138.6 12.2 %shard_map.378 = (bf16[2048,72]{1,0:T(8,128)(2,1)}, f32[1,2048]{1,0:T(1,128)}) custom-call(s32[2048,1]{1,0:T(8,128)} %copy.114.seg_q.seg_k, s32[1,2048]{1,0:T(1,128)} %bitcast.88, bf16[2048,768]{1,0:T(8,128)(2,1)} %convolution_convert_fusion.q.kv, bf16[2048,768]{1,0:T(8,128)(2,1)} %convolution_convert_fusion.q.kv), custom_call_target="tpu_custom_call" | custom-call | tf_op jit(solution)/shard_map/pallas_call | solution.py:279
  190.4 14.3 %all-to-all-done.3 = bf16[8,64,1152]{2,1,0:T(8,128)(2,1)S(1)} async-done(((bf16[8,64,1152]{2,1,0:T(8,128)(2,1)}), bf16[8,64,1152]{2,1,0:T(8,128)(2,1)S(1)}, u32[]{:S(2)}, u32[]{:S(2)}) %all-to-all-start.3) | async-done | bytes 1179680 | tf_op jit(solution)/shard_map/all_to_all | solution.py:114
  228.2 8.4 %shard_map.381 = (bf16[512,1152]{1,0:T(8,128)(2,1)}, bf16[512,1152]{1,0:T(8,128)(2,1)}) custom-call(s32[1]{0:T(128)} %bitcast.core, bf16[512,1152]{1,0:T(8,128)(2,1)} %bitcast.70, bf16[1152,3072]{1,0:T(8,128)(2,1)} %shard_map.379.mine, bf16[1152,3072]{1,0:T(8,128)(2,1)} %collective-permute-done.12.other), custom_call_target="tpu_custom_call" | custom-call | tf_op jit(solution)/shard_map/pallas_call | solution.py:569
  236.7 11.7 %shard_map.382.mixed = bf16[256,1152]{1,0:T(8,128)(2,1)} custom-call(s32[256,1]{1,0:T(8,128)} %copy.118.cap_q, s32[1,512]{1,0:T(1,128)} %and_select_fusion.1.cap_t, bf16[256,1152]{1,0:T(8,128)(2,1)} %get-tuple-element.169.q, bf16[512,1152]{1,0:T(8,128)(2,1)} %get-tuple-element.173.k, bf16[512,1152]{1,0:T(8,128)(2,1)} %get-tuple-element.174.v), custom_call_target="tpu_custom_call" | custom-call | tf_op jit(solution)/shard_map/pallas_call | solution.py:370
  266.0 8.2 %shard_map.384 = (bf16[256,1152]{1,0:T(8,128)(2,1)}, bf16[256,1152]{1,0:T(8,128)(2,1)}, bf16[256,1152]{1,0:T(8,128)(2,1)}, bf16[256,1152]{1,0:T(8,128)(2,1)}) custom-call(s32[1]{0:T(128)} %bitcast.core, bf16[256,1152]{1,0:T(8,128)(2,1)} %get-tuple-element.176.refs_0_, bf16[256,1152]{1,0:T(8,128)(2,1)} %copy-done.2, bf16[1152,1152]{1,0:T(8,128)(2,1)} %bitcast.62, ...), custom_call_target="tpu_custom_call" | custom-call | tf_op jit(solution)/shard_map/pallas_call | solution.py:476
  279.8 12.3 %shard_map.385 = (bf16[256,1152]{1,0:T(8,128)(2,1)}, bf16[256,1152]{1,0:T(8,128)(2,1)}, bf16[256,1152]{1,0:T(8,128)(2,1)}, bf16[256,1152]{1,0:T(8,128)(2,1)}, bf...) custom-call(s32[1]{0:T(128)} %bitcast.core, ...), custom_call_target="tpu_custom_call" | custom-call | tf_op jit(solution)/shard_map/pallas_call | solution.py:476
  292.9 8.2 %shard_map.386 = (bf16[256,1152]{1,0:T(8,128)(2,1)}, bf16[256,1152]{1,0:T(8,128)(2,1)}, bf16[256,1152]{1,0:T(8,128)(2,1)}, bf16[256,1152]{1,0:T(8,128)(2,1)}) custom-call(s32[1]{0:T(128)} %bitcast.core, bf16[128,1152]{1,0:T(8,128)(2,1)} %copy-done.25, bf16[128,1152]{1,0:T(8,128)(2,1)} %copy-done.26, bf16[128,1152]{1,0:T(8,128)(2,1)} %copy-done.23, ...), custom_call_target="tpu_custom_call" | custom-call | tf_op jit(solution)/shard_map/pallas_call | solution.py:476
  306.8 8.7 %shard_map.387 = bf16[1152,1152]{1,0:T(8,128)(2,1)} custom-call(s32[1]{0:T(128)} %bitcast.core, bf16[256,1152]{1,0:T(8,128)(2,1)} %get-tuple-element.176.refs_0_, bf16[256,1152]{1,0:T(8,128)(2,1)} %copy-done.5, bf16[256,1152]{1,0:T(8,128)(2,1)} %collective-permute-done.16.refs_1_.refs_2_, bf16[256,1152]{1,0:T(8,128)(2,1)} %copy-done.13, ...), custom_call_target="tpu_custom_call" | custom-call | tf_op jit(solution)/shard_map/pallas_call | solution.py:510
  323.9 8.7 %shard_map.388 = bf16[1152,1152]{1,0:T(8,128)(2,1)} custom-call(s32[1]{0:T(128)} %bitcast.core, bf16[256,1152]{1,0:T(8,128)(2,1)} %get-tuple-element.176.refs_0_, bf16[256,1152]{1,0:T(8,128)(2,1)} %copy-done.5, bf16[256,1152]{1,0:T(8,128)(2,1)} %collective-permute-done.16.refs_1_.refs_2_, bf16[256,1152]{1,0:T(8,128)(2,1)} %copy-done.13, ...), custom_call_target="tpu_custom_call" | custom-call | tf_op jit(solution)/shard_map/pallas_call | solution.py:510
  354.2 15.3 %shard_map.390 = (bf16[256,1152]{1,0:T(8,128)(2,1)}, bf16[512,2304]{1,0:T(8,128)(2,1)}) custom-call(s32[512,1]{1,0:T(8,128)} %fusion.26.cap_t, s32[1,256]{1,0:T(1,128)} %bitcast.94, bf16[256,1152]{1,0:T(8,128)(2,1)} %get-tuple-element.169.q, bf16[512,1152]{1,0:T(8,128)(2,1)} %get-tuple-element.173.k, bf16[512,1152]{1,0:T(8,128)(2,1)} %get-tuple-element.174.v, ...), custom_call_target="tpu_custom_call" | custom-call | tf_op jit(solution)/shard_map/pallas_call | solution.py:398
  428.0 18.7 %shard_map.392.refs_0_ = bf16[2048,768]{1,0:T(8,128)(2,1)} custom-call(s32[2048,1]{1,0:T(8,128)} %copy.114.seg_q.seg_k, s32[1,2048]{1,0:T(1,128)} %bitcast.89, f32[1,2048]{1,0:T(1,128)} %get-tuple-element.211.total, bf16[2048,768]{1,0:T(8,128)(2,1)} %convolution_convert_fusion.q.kv, bf16[2048,768]{1,0:T(8,128)(2,1)} %convolution_convert_fusion.q.kv, ...), custom_call_target="tpu_custom_call" | custom-call | tf_op jit(solution)/shard_map/pallas_call | solution.py:331
  467.0 18.5 %shard_map.393.g = bf16[2048,768]{1,0:T(8,128)(2,1)} custom-call(s32[2048,1]{1,0:T(8,128)} %copy.114.seg_q.seg_k, s32[1,2048]{1,0:T(1,128)} %bitcast.90, f32[1,2048]{1,0:T(1,128)} %get-tuple-element.233.total, bf16[2048,768]{1,0:T(8,128)(2,1)} %convolution_convert_fusion.q.kv, ...), custom_call_target="tpu_custom_call", output_to_operand_aliasing={{}: (6, {})} | custom-call | tf_op jit(solution)/shard_map/pallas_call | solution.py:331
  508.7 10.7 %shard_map.395 = (bf16[2048,1152]{1,0:T(8,128)(2,1)}, f32[8,1152]{1,0:T(8,128)}) custom-call(bf16[2048,768]{1,0:T(8,128)(2,1)} %shard_map.393.g, bf16[1152,768]{1,0:T(8,128)(2,1)} %shard_map.376.w, bf16[2048,1152]{1,0:T(8,128)(2,1)} %get-tuple-element.241.plain), custom_call_target="tpu_custom_call" | custom-call | tf_op jit(solution)/shard_map/pallas_call | solution.py:672
  540.7 11.1 %shard_map.397 = (bf16[512,512]{1,0:T(8,128)(2,1)}, bf16[512,1152]{1,0:T(8,128)(2,1)}, bf16[144,2304]{1,0:T(8,128)(2,1)}) custom-call(s32[1]{0:T(128)} %bitcast.core, bf16[512,2304]{1,0:T(8,128)(2,1)} %bitcast.67, bf16[512,144]{1,0:T(8,128)(2,1)} %constant_dynamic-slice_fusion.9.cols, bf16[512,512]{1,0:T(8,128)(2,1)} %bitcast.81, bf16[512,1152]{1,0:T(8,128)(2,1)} %w_text.1, ...), custom_call_target="tpu_custom_call" | custom-call | tf_op jit(solution)/shard_map/pallas_call | solution.py:569
  553.4 31.0 %collective-permute-done.51 = bf16[144,1920]{1,0:T(8,128)(2,1)S(1)} collective-permute-done((bf16[144,1920]{1,0:T(8,128)(2,1)S(1)}, bf16[144,1920]{1,0:T(8,128)(2,1)S(1)}, u32[]{:S(2)}, u32[]{:S(2)}) %collective-permute-start.51) | collective-permute-done | bytes 552992 | tf_op jit(solution)/shard_map/ppermute | solution.py:57
  634.5 16.0 %reduce-scatter.11.cloned.1.call-done = bf16[128,1792]{1,0:T(8,128)(2,1)} async-done(((bf16[512,1792]{1,0:T(8,128)(2,1)}), bf16[128,1792]{1,0:T(8,128)(2,1)}) %reduce-scatter.11.cloned.1.call-update) | async-done | bytes 458768 | tf_op jit(solution)/shard_map/reduce_scatter | solution.py:1063
  695.9 8.0 %collective-permute-done.74.refs_1_ = bf16[128,1792]{1,0:T(8,128)(2,1)S(1)} collective-permute-done((bf16[128,1792]{1,0:T(8,128)(2,1)S(1)}, bf16[128,1792]{1,0:T(8,128)(2,1)S(1)}, u32[]{:S(2)}, u32[]{:S(2)}) %collective-permute-start.74) | collective-permute-done | bytes 458784 | tf_op jit(solution)/shard_map/ppermute | solution.py:57
  703.9 12.3 %collective-permute-start.78 = (bf16[576,1152]{1,0:T(8,128)(2,1)}, bf16[576,1152]{1,0:T(8,128)(2,1)}, u32[]{:S(2)}, u32[]{:S(2)}) collective-permute-start(bf16[576,1152]{1,0:T(8,128)(2,1)} %shard_map.401.mine), channel_id=1, source_target_pairs={{0,8},{8,0},{1,9},{9,1},{2,10},{10,2},{3,11},{11,3},{4,12},{12,4},... | collective-permute-start | bytes 3981320 | tf_op jit(solution)/shard_map/ppermute | solution.py:57
  (485 shorter events, 432.9 us)
Async XLA Ops:
  7.2 102.5 %all-gather.2.cloned.1.call-start = ((), (), s32[]{:S(2)}) async-start(), calls=%async_computation.14 | async-start | bytes 1990656 | tf_op jit(solution)/shard_map/all_gather | solution.py:824
  37.1 36.8 %collective-permute-start.3 = (bf16[256,1152]{1,0:T(8,128)(2,1)S(1)}, bf16[256,1152]{1,0:T(8,128)(2,1)S(1)}, u32[]{:S(2)}, u32[]{:S(2)}) collective-permute-start(bf16[256,1152]{1,0:T(8,128)(2,1)S(1)} %collective-permute-done.refs_1_), channel_id=1, source_target_pairs={{0,2},{2,4},{4,6},{6,0},{1,3},{3,5},{5,7},{7,1},{8,10},{10,12},{12... | collective-permute-start | bytes 1769480 | tf_op jit(solution)/shard_map/ppermute | solution.py:57
  38.5 35.4 %collective-permute-start.4 = (bf16[256,1152]{1,0:T(8,128)(2,1)}, bf16[256,1152]{1,0:T(8,128)(2,1)}, u32[]{:S(2)}, u32[]{:S(2)}) collective-permute-start(bf16[256,1152]{1,0:T(8,128)(2,1)} %collective-permute-done.1.refs_2_), channel_id=1, source_target_pairs={{0,6},{2,0},{4,2},{6,4},{1,7},{3,1},{5,3},{7,5},{8,14},{10,8},{12,... | collective-permute-start | bytes 1769480 | tf_op jit(solution)/shard_map/ppermute | solution.py:57
  39.9 44.6 %collective-permute-start.5 = (bf16[256,1152]{1,0:T(8,128)(2,1)}, bf16[256,1152]{1,0:T(8,128)(2,1)S(1)}, u32[]{:S(2)}, u32[]{:S(2)}) collective-permute-start(bf16[256,1152]{1,0:T(8,128)(2,1)} %collective-permute-done.1.refs_2_), channel_id=1, source_target_pairs={{0,1},{1,0},{2,3},{3,2},{4,5},{5,4},{6,7},{7,6},{8,9},{9,8},{10,11... | collective-permute-start | bytes 1769480 | tf_op jit(solution)/shard_map/ppermute | solution.py:57
  71.9 90.5 %reduce-scatter.5.cloned.1.call-start = ((), (), s32[]{:S(2)}) async-start(), calls=%async_computation.15 | async-start | bytes 1327104 | tf_op jit(solution)/shard_map/reduce_scatter | solution.py:841
  109.7 41.0 %collective-permute-start.8 = (bf16[1152,768]{1,0:T(8,128)(2,1)}, bf16[1152,768]{1,0:T(8,128)(2,1)S(1)}, u32[]{:S(2)}, u32[]{:S(2)}) collective-permute-start(bf16[1152,768]{1,0:T(8,128)(2,1)} %all-gather.2.cloned.1.call-done.own), channel_id=1, source_target_pairs={{0,16},{16,32},{32,48},{48,0},{1,17},{17,33},{33,49},{49,1},{2,18}... | collective-permute-start | bytes 5308424 | tf_op jit(solution)/shard_map/ppermute | solution.py:57
  111.4 39.3 %collective-permute-start.9 = (bf16[1152,768]{1,0:T(8,128)(2,1)}, bf16[1152,768]{1,0:T(8,128)(2,1)}, u32[]{:S(2)}, u32[]{:S(2)}) collective-permute-start(bf16[1152,768]{1,0:T(8,128)(2,1)} %all-gather.2.cloned.1.call-done.own), channel_id=1, source_target_pairs={{0,48},{16,0},{32,16},{48,32},{1,49},{17,1},{33,17},{49,33},{2,50}... | collective-permute-start | bytes 5308424 | tf_op jit(solution)/shard_map/ppermute | solution.py:57
  178.2 43.0 %collective-permute-start.12 = (bf16[1152,3072]{1,0:T(8,128)(2,1)}, bf16[1152,3072]{1,0:T(8,128)(2,1)}, u32[]{:S(2)}, u32[]{:S(2)}) collective-permute-start(bf16[1152,3072]{1,0:T(8,128)(2,1)} %shard_map.379.mine), channel_id=1, source_target_pairs={{0,8},{8,0},{1,9},{9,1},{2,10},{10,2},{3,11},{11,3},{4,12},{12,4},... | collective-permute-start | bytes 21233672 | tf_op jit(solution)/shard_map/ppermute | solution.py:57
  206.6 41.7 %all-to-all-start.4 = ((bf16[8,144,1152]{2,1,0:T(8,128)(2,1)}), bf16[8,144,1152]{2,1,0:T(8,128)(2,1)S(1)}, u32[]{:S(2)}, u32[]{:S(2)}) async-start(bf16[8,144,1152]{2,1,0:T(8,128)(2,1)} %broadcast_in_dim.136), calls=%async_computation.5 | async-start | bytes 5308416 | tf_op jit(solution)/shard_map/all_to_all | solution.py:114
  210.3 237.7 %reduce-scatter.7.cloned.1.call-start = ((), (), s32[]{:S(2)}) async-start(), calls=%async_computation.16 | async-start | bytes 2654208 | tf_op jit(solution)/shard_map/reduce_scatter | solution.py:980
  378.4 37.4 %collective-permute-start.32 = (bf16[256,1152]{1,0:T(8,128)(2,1)}, bf16[256,1152]{1,0:T(8,128)(2,1)}, u32[]{:S(2)}, u32[]{:S(2)}) collective-permute-start(bf16[256,1152]{1,0:T(8,128)(2,1)} %shard_map.382.mixed), channel_id=1, source_target_pairs={{0,8},{8,0},{1,9},{9,1},{2,10},{10,2},{3,11},{11,3},{4,12},{12,4},... | collective-permute-start | bytes 1769480 | tf_op jit(solution)/shard_map/ppermute | solution.py:57
  450.6 47.6 %all-to-all-start.6 = ((bf16[8,64,2304]{2,1,0:T(8,128)(2,1)}), bf16[8,64,2304]{2,1,0:T(8,128)(2,1)S(1)}, u32[]{:S(2)}, u32[]{:S(2)}) async-start(bf16[8,64,2304]{2,1,0:T(8,128)(2,1)} %broadcast_in_dim.139), calls=%async_computation.8 | async-start | bytes 4718592 | tf_op jit(solution)/shard_map/all_to_all | solution.py:114
  505.6 47.7 %collective-permute-start.50 = (bf16[144,1920]{1,0:T(8,128)(2,1)}, bf16[144,1920]{1,0:T(8,128)(2,1)}, u32[]{:S(2)}, u32[]{:S(2)}) collective-permute-start(bf16[144,1920]{1,0:T(8,128)(2,1)} %constant_dynamic-slice_fusion.6), channel_id=1, source_target_pairs={{0,2},{2,4},{4,6},{6,0},{1,3},{3,5},{5,7},{7,1},{8,10},{10,12},{12... | collective-permute-start | bytes 1658888 | tf_op jit(solution)/shard_map/ppermute | solution.py:57
  520.5 114.0 %all-to-all-start.8 = ((bf16[8,256,1152]{2,1,0:T(8,128)(2,1)}), bf16[8,256,1152]{2,1,0:T(8,128)(2,1)}, u32[]{:S(2)}, u32[]{:S(2)}) async-start(bf16[8,256,1152]{2,1,0:T(8,128)(2,1)} %bitcast.74), calls=%async_computation.10 | async-start | bytes 9437184 | tf_op jit(solution)/shard_map/all_to_all | solution.py:118
  525.1 109.4 %reduce-scatter.9.cloned.1.call-start = ((), (), s32[]{:S(2)}) async-start(), calls=%async_computation.17 | async-start | bytes 737280 | tf_op jit(solution)/shard_map/reduce_scatter | solution.py:1054
  529.7 67.7 %collective-permute-start.48 = (bf16[216,1152]{1,0:T(8,128)(2,1)}, bf16[216,1152]{1,0:T(8,128)(2,1)}, u32[]{:S(2)}, u32[]{:S(2)}) collective-permute-start(bf16[216,1152]{1,0:T(8,128)(2,1)} %constant_dynamic-slice_fusion.10), channel_id=1, source_target_pairs={{0,8},{8,0},{1,9},{9,1},{2,10},{10,2},{3,11},{11,3},{4,12},{12,4},... | collective-permute-start | bytes 1493000 | tf_op jit(solution)/shard_map/ppermute | solution.py:57
  536.4 47.9 %collective-permute-start.51 = (bf16[144,1920]{1,0:T(8,128)(2,1)S(1)}, bf16[144,1920]{1,0:T(8,128)(2,1)S(1)}, u32[]{:S(2)}, u32[]{:S(2)}) collective-permute-start(bf16[144,1920]{1,0:T(8,128)(2,1)S(1)} %pad_maximum_fusion.11), channel_id=1, source_target_pairs={{0,1},{1,0},{2,3},{3,2},{4,5},{5,4},{6,7},{7,6},{8,9},{9,8},{10,11... | collective-permute-start | bytes 1658888 | tf_op jit(solution)/shard_map/ppermute | solution.py:57
  538.3 47.2 %collective-permute-start.53 = (bf16[144,1920]{1,0:T(8,128)(2,1)S(1)}, bf16[144,1920]{1,0:T(8,128)(2,1)S(1)}, u32[]{:S(2)}, u32[]{:S(2)}) collective-permute-start(bf16[144,1920]{1,0:T(8,128)(2,1)S(1)} %pad_maximum_fusion.12), channel_id=1, source_target_pairs={{0,6},{2,0},{4,2},{6,4},{1,7},{3,1},{5,3},{7,5},{8,14},{10,8},{12,... | collective-permute-start | bytes 1658888 | tf_op jit(solution)/shard_map/ppermute | solution.py:57
  599.5 51.0 %reduce-scatter.11.cloned.1.call-start = ((), (), s32[]{:S(2)}) async-start(), calls=%async_computation.18 | async-start | bytes 2293760 | tf_op jit(solution)/shard_map/reduce_scatter | solution.py:1063
  679.7 42.3 %collective-permute-start.47 = (bf16[256,1152]{1,0:T(8,128)(2,1)S(1)}, bf16[256,1152]{1,0:T(8,128)(2,1)}, u32[]{:S(2)}, u32[]{:S(2)}) collective-permute-start(bf16[256,1152]{1,0:T(8,128)(2,1)S(1)} %copy-done.31), channel_id=1, source_target_pairs={{0,16},{16,32},{32,48},{48,0},{1,17},{17,33},{33,49},{49,1},{2,18}... | collective-permute-start | bytes 1769480 | tf_op jit(solution)/shard_map/ppermute | solution.py:57
  680.3 42.1 %collective-permute-start.46 = (bf16[256,1152]{1,0:T(8,128)(2,1)}, bf16[256,1152]{1,0:T(8,128)(2,1)}, u32[]{:S(2)}, u32[]{:S(2)}) collective-permute-start(bf16[256,1152]{1,0:T(8,128)(2,1)} %pad_maximum_fusion.9), channel_id=1, source_target_pairs={{0,48},{16,0},{32,16},{48,32},{1,49},{17,1},{33,17},{49,33},{2,50}... | collective-permute-start | bytes 1769480 | tf_op jit(solution)/shard_map/ppermute | solution.py:57
  684.9 33.6 %collective-permute-start.76 = (bf16[128,1792]{1,0:T(8,128)(2,1)S(1)}, bf16[128,1792]{1,0:T(8,128)(2,1)S(1)}, u32[]{:S(2)}, u32[]{:S(2)}) collective-permute-start(bf16[128,1792]{1,0:T(8,128)(2,1)S(1)} %add.556.refs_0_), channel_id=1, source_target_pairs={{0,48},{16,0},{32,16},{48,32},{1,49},{17,1},{33,17},{49,33},{2,50}... | collective-permute-start | bytes 1376264 | tf_op jit(solution)/shard_map/ppermute | solution.py:57
  686.5 45.2 %all-to-all-start.9 = ((bf16[8,64,512]{2,1,0:T(8,128)(2,1)}), bf16[8,64,512]{2,1,0:T(8,128)(2,1)S(1)}, u32[]{:S(2)}, u32[]{:S(2)}) async-start(bf16[8,64,512]{2,1,0:T(8,128)(2,1)} %bitcast.42), calls=%async_computation.13 | async-start | bytes 1048576 | tf_op jit(solution)/shard_map/all_to_all | solution.py:1109
  703.9 34.2 %collective-permute-start.78 = (bf16[576,1152]{1,0:T(8,128)(2,1)}, bf16[576,1152]{1,0:T(8,128)(2,1)}, u32[]{:S(2)}, u32[]{:S(2)}) collective-permute-start(bf16[576,1152]{1,0:T(8,128)(2,1)} %shard_map.401.mine), channel_id=1, source_target_pairs={{0,8},{8,0},{1,9},{9,1},{2,10},{10,2},{3,11},{11,3},{4,12},{12,4},... | collective-permute-start | bytes 3981320 | tf_op jit(solution)/shard_map/ppermute | solution.py:57
  (144 other events, 1854.2 us)
Sparse Core Ops, SparseCore 0:
  10.6 71.7 all-gather.1
  112.9 37.7 reduce-scatter.4
  369.6 71.7 reduce-scatter.6
  599.6 18.2 reduce-scatter.8
  620.8 29.6 reduce-scatter.10

commit v9 on v8

--- a/solution.py
+++ b/solution.py
@@ -50,6 +50,10 @@
 
 def params():
     return pltpu.CompilerParams(vmem_limit_bytes=VMEM)
+
+
+def cost(micros):
+    return pl.CostEstimate(flops=int(micros * 1.15e9), bytes_accessed=0, transcendentals=0)
 
 
 def shift(x, axis, by):
@@ -683,6 +687,7 @@
         ],
         out_shape=[jax.ShapeDtypeStruct((ROW // SPLIT, D), bf16)] * SPLIT
         + [jax.ShapeDtypeStruct((8, D), f32)],
+        cost_estimate=cost(11),
         compiler_params=params(),
     )(g, w, plain)
 
@@ -709,6 +714,7 @@
         ],
         out_specs=pl.BlockSpec((384, 3 * SHARD), lambda i: (i, 0)),
         out_shape=jax.ShapeDtypeStruct((D, 3 * SHARD), bf16),
+        cost_estimate=cost(8),
         compiler_params=params(),
     )(x, g)
 
@@ -832,23 +838,22 @@
     heads_w = peers_parts(heads_pack)
     n31, n20, n11 = gather_second(n01, n10)
 
-    text_own = jnp.pad(after(text_states[0], heads_w), ((0, TXT_OWN - CAP_TOK), (0, 0)))
-    text_columns = lax.all_to_all(text_own, FS, split_axis=1, concat_axis=0, tiled=True)
-    n31, n20, n11, text_columns = lax.optimization_barrier((n31, n20, n11, text_columns))
+    n31, n20, n11 = lax.optimization_barrier((n31, n20, n11))
     n21 = gather_third(n31, n11)
-    heads_w = spread_heads(heads_w)
-    context_part = dot_nn(text_columns, w_text).astype(bf16)
-    context_own = lax.psum_scatter(context_part, FS, scatter_dimension=0, tiled=True)
     plain_all, normed_all = place_rows(
-        after(plain, context_part),
+        plain,
         (n01, n10, n30),
         (n31, n20, n11),
         n21,
         row(ln1_gain),
         row(ln1_bias),
     )
-    quarter_own, normed_all = lax.optimization_barrier((quarter_own, normed_all))
+    heads_w = spread_heads(heads_w)
+    quarter_own, normed_all, heads_w = lax.optimization_barrier((quarter_own, normed_all, heads_w))
     quarter_minus, quarter_plus = shift(quarter_own, "z", 1), shift(quarter_own, "z", -1)
+
+    text_own = jnp.pad(after(text_states[0], normed_all), ((0, TXT_OWN - CAP_TOK), (0, 0)))
+    text_columns = lax.all_to_all(text_own, FS, split_axis=1, concat_axis=0, tiled=True)
 
     up_own = jnp.concatenate(
         [
@@ -861,7 +866,10 @@
 
     seg_col, seg_row = segment[:, None], segment[None, :]
     qkv = dot_nn(normed_all, heads_w).astype(bf16)
-    head0, total0 = self_forward(0, seg_col, seg_row, qkv)
+    text_columns, qkv = lax.optimization_barrier((text_columns, qkv))
+    context_part = dot_nn(text_columns, w_text).astype(bf16)
+    context_own = lax.psum_scatter(context_part, FS, scatter_dimension=0, tiled=True)
+    head0, total0 = self_forward(0, seg_col, seg_row, after(qkv, context_part))
     head1, total1 = self_forward(1, seg_col, seg_row, after(qkv, head0))
     quarter_minus, quarter_plus, head1 = lax.optimization_barrier(
         (quarter_minus, quarter_plus, head1)
@@ -952,11 +960,6 @@
     )
     back_minus, back_plus, keep = lax.optimization_barrier((back_minus, back_plus, keep))
     hidden_sum = keep + shift(send, "c", 1)
-
-    def hidden_chunk(dy, dx):
-        return row_block(hidden_sum, peer(dy, dx), SHARD)
-
-    h_lo, h_hi, h20 = reduce_first(hidden_chunk)
     grad_after_cross, grad_cross_branch, grad_cross_mixed, sums_three = call(
         third_back_body,
         [
@@ -974,21 +977,19 @@
         cross_query,
         cross_key,
         cross_value,
-        after(grad_cross_mixed, h_lo, h_hi),
-    )
-    h11, h31 = reduce_second(hidden_chunk, h_lo, h_hi)
+        grad_cross_mixed,
+    )
     kv_own = lax.psum_scatter(grad_kv, FS, scatter_dimension=0, tiled=True)
     grad_after_self, grad_self_branch, grad_attended, sums_two = call(
         second_back_body,
         [
-            (core_index, "smem"), (after_self, "vmem"), (after(grad_cquery_rows, h11, h31, h20), "vmem"),
+            (core_index, "smem"), (after_self, "vmem"), (grad_cquery_rows, "vmem"),
             (grad_after_cross, "vmem"), (row(ln2_gain), "vmem"),
             (square_mine, "hbm"), (square_other, "hbm"),
         ],
         [((TOK, D), f32), ((TOK, D), bf16), ((TOK, D), bf16), ((8, D), f32)],
         square_scratch(2),
     )
-    hidden_parts = reduce_third(hidden_chunk, h20, h11, h31)
     grad_heads = lax.all_to_all(grad_attended, FS, split_axis=1, concat_axis=0, tiled=True)
 
     square = jnp.concatenate(
@@ -1003,40 +1004,48 @@
     def square_chunk(dy, dx):
         return row_block(square, peer(dy, dx), SHARD)
 
-    grad_heads, square, *hidden_parts = lax.optimization_barrier(
-        (grad_heads, square, *hidden_parts)
-    )
-    hidden_grad = reduce_last(hidden_chunk, *hidden_parts).astype(bf16)
+    grad_heads, square = lax.optimization_barrier((grad_heads, square))
     grad_qkv = self_backward(0, seg_col, seg_row, total0, qkv, grad_heads)
-    kv_own, grad_qkv, square = lax.optimization_barrier((kv_own, grad_qkv, square))
+    kv_own, square, grad_qkv = lax.optimization_barrier((kv_own, square, grad_qkv))
     s_lo, s_hi, s20 = reduce_first(square_chunk)
     kv_all = every_peer(kv_own)
-    hidden_grad = after(hidden_grad, kv_own)
-    hidden_grad = hidden_grad + shift(hidden_grad, "xh", 1)
-    out_minus, out_plus = reduce_z(after(out_far, kv_own), out_m, out_p)
+    hidden_grad = lax.psum_scatter(after(hidden_sum, kv_own), FS, scatter_dimension=0, tiled=True)
+    out_minus, out_plus = reduce_z(after(out_far, grad_qkv), out_m, out_p)
     grad_qkv = self_backward(
         1, seg_col, seg_row, total1, qkv, after(grad_heads, kv_own), (grad_qkv,)
     )
-    s_lo, s_hi, out_minus, out_plus, hidden_grad, grad_qkv = lax.optimization_barrier(
-        (s_lo, s_hi, out_minus, out_plus, hidden_grad, grad_qkv)
-    )
+    s_lo, s_hi, s20, out_minus, out_plus, grad_qkv = lax.optimization_barrier(
+        (s_lo, s_hi, s20, out_minus, out_plus, grad_qkv)
+    )
+    s11, s31 = reduce_second(square_chunk, s_lo, s_hi)
+
     heads_own = heads_grad(normed_all, grad_qkv)
-    heads_own, kv_all = lax.optimization_barrier((heads_own, kv_all))
+    heads_own, s11, s31, kv_all = lax.optimization_barrier((heads_own, s11, s31, kv_all))
     heads_part = peers_parts(heads_own)
+    square_parts = reduce_third(square_chunk, s20, s11, s31)
     part, sums_one = first_part(after(grad_qkv, heads_own), heads_w, plain_all)
-    part, heads_part = lax.optimization_barrier((part, heads_part))
+    part, heads_part, kv_all, *square_parts = lax.optimization_barrier(
+        (part, heads_part, kv_all, *square_parts)
+    )
     sent = peers_parts(part)
 
-    s11, s31 = reduce_second(square_chunk, after(s_lo, part), s_hi)
-    hidden_z = neighbours(after(hidden_grad, part))
+    square = reduce_last(square_chunk, *square_parts).astype(bf16)
     heads_rows = unpack_heads(heads_part)
     early = row_block(heads_rows, core, 216) + shift(row_block(heads_rows, 1 - core, 216), "c", 1)
     early = jnp.concatenate([early, jnp.zeros((256 - 216, D), bf16)], axis=0)
+    square = jnp.concatenate([square[:, WIN * k : WIN * (k + 1)] for k in range(3)], axis=0)
+    square = jnp.concatenate([square[:216], square[216:]], axis=1)
+    early = jnp.concatenate(
+        [early, jnp.concatenate([square, jnp.zeros((256 - 216, 2 * WIN), bf16)], axis=0)], axis=1
+    )
+    early = lax.psum_scatter(early, "z", scatter_dimension=0, tiled=True)
+    norms = jnp.concatenate([sums_one[:2], sums_two[:2], sums_three[:2], jnp.zeros((2, D), f32)])
+    norms = sum_over(norms, "z", "c")
     own_columns = lax.dynamic_slice_in_dim(context, peer(0, 0) * SHARD, SHARD, axis=1)
     text_part, grad_w_text, grad_w_kv = call(
         text_back_body,
         [
-            (core_index, "smem"), (after(kv_all, part), "vmem"), (own_columns, "vmem"),
+            (core_index, "smem"), (kv_all, "vmem"), (own_columns, "vmem"),
             (text_columns, "vmem"), (w_text, "vmem"),
             (square_mine, "hbm"), (square_other, "hbm"),
         ],
@@ -1047,31 +1056,23 @@
     def half(which):
         kv = jnp.where(which == 0, grad_w_kv[:, :D], grad_w_kv[:, D:])
         return jnp.concatenate(
-            [row_block(grad_w_text, which, 256), kv, jnp.zeros((512 - 400, D), bf16)], axis=0
+            [row_block(grad_w_text, which, 256), kv, jnp.zeros((448 - 400, D), bf16)], axis=0
         )
 
     late = half(core) + shift(half(1 - core), "c", 1)
-    early = lax.psum_scatter(early, "z", scatter_dimension=0, tiled=True)
-    square_parts = reduce_third(square_chunk, s20, s11, s31)
-    square = reduce_last(square_chunk, *square_parts).astype(bf16)
-    square = jnp.concatenate(
-        [square[:, WIN * k : WIN * (k + 1)] for k in range(3)]
-        + [jnp.zeros((512 - 3 * SHARD, WIN), bf16)],
-        axis=0,
-    )
-    late = jnp.concatenate([late, square], axis=1)
     late = lax.psum_scatter(late, "z", scatter_dimension=0, tiled=True)
-    part, early, late, *hidden_z = lax.optimization_barrier((sent, early, late, *hidden_z))
+    hidden_grad = after(hidden_grad, part)
+    hidden_grad = hidden_grad + shift(hidden_grad, "xh", 1)
+    part, norms, late = lax.optimization_barrier((sent, norms, late))
+    early = after(early, part)
     early = early + shift(early, "xh", 1)
-    norms = jnp.concatenate([sums_one[:2], sums_two[:2], sums_three[:2], jnp.zeros((2, D), f32)])
-    norms = sum_over(after(norms, part), "z", "c")
+    hidden_grad = in_order(*neighbours(after(hidden_grad, part)))
+    grad_w_up, grad_w_down = sort_hidden(core_index, hidden_grad, shift(hidden_grad, "c", 1))
 
     norms = sum_over(norms, "y", "xl", "xh")
     late = late + shift(late, "xh", 1)
     early = in_order(*neighbours(early))
     late = in_order(*neighbours(late))
-    hidden_grad = in_order(*hidden_z)
-    grad_w_up, grad_w_down = sort_hidden(core_index, hidden_grad, shift(hidden_grad, "c", 1))
 
     def by_core(x):
         other = shift(x, "c", 1)
@@ -1079,19 +1080,20 @@
         return low.astype(f32), high.astype(f32)
 
     low, high = by_core(early)
-    grad_w_query = low[:144]
-    grad_w_key = jnp.concatenate([low[144:216], high[:72]], axis=0)
-    grad_w_value = high[72:216]
-    low, high = by_core(late)
-    grad_w_text = jnp.concatenate([low[:256, :D], high[:256, :D]], axis=0)
-    grad_c_key, grad_c_value = low[256:400, :D], high[256:400, :D]
+    grad_w_query = low[:144, :D]
+    grad_w_key = jnp.concatenate([low[144:216, :D], high[:72, :D]], axis=0)
+    grad_w_value = high[72:216, :D]
+    low = jnp.concatenate([low[:216, D : D + WIN], low[:216, D + WIN :]], axis=0)
+    high = jnp.concatenate([high[:216, D : D + WIN], high[:216, D + WIN :]], axis=0)
     grad_c_out, grad_c_query, grad_w_out = (
         jnp.concatenate(
-            [low[SHARD * k : SHARD * (k + 1), D:], high[SHARD * k : SHARD * (k + 1), D + 128 :]],
-            axis=1,
+            [low[SHARD * k : SHARD * (k + 1)], high[SHARD * k : SHARD * (k + 1), 128:]], axis=1
         )
         for k in range(3)
     )
+    low, high = by_core(late)
+    grad_w_text = jnp.concatenate([low[:256], high[:256]], axis=0)
+    grad_c_key, grad_c_value = low[256:400], high[256:400]
     out_minus, out_plus = shift(out_minus, "z", -1), shift(out_plus, "z", 1)
     outputs = (
         after_cross + out_own.astype(f32) + out_minus.astype(f32) + out_plus.astype(f32)

time: 766 us -> 775 us (1.012)
  waiting for transfers between devices: 196 us -> 244 us
  starting transfers between devices: 173 us -> 126 us
  blocking collectives: 0 us -> 14 us
    all_to_all x3, waiting for transfers between devices: 24.9 us -> 76.8 us  [peers_parts(): return lax.all_to_all(x, axes, 0, 0, tiled=True)]
    ppermute x79 -> x71, starting transfers between devices: 133 us -> 88.7 us  [shift(): return lax.ppermute(x, axis, [(i, (i + by) % n) for i in range(n)])]
    ppermute x79 -> x71, waiting for transfers between devices: 124 us -> 80.9 us  [shift(): return lax.ppermute(x, axis, [(i, (i + by) % n) for i in range(n)])]
    reduce_scatter x0 -> x1, waiting for transfers between devices: none -> 31.1 us  [local(): lax.psum_scatter(after(hidden_sum, kv_own), FS, scatter_dimension=0, tile...]
    reduce_scatter x1, waiting for transfers between devices: 0.01 us -> 28.8 us  [local(): early = lax.psum_scatter(early, 'z', scatter_dimension=0, tiled=True)]
    reduce_scatter x1, waiting for transfers between devices: 16 us -> 0.01 us  [local(): late = lax.psum_scatter(late, 'z', scatter_dimension=0, tiled=True)]
    all_to_all x0 -> x1, blocking collectives: none -> 14 us  [local(): lax.all_to_all(jnp.concatenate([head0, head1], axis=1), FS, split_axis=0,...]
    all_to_all x1, waiting for transfers between devices: 8.3 us -> 0.01 us  [local(): lax.all_to_all(text_own, FS, split_axis=1, concat_axis=0, tiled=True)]
  transfers between devices with their start and end apart: 94 -> 86, of which waited for: 34 -> 26; matrix products, arithmetic and copies ran while one was open for 14% -> 12% of each run, Pallas kernels for 28% -> 25%
where the time goes in v9:
time: 775 us; the launch traced here: 767 us
  waiting for transfers between devices  244 us (31%)
  Pallas kernels  240 us (31%)
  starting transfers between devices  126 us (16%)
  local copies, waits for them, and re-layouts  59.1 us (8%)
  other arithmetic  49.3 us (6%)
  matrix products  19.2 us (2%)
  between operations  15.6 us (2%)
  blocking collectives  14 us (2%)
    ppermute x71, starting transfers between devices, shift(): return lax.ppermute(x, axis, [(i, (i + by) % n) for i in range(n)])  88.7 us
    ppermute x71, waiting for transfers between devices, shift(): return lax.ppermute(x, axis, [(i, (i + by) % n) for i in range(n)])  80.9 us
    all_to_all x3, waiting for transfers between devices, peers_parts(): return lax.all_to_all(x, axes, 0, 0, tiled=True)  76.8 us
    pallas_call x7, Pallas kernels, call(): pl.pallas_call(body, in_specs=[pl.BlockSpec(memory_space=spaces[where]) f...  51.7 us
    pallas_call x2, Pallas kernels, self_backward(): pl.pallas_call(functools.partial(self_backward_body, head), grid=(ROW //...  37.3 us
    reduce_scatter x1, waiting for transfers between devices, local(): lax.psum_scatter(after(hidden_sum, kv_own), FS, scatter_dimension=0, tile...  31.1 us
    reduce_scatter x1, waiting for transfers between devices, local(): early = lax.psum_scatter(early, 'z', scatter_dimension=0, tiled=True)  28.8 us
    pallas_call x3, Pallas kernels, mlp(): pl.pallas_call(functools.partial(mlp_body, parts, count), in_specs=[pl.Bl...  28.6 us
  transfers between devices with their start and end apart: 86, of which 26 were waited for; matrix products, arithmetic and copies ran while one was open for 12% of the time, Pallas kernels for 25%

profile of v9, /device:TPU:1, one launch (start us, length us, event | category | flops | bytes accessed | tf_op | source)
XLA Modules:
  0.0 766.8 jit_solution(3673843534677067469)
XLA Ops:
  18.8 9.6 %collective-permute-done.refs_1_ = bf16[256,1152]{1,0:T(8,128)(2,1)S(1)} collective-permute-done((bf16[256,1152]{1,0:T(8,128)(2,1)S(1)}, bf16[256,1152]{1,0:T(8,128)(2,1)S(1)}, u32[]{:S(2)}, u32[]{:S(2)}) %collective-permute-start) | collective-permute-done | bytes 589856 | tf_op jit(solution)/shard_map/ppermute | solution.py:61
  39.2 11.9 %collective-permute-done.3.refs_4_ = bf16[256,1152]{1,0:T(8,128)(2,1)S(1)} collective-permute-done((bf16[256,1152]{1,0:T(8,128)(2,1)S(1)}, bf16[256,1152]{1,0:T(8,128)(2,1)S(1)}, u32[]{:S(2)}, u32[]{:S(2)}) %collective-permute-start.3) | collective-permute-done | bytes 589856 | tf_op jit(solution)/shard_map/ppermute | solution.py:61
  51.1 11.0 %collective-permute-done.5.refs_6_ = bf16[256,1152]{1,0:T(8,128)(2,1)S(1)} collective-permute-done((bf16[256,1152]{1,0:T(8,128)(2,1)}, bf16[256,1152]{1,0:T(8,128)(2,1)S(1)}, u32[]{:S(2)}, u32[]{:S(2)}) %collective-permute-start.5) | collective-permute-done | bytes 589856 | tf_op jit(solution)/shard_map/ppermute | solution.py:61
  65.6 21.5 %all-to-all-done = bf16[8,144,432]{2,1,0:T(8,128)(2,1)S(1)} async-done(((bf16[8,144,432]{2,1,0:T(8,128)(2,1)}), bf16[8,144,432]{2,1,0:T(8,128)(2,1)S(1)}, u32[]{:S(2)}, u32[]{:S(2)}) %all-to-all-start) | async-done | bytes 995360 | tf_op jit(solution)/shard_map/all_to_all | solution.py:122
  107.3 8.8 %convolution_convert_fusion.q.kv = bf16[2048,768]{1,0:T(8,128)(2,1)} fusion(bf16[2048,1152]{1,0:T(8,128)(2,1)} %get-tuple-element.152.x, bf16[1152,768]{1,0:T(8,128)(2,1)} %shard_map.376.w), kind=kOutput, calls=%fused_computation.1 | convolution fusion | flops 3625451520 | bytes 9633792 | tf_op jit(solution)/shard_map/dot_general | solution.py:40
  121.1 12.1 %shard_map.377 = (bf16[2048,72]{1,0:T(8,128)(2,1)}, f32[1,2048]{1,0:T(1,128)}) custom-call(s32[2048,1]{1,0:T(8,128)} %copy.114.seg_q.seg_k, s32[1,2048]{1,0:T(1,128)} %bitcast.91, bf16[2048,768]{1,0:T(8,128)(2,1)} %convolution_convert_fusion.q.kv, bf16[2048,768]{1,0:T(8,128)(2,1)} %convolution_convert_fusion.q.kv), custom_call_target="tpu_custom_call" | custom-call | tf_op jit(solution)/shard_map/pallas_call | solution.py:283
  133.2 12.2 %shard_map.378 = (bf16[2048,72]{1,0:T(8,128)(2,1)}, f32[1,2048]{1,0:T(1,128)}) custom-call(s32[2048,1]{1,0:T(8,128)} %copy.114.seg_q.seg_k, s32[1,2048]{1,0:T(1,128)} %bitcast.92, bf16[2048,768]{1,0:T(8,128)(2,1)} %convolution_convert_fusion.q.kv, bf16[2048,768]{1,0:T(8,128)(2,1)} %convolution_convert_fusion.q.kv), custom_call_target="tpu_custom_call" | custom-call | tf_op jit(solution)/shard_map/pallas_call | solution.py:283
  152.3 14.0 %all_to_all.135 = bf16[8,256,144]{1,2,0:T(8,128)(2,1)} all-to-all(bf16[8,256,144]{1,2,0:T(8,128)(2,1)S(1)} %copy.116), channel_id=1, replica_groups=mesh['xh'=2,'z'=4,'c'=2,'y'=4,'xl'=2] {'y','xl'}, dimensions={0} | all-to-all | bytes 1179648 | tf_op jit(solution)/shard_map/all_to_all | solution.py:881
  186.7 14.1 %all-to-all-done.3 = bf16[8,64,1152]{2,1,0:T(8,128)(2,1)S(1)} async-done(((bf16[8,64,1152]{2,1,0:T(8,128)(2,1)}), bf16[8,64,1152]{2,1,0:T(8,128)(2,1)S(1)}, u32[]{:S(2)}, u32[]{:S(2)}) %all-to-all-start.3) | async-done | bytes 1179680 | tf_op jit(solution)/shard_map/all_to_all | solution.py:118
  224.2 8.4 %shard_map.381 = (bf16[512,1152]{1,0:T(8,128)(2,1)}, bf16[512,1152]{1,0:T(8,128)(2,1)}) custom-call(s32[1]{0:T(128)} %bitcast.core, bf16[512,1152]{1,0:T(8,128)(2,1)} %bitcast.70, bf16[1152,3072]{1,0:T(8,128)(2,1)} %shard_map.379.mine, bf16[1152,3072]{1,0:T(8,128)(2,1)} %collective-permute-done.12.other), custom_call_target="tpu_custom_call" | custom-call | tf_op jit(solution)/shard_map/pallas_call | solution.py:573
  232.6 11.7 %shard_map.382.mixed = bf16[256,1152]{1,0:T(8,128)(2,1)} custom-call(s32[256,1]{1,0:T(8,128)} %copy.118.cap_q, s32[1,512]{1,0:T(1,128)} %and_select_fusion.1.cap_t, bf16[256,1152]{1,0:T(8,128)(2,1)} %get-tuple-element.169.q, bf16[512,1152]{1,0:T(8,128)(2,1)} %get-tuple-element.173.k, bf16[512,1152]{1,0:T(8,128)(2,1)} %get-tuple-element.174.v), custom_call_target="tpu_custom_call" | custom-call | tf_op jit(solution)/shard_map/pallas_call | solution.py:374
  262.0 8.2 %shard_map.384 = (bf16[256,1152]{1,0:T(8,128)(2,1)}, bf16[256,1152]{1,0:T(8,128)(2,1)}, bf16[256,1152]{1,0:T(8,128)(2,1)}, bf16[256,1152]{1,0:T(8,128)(2,1)}) custom-call(s32[1]{0:T(128)} %bitcast.core, bf16[256,1152]{1,0:T(8,128)(2,1)} %get-tuple-element.176.refs_0_, bf16[256,1152]{1,0:T(8,128)(2,1)} %copy-done.2, bf16[1152,1152]{1,0:T(8,128)(2,1)} %bitcast.62, ...), custom_call_target="tpu_custom_call" | custom-call | tf_op jit(solution)/shard_map/pallas_call | solution.py:480
  276.0 12.3 %shard_map.385 = (bf16[256,1152]{1,0:T(8,128)(2,1)}, bf16[256,1152]{1,0:T(8,128)(2,1)}, bf16[256,1152]{1,0:T(8,128)(2,1)}, bf16[256,1152]{1,0:T(8,128)(2,1)}, bf...) custom-call(s32[1]{0:T(128)} %bitcast.core, ...), custom_call_target="tpu_custom_call" | custom-call | tf_op jit(solution)/shard_map/pallas_call | solution.py:480
  302.0 8.7 %shard_map.387 = bf16[1152,1152]{1,0:T(8,128)(2,1)} custom-call(s32[1]{0:T(128)} %bitcast.core, bf16[256,1152]{1,0:T(8,128)(2,1)} %get-tuple-element.176.refs_0_, bf16[256,1152]{1,0:T(8,128)(2,1)} %copy-done.4, bf16[256,1152]{1,0:T(8,128)(2,1)} %collective-permute-done.16.refs_1_.refs_2_, bf16[256,1152]{1,0:T(8,128)(2,1)} %copy-done.14, ...), custom_call_target="tpu_custom_call" | custom-call | tf_op jit(solution)/shard_map/pallas_call | solution.py:514
  320.0 9.1 %shard_map.388 = bf16[1152,1152]{1,0:T(8,128)(2,1)} custom-call(s32[1]{0:T(128)} %bitcast.core, bf16[256,1152]{1,0:T(8,128)(2,1)} %get-tuple-element.176.refs_0_, bf16[256,1152]{1,0:T(8,128)(2,1)} %copy-done.4, bf16[256,1152]{1,0:T(8,128)(2,1)} %collective-permute-done.16.refs_1_.refs_2_, bf16[256,1152]{1,0:T(8,128)(2,1)} %copy-done.14, ...), custom_call_target="tpu_custom_call" | custom-call | tf_op jit(solution)/shard_map/pallas_call | solution.py:514
  346.4 15.3 %shard_map.390 = (bf16[256,1152]{1,0:T(8,128)(2,1)}, bf16[512,2304]{1,0:T(8,128)(2,1)}) custom-call(s32[512,1]{1,0:T(8,128)} %fusion.36.cap_t, s32[1,256]{1,0:T(1,128)} %bitcast.98, bf16[256,1152]{1,0:T(8,128)(2,1)} %get-tuple-element.169.q, bf16[512,1152]{1,0:T(8,128)(2,1)} %get-tuple-element.173.k, bf16[512,1152]{1,0:T(8,128)(2,1)} %get-tuple-element.174.v, ...), custom_call_target="tpu_custom_call" | custom-call | tf_op jit(solution)/shard_map/pallas_call | solution.py:402
  402.6 18.7 %shard_map.392.refs_0_ = bf16[2048,768]{1,0:T(8,128)(2,1)} custom-call(s32[2048,1]{1,0:T(8,128)} %copy.114.seg_q.seg_k, s32[1,2048]{1,0:T(1,128)} %bitcast.93, f32[1,2048]{1,0:T(1,128)} %get-tuple-element.219.total, bf16[2048,768]{1,0:T(8,128)(2,1)} %convolution_convert_fusion.q.kv, bf16[2048,768]{1,0:T(8,128)(2,1)} %convolution_convert_fusion.q.kv, ...), custom_call_target="tpu_custom_call" | custom-call | tf_op jit(solution)/shard_map/pallas_call | solution.py:335
  441.1 18.6 %shard_map.393.g = bf16[2048,768]{1,0:T(8,128)(2,1)} custom-call(s32[2048,1]{1,0:T(8,128)} %copy.114.seg_q.seg_k, s32[1,2048]{1,0:T(1,128)} %bitcast.94, f32[1,2048]{1,0:T(1,128)} %get-tuple-element.227.total, bf16[2048,768]{1,0:T(8,128)(2,1)} %convolution_convert_fusion.q.kv, ...), custom_call_target="tpu_custom_call", output_to_operand_aliasing={{}: (6, {})} | custom-call | tf_op jit(solution)/shard_map/pallas_call | solution.py:335
  491.8 10.8 %shard_map.395 = (bf16[2048,1152]{1,0:T(8,128)(2,1)}, f32[8,1152]{1,0:T(8,128)}) custom-call(bf16[2048,768]{1,0:T(8,128)(2,1)} %shard_map.393.g, bf16[1152,768]{1,0:T(8,128)(2,1)} %shard_map.376.w, bf16[2048,1152]{1,0:T(8,128)(2,1)} %get-tuple-element.237.plain), custom_call_target="tpu_custom_call" | custom-call | flops 12650000384 | tf_op jit(solution)/shard_map/pallas_call | solution.py:676
  502.6 8.7 %collective-permute-done.42 = bf16[144,1920]{1,0:T(8,128)(2,1)S(1)} collective-permute-done((bf16[144,1920]{1,0:T(8,128)(2,1)}, bf16[144,1920]{1,0:T(8,128)(2,1)S(1)}, u32[]{:S(2)}, u32[]{:S(2)}) %collective-permute-start.42) | collective-permute-done | bytes 552992 | tf_op jit(solution)/shard_map/ppermute | solution.py:61
  511.3 11.5 %shard_map.396 = (bf16[512,512]{1,0:T(8,128)(2,1)}, bf16[512,1152]{1,0:T(8,128)(2,1)}, bf16[144,2304]{1,0:T(8,128)(2,1)}) custom-call(s32[1]{0:T(128)} %bitcast.core, bf16[512,2304]{1,0:T(8,128)(2,1)} %bitcast.67, bf16[512,144]{1,0:T(8,128)(2,1)} %constant_dynamic-slice_fusion.5.cols, bf16[512,512]{1,0:T(8,128)(2,1)} %bitcast.83, bf16[512,1152]{1,0:T(8,128)(2,1)} %w_text.1, ...), custom_call_target="tpu_custom_call" | custom-call | tf_op jit(solution)/shard_map/pallas_call | solution.py:573
  555.8 55.3 %all-to-all-done.8 = bf16[8,256,1152]{2,1,0:T(8,128)(2,1)} async-done(((bf16[8,256,1152]{2,1,0:T(8,128)(2,1)}), bf16[8,256,1152]{2,1,0:T(8,128)(2,1)}, u32[]{:S(2)}, u32[]{:S(2)}) %all-to-all-start.8) | async-done | bytes 4718624 | tf_op jit(solution)/shard_map/all_to_all | solution.py:122
  616.0 31.1 %reduce-scatter.14.cloned.1.call-done = bf16[144,1152]{1,0:T(8,128)(2,1)} async-done(((bf16[1152,1152]{1,0:T(8,128)(2,1)}), bf16[144,1152]{1,0:T(8,128)(2,1)}) %reduce-scatter.14.cloned.1.call-update) | async-done | bytes 331792 | tf_op jit(solution)/shard_map/reduce_scatter | solution.py:1012
  664.3 28.8 %reduce-scatter.12.cloned.1.call-done = bf16[64,2432]{1,0:T(8,128)(2,1)} async-done(((bf16[256,2432]{1,0:T(8,128)(2,1)}), bf16[64,2432]{1,0:T(8,128)(2,1)}) %reduce-scatter.12.cloned.1.call-update) | async-done | bytes 311312 | tf_op jit(solution)/shard_map/reduce_scatter | solution.py:1041
  (451 shorter events, 379.0 us)
Async XLA Ops:
  7.2 92.6 %all-gather.2.cloned.1.call-start = ((), (), s32[]{:S(2)}) async-start(), calls=%async_computation.15 | async-start | bytes 1990656 | tf_op jit(solution)/shard_map/all_gather | solution.py:830
  35.5 51.6 %all-to-all-start = ((bf16[8,144,432]{2,1,0:T(8,128)(2,1)}), bf16[8,144,432]{2,1,0:T(8,128)(2,1)S(1)}, u32[]{:S(2)}, u32[]{:S(2)}) async-start(bf16[8,144,432]{2,1,0:T(8,128)(2,1)} %bitcast.74), calls=%async_computation | async-start | bytes 2359296 | tf_op jit(solution)/shard_map/all_to_all | solution.py:122
  99.8 45.6 %collective-permute-start.8 = (bf16[1152,768]{1,0:T(8,128)(2,1)}, bf16[1152,768]{1,0:T(8,128)(2,1)S(1)}, u32[]{:S(2)}, u32[]{:S(2)}) collective-permute-start(bf16[1152,768]{1,0:T(8,128)(2,1)} %all-gather.2.cloned.1.call-done.own), channel_id=1, source_target_pairs={{0,16},{16,32},{32,48},{48,0},{1,17},{17,33},{33,49},{49,1},{2,18}... | collective-permute-start | bytes 5308424 | tf_op jit(solution)/shard_map/ppermute | solution.py:61
  101.5 43.9 %collective-permute-start.9 = (bf16[1152,768]{1,0:T(8,128)(2,1)}, bf16[1152,768]{1,0:T(8,128)(2,1)}, u32[]{:S(2)}, u32[]{:S(2)}) collective-permute-start(bf16[1152,768]{1,0:T(8,128)(2,1)} %all-gather.2.cloned.1.call-done.own), channel_id=1, source_target_pairs={{0,48},{16,0},{32,16},{48,32},{1,49},{17,1},{33,17},{49,33},{2,50}... | collective-permute-start | bytes 5308424 | tf_op jit(solution)/shard_map/ppermute | solution.py:61
  107.1 61.1 %reduce-scatter.6.cloned.1.call-start = ((), (), s32[]{:S(2)}) async-start(), calls=%async_computation.16 | async-start | bytes 1327104 | tf_op jit(solution)/shard_map/reduce_scatter | solution.py:871
  174.2 43.0 %collective-permute-start.12 = (bf16[1152,3072]{1,0:T(8,128)(2,1)}, bf16[1152,3072]{1,0:T(8,128)(2,1)}, u32[]{:S(2)}, u32[]{:S(2)}) collective-permute-start(bf16[1152,3072]{1,0:T(8,128)(2,1)} %shard_map.379.mine), channel_id=1, source_target_pairs={{0,8},{8,0},{1,9},{9,1},{2,10},{10,2},{3,11},{11,3},{4,12},{12,4},... | collective-permute-start | bytes 21233672 | tf_op jit(solution)/shard_map/ppermute | solution.py:61
  202.7 41.6 %all-to-all-start.4 = ((bf16[8,144,1152]{2,1,0:T(8,128)(2,1)}), bf16[8,144,1152]{2,1,0:T(8,128)(2,1)S(1)}, u32[]{:S(2)}, u32[]{:S(2)}) async-start(bf16[8,144,1152]{2,1,0:T(8,128)(2,1)} %broadcast_in_dim.134), calls=%async_computation.5 | async-start | bytes 5308416 | tf_op jit(solution)/shard_map/all_to_all | solution.py:118
  206.4 218.2 %reduce-scatter.8.cloned.1.call-start = ((), (), s32[]{:S(2)}) async-start(), calls=%async_computation.17 | async-start | bytes 2654208 | tf_op jit(solution)/shard_map/reduce_scatter | solution.py:982
  426.3 37.3 %collective-permute-start.33 = (bf16[80,1920]{1,0:T(8,128)(2,1)}, bf16[80,1920]{1,0:T(8,128)(2,1)}, u32[]{:S(2)}, u32[]{:S(2)}) collective-permute-start(bf16[80,1920]{1,0:T(8,128)(2,1)} %constant_dynamic-slice_fusion), channel_id=1, source_target_pairs={{0,2},{2,4},{4,6},{6,0},{1,3},{3,5},{5,7},{7,1},{8,10},{10,12},{12... | collective-permute-start | bytes 921608 | tf_op jit(solution)/shard_map/ppermute | solution.py:61
  437.2 42.1 %all-to-all-start.6 = ((bf16[8,64,2304]{2,1,0:T(8,128)(2,1)}), bf16[8,64,2304]{2,1,0:T(8,128)(2,1)S(1)}, u32[]{:S(2)}, u32[]{:S(2)}) async-start(bf16[8,64,2304]{2,1,0:T(8,128)(2,1)} %broadcast_in_dim.137), calls=%async_computation.8 | async-start | bytes 4718592 | tf_op jit(solution)/shard_map/all_to_all | solution.py:118
  484.1 71.7 %reduce-scatter.10.cloned.1.call-start = ((), (), s32[]{:S(2)}) async-start(), calls=%async_computation.18 | async-start | bytes 1290240 | tf_op jit(solution)/shard_map/reduce_scatter | solution.py:1063
  530.4 116.7 %reduce-scatter.14.cloned.1.call-start = ((), (), s32[]{:S(2)}) async-start(), calls=%async_computation.20 | async-start | bytes 2985984 | tf_op jit(solution)/shard_map/reduce_scatter | solution.py:1012
  531.0 80.0 %all-to-all-start.8 = ((bf16[8,256,1152]{2,1,0:T(8,128)(2,1)}), bf16[8,256,1152]{2,1,0:T(8,128)(2,1)}, u32[]{:S(2)}, u32[]{:S(2)}) async-start(bf16[8,256,1152]{2,1,0:T(8,128)(2,1)} %bitcast.73), calls=%async_computation.10 | async-start | bytes 9437184 | tf_op jit(solution)/shard_map/all_to_all | solution.py:122
  535.6 157.5 %reduce-scatter.12.cloned.1.call-start = ((), (), s32[]{:S(2)}) async-start(), calls=%async_computation.19 | async-start | bytes 1556480 | tf_op jit(solution)/shard_map/reduce_scatter | solution.py:1041
  611.0 36.0 %collective-permute-start.61 = (bf16[112,1152]{1,0:T(8,128)(2,1)}, bf16[112,1152]{1,0:T(8,128)(2,1)S(1)}, u32[]{:S(2)}, u32[]{:S(2)}) collective-permute-start(bf16[112,1152]{1,0:T(8,128)(2,1)} %reduce-scatter.10.cloned.1.call-done), channel_id=1, source_target_pairs={{0,64},{64,0},{1,65},{65,1},{2,66},{66,2},{3,67},{67,3},{4,68},{68... | collective-permute-start | bytes 774152 | tf_op jit(solution)/shard_map/ppermute | solution.py:61
  613.3 48.9 %collective-permute-start.39 = (bf16[256,1152]{1,0:T(8,128)(2,1)S(1)}, bf16[256,1152]{1,0:T(8,128)(2,1)S(1)}, u32[]{:S(2)}, u32[]{:S(2)}) collective-permute-start(bf16[256,1152]{1,0:T(8,128)(2,1)S(1)} %copy-done.36), channel_id=1, source_target_pairs={{0,16},{16,32},{32,48},{48,0},{1,17},{17,33},{33,49},{49,1},{2,18}... | collective-permute-start | bytes 1769480 | tf_op jit(solution)/shard_map/ppermute | solution.py:61
  613.3 37.2 %collective-permute-start.52 = (f32[8,1152]{1,0:T(8,128)S(1)}, f32[8,1152]{1,0:T(8,128)S(1)}, u32[]{:S(2)}, u32[]{:S(2)}) collective-permute-start(f32[8,1152]{1,0:T(8,128)S(1)} %add.480), channel_id=1, source_target_pairs={{0,6},{2,0},{4,2},{6,4},{1,7},{3,1},{5,3},{7,5},{8,14},{10,8},{12,... | collective-permute-start | bytes 110600 | tf_op jit(solution)/shard_map/ppermute | solution.py:61
  615.1 37.8 %collective-permute-start.51 = (f32[8,1152]{1,0:T(8,128)S(1)}, f32[8,1152]{1,0:T(8,128)S(1)}, u32[]{:S(2)}, u32[]{:S(2)}) collective-permute-start(f32[8,1152]{1,0:T(8,128)S(1)} %add.480), channel_id=1, source_target_pairs={{0,4},{2,6},{4,0},{6,2},{1,5},{3,7},{5,1},{7,3},{8,12},{10,14},{12... | collective-permute-start | bytes 110600 | tf_op jit(solution)/shard_map/ppermute | solution.py:61
  616.0 36.9 %collective-permute-start.50 = (f32[8,1152]{1,0:T(8,128)S(1)}, f32[8,1152]{1,0:T(8,128)S(1)}, u32[]{:S(2)}, u32[]{:S(2)}) collective-permute-start(f32[8,1152]{1,0:T(8,128)S(1)} %add.480), channel_id=1, source_target_pairs={{0,2},{2,4},{4,6},{6,0},{1,3},{3,5},{5,7},{7,1},{8,10},{10,12},{12... | collective-permute-start | bytes 110600 | tf_op jit(solution)/shard_map/ppermute | solution.py:61
  647.1 65.8 %collective-permute-start.38 = (bf16[256,1152]{1,0:T(8,128)(2,1)S(1)}, bf16[256,1152]{1,0:T(8,128)(2,1)}, u32[]{:S(2)}, u32[]{:S(2)}) collective-permute-start(bf16[256,1152]{1,0:T(8,128)(2,1)S(1)} %copy-done.35), channel_id=1, source_target_pairs={{0,48},{16,0},{32,16},{48,32},{1,49},{17,1},{33,17},{49,33},{2,50}... | collective-permute-start | bytes 1769480 | tf_op jit(solution)/shard_map/ppermute | solution.py:61
  652.9 40.1 %collective-permute-start.62 = (bf16[112,1152]{1,0:T(8,128)(2,1)S(1)}, bf16[112,1152]{1,0:T(8,128)(2,1)S(1)}, u32[]{:S(2)}, u32[]{:S(2)}) collective-permute-start(bf16[112,1152]{1,0:T(8,128)(2,1)S(1)} %add.497.refs_0_), channel_id=1, source_target_pairs={{0,16},{16,32},{32,48},{48,0},{1,17},{17,33},{33,49},{49,1},{2,18}... | collective-permute-start | bytes 774152 | tf_op jit(solution)/shard_map/ppermute | solution.py:61
  652.9 40.8 %collective-permute-start.63 = (bf16[112,1152]{1,0:T(8,128)(2,1)S(1)}, bf16[112,1152]{1,0:T(8,128)(2,1)S(1)}, u32[]{:S(2)}, u32[]{:S(2)}) collective-permute-start(bf16[112,1152]{1,0:T(8,128)(2,1)S(1)} %add.497.refs_0_), channel_id=1, source_target_pairs={{0,32},{16,48},{32,0},{48,16},{1,33},{17,49},{33,1},{49,17},{2,34}... | collective-permute-start | bytes 774152 | tf_op jit(solution)/shard_map/ppermute | solution.py:61
  662.2 52.1 %collective-permute-start.67 = (bf16[144,1152]{1,0:T(8,128)(2,1)S(1)}, bf16[144,1152]{1,0:T(8,128)(2,1)S(1)}, u32[]{:S(2)}, u32[]{:S(2)}) collective-permute-start(bf16[144,1152]{1,0:T(8,128)(2,1)S(1)} %add.498.refs_0_), channel_id=1, source_target_pairs={{0,16},{16,32},{32,48},{48,0},{1,17},{17,33},{33,49},{49,1},{2,18}... | collective-permute-start | bytes 995336 | tf_op jit(solution)/shard_map/ppermute | solution.py:61
  664.3 51.0 %collective-permute-start.68 = (bf16[144,1152]{1,0:T(8,128)(2,1)S(1)}, bf16[144,1152]{1,0:T(8,128)(2,1)}, u32[]{:S(2)}, u32[]{:S(2)}) collective-permute-start(bf16[144,1152]{1,0:T(8,128)(2,1)S(1)} %add.498.refs_0_), channel_id=1, source_target_pairs={{0,32},{16,48},{32,0},{48,16},{1,33},{17,49},{33,1},{49,17},{2,34}... | collective-permute-start | bytes 995336 | tf_op jit(solution)/shard_map/ppermute | solution.py:61
  (130 other events, 1923.0 us)
Sparse Core Ops, SparseCore 0:
  10.6 75.5 all-gather.1
  119.6 39.3 reduce-scatter.5
  361.8 62.7 reduce-scatter.7
  530.5 21.3 reduce-scatter.9
  554.8 92.1 reduce-scatter.13
  650.1 42.9 reduce-scatter.11

commit v10 on v9

--- a/solution.py
+++ b/solution.py
@@ -871,8 +871,9 @@
     context_own = lax.psum_scatter(context_part, FS, scatter_dimension=0, tiled=True)
     head0, total0 = self_forward(0, seg_col, seg_row, after(qkv, context_part))
     head1, total1 = self_forward(1, seg_col, seg_row, after(qkv, head0))
-    quarter_minus, quarter_plus, head1 = lax.optimization_barrier(
-        (quarter_minus, quarter_plus, head1)
+    hidden_mine = every_peer(after(hidden_own, text_columns))
+    quarter_minus, quarter_plus, hidden_mine, head1 = lax.optimization_barrier(
+        (quarter_minus, quarter_plus, hidden_mine, head1)
     )
     quarter_far = (
         shift(halves(quarter_minus)[0], "z", 1),
@@ -891,7 +892,6 @@
     grad_mlp = grad_out.astype(bf16)
     grad_sent = after(grad_mlp, square_mine)
     mlp_minus, mlp_plus = shift(grad_sent, "z", 1), shift(grad_sent, "z", -1)
-    hidden_mine = every_peer(after(hidden_own, context))
 
     after_self, normed_two, cross_query = call(
         after_self_body,
@@ -1024,8 +1024,8 @@
     heads_part = peers_parts(heads_own)
     square_parts = reduce_third(square_chunk, s20, s11, s31)
     part, sums_one = first_part(after(grad_qkv, heads_own), heads_w, plain_all)
-    part, heads_part, kv_all, *square_parts = lax.optimization_barrier(
-        (part, heads_part, kv_all, *square_parts)
+    part, heads_part, kv_all, hidden_grad, *square_parts = lax.optimization_barrier(
+        (part, heads_part, kv_all, hidden_grad, *square_parts)
     )
     sent = peers_parts(part)
 

time: 775 us -> 744 us (0.960)
  waiting for transfers between devices: 244 us -> 210 us
  blocking collectives: 14 us -> 0 us
  starting transfers between devices: 126 us -> 135 us
    ppermute x71, waiting for transfers between devices: 80.9 us -> 134 us  [shift(): return lax.ppermute(x, axis, [(i, (i + by) % n) for i in range(n)])]
    all_to_all x3, waiting for transfers between devices: 76.8 us -> 46.4 us  [peers_parts(): return lax.all_to_all(x, axes, 0, 0, tiled=True)]
    reduce_scatter x1, waiting for transfers between devices: 31.1 us -> 1.75 us  [local(): lax.psum_scatter(after(hidden_sum, kv_own), FS, scatter_dimension=0, tile...]
    reduce_scatter x1, waiting for transfers between devices: 28.8 us -> 0.01 us  [local(): early = lax.psum_scatter(early, 'z', scatter_dimension=0, tiled=True)]
    all_to_all x3, waiting for transfers between devices: 14.1 us -> 0.01 us  [every_peer(): return lax.all_to_all(copies, axes, 0, 0, tiled=True)]
    all_to_all x1 -> x0, blocking collectives: 14 us -> none  [local(): lax.all_to_all(jnp.concatenate([head0, head1], axis=1), FS, split_axis=0,...]
  transfers between devices with their start and end apart: 86 -> 87, of which waited for: 26 -> 34; matrix products, arithmetic and copies ran while one was open for 12% -> 13% of each run, Pallas kernels for 25% -> 23%
where the time goes in v10:
time: 744 us; the launch traced here: 734 us
  Pallas kernels  240 us (32%)
  waiting for transfers between devices  210 us (28%)
  starting transfers between devices  135 us (18%)
  local copies, waits for them, and re-layouts  64.4 us (9%)
  other arithmetic  51.3 us (7%)
  matrix products  18.2 us (2%)
  between operations  15.9 us (2%)
    ppermute x71, waiting for transfers between devices, shift(): return lax.ppermute(x, axis, [(i, (i + by) % n) for i in range(n)])  134 us
    ppermute x71, starting transfers between devices, shift(): return lax.ppermute(x, axis, [(i, (i + by) % n) for i in range(n)])  92.6 us
    pallas_call x7, Pallas kernels, call(): pl.pallas_call(body, in_specs=[pl.BlockSpec(memory_space=spaces[where]) f...  51.3 us
    all_to_all x3, waiting for transfers between devices, peers_parts(): return lax.all_to_all(x, axes, 0, 0, tiled=True)  46.4 us
    pallas_call x2, Pallas kernels, self_backward(): pl.pallas_call(functools.partial(self_backward_body, head), grid=(ROW //...  37.4 us
    pallas_call x3, Pallas kernels, mlp(): pl.pallas_call(functools.partial(mlp_body, parts, count), in_specs=[pl.Bl...  28.6 us
    pallas_call x2, Pallas kernels, self_forward(): pl.pallas_call(self_forward_body, grid=(ROW // TOK,), in_specs=[pl.BlockS...  24.3 us
    pallas_call x2, Pallas kernels, mlp_grad(): pl.pallas_call(functools.partial(mlp_grad_body, which), grid=(3,), in_spe...  17.6 us
  transfers between devices with their start and end apart: 87, of which 34 were waited for; matrix products, arithmetic and copies ran while one was open for 13% of the time, Pallas kernels for 23%

profile of v10, /device:TPU:1, one launch (start us, length us, event | category | flops | bytes accessed | tf_op | source)
XLA Modules:
  0.0 734.4 jit_solution(7133071049749500292)
XLA Ops:
  18.8 9.6 %collective-permute-done.refs_1_ = bf16[256,1152]{1,0:T(8,128)(2,1)} collective-permute-done((bf16[256,1152]{1,0:T(8,128)(2,1)S(1)}, bf16[256,1152]{1,0:T(8,128)(2,1)}, u32[]{:S(2)}, u32[]{:S(2)}) %collective-permute-start) | collective-permute-done | bytes 589856 | tf_op jit(solution)/shard_map/ppermute | solution.py:61
  42.6 8.6 %collective-permute-done.3.refs_4_ = bf16[256,1152]{1,0:T(8,128)(2,1)S(1)} collective-permute-done((bf16[256,1152]{1,0:T(8,128)(2,1)}, bf16[256,1152]{1,0:T(8,128)(2,1)S(1)}, u32[]{:S(2)}, u32[]{:S(2)}) %collective-permute-start.3) | collective-permute-done | bytes 589856 | tf_op jit(solution)/shard_map/ppermute | solution.py:61
  51.3 10.7 %collective-permute-done.5.refs_6_ = bf16[256,1152]{1,0:T(8,128)(2,1)S(1)} collective-permute-done((bf16[256,1152]{1,0:T(8,128)(2,1)}, bf16[256,1152]{1,0:T(8,128)(2,1)S(1)}, u32[]{:S(2)}, u32[]{:S(2)}) %collective-permute-start.5) | collective-permute-done | bytes 589856 | tf_op jit(solution)/shard_map/ppermute | solution.py:61
  66.0 21.1 %all-to-all-done = bf16[8,144,432]{2,1,0:T(8,128)(2,1)S(1)} async-done(((bf16[8,144,432]{2,1,0:T(8,128)(2,1)}), bf16[8,144,432]{2,1,0:T(8,128)(2,1)S(1)}, u32[]{:S(2)}, u32[]{:S(2)}) %all-to-all-start) | async-done | bytes 995360 | tf_op jit(solution)/shard_map/all_to_all | solution.py:122
  126.3 12.1 %shard_map.377 = (bf16[2048,72]{1,0:T(8,128)(2,1)}, f32[1,2048]{1,0:T(1,128)}) custom-call(s32[2048,1]{1,0:T(8,128)} %copy.114.seg_q.seg_k, s32[1,2048]{1,0:T(1,128)} %bitcast.89, bf16[2048,768]{1,0:T(8,128)(2,1)} %convolution_convert_fusion.q.kv, bf16[2048,768]{1,0:T(8,128)(2,1)} %convolution_convert_fusion.q.kv), custom_call_target="tpu_custom_call" | custom-call | tf_op jit(solution)/shard_map/pallas_call | solution.py:283
  138.4 12.1 %shard_map.378 = (bf16[2048,72]{1,0:T(8,128)(2,1)}, f32[1,2048]{1,0:T(1,128)}) custom-call(s32[2048,1]{1,0:T(8,128)} %copy.114.seg_q.seg_k, s32[1,2048]{1,0:T(1,128)} %bitcast.90, bf16[2048,768]{1,0:T(8,128)(2,1)} %convolution_convert_fusion.q.kv, bf16[2048,768]{1,0:T(8,128)(2,1)} %convolution_convert_fusion.q.kv), custom_call_target="tpu_custom_call" | custom-call | tf_op jit(solution)/shard_map/pallas_call | solution.py:283
  220.0 8.4 %shard_map.381 = (bf16[512,1152]{1,0:T(8,128)(2,1)}, bf16[512,1152]{1,0:T(8,128)(2,1)}) custom-call(s32[1]{0:T(128)} %bitcast.core, bf16[512,1152]{1,0:T(8,128)(2,1)} %bitcast.28.context, bf16[1152,3072]{1,0:T(8,128)(2,1)} %shard_map.379.mine, bf16[1152,3072]{1,0:T(8,128)(2,1)} %collective-permute-done.12.other), custom_call_target="tpu_custom_call" | custom-call | tf_op jit(solution)/shard_map/pallas_call | solution.py:573
  228.4 11.7 %shard_map.382.mixed = bf16[256,1152]{1,0:T(8,128)(2,1)} custom-call(s32[256,1]{1,0:T(8,128)} %copy.118.cap_q, s32[1,512]{1,0:T(1,128)} %and_select_fusion.1.cap_t, bf16[256,1152]{1,0:T(8,128)(2,1)} %get-tuple-element.172.q, bf16[512,1152]{1,0:T(8,128)(2,1)} %get-tuple-element.176.k, bf16[512,1152]{1,0:T(8,128)(2,1)} %get-tuple-element.177.v), custom_call_target="tpu_custom_call" | custom-call | tf_op jit(solution)/shard_map/pallas_call | solution.py:374
  256.7 8.2 %shard_map.384 = (bf16[256,1152]{1,0:T(8,128)(2,1)}, bf16[256,1152]{1,0:T(8,128)(2,1)}, bf16[256,1152]{1,0:T(8,128)(2,1)}, bf16[256,1152]{1,0:T(8,128)(2,1)}) custom-call(s32[1]{0:T(128)} %bitcast.core, bf16[256,1152]{1,0:T(8,128)(2,1)} %get-tuple-element.179.refs_0_, bf16[256,1152]{1,0:T(8,128)(2,1)} %copy-done.2, bf16[1152,1152]{1,0:T(8,128)(2,1)} %bitcast.62, ...), custom_call_target="tpu_custom_call" | custom-call | tf_op jit(solution)/shard_map/pallas_call | solution.py:480
  270.7 12.3 %shard_map.385 = (bf16[256,1152]{1,0:T(8,128)(2,1)}, bf16[256,1152]{1,0:T(8,128)(2,1)}, bf16[256,1152]{1,0:T(8,128)(2,1)}, bf16[256,1152]{1,0:T(8,128)(2,1)}, bf...) custom-call(s32[1]{0:T(128)} %bitcast.core, ...), custom_call_target="tpu_custom_call" | custom-call | tf_op jit(solution)/shard_map/pallas_call | solution.py:480
  283.8 8.2 %shard_map.386 = (bf16[256,1152]{1,0:T(8,128)(2,1)}, bf16[256,1152]{1,0:T(8,128)(2,1)}, bf16[256,1152]{1,0:T(8,128)(2,1)}, bf16[256,1152]{1,0:T(8,128)(2,1)}) custom-call(s32[1]{0:T(128)} %bitcast.core, bf16[128,1152]{1,0:T(8,128)(2,1)} %copy-done.27, bf16[128,1152]{1,0:T(8,128)(2,1)} %copy-done.29, bf16[128,1152]{1,0:T(8,128)(2,1)} %copy-done.25, ...), custom_call_target="tpu_custom_call" | custom-call | tf_op jit(solution)/shard_map/pallas_call | solution.py:480
  296.6 8.7 %shard_map.387 = bf16[1152,1152]{1,0:T(8,128)(2,1)} custom-call(s32[1]{0:T(128)} %bitcast.core, bf16[256,1152]{1,0:T(8,128)(2,1)} %get-tuple-element.179.refs_0_, bf16[256,1152]{1,0:T(8,128)(2,1)} %copy-done.4, bf16[256,1152]{1,0:T(8,128)(2,1)} %collective-permute-done.16.refs_1_.refs_2_, bf16[256,1152]{1,0:T(8,128)(2,1)} %copy-done.12, ...), custom_call_target="tpu_custom_call" | custom-call | tf_op jit(solution)/shard_map/pallas_call | solution.py:514
  314.5 8.9 %shard_map.388 = bf16[1152,1152]{1,0:T(8,128)(2,1)} custom-call(s32[1]{0:T(128)} %bitcast.core, bf16[256,1152]{1,0:T(8,128)(2,1)} %get-tuple-element.179.refs_0_, bf16[256,1152]{1,0:T(8,128)(2,1)} %copy-done.4, bf16[256,1152]{1,0:T(8,128)(2,1)} %collective-permute-done.16.refs_1_.refs_2_, bf16[256,1152]{1,0:T(8,128)(2,1)} %copy-done.12, ...), custom_call_target="tpu_custom_call" | custom-call | tf_op jit(solution)/shard_map/pallas_call | solution.py:514
  340.8 15.5 %shard_map.390 = (bf16[256,1152]{1,0:T(8,128)(2,1)}, bf16[512,2304]{1,0:T(8,128)(2,1)}) custom-call(s32[512,1]{1,0:T(8,128)} %fusion.36.cap_t, s32[1,256]{1,0:T(1,128)} %bitcast.96, bf16[256,1152]{1,0:T(8,128)(2,1)} %get-tuple-element.172.q, bf16[512,1152]{1,0:T(8,128)(2,1)} %get-tuple-element.176.k, bf16[512,1152]{1,0:T(8,128)(2,1)} %get-tuple-element.177.v, ...), custom_call_target="tpu_custom_call" | custom-call | tf_op jit(solution)/shard_map/pallas_call | solution.py:402
  387.9 8.1 %all-to-all-done.5 = bf16[256,8,144]{0,2,1:T(8,128)(2,1)S(1)} async-done(((bf16[256,8,144]{0,2,1:T(8,128)(2,1)}), bf16[256,8,144]{0,2,1:T(8,128)(2,1)S(1)}, u32[]{:S(2)}, u32[]{:S(2)}) %all-to-all-start.5) | async-done | bytes 589856 | tf_op jit(solution)/shard_map/all_to_all | solution.py:993
  397.2 18.8 %shard_map.392.refs_0_ = bf16[2048,768]{1,0:T(8,128)(2,1)} custom-call(s32[2048,1]{1,0:T(8,128)} %copy.114.seg_q.seg_k, s32[1,2048]{1,0:T(1,128)} %bitcast.91, f32[1,2048]{1,0:T(1,128)} %get-tuple-element.222.total, bf16[2048,768]{1,0:T(8,128)(2,1)} %convolution_convert_fusion.q.kv, bf16[2048,768]{1,0:T(8,128)(2,1)} %convolution_convert_fusion.q.kv, ...), custom_call_target="tpu_custom_call" | custom-call | tf_op jit(solution)/shard_map/pallas_call | solution.py:335
  436.6 18.6 %shard_map.393.g = bf16[2048,768]{1,0:T(8,128)(2,1)} custom-call(s32[2048,1]{1,0:T(8,128)} %copy.114.seg_q.seg_k, s32[1,2048]{1,0:T(1,128)} %bitcast.92, f32[1,2048]{1,0:T(1,128)} %get-tuple-element.230.total, bf16[2048,768]{1,0:T(8,128)(2,1)} %convolution_convert_fusion.q.kv, ...), custom_call_target="tpu_custom_call", output_to_operand_aliasing={{}: (6, {})} | custom-call | tf_op jit(solution)/shard_map/pallas_call | solution.py:335
  473.4 19.7 %collective-permute-done.40 = bf16[144,1920]{1,0:T(8,128)(2,1)S(1)} collective-permute-done((bf16[144,1920]{1,0:T(8,128)(2,1)S(1)}, bf16[144,1920]{1,0:T(8,128)(2,1)S(1)}, u32[]{:S(2)}, u32[]{:S(2)}) %collective-permute-start.40) | collective-permute-done | bytes 552992 | tf_op jit(solution)/shard_map/ppermute | solution.py:61
  505.6 10.8 %shard_map.395 = (bf16[2048,1152]{1,0:T(8,128)(2,1)}, f32[8,1152]{1,0:T(8,128)}) custom-call(bf16[2048,768]{1,0:T(8,128)(2,1)} %shard_map.393.g, bf16[1152,768]{1,0:T(8,128)(2,1)} %shard_map.376.w, bf16[2048,1152]{1,0:T(8,128)(2,1)} %get-tuple-element.240.plain), custom_call_target="tpu_custom_call" | custom-call | flops 12650000384 | tf_op jit(solution)/shard_map/pallas_call | solution.py:676
  516.4 12.5 %collective-permute-done.42 = bf16[144,1920]{1,0:T(8,128)(2,1)S(1)} collective-permute-done((bf16[144,1920]{1,0:T(8,128)(2,1)}, bf16[144,1920]{1,0:T(8,128)(2,1)S(1)}, u32[]{:S(2)}, u32[]{:S(2)}) %collective-permute-start.42) | collective-permute-done | bytes 552992 | tf_op jit(solution)/shard_map/ppermute | solution.py:61
  528.9 18.4 %collective-permute-done.43 = bf16[144,1920]{1,0:T(8,128)(2,1)S(1)} collective-permute-done((bf16[144,1920]{1,0:T(8,128)(2,1)}, bf16[144,1920]{1,0:T(8,128)(2,1)S(1)}, u32[]{:S(2)}, u32[]{:S(2)}) %collective-permute-start.43) | collective-permute-done | bytes 552992 | tf_op jit(solution)/shard_map/ppermute | solution.py:61
  549.9 11.0 %shard_map.396 = (bf16[512,512]{1,0:T(8,128)(2,1)}, bf16[512,1152]{1,0:T(8,128)(2,1)}, bf16[144,2304]{1,0:T(8,128)(2,1)}) custom-call(s32[1]{0:T(128)} %bitcast.core, bf16[512,2304]{1,0:T(8,128)(2,1)} %bitcast.67, bf16[512,144]{1,0:T(8,128)(2,1)} %constant_dynamic-slice_fusion.5.cols, bf16[512,512]{1,0:T(8,128)(2,1)} %bitcast.81, bf16[512,1152]{1,0:T(8,128)(2,1)} %w_text.1, ...), custom_call_target="tpu_custom_call" | custom-call | tf_op jit(solution)/shard_map/pallas_call | solution.py:573
  600.2 25.3 %all-to-all-done.8 = bf16[8,256,1152]{2,1,0:T(8,128)(2,1)} async-done(((bf16[8,256,1152]{2,1,0:T(8,128)(2,1)}), bf16[8,256,1152]{2,1,0:T(8,128)(2,1)}, u32[]{:S(2)}, u32[]{:S(2)}) %all-to-all-start.8) | async-done | bytes 4718624 | tf_op jit(solution)/shard_map/all_to_all | solution.py:122
  656.7 10.2 %collective-permute-done.64.refs_3_ = bf16[112,1152]{1,0:T(8,128)(2,1)S(1)} collective-permute-done((bf16[112,1152]{1,0:T(8,128)(2,1)S(1)}, bf16[112,1152]{1,0:T(8,128)(2,1)S(1)}, u32[]{:S(2)}, u32[]{:S(2)}) %collective-permute-start.64) | collective-permute-done | bytes 258080 | tf_op jit(solution)/shard_map/ppermute | solution.py:61
  (468 shorter events, 409.1 us)
Async XLA Ops:
  7.2 92.0 %all-gather.2.cloned.1.call-start = ((), (), s32[]{:S(2)}) async-start(), calls=%async_computation.15 | async-start | bytes 1990656 | tf_op jit(solution)/shard_map/all_gather | solution.py:830
  35.4 51.7 %all-to-all-start = ((bf16[8,144,432]{2,1,0:T(8,128)(2,1)}), bf16[8,144,432]{2,1,0:T(8,128)(2,1)S(1)}, u32[]{:S(2)}, u32[]{:S(2)}) async-start(bf16[8,144,432]{2,1,0:T(8,128)(2,1)} %bitcast.72), calls=%async_computation | async-start | bytes 2359296 | tf_op jit(solution)/shard_map/all_to_all | solution.py:122
  113.6 44.9 %all-to-all-start.2 = ((bf16[8,144,1152]{2,1,0:T(8,128)(2,1)}), bf16[8,144,1152]{2,1,0:T(8,128)(2,1)S(1)}, u32[]{:S(2)}, u32[]{:S(2)}) async-start(bf16[8,144,1152]{2,1,0:T(8,128)(2,1)} %broadcast_in_dim.121), calls=%async_computation.2 | async-start | bytes 5308416 | tf_op jit(solution)/shard_map/all_to_all | solution.py:118
  118.4 56.6 %reduce-scatter.6.cloned.1.call-start = ((), (), s32[]{:S(2)}) async-start(), calls=%async_computation.16 | async-start | bytes 1327104 | tf_op jit(solution)/shard_map/reduce_scatter | solution.py:871
  118.4 39.5 %collective-permute-start.8 = (bf16[1152,768]{1,0:T(8,128)(2,1)}, bf16[1152,768]{1,0:T(8,128)(2,1)}, u32[]{:S(2)}, u32[]{:S(2)}) collective-permute-start(bf16[1152,768]{1,0:T(8,128)(2,1)} %all-gather.2.cloned.1.call-done.own), channel_id=1, source_target_pairs={{0,16},{16,32},{32,48},{48,0},{1,17},{17,33},{33,49},{49,1},{2,18}... | collective-permute-start | bytes 5308424 | tf_op jit(solution)/shard_map/ppermute | solution.py:61
  120.1 38.3 %collective-permute-start.9 = (bf16[1152,768]{1,0:T(8,128)(2,1)}, bf16[1152,768]{1,0:T(8,128)(2,1)}, u32[]{:S(2)}, u32[]{:S(2)}) collective-permute-start(bf16[1152,768]{1,0:T(8,128)(2,1)} %all-gather.2.cloned.1.call-done.own), channel_id=1, source_target_pairs={{0,48},{16,0},{32,16},{48,32},{1,49},{17,1},{33,17},{49,33},{2,50}... | collective-permute-start | bytes 5308424 | tf_op jit(solution)/shard_map/ppermute | solution.py:61
  202.1 217.5 %reduce-scatter.8.cloned.1.call-start = ((), (), s32[]{:S(2)}) async-start(), calls=%async_computation.17 | async-start | bytes 2654208 | tf_op jit(solution)/shard_map/reduce_scatter | solution.py:982
  421.2 37.9 %collective-permute-start.33 = (bf16[80,1920]{1,0:T(8,128)(2,1)}, bf16[80,1920]{1,0:T(8,128)(2,1)}, u32[]{:S(2)}, u32[]{:S(2)}) collective-permute-start(bf16[80,1920]{1,0:T(8,128)(2,1)} %constant_dynamic-slice_fusion), channel_id=1, source_target_pairs={{0,2},{2,4},{4,6},{6,0},{1,3},{3,5},{5,7},{7,1},{8,10},{10,12},{12... | collective-permute-start | bytes 921608 | tf_op jit(solution)/shard_map/ppermute | solution.py:61
  422.3 32.9 %collective-permute-start.36 = (bf16[128,1152]{1,0:T(8,128)(2,1)}, bf16[128,1152]{1,0:T(8,128)(2,1)}, u32[]{:S(2)}, u32[]{:S(2)}) collective-permute-start(bf16[128,1152]{1,0:T(8,128)(2,1)} %get-tuple-element.370), channel_id=1, source_target_pairs={{0,48},{16,0},{32,16},{48,32},{1,49},{17,1},{33,17},{49,33},{2,50}... | collective-permute-start | bytes 884744 | tf_op jit(solution)/shard_map/ppermute | solution.py:61
  426.7 32.5 %collective-permute-start.34 = (bf16[64,1920]{1,0:T(8,128)(2,1)}, bf16[64,1920]{1,0:T(8,128)(2,1)}, u32[]{:S(2)}, u32[]{:S(2)}) collective-permute-start(bf16[64,1920]{1,0:T(8,128)(2,1)} %constant_dynamic-slice_fusion.9), channel_id=1, source_target_pairs={{0,6},{2,0},{4,2},{6,4},{1,7},{3,1},{5,3},{7,5},{8,14},{10,8},{12,... | collective-permute-start | bytes 737288 | tf_op jit(solution)/shard_map/ppermute | solution.py:61
  432.1 61.0 %all-to-all-start.6 = ((bf16[8,64,2304]{2,1,0:T(8,128)(2,1)}), bf16[8,64,2304]{2,1,0:T(8,128)(2,1)S(1)}, u32[]{:S(2)}, u32[]{:S(2)}) async-start(bf16[8,64,2304]{2,1,0:T(8,128)(2,1)} %broadcast_in_dim.137), calls=%async_computation.8 | async-start | bytes 4718592 | tf_op jit(solution)/shard_map/all_to_all | solution.py:118
  436.0 113.9 %reduce-scatter.10.cloned.1.call-start = ((), (), s32[]{:S(2)}) async-start(), calls=%async_computation.18 | async-start | bytes 2985984 | tf_op jit(solution)/shard_map/reduce_scatter | solution.py:1012
  461.7 31.4 %collective-permute-start.40 = (bf16[144,1920]{1,0:T(8,128)(2,1)S(1)}, bf16[144,1920]{1,0:T(8,128)(2,1)S(1)}, u32[]{:S(2)}, u32[]{:S(2)}) collective-permute-start(bf16[144,1920]{1,0:T(8,128)(2,1)S(1)} %pad_maximum_fusion.11), channel_id=1, source_target_pairs={{0,1},{1,0},{2,3},{3,2},{4,5},{5,4},{6,7},{7,6},{8,9},{9,8},{10,11... | collective-permute-start | bytes 1658888 | tf_op jit(solution)/shard_map/ppermute | solution.py:61
  463.2 29.9 %collective-permute-start.41 = (bf16[144,1920]{1,0:T(8,128)(2,1)S(1)}, bf16[144,1920]{1,0:T(8,128)(2,1)}, u32[]{:S(2)}, u32[]{:S(2)}) collective-permute-start(bf16[144,1920]{1,0:T(8,128)(2,1)S(1)} %pad_maximum_fusion.12), channel_id=1, source_target_pairs={{0,6},{2,0},{4,2},{6,4},{1,7},{3,1},{5,3},{7,5},{8,14},{10,8},{12,... | collective-permute-start | bytes 1658888 | tf_op jit(solution)/shard_map/ppermute | solution.py:61
  493.9 54.2 %all-to-all-start.7 = ((bf16[8,144,432]{2,1,0:T(8,128)(2,1)}), bf16[8,144,432]{2,1,0:T(8,128)(2,1)S(1)}, u32[]{:S(2)}, u32[]{:S(2)}) async-start(bf16[8,144,432]{2,1,0:T(8,128)(2,1)} %bitcast.85), calls=%async_computation.9 | async-start | bytes 2359296 | tf_op jit(solution)/shard_map/all_to_all | solution.py:122
  502.7 44.5 %collective-permute-start.43 = (bf16[144,1920]{1,0:T(8,128)(2,1)}, bf16[144,1920]{1,0:T(8,128)(2,1)S(1)}, u32[]{:S(2)}, u32[]{:S(2)}) collective-permute-start(bf16[144,1920]{1,0:T(8,128)(2,1)} %get-tuple-element.337), channel_id=1, source_target_pairs={{0,1},{1,0},{2,3},{3,2},{4,5},{5,4},{6,7},{7,6},{8,9},{9,8},{10,11... | collective-permute-start | bytes 1658888 | tf_op jit(solution)/shard_map/ppermute | solution.py:61
  503.9 44.2 %collective-permute-start.44 = (bf16[144,1920]{1,0:T(8,128)(2,1)}, bf16[144,1920]{1,0:T(8,128)(2,1)S(1)}, u32[]{:S(2)}, u32[]{:S(2)}) collective-permute-start(bf16[144,1920]{1,0:T(8,128)(2,1)} %get-tuple-element.336), channel_id=1, source_target_pairs={{0,6},{2,0},{4,2},{6,4},{1,7},{3,1},{5,3},{7,5},{8,14},{10,8},{12,... | collective-permute-start | bytes 1658888 | tf_op jit(solution)/shard_map/ppermute | solution.py:61
  565.7 59.8 %all-to-all-start.8 = ((bf16[8,256,1152]{2,1,0:T(8,128)(2,1)}), bf16[8,256,1152]{2,1,0:T(8,128)(2,1)}, u32[]{:S(2)}, u32[]{:S(2)}) async-start(bf16[8,256,1152]{2,1,0:T(8,128)(2,1)} %bitcast.71), calls=%async_computation.11 | async-start | bytes 9437184 | tf_op jit(solution)/shard_map/all_to_all | solution.py:122
  570.3 29.9 %reduce-scatter.12.cloned.1.call-start = ((), (), s32[]{:S(2)}) async-start(), calls=%async_computation.19 | async-start | bytes 1290240 | tf_op jit(solution)/shard_map/reduce_scatter | solution.py:1063
  575.7 75.1 %reduce-scatter.14.cloned.1.call-start = ((), (), s32[]{:S(2)}) async-start(), calls=%async_computation.20 | async-start | bytes 1556480 | tf_op jit(solution)/shard_map/reduce_scatter | solution.py:1041
  634.2 44.9 %collective-permute-start.38 = (bf16[256,1152]{1,0:T(8,128)(2,1)S(1)}, bf16[256,1152]{1,0:T(8,128)(2,1)}, u32[]{:S(2)}, u32[]{:S(2)}) collective-permute-start(bf16[256,1152]{1,0:T(8,128)(2,1)S(1)} %copy-done.35), channel_id=1, source_target_pairs={{0,48},{16,0},{32,16},{48,32},{1,49},{17,1},{33,17},{49,33},{2,50}... | collective-permute-start | bytes 1769480 | tf_op jit(solution)/shard_map/ppermute | solution.py:61
  647.6 34.8 %collective-permute-start.67 = (bf16[144,1152]{1,0:T(8,128)(2,1)S(1)}, bf16[144,1152]{1,0:T(8,128)(2,1)S(1)}, u32[]{:S(2)}, u32[]{:S(2)}) collective-permute-start(bf16[144,1152]{1,0:T(8,128)(2,1)S(1)} %add.498.refs_0_), channel_id=1, source_target_pairs={{0,16},{16,32},{32,48},{48,0},{1,17},{17,33},{33,49},{49,1},{2,18}... | collective-permute-start | bytes 995336 | tf_op jit(solution)/shard_map/ppermute | solution.py:61
  650.8 32.9 %collective-permute-start.68 = (bf16[144,1152]{1,0:T(8,128)(2,1)S(1)}, bf16[144,1152]{1,0:T(8,128)(2,1)}, u32[]{:S(2)}, u32[]{:S(2)}) collective-permute-start(bf16[144,1152]{1,0:T(8,128)(2,1)S(1)} %add.498.refs_0_), channel_id=1, source_target_pairs={{0,32},{16,48},{32,0},{48,16},{1,33},{17,49},{33,1},{49,17},{2,34}... | collective-permute-start | bytes 995336 | tf_op jit(solution)/shard_map/ppermute | solution.py:61
  671.6 37.0 %collective-permute-start.65 = (bf16[448,1152]{1,0:T(8,128)(2,1)}, bf16[448,1152]{1,0:T(8,128)(2,1)}, u32[]{:S(2)}, u32[]{:S(2)}) collective-permute-start(bf16[448,1152]{1,0:T(8,128)(2,1)} %shard_map.400), channel_id=1, source_target_pairs={{0,8},{8,0},{1,9},{9,1},{2,10},{10,2},{3,11},{11,3},{4,12},{12,4},... | collective-permute-start | bytes 3096584 | tf_op jit(solution)/shard_map/ppermute | solution.py:61
  (139 other events, 1894.1 us)
Sparse Core Ops, SparseCore 0:
  10.6 75.6 all-gather.1
  124.8 50.2 reduce-scatter.5
  356.5 63.0 reduce-scatter.7
  439.5 110.3 reduce-scatter.9
  575.8 24.3 reduce-scatter.11
  603.2 24.1 reduce-scatter.13

commit v11 on v10

--- a/solution.py
+++ b/solution.py
@@ -960,6 +960,7 @@
     )
     back_minus, back_plus, keep = lax.optimization_barrier((back_minus, back_plus, keep))
     hidden_sum = keep + shift(send, "c", 1)
+    hidden_grad = lax.psum_scatter(hidden_sum, FS, scatter_dimension=0, tiled=True)
     grad_after_cross, grad_cross_branch, grad_cross_mixed, sums_three = call(
         third_back_body,
         [
@@ -979,7 +980,6 @@
         cross_value,
         grad_cross_mixed,
     )
-    kv_own = lax.psum_scatter(grad_kv, FS, scatter_dimension=0, tiled=True)
     grad_after_self, grad_self_branch, grad_attended, sums_two = call(
         second_back_body,
         [
@@ -1006,41 +1006,47 @@
 
     grad_heads, square = lax.optimization_barrier((grad_heads, square))
     grad_qkv = self_backward(0, seg_col, seg_row, total0, qkv, grad_heads)
-    kv_own, square, grad_qkv = lax.optimization_barrier((kv_own, square, grad_qkv))
+    square, hidden_grad, grad_kv, grad_qkv = lax.optimization_barrier(
+        (square, hidden_grad, grad_kv, grad_qkv)
+    )
+    kv_own = lax.psum_scatter(grad_kv, FS, scatter_dimension=0, tiled=True)
     s_lo, s_hi, s20 = reduce_first(square_chunk)
-    kv_all = every_peer(kv_own)
-    hidden_grad = lax.psum_scatter(after(hidden_sum, kv_own), FS, scatter_dimension=0, tiled=True)
+    hidden_grad = hidden_grad + shift(hidden_grad, "xh", 1)
     out_minus, out_plus = reduce_z(after(out_far, grad_qkv), out_m, out_p)
-    grad_qkv = self_backward(
-        1, seg_col, seg_row, total1, qkv, after(grad_heads, kv_own), (grad_qkv,)
-    )
+    grad_qkv = self_backward(1, seg_col, seg_row, total1, qkv, grad_heads, (grad_qkv,))
     s_lo, s_hi, s20, out_minus, out_plus, grad_qkv = lax.optimization_barrier(
         (s_lo, s_hi, s20, out_minus, out_plus, grad_qkv)
     )
     s11, s31 = reduce_second(square_chunk, s_lo, s_hi)
 
     heads_own = heads_grad(normed_all, grad_qkv)
-    heads_own, s11, s31, kv_all = lax.optimization_barrier((heads_own, s11, s31, kv_all))
+    heads_own, kv_own = lax.optimization_barrier((heads_own, kv_own))
     heads_part = peers_parts(heads_own)
+    kv_all = lax.all_gather(kv_own, FS, axis=0, tiled=True)
+    part, sums_one = first_part(after(grad_qkv, heads_own), heads_w, plain_all)
+    part, heads_part, s11, s31, hidden_grad = lax.optimization_barrier(
+        (part, heads_part, s11, s31, hidden_grad)
+    )
+    sent = peers_parts(part)
+
     square_parts = reduce_third(square_chunk, s20, s11, s31)
-    part, sums_one = first_part(after(grad_qkv, heads_own), heads_w, plain_all)
-    part, heads_part, kv_all, hidden_grad, *square_parts = lax.optimization_barrier(
-        (part, heads_part, kv_all, hidden_grad, *square_parts)
-    )
-    sent = peers_parts(part)
-
-    square = reduce_last(square_chunk, *square_parts).astype(bf16)
+    hidden_z = neighbours(after(hidden_grad, part))
     heads_rows = unpack_heads(heads_part)
     early = row_block(heads_rows, core, 216) + shift(row_block(heads_rows, 1 - core, 216), "c", 1)
-    early = jnp.concatenate([early, jnp.zeros((256 - 216, D), bf16)], axis=0)
+    norms = jnp.concatenate([sums_one[:2], sums_two[:2], sums_three[:2], jnp.zeros((2, D), f32)])
+    norms = sum_over(norms, "z", "c")
+    part, early, norms, kv_all, *rest = lax.optimization_barrier(
+        (sent, early, norms, kv_all, *square_parts, *hidden_z)
+    )
+    square_parts, hidden_z = rest[:3], rest[3:]
+
+    square = reduce_last(square_chunk, *square_parts).astype(bf16)
     square = jnp.concatenate([square[:, WIN * k : WIN * (k + 1)] for k in range(3)], axis=0)
     square = jnp.concatenate([square[:216], square[216:]], axis=1)
-    early = jnp.concatenate(
-        [early, jnp.concatenate([square, jnp.zeros((256 - 216, 2 * WIN), bf16)], axis=0)], axis=1
-    )
+    early = jnp.concatenate([early, square], axis=1)
+    early = jnp.concatenate([early, jnp.zeros((256 - 216, D + 2 * WIN), bf16)], axis=0)
     early = lax.psum_scatter(early, "z", scatter_dimension=0, tiled=True)
-    norms = jnp.concatenate([sums_one[:2], sums_two[:2], sums_three[:2], jnp.zeros((2, D), f32)])
-    norms = sum_over(norms, "z", "c")
+    early = early + shift(early, "xh", 1)
     own_columns = lax.dynamic_slice_in_dim(context, peer(0, 0) * SHARD, SHARD, axis=1)
     text_part, grad_w_text, grad_w_kv = call(
         text_back_body,
@@ -1061,12 +1067,7 @@
 
     late = half(core) + shift(half(1 - core), "c", 1)
     late = lax.psum_scatter(late, "z", scatter_dimension=0, tiled=True)
-    hidden_grad = after(hidden_grad, part)
-    hidden_grad = hidden_grad + shift(hidden_grad, "xh", 1)
-    part, norms, late = lax.optimization_barrier((sent, norms, late))
-    early = after(early, part)
-    early = early + shift(early, "xh", 1)
-    hidden_grad = in_order(*neighbours(after(hidden_grad, part)))
+    hidden_grad = in_order(*hidden_z)
     grad_w_up, grad_w_down = sort_hidden(core_index, hidden_grad, shift(hidden_grad, "c", 1))
 
     norms = sum_over(norms, "y", "xl", "xh")

time: 744 us -> 763 us (1.026)
  waiting for transfers between devices: 210 us -> 233 us
  other arithmetic: 51.3 us -> 41.1 us
    ppermute x71, waiting for transfers between devices: 134 us -> 166 us  [shift(): return lax.ppermute(x, axis, [(i, (i + by) % n) for i in range(n)])]
    all_to_all x3, waiting for transfers between devices: 46.4 us -> 25.4 us  [peers_parts(): return lax.all_to_all(x, axes, 0, 0, tiled=True)]
    reduce_scatter x1, waiting for transfers between devices: 3.54 us -> 17 us  [local(): kv_own = lax.psum_scatter(grad_kv, FS, scatter_dimension=0, tiled=True)]
    ppermute x71, starting transfers between devices: 92.6 us -> 102 us  [shift(): return lax.ppermute(x, axis, [(i, (i + by) % n) for i in range(n)])]
  transfers between devices with their start and end apart: 87 -> 87, of which waited for: 34 -> 35; matrix products, arithmetic and copies ran while one was open for 13% -> 12% of each run, Pallas kernels for 23% -> 27%
where the time goes in v11:
time: 763 us; the launch traced here: 753 us
  Pallas kernels  240 us (31%)
  waiting for transfers between devices  233 us (31%)
  starting transfers between devices  141 us (18%)
  local copies, waits for them, and re-layouts  63.8 us (8%)
  other arithmetic  41.1 us (5%)
  matrix products  18.2 us (2%)
  between operations  15.6 us (2%)
    ppermute x71, waiting for transfers between devices, shift(): return lax.ppermute(x, axis, [(i, (i + by) % n) for i in range(n)])  166 us
    ppermute x71, starting transfers between devices, shift(): return lax.ppermute(x, axis, [(i, (i + by) % n) for i in range(n)])  102 us
    pallas_call x7, Pallas kernels, call(): pl.pallas_call(body, in_specs=[pl.BlockSpec(memory_space=spaces[where]) f...  51.5 us
    pallas_call x2, Pallas kernels, self_backward(): pl.pallas_call(functools.partial(self_backward_body, head), grid=(ROW //...  37.5 us
    pallas_call x3, Pallas kernels, mlp(): pl.pallas_call(functools.partial(mlp_body, parts, count), in_specs=[pl.Bl...  28.5 us
    all_to_all x3, waiting for transfers between devices, peers_parts(): return lax.all_to_all(x, axes, 0, 0, tiled=True)  25.4 us
    pallas_call x2, Pallas kernels, self_forward(): pl.pallas_call(self_forward_body, grid=(ROW // TOK,), in_specs=[pl.BlockS...  24.3 us
    pallas_call x2, Pallas kernels, mlp_grad(): pl.pallas_call(functools.partial(mlp_grad_body, which), grid=(3,), in_spe...  17.4 us
  transfers between devices with their start and end apart: 87, of which 35 were waited for; matrix products, arithmetic and copies ran while one was open for 12% of the time, Pallas kernels for 27%

profile of v11, /device:TPU:1, one launch (start us, length us, event | category | flops | bytes accessed | tf_op | source)
XLA Modules:
  0.0 752.8 jit_solution(6794236508040034442)
XLA Ops:
  18.8 9.6 %collective-permute-done.refs_1_ = bf16[256,1152]{1,0:T(8,128)(2,1)} collective-permute-done((bf16[256,1152]{1,0:T(8,128)(2,1)S(1)}, bf16[256,1152]{1,0:T(8,128)(2,1)}, u32[]{:S(2)}, u32[]{:S(2)}) %collective-permute-start) | collective-permute-done | bytes 589856 | tf_op jit(solution)/shard_map/ppermute | solution.py:61
  42.6 8.6 %collective-permute-done.3.refs_4_ = bf16[256,1152]{1,0:T(8,128)(2,1)S(1)} collective-permute-done((bf16[256,1152]{1,0:T(8,128)(2,1)}, bf16[256,1152]{1,0:T(8,128)(2,1)S(1)}, u32[]{:S(2)}, u32[]{:S(2)}) %collective-permute-start.3) | collective-permute-done | bytes 589856 | tf_op jit(solution)/shard_map/ppermute | solution.py:61
  51.3 10.7 %collective-permute-done.5.refs_6_ = bf16[256,1152]{1,0:T(8,128)(2,1)S(1)} collective-permute-done((bf16[256,1152]{1,0:T(8,128)(2,1)}, bf16[256,1152]{1,0:T(8,128)(2,1)S(1)}, u32[]{:S(2)}, u32[]{:S(2)}) %collective-permute-start.5) | collective-permute-done | bytes 589856 | tf_op jit(solution)/shard_map/ppermute | solution.py:61
  66.0 21.1 %all-to-all-done = bf16[8,144,432]{2,1,0:T(8,128)(2,1)S(1)} async-done(((bf16[8,144,432]{2,1,0:T(8,128)(2,1)}), bf16[8,144,432]{2,1,0:T(8,128)(2,1)S(1)}, u32[]{:S(2)}, u32[]{:S(2)}) %all-to-all-start) | async-done | bytes 995360 | tf_op jit(solution)/shard_map/all_to_all | solution.py:122
  126.4 12.1 %shard_map.377 = (bf16[2048,72]{1,0:T(8,128)(2,1)}, f32[1,2048]{1,0:T(1,128)}) custom-call(s32[2048,1]{1,0:T(8,128)} %copy.114.seg_q.seg_k, s32[1,2048]{1,0:T(1,128)} %bitcast.86, bf16[2048,768]{1,0:T(8,128)(2,1)} %convolution_convert_fusion.q.kv, bf16[2048,768]{1,0:T(8,128)(2,1)} %convolution_convert_fusion.q.kv), custom_call_target="tpu_custom_call" | custom-call | tf_op jit(solution)/shard_map/pallas_call | solution.py:283
  138.5 12.2 %shard_map.378 = (bf16[2048,72]{1,0:T(8,128)(2,1)}, f32[1,2048]{1,0:T(1,128)}) custom-call(s32[2048,1]{1,0:T(8,128)} %copy.114.seg_q.seg_k, s32[1,2048]{1,0:T(1,128)} %bitcast.87, bf16[2048,768]{1,0:T(8,128)(2,1)} %convolution_convert_fusion.q.kv, bf16[2048,768]{1,0:T(8,128)(2,1)} %convolution_convert_fusion.q.kv), custom_call_target="tpu_custom_call" | custom-call | tf_op jit(solution)/shard_map/pallas_call | solution.py:283
  220.2 8.4 %shard_map.381 = (bf16[512,1152]{1,0:T(8,128)(2,1)}, bf16[512,1152]{1,0:T(8,128)(2,1)}) custom-call(s32[1]{0:T(128)} %bitcast.core, bf16[512,1152]{1,0:T(8,128)(2,1)} %bitcast.28.context, bf16[1152,3072]{1,0:T(8,128)(2,1)} %shard_map.379.mine, bf16[1152,3072]{1,0:T(8,128)(2,1)} %collective-permute-done.12.other), custom_call_target="tpu_custom_call" | custom-call | tf_op jit(solution)/shard_map/pallas_call | solution.py:573
  228.7 11.7 %shard_map.382.mixed = bf16[256,1152]{1,0:T(8,128)(2,1)} custom-call(s32[256,1]{1,0:T(8,128)} %copy.118.cap_q, s32[1,512]{1,0:T(1,128)} %and_select_fusion.1.cap_t, bf16[256,1152]{1,0:T(8,128)(2,1)} %get-tuple-element.173.q, bf16[512,1152]{1,0:T(8,128)(2,1)} %get-tuple-element.177.k, bf16[512,1152]{1,0:T(8,128)(2,1)} %get-tuple-element.178.v), custom_call_target="tpu_custom_call" | custom-call | tf_op jit(solution)/shard_map/pallas_call | solution.py:374
  256.4 8.2 %shard_map.384 = (bf16[256,1152]{1,0:T(8,128)(2,1)}, bf16[256,1152]{1,0:T(8,128)(2,1)}, bf16[256,1152]{1,0:T(8,128)(2,1)}, bf16[256,1152]{1,0:T(8,128)(2,1)}) custom-call(s32[1]{0:T(128)} %bitcast.core, bf16[256,1152]{1,0:T(8,128)(2,1)} %get-tuple-element.180.refs_0_, bf16[256,1152]{1,0:T(8,128)(2,1)} %copy-done.2, bf16[1152,1152]{1,0:T(8,128)(2,1)} %bitcast.61, ...), custom_call_target="tpu_custom_call" | custom-call | tf_op jit(solution)/shard_map/pallas_call | solution.py:480
  272.2 12.2 %shard_map.385 = (bf16[256,1152]{1,0:T(8,128)(2,1)}, bf16[256,1152]{1,0:T(8,128)(2,1)}, bf16[256,1152]{1,0:T(8,128)(2,1)}, bf16[256,1152]{1,0:T(8,128)(2,1)}, bf...) custom-call(s32[1]{0:T(128)} %bitcast.core, ...), custom_call_target="tpu_custom_call" | custom-call | tf_op jit(solution)/shard_map/pallas_call | solution.py:480
  285.2 8.2 %shard_map.386 = (bf16[256,1152]{1,0:T(8,128)(2,1)}, bf16[256,1152]{1,0:T(8,128)(2,1)}, bf16[256,1152]{1,0:T(8,128)(2,1)}, bf16[256,1152]{1,0:T(8,128)(2,1)}) custom-call(s32[1]{0:T(128)} %bitcast.core, bf16[128,1152]{1,0:T(8,128)(2,1)} %copy-done.26, bf16[128,1152]{1,0:T(8,128)(2,1)} %copy-done.28, bf16[128,1152]{1,0:T(8,128)(2,1)} %copy-done.25, ...), custom_call_target="tpu_custom_call" | custom-call | tf_op jit(solution)/shard_map/pallas_call | solution.py:480
  298.1 8.8 %shard_map.387 = bf16[1152,1152]{1,0:T(8,128)(2,1)} custom-call(s32[1]{0:T(128)} %bitcast.core, bf16[256,1152]{1,0:T(8,128)(2,1)} %get-tuple-element.180.refs_0_, bf16[256,1152]{1,0:T(8,128)(2,1)} %copy-done.3, bf16[256,1152]{1,0:T(8,128)(2,1)} %collective-permute-done.16.refs_1_.refs_2_, bf16[256,1152]{1,0:T(8,128)(2,1)} %copy-done.12, ...), custom_call_target="tpu_custom_call" | custom-call | tf_op jit(solution)/shard_map/pallas_call | solution.py:514
  315.5 8.7 %shard_map.388 = bf16[1152,1152]{1,0:T(8,128)(2,1)} custom-call(s32[1]{0:T(128)} %bitcast.core, bf16[256,1152]{1,0:T(8,128)(2,1)} %get-tuple-element.180.refs_0_, bf16[256,1152]{1,0:T(8,128)(2,1)} %copy-done.3, bf16[256,1152]{1,0:T(8,128)(2,1)} %collective-permute-done.16.refs_1_.refs_2_, bf16[256,1152]{1,0:T(8,128)(2,1)} %copy-done.12, ...), custom_call_target="tpu_custom_call" | custom-call | tf_op jit(solution)/shard_map/pallas_call | solution.py:514
  346.8 15.3 %shard_map.390 = (bf16[256,1152]{1,0:T(8,128)(2,1)}, bf16[512,2304]{1,0:T(8,128)(2,1)}) custom-call(s32[512,1]{1,0:T(8,128)} %fusion.36.cap_t, s32[1,256]{1,0:T(1,128)} %bitcast.93, bf16[256,1152]{1,0:T(8,128)(2,1)} %get-tuple-element.173.q, bf16[512,1152]{1,0:T(8,128)(2,1)} %get-tuple-element.177.k, bf16[512,1152]{1,0:T(8,128)(2,1)} %get-tuple-element.178.v, ...), custom_call_target="tpu_custom_call" | custom-call | tf_op jit(solution)/shard_map/pallas_call | solution.py:402
  399.2 18.7 %shard_map.392.refs_0_ = bf16[2048,768]{1,0:T(8,128)(2,1)} custom-call(s32[2048,1]{1,0:T(8,128)} %copy.114.seg_q.seg_k, s32[1,2048]{1,0:T(1,128)} %bitcast.88, f32[1,2048]{1,0:T(1,128)} %get-tuple-element.223.total, bf16[2048,768]{1,0:T(8,128)(2,1)} %convolution_convert_fusion.q.kv, bf16[2048,768]{1,0:T(8,128)(2,1)} %convolution_convert_fusion.q.kv, ...), custom_call_target="tpu_custom_call" | custom-call | tf_op jit(solution)/shard_map/pallas_call | solution.py:335
  426.4 18.8 %shard_map.393.g = bf16[2048,768]{1,0:T(8,128)(2,1)} custom-call(s32[2048,1]{1,0:T(8,128)} %copy.114.seg_q.seg_k, s32[1,2048]{1,0:T(1,128)} %bitcast.89, f32[1,2048]{1,0:T(1,128)} %get-tuple-element.231.total, bf16[2048,768]{1,0:T(8,128)(2,1)} %convolution_convert_fusion.q.kv, ...), custom_call_target="tpu_custom_call", output_to_operand_aliasing={{}: (6, {})} | custom-call | tf_op jit(solution)/shard_map/pallas_call | solution.py:335
  450.2 12.8 %collective-permute-done.42 = bf16[144,1152]{1,0:T(8,128)(2,1)S(1)} collective-permute-done((bf16[144,1152]{1,0:T(8,128)(2,1)S(1)}, bf16[144,1152]{1,0:T(8,128)(2,1)S(1)}, u32[]{:S(2)}, u32[]{:S(2)}) %collective-permute-start.42) | collective-permute-done | bytes 331808 | tf_op jit(solution)/shard_map/ppermute | solution.py:61
  476.2 17.0 %reduce-scatter.10.cloned.1.call-done = bf16[64,2304]{1,0:T(8,128)(2,1)} async-done(((bf16[512,2304]{1,0:T(8,128)(2,1)}), bf16[64,2304]{1,0:T(8,128)(2,1)}) %reduce-scatter.10.cloned.1.call-update) | async-done | bytes 294928 | tf_op jit(solution)/shard_map/reduce_scatter | solution.py:1012
  498.0 10.8 %shard_map.395 = (bf16[2048,1152]{1,0:T(8,128)(2,1)}, f32[8,1152]{1,0:T(8,128)}) custom-call(bf16[2048,768]{1,0:T(8,128)(2,1)} %shard_map.393.g, bf16[1152,768]{1,0:T(8,128)(2,1)} %shard_map.376.w, bf16[2048,1152]{1,0:T(8,128)(2,1)} %get-tuple-element.238.plain), custom_call_target="tpu_custom_call" | custom-call | flops 12650000384 | tf_op jit(solution)/shard_map/pallas_call | solution.py:676
  550.5 8.2 %collective-permute-done.52.refs_2_ = bf16[144,1152]{1,0:T(8,128)(2,1)S(1)} collective-permute-done((bf16[144,1152]{1,0:T(8,128)(2,1)S(1)}, bf16[144,1152]{1,0:T(8,128)(2,1)S(1)}, u32[]{:S(2)}, u32[]{:S(2)}) %collective-permute-start.52) | collective-permute-done | bytes 331808 | tf_op jit(solution)/shard_map/ppermute | solution.py:61
  564.6 25.7 %collective-permute-done.48 = bf16[144,1920]{1,0:T(8,128)(2,1)S(1)} collective-permute-done((bf16[144,1920]{1,0:T(8,128)(2,1)S(1)}, bf16[144,1920]{1,0:T(8,128)(2,1)S(1)}, u32[]{:S(2)}, u32[]{:S(2)}) %collective-permute-start.48) | collective-permute-done | bytes 552992 | tf_op jit(solution)/shard_map/ppermute | solution.py:61
  590.3 28.6 %collective-permute-done.49 = bf16[144,1920]{1,0:T(8,128)(2,1)S(1)} collective-permute-done((bf16[144,1920]{1,0:T(8,128)(2,1)S(1)}, bf16[144,1920]{1,0:T(8,128)(2,1)S(1)}, u32[]{:S(2)}, u32[]{:S(2)}) %collective-permute-start.49) | collective-permute-done | bytes 552992 | tf_op jit(solution)/shard_map/ppermute | solution.py:61
  622.0 11.1 %shard_map.398 = (bf16[512,512]{1,0:T(8,128)(2,1)}, bf16[512,1152]{1,0:T(8,128)(2,1)}, bf16[144,2304]{1,0:T(8,128)(2,1)}) custom-call(s32[1]{0:T(128)} %bitcast.core, bf16[512,2304]{1,0:T(8,128)(2,1)} %all-gather.5.cloned.1.call-done.kv, bf16[512,144]{1,0:T(8,128)(2,1)} %constant_dynamic-slice_fusion.4.cols, bf16[512,512]{1,0:T(8,128)(2,1)} %bitcast.79, ...), custom_call_target="tpu_custom_call" | custom-call | tf_op jit(solution)/shard_map/pallas_call | solution.py:573
  669.8 9.4 %collective-permute-done.61.refs_2_ = bf16[64,2432]{1,0:T(8,128)(2,1)S(1)} collective-permute-done((bf16[64,2432]{1,0:T(8,128)(2,1)S(1)}, bf16[64,2432]{1,0:T(8,128)(2,1)S(1)}, u32[]{:S(2)}, u32[]{:S(2)}) %collective-permute-start.61) | collective-permute-done | bytes 311328 | tf_op jit(solution)/shard_map/ppermute | solution.py:61
  (457 shorter events, 420.4 us)
Async XLA Ops:
  7.2 92.0 %all-gather.3.cloned.1.call-start = ((), (), s32[]{:S(2)}) async-start(), calls=%async_computation.14 | async-start | bytes 1990656 | tf_op jit(solution)/shard_map/all_gather | solution.py:830
  35.4 51.7 %all-to-all-start = ((bf16[8,144,432]{2,1,0:T(8,128)(2,1)}), bf16[8,144,432]{2,1,0:T(8,128)(2,1)S(1)}, u32[]{:S(2)}, u32[]{:S(2)}) async-start(bf16[8,144,432]{2,1,0:T(8,128)(2,1)} %bitcast.70), calls=%async_computation | async-start | bytes 2359296 | tf_op jit(solution)/shard_map/all_to_all | solution.py:122
  113.6 44.9 %all-to-all-start.2 = ((bf16[8,144,1152]{2,1,0:T(8,128)(2,1)}), bf16[8,144,1152]{2,1,0:T(8,128)(2,1)S(1)}, u32[]{:S(2)}, u32[]{:S(2)}) async-start(bf16[8,144,1152]{2,1,0:T(8,128)(2,1)} %broadcast_in_dim.114), calls=%async_computation.2 | async-start | bytes 5308416 | tf_op jit(solution)/shard_map/all_to_all | solution.py:118
  118.4 56.6 %reduce-scatter.6.cloned.1.call-start = ((), (), s32[]{:S(2)}) async-start(), calls=%async_computation.15 | async-start | bytes 1327104 | tf_op jit(solution)/shard_map/reduce_scatter | solution.py:871
  118.5 39.5 %collective-permute-start.8 = (bf16[1152,768]{1,0:T(8,128)(2,1)}, bf16[1152,768]{1,0:T(8,128)(2,1)}, u32[]{:S(2)}, u32[]{:S(2)}) collective-permute-start(bf16[1152,768]{1,0:T(8,128)(2,1)} %all-gather.3.cloned.1.call-done.own), channel_id=1, source_target_pairs={{0,16},{16,32},{32,48},{48,0},{1,17},{17,33},{33,49},{49,1},{2,18}... | collective-permute-start | bytes 5308424 | tf_op jit(solution)/shard_map/ppermute | solution.py:61
  120.2 38.3 %collective-permute-start.9 = (bf16[1152,768]{1,0:T(8,128)(2,1)}, bf16[1152,768]{1,0:T(8,128)(2,1)}, u32[]{:S(2)}, u32[]{:S(2)}) collective-permute-start(bf16[1152,768]{1,0:T(8,128)(2,1)} %all-gather.3.cloned.1.call-done.own), channel_id=1, source_target_pairs={{0,48},{16,0},{32,16},{48,32},{1,49},{17,1},{33,17},{49,33},{2,50}... | collective-permute-start | bytes 5308424 | tf_op jit(solution)/shard_map/ppermute | solution.py:61
  202.1 215.8 %reduce-scatter.8.cloned.1.call-start = ((), (), s32[]{:S(2)}) async-start(), calls=%async_computation.16 | async-start | bytes 2985984 | tf_op jit(solution)/shard_map/reduce_scatter | solution.py:963
  339.7 43.1 %collective-permute-start.29 = (bf16[256,1152]{1,0:T(8,128)(2,1)}, bf16[256,1152]{1,0:T(8,128)(2,1)}, u32[]{:S(2)}, u32[]{:S(2)}) collective-permute-start(bf16[256,1152]{1,0:T(8,128)(2,1)} %get-tuple-element.218), channel_id=1, source_target_pairs={{0,8},{8,0},{1,9},{9,1},{2,10},{10,2},{3,11},{11,3},{4,12},{12,4},... | collective-permute-start | bytes 1769480 | tf_op jit(solution)/shard_map/ppermute | solution.py:61
  380.5 112.7 %reduce-scatter.10.cloned.1.call-start = ((), (), s32[]{:S(2)}) async-start(), calls=%async_computation.17 | async-start | bytes 2654208 | tf_op jit(solution)/shard_map/reduce_scatter | solution.py:1012
  418.9 44.2 %collective-permute-start.33 = (bf16[80,1920]{1,0:T(8,128)(2,1)S(1)}, bf16[80,1920]{1,0:T(8,128)(2,1)S(1)}, u32[]{:S(2)}, u32[]{:S(2)}) collective-permute-start(bf16[80,1920]{1,0:T(8,128)(2,1)S(1)} %constant_dynamic-slice_fusion), channel_id=1, source_target_pairs={{0,2},{2,4},{4,6},{6,0},{1,3},{3,5},{5,7},{7,1},{8,10},{10,12},{12... | collective-permute-start | bytes 921608 | tf_op jit(solution)/shard_map/ppermute | solution.py:61
  422.1 41.0 %collective-permute-start.34 = (bf16[64,1920]{1,0:T(8,128)(2,1)}, bf16[64,1920]{1,0:T(8,128)(2,1)}, u32[]{:S(2)}, u32[]{:S(2)}) collective-permute-start(bf16[64,1920]{1,0:T(8,128)(2,1)} %constant_dynamic-slice_fusion.9), channel_id=1, source_target_pairs={{0,6},{2,0},{4,2},{6,4},{1,7},{3,1},{5,3},{7,5},{8,14},{10,8},{12,... | collective-permute-start | bytes 737288 | tf_op jit(solution)/shard_map/ppermute | solution.py:61
  425.0 38.2 %collective-permute-start.35 = (bf16[144,1920]{1,0:T(8,128)(2,1)S(1)}, bf16[144,1920]{1,0:T(8,128)(2,1)S(1)}, u32[]{:S(2)}, u32[]{:S(2)}) collective-permute-start(bf16[144,1920]{1,0:T(8,128)(2,1)S(1)} %constant_dynamic-slice_fusion.8), channel_id=1, source_target_pairs={{0,2},{2,4},{4,6},{6,0},{1,3},{3,5},{5,7},{7,1},{8,10},{10,12},{12... | collective-permute-start | bytes 1658888 | tf_op jit(solution)/shard_map/ppermute | solution.py:61
  465.8 43.1 %collective-permute-start.40 = (bf16[144,1920]{1,0:T(8,128)(2,1)S(1)}, bf16[144,1920]{1,0:T(8,128)(2,1)}, u32[]{:S(2)}, u32[]{:S(2)}) collective-permute-start(bf16[144,1920]{1,0:T(8,128)(2,1)S(1)} %pad_maximum_fusion.11), channel_id=1, source_target_pairs={{0,1},{1,0},{2,3},{3,2},{4,5},{5,4},{6,7},{7,6},{8,9},{9,8},{10,11... | collective-permute-start | bytes 1658888 | tf_op jit(solution)/shard_map/ppermute | solution.py:61
  465.9 42.9 %collective-permute-start.41 = (bf16[144,1920]{1,0:T(8,128)(2,1)S(1)}, bf16[144,1920]{1,0:T(8,128)(2,1)}, u32[]{:S(2)}, u32[]{:S(2)}) collective-permute-start(bf16[144,1920]{1,0:T(8,128)(2,1)S(1)} %pad_maximum_fusion.12), channel_id=1, source_target_pairs={{0,6},{2,0},{4,2},{6,4},{1,7},{3,1},{5,3},{7,5},{8,14},{10,8},{12,... | collective-permute-start | bytes 1658888 | tf_op jit(solution)/shard_map/ppermute | solution.py:61
  497.4 121.5 %all-gather.5.cloned.1.call-start = ((), (), s32[]{:S(2)}) async-start(), calls=%async_computation.18 | async-start | bytes 2654208 | tf_op jit(solution)/shard_map/all_gather | solution.py:1025
  514.2 104.8 %all-to-all-start.7 = ((bf16[8,256,1152]{2,1,0:T(8,128)(2,1)}), bf16[8,256,1152]{2,1,0:T(8,128)(2,1)}, u32[]{:S(2)}, u32[]{:S(2)}) async-start(bf16[8,256,1152]{2,1,0:T(8,128)(2,1)} %bitcast.69), calls=%async_computation.10 | async-start | bytes 9437184 | tf_op jit(solution)/shard_map/all_to_all | solution.py:122
  518.8 128.7 %reduce-scatter.12.cloned.1.call-start = ((), (), s32[]{:S(2)}) async-start(), calls=%async_computation.19 | async-start | bytes 1556480 | tf_op jit(solution)/shard_map/reduce_scatter | solution.py:1048
  540.9 49.4 %collective-permute-start.48 = (bf16[144,1920]{1,0:T(8,128)(2,1)S(1)}, bf16[144,1920]{1,0:T(8,128)(2,1)S(1)}, u32[]{:S(2)}, u32[]{:S(2)}) collective-permute-start(bf16[144,1920]{1,0:T(8,128)(2,1)S(1)} %get-tuple-element.340), channel_id=1, source_target_pairs={{0,2},{2,4},{4,6},{6,0},{1,3},{3,5},{5,7},{7,1},{8,10},{10,12},{12... | collective-permute-start | bytes 1658888 | tf_op jit(solution)/shard_map/ppermute | solution.py:61
  542.5 76.4 %collective-permute-start.49 = (bf16[144,1920]{1,0:T(8,128)(2,1)S(1)}, bf16[144,1920]{1,0:T(8,128)(2,1)S(1)}, u32[]{:S(2)}, u32[]{:S(2)}) collective-permute-start(bf16[144,1920]{1,0:T(8,128)(2,1)S(1)} %get-tuple-element.339), channel_id=1, source_target_pairs={{0,1},{1,0},{2,3},{3,2},{4,5},{5,4},{6,7},{7,6},{8,9},{9,8},{10,11... | collective-permute-start | bytes 1658888 | tf_op jit(solution)/shard_map/ppermute | solution.py:61
  543.7 75.2 %collective-permute-start.50 = (bf16[144,1920]{1,0:T(8,128)(2,1)S(1)}, bf16[144,1920]{1,0:T(8,128)(2,1)S(1)}, u32[]{:S(2)}, u32[]{:S(2)}) collective-permute-start(bf16[144,1920]{1,0:T(8,128)(2,1)S(1)} %get-tuple-element.338), channel_id=1, source_target_pairs={{0,6},{2,0},{4,2},{6,4},{1,7},{3,1},{5,3},{7,5},{8,14},{10,8},{12,... | collective-permute-start | bytes 1658888 | tf_op jit(solution)/shard_map/ppermute | solution.py:61
  621.5 81.0 %reduce-scatter.14.cloned.1.call-start = ((), (), s32[]{:S(2)}) async-start(), calls=%async_computation.20 | async-start | bytes 1290240 | tf_op jit(solution)/shard_map/reduce_scatter | solution.py:1069
  660.5 42.0 %collective-permute-start.39 = (bf16[256,1152]{1,0:T(8,128)(2,1)}, bf16[256,1152]{1,0:T(8,128)(2,1)}, u32[]{:S(2)}, u32[]{:S(2)}) collective-permute-start(bf16[256,1152]{1,0:T(8,128)(2,1)} %pad_maximum_fusion.10), channel_id=1, source_target_pairs={{0,16},{16,32},{32,48},{48,0},{1,17},{17,33},{33,49},{49,1},{2,18}... | collective-permute-start | bytes 1769480 | tf_op jit(solution)/shard_map/ppermute | solution.py:61
  661.6 41.4 %collective-permute-start.38 = (bf16[256,1152]{1,0:T(8,128)(2,1)}, bf16[256,1152]{1,0:T(8,128)(2,1)}, u32[]{:S(2)}, u32[]{:S(2)}) collective-permute-start(bf16[256,1152]{1,0:T(8,128)(2,1)} %pad_maximum_fusion.9), channel_id=1, source_target_pairs={{0,48},{16,0},{32,16},{48,32},{1,49},{17,1},{33,17},{49,33},{2,50}... | collective-permute-start | bytes 1769480 | tf_op jit(solution)/shard_map/ppermute | solution.py:61
  694.7 39.3 %collective-permute-start.63 = (bf16[256,2432]{1,0:T(8,128)(2,1)}, bf16[256,2432]{1,0:T(8,128)(2,1)}, u32[]{:S(2)}, u32[]{:S(2)}) collective-permute-start(bf16[256,2432]{1,0:T(8,128)(2,1)} %shard_map.399), channel_id=1, source_target_pairs={{0,8},{8,0},{1,9},{9,1},{2,10},{10,2},{3,11},{11,3},{4,12},{12,4},... | collective-permute-start | bytes 3735560 | tf_op jit(solution)/shard_map/ppermute | solution.py:61
  (134 other events, 1901.3 us)
Sparse Core Ops, SparseCore 0:
  10.6 75.6 all-gather.2
  124.8 50.1 reduce-scatter.5
  336.6 68.8 reduce-scatter.7
  419.2 73.9 reduce-scatter.9
  499.6 93.5 all-gather.4
  621.7 25.7 reduce-scatter.11
  650.6 37.3 reduce-scatter.13

commit v12 on v10

--- a/solution.py
+++ b/solution.py
@@ -1020,14 +1020,14 @@
     s11, s31 = reduce_second(square_chunk, s_lo, s_hi)
 
     heads_own = heads_grad(normed_all, grad_qkv)
-    heads_own, s11, s31, kv_all = lax.optimization_barrier((heads_own, s11, s31, kv_all))
+    heads_own, kv_all = lax.optimization_barrier((heads_own, kv_all))
     heads_part = peers_parts(heads_own)
+    part, sums_one = first_part(after(grad_qkv, heads_own), heads_w, plain_all)
+    part, heads_part, kv_all, hidden_grad, s11, s31 = lax.optimization_barrier(
+        (part, heads_part, kv_all, hidden_grad, s11, s31)
+    )
+    sent = peers_parts(part)
     square_parts = reduce_third(square_chunk, s20, s11, s31)
-    part, sums_one = first_part(after(grad_qkv, heads_own), heads_w, plain_all)
-    part, heads_part, kv_all, hidden_grad, *square_parts = lax.optimization_barrier(
-        (part, heads_part, kv_all, hidden_grad, *square_parts)
-    )
-    sent = peers_parts(part)
 
     square = reduce_last(square_chunk, *square_parts).astype(bf16)
     heads_rows = unpack_heads(heads_part)

time: 744 us -> 757 us (1.017)
    all_to_all x3, waiting for transfers between devices: 0.01 us -> 16.4 us  [every_peer(): return lax.all_to_all(copies, axes, 0, 0, tiled=True)]
  transfers between devices with their start and end apart: 87 -> 87, of which waited for: 34 -> 34; matrix products, arithmetic and copies ran while one was open for 13% -> 14% of each run, Pallas kernels for 23% -> 23%
where the time goes in v12:
time: 757 us; the launch traced here: 747 us
  Pallas kernels  240 us (32%)
  waiting for transfers between devices  215 us (28%)
  starting transfers between devices  142 us (19%)
  local copies, waits for them, and re-layouts  63.4 us (8%)
  other arithmetic  52.6 us (7%)
  matrix products  18.4 us (2%)
  between operations  15.6 us (2%)
    ppermute x71, waiting for transfers between devices, shift(): return lax.ppermute(x, axis, [(i, (i + by) % n) for i in range(n)])  134 us
    ppermute x71, starting transfers between devices, shift(): return lax.ppermute(x, axis, [(i, (i + by) % n) for i in range(n)])  99.3 us
    pallas_call x7, Pallas kernels, call(): pl.pallas_call(body, in_specs=[pl.BlockSpec(memory_space=spaces[where]) f...  51.8 us
    all_to_all x3, waiting for transfers between devices, peers_parts(): return lax.all_to_all(x, axes, 0, 0, tiled=True)  45.1 us
    pallas_call x2, Pallas kernels, self_backward(): pl.pallas_call(functools.partial(self_backward_body, head), grid=(ROW //...  37.3 us
    pallas_call x3, Pallas kernels, mlp(): pl.pallas_call(functools.partial(mlp_body, parts, count), in_specs=[pl.Bl...  28.6 us
    pallas_call x2, Pallas kernels, self_forward(): pl.pallas_call(self_forward_body, grid=(ROW // TOK,), in_specs=[pl.BlockS...  24.3 us
    pallas_call x2, Pallas kernels, mlp_grad(): pl.pallas_call(functools.partial(mlp_grad_body, which), grid=(3,), in_spe...  17.8 us
  transfers between devices with their start and end apart: 87, of which 34 were waited for; matrix products, arithmetic and copies ran while one was open for 14% of the time, Pallas kernels for 23%

profile of v12, /device:TPU:1, one launch (start us, length us, event | category | flops | bytes accessed | tf_op | source)
XLA Modules:
  0.0 747.0 jit_solution(14893137999585888473)
XLA Ops:
  18.8 9.6 %collective-permute-done.refs_1_ = bf16[256,1152]{1,0:T(8,128)(2,1)} collective-permute-done((bf16[256,1152]{1,0:T(8,128)(2,1)S(1)}, bf16[256,1152]{1,0:T(8,128)(2,1)}, u32[]{:S(2)}, u32[]{:S(2)}) %collective-permute-start) | collective-permute-done | bytes 589856 | tf_op jit(solution)/shard_map/ppermute | solution.py:61
  42.6 8.6 %collective-permute-done.3.refs_4_ = bf16[256,1152]{1,0:T(8,128)(2,1)S(1)} collective-permute-done((bf16[256,1152]{1,0:T(8,128)(2,1)}, bf16[256,1152]{1,0:T(8,128)(2,1)S(1)}, u32[]{:S(2)}, u32[]{:S(2)}) %collective-permute-start.3) | collective-permute-done | bytes 589856 | tf_op jit(solution)/shard_map/ppermute | solution.py:61
  51.3 10.7 %collective-permute-done.5.refs_6_ = bf16[256,1152]{1,0:T(8,128)(2,1)S(1)} collective-permute-done((bf16[256,1152]{1,0:T(8,128)(2,1)}, bf16[256,1152]{1,0:T(8,128)(2,1)S(1)}, u32[]{:S(2)}, u32[]{:S(2)}) %collective-permute-start.5) | collective-permute-done | bytes 589856 | tf_op jit(solution)/shard_map/ppermute | solution.py:61
  66.0 21.1 %all-to-all-done = bf16[8,144,432]{2,1,0:T(8,128)(2,1)S(1)} async-done(((bf16[8,144,432]{2,1,0:T(8,128)(2,1)}), bf16[8,144,432]{2,1,0:T(8,128)(2,1)S(1)}, u32[]{:S(2)}, u32[]{:S(2)}) %all-to-all-start) | async-done | bytes 995360 | tf_op jit(solution)/shard_map/all_to_all | solution.py:122
  103.6 8.2 %convolution_convert_fusion.q.kv = bf16[2048,768]{1,0:T(8,128)(2,1)} fusion(bf16[2048,1152]{1,0:T(8,128)(2,1)} %get-tuple-element.151.x, bf16[1152,768]{1,0:T(8,128)(2,1)S(1)} %copy-done.20), kind=kOutput, calls=%fused_computation.1 | convolution fusion | flops 3625451520 | bytes 9633792 | tf_op jit(solution)/shard_map/dot_general | solution.py:40
  126.5 12.1 %shard_map.377 = (bf16[2048,72]{1,0:T(8,128)(2,1)}, f32[1,2048]{1,0:T(1,128)}) custom-call(s32[2048,1]{1,0:T(8,128)} %copy.114.seg_q.seg_k, s32[1,2048]{1,0:T(1,128)} %bitcast.89, bf16[2048,768]{1,0:T(8,128)(2,1)} %convolution_convert_fusion.q.kv, bf16[2048,768]{1,0:T(8,128)(2,1)} %convolution_convert_fusion.q.kv), custom_call_target="tpu_custom_call" | custom-call | tf_op jit(solution)/shard_map/pallas_call | solution.py:283
  138.6 12.2 %shard_map.378 = (bf16[2048,72]{1,0:T(8,128)(2,1)}, f32[1,2048]{1,0:T(1,128)}) custom-call(s32[2048,1]{1,0:T(8,128)} %copy.114.seg_q.seg_k, s32[1,2048]{1,0:T(1,128)} %bitcast.90, bf16[2048,768]{1,0:T(8,128)(2,1)} %convolution_convert_fusion.q.kv, bf16[2048,768]{1,0:T(8,128)(2,1)} %convolution_convert_fusion.q.kv), custom_call_target="tpu_custom_call" | custom-call | tf_op jit(solution)/shard_map/pallas_call | solution.py:283
  188.7 7.8 %collective-permute-start.12 = (bf16[1152,3072]{1,0:T(8,128)(2,1)}, bf16[1152,3072]{1,0:T(8,128)(2,1)}, u32[]{:S(2)}, u32[]{:S(2)}) collective-permute-start(bf16[1152,3072]{1,0:T(8,128)(2,1)} %shard_map.379.mine), channel_id=1, source_target_pairs={{0,8},{8,0},{1,9},{9,1},{2,10},{10,2},{3,11},{11,3},{4,12},{12,4},... | collective-permute-start | bytes 21233672 | tf_op jit(solution)/shard_map/ppermute | solution.py:61
  220.0 8.4 %shard_map.381 = (bf16[512,1152]{1,0:T(8,128)(2,1)}, bf16[512,1152]{1,0:T(8,128)(2,1)}) custom-call(s32[1]{0:T(128)} %bitcast.core, bf16[512,1152]{1,0:T(8,128)(2,1)} %bitcast.28.context, bf16[1152,3072]{1,0:T(8,128)(2,1)} %shard_map.379.mine, bf16[1152,3072]{1,0:T(8,128)(2,1)} %collective-permute-done.12.other), custom_call_target="tpu_custom_call" | custom-call | tf_op jit(solution)/shard_map/pallas_call | solution.py:573
  228.5 11.7 %shard_map.382.mixed = bf16[256,1152]{1,0:T(8,128)(2,1)} custom-call(s32[256,1]{1,0:T(8,128)} %copy.118.cap_q, s32[1,512]{1,0:T(1,128)} %and_select_fusion.1.cap_t, bf16[256,1152]{1,0:T(8,128)(2,1)} %get-tuple-element.169.q, bf16[512,1152]{1,0:T(8,128)(2,1)} %get-tuple-element.173.k, bf16[512,1152]{1,0:T(8,128)(2,1)} %get-tuple-element.174.v), custom_call_target="tpu_custom_call" | custom-call | tf_op jit(solution)/shard_map/pallas_call | solution.py:374
  256.9 8.2 %shard_map.384 = (bf16[256,1152]{1,0:T(8,128)(2,1)}, bf16[256,1152]{1,0:T(8,128)(2,1)}, bf16[256,1152]{1,0:T(8,128)(2,1)}, bf16[256,1152]{1,0:T(8,128)(2,1)}) custom-call(s32[1]{0:T(128)} %bitcast.core, bf16[256,1152]{1,0:T(8,128)(2,1)} %get-tuple-element.176.refs_0_, bf16[256,1152]{1,0:T(8,128)(2,1)} %copy-done.2, bf16[1152,1152]{1,0:T(8,128)(2,1)} %bitcast.62, ...), custom_call_target="tpu_custom_call" | custom-call | tf_op jit(solution)/shard_map/pallas_call | solution.py:480
  270.9 12.3 %shard_map.385 = (bf16[256,1152]{1,0:T(8,128)(2,1)}, bf16[256,1152]{1,0:T(8,128)(2,1)}, bf16[256,1152]{1,0:T(8,128)(2,1)}, bf16[256,1152]{1,0:T(8,128)(2,1)}, bf...) custom-call(s32[1]{0:T(128)} %bitcast.core, ...), custom_call_target="tpu_custom_call" | custom-call | tf_op jit(solution)/shard_map/pallas_call | solution.py:480
  284.0 8.2 %shard_map.386 = (bf16[256,1152]{1,0:T(8,128)(2,1)}, bf16[256,1152]{1,0:T(8,128)(2,1)}, bf16[256,1152]{1,0:T(8,128)(2,1)}, bf16[256,1152]{1,0:T(8,128)(2,1)}) custom-call(s32[1]{0:T(128)} %bitcast.core, bf16[128,1152]{1,0:T(8,128)(2,1)} %copy-done.27, bf16[128,1152]{1,0:T(8,128)(2,1)} %copy-done.29, bf16[128,1152]{1,0:T(8,128)(2,1)} %copy-done.25, ...), custom_call_target="tpu_custom_call" | custom-call | tf_op jit(solution)/shard_map/pallas_call | solution.py:480
  297.0 8.7 %shard_map.387 = bf16[1152,1152]{1,0:T(8,128)(2,1)} custom-call(s32[1]{0:T(128)} %bitcast.core, bf16[256,1152]{1,0:T(8,128)(2,1)} %get-tuple-element.176.refs_0_, bf16[256,1152]{1,0:T(8,128)(2,1)} %copy-done.4, bf16[256,1152]{1,0:T(8,128)(2,1)} %collective-permute-done.16.refs_1_.refs_2_, bf16[256,1152]{1,0:T(8,128)(2,1)} %copy-done.12, ...), custom_call_target="tpu_custom_call" | custom-call | tf_op jit(solution)/shard_map/pallas_call | solution.py:514
  314.9 9.1 %shard_map.388 = bf16[1152,1152]{1,0:T(8,128)(2,1)} custom-call(s32[1]{0:T(128)} %bitcast.core, bf16[256,1152]{1,0:T(8,128)(2,1)} %get-tuple-element.176.refs_0_, bf16[256,1152]{1,0:T(8,128)(2,1)} %copy-done.4, bf16[256,1152]{1,0:T(8,128)(2,1)} %collective-permute-done.16.refs_1_.refs_2_, bf16[256,1152]{1,0:T(8,128)(2,1)} %copy-done.12, ...), custom_call_target="tpu_custom_call" | custom-call | tf_op jit(solution)/shard_map/pallas_call | solution.py:514
  341.2 15.3 %shard_map.390 = (bf16[256,1152]{1,0:T(8,128)(2,1)}, bf16[512,2304]{1,0:T(8,128)(2,1)}) custom-call(s32[512,1]{1,0:T(8,128)} %fusion.36.cap_t, s32[1,256]{1,0:T(1,128)} %bitcast.96, bf16[256,1152]{1,0:T(8,128)(2,1)} %get-tuple-element.169.q, bf16[512,1152]{1,0:T(8,128)(2,1)} %get-tuple-element.173.k, bf16[512,1152]{1,0:T(8,128)(2,1)} %get-tuple-element.174.v, ...), custom_call_target="tpu_custom_call" | custom-call | tf_op jit(solution)/shard_map/pallas_call | solution.py:402
  388.0 8.2 %all-to-all-done.5 = bf16[256,8,144]{0,2,1:T(8,128)(2,1)S(1)} async-done(((bf16[256,8,144]{0,2,1:T(8,128)(2,1)}), bf16[256,8,144]{0,2,1:T(8,128)(2,1)S(1)}, u32[]{:S(2)}, u32[]{:S(2)}) %all-to-all-start.5) | async-done | bytes 589856 | tf_op jit(solution)/shard_map/all_to_all | solution.py:993
  397.5 18.7 %shard_map.392.refs_0_ = bf16[2048,768]{1,0:T(8,128)(2,1)} custom-call(s32[2048,1]{1,0:T(8,128)} %copy.114.seg_q.seg_k, s32[1,2048]{1,0:T(1,128)} %bitcast.91, f32[1,2048]{1,0:T(1,128)} %get-tuple-element.219.total, bf16[2048,768]{1,0:T(8,128)(2,1)} %convolution_convert_fusion.q.kv, bf16[2048,768]{1,0:T(8,128)(2,1)} %convolution_convert_fusion.q.kv, ...), custom_call_target="tpu_custom_call" | custom-call | tf_op jit(solution)/shard_map/pallas_call | solution.py:335
  436.3 18.6 %shard_map.393.g = bf16[2048,768]{1,0:T(8,128)(2,1)} custom-call(s32[2048,1]{1,0:T(8,128)} %copy.114.seg_q.seg_k, s32[1,2048]{1,0:T(1,128)} %bitcast.92, f32[1,2048]{1,0:T(1,128)} %get-tuple-element.227.total, bf16[2048,768]{1,0:T(8,128)(2,1)} %convolution_convert_fusion.q.kv, ...), custom_call_target="tpu_custom_call", output_to_operand_aliasing={{}: (6, {})} | custom-call | tf_op jit(solution)/shard_map/pallas_call | solution.py:335
  474.7 16.4 %all-to-all-done.6 = bf16[8,64,2304]{2,1,0:T(8,128)(2,1)S(1)} async-done(((bf16[8,64,2304]{2,1,0:T(8,128)(2,1)}), bf16[8,64,2304]{2,1,0:T(8,128)(2,1)S(1)}, u32[]{:S(2)}, u32[]{:S(2)}) %all-to-all-start.6) | async-done | bytes 2359328 | tf_op jit(solution)/shard_map/all_to_all | solution.py:118
  494.7 10.8 %shard_map.395 = (bf16[2048,1152]{1,0:T(8,128)(2,1)}, f32[8,1152]{1,0:T(8,128)}) custom-call(bf16[2048,768]{1,0:T(8,128)(2,1)} %shard_map.393.g, bf16[1152,768]{1,0:T(8,128)(2,1)} %shard_map.376.w, bf16[2048,1152]{1,0:T(8,128)(2,1)} %get-tuple-element.235.plain), custom_call_target="tpu_custom_call" | custom-call | flops 12650000384 | tf_op jit(solution)/shard_map/pallas_call | solution.py:676
  512.7 24.1 %all-to-all-done.7 = bf16[8,144,432]{2,1,0:T(8,128)(2,1)S(1)} async-done(((bf16[8,144,432]{2,1,0:T(8,128)(2,1)}), bf16[8,144,432]{2,1,0:T(8,128)(2,1)S(1)}, u32[]{:S(2)}, u32[]{:S(2)}) %all-to-all-start.7) | async-done | bytes 995360 | tf_op jit(solution)/shard_map/all_to_all | solution.py:122
  536.8 11.5 %shard_map.396 = (bf16[512,512]{1,0:T(8,128)(2,1)}, bf16[512,1152]{1,0:T(8,128)(2,1)}, bf16[144,2304]{1,0:T(8,128)(2,1)}) custom-call(s32[1]{0:T(128)} %bitcast.core, bf16[512,2304]{1,0:T(8,128)(2,1)} %bitcast.67, bf16[512,144]{1,0:T(8,128)(2,1)} %constant_dynamic-slice_fusion.6.cols, bf16[512,512]{1,0:T(8,128)(2,1)} %bitcast.81, bf16[512,1152]{1,0:T(8,128)(2,1)} %w_text.1, ...), custom_call_target="tpu_custom_call" | custom-call | tf_op jit(solution)/shard_map/pallas_call | solution.py:573
  570.7 50.4 %collective-permute-done.55 = bf16[144,1920]{1,0:T(8,128)(2,1)S(1)} collective-permute-done((bf16[144,1920]{1,0:T(8,128)(2,1)}, bf16[144,1920]{1,0:T(8,128)(2,1)S(1)}, u32[]{:S(2)}, u32[]{:S(2)}) %collective-permute-start.55) | collective-permute-done | bytes 552992 | tf_op jit(solution)/shard_map/ppermute | solution.py:61
  (454 shorter events, 400.6 us)
Async XLA Ops:
  7.2 92.0 %all-gather.2.cloned.1.call-start = ((), (), s32[]{:S(2)}) async-start(), calls=%async_computation.15 | async-start | bytes 1990656 | tf_op jit(solution)/shard_map/all_gather | solution.py:830
  35.4 51.7 %all-to-all-start = ((bf16[8,144,432]{2,1,0:T(8,128)(2,1)}), bf16[8,144,432]{2,1,0:T(8,128)(2,1)S(1)}, u32[]{:S(2)}, u32[]{:S(2)}) async-start(bf16[8,144,432]{2,1,0:T(8,128)(2,1)} %bitcast.72), calls=%async_computation | async-start | bytes 2359296 | tf_op jit(solution)/shard_map/all_to_all | solution.py:122
  113.6 45.0 %all-to-all-start.2 = ((bf16[8,144,1152]{2,1,0:T(8,128)(2,1)}), bf16[8,144,1152]{2,1,0:T(8,128)(2,1)S(1)}, u32[]{:S(2)}, u32[]{:S(2)}) async-start(bf16[8,144,1152]{2,1,0:T(8,128)(2,1)} %broadcast_in_dim.121), calls=%async_computation.2 | async-start | bytes 5308416 | tf_op jit(solution)/shard_map/all_to_all | solution.py:118
  118.5 56.6 %reduce-scatter.6.cloned.1.call-start = ((), (), s32[]{:S(2)}) async-start(), calls=%async_computation.16 | async-start | bytes 1327104 | tf_op jit(solution)/shard_map/reduce_scatter | solution.py:871
  118.5 39.5 %collective-permute-start.8 = (bf16[1152,768]{1,0:T(8,128)(2,1)}, bf16[1152,768]{1,0:T(8,128)(2,1)}, u32[]{:S(2)}, u32[]{:S(2)}) collective-permute-start(bf16[1152,768]{1,0:T(8,128)(2,1)} %all-gather.2.cloned.1.call-done.own), channel_id=1, source_target_pairs={{0,16},{16,32},{32,48},{48,0},{1,17},{17,33},{33,49},{49,1},{2,18}... | collective-permute-start | bytes 5308424 | tf_op jit(solution)/shard_map/ppermute | solution.py:61
  120.3 38.3 %collective-permute-start.9 = (bf16[1152,768]{1,0:T(8,128)(2,1)}, bf16[1152,768]{1,0:T(8,128)(2,1)}, u32[]{:S(2)}, u32[]{:S(2)}) collective-permute-start(bf16[1152,768]{1,0:T(8,128)(2,1)} %all-gather.2.cloned.1.call-done.own), channel_id=1, source_target_pairs={{0,48},{16,0},{32,16},{48,32},{1,49},{17,1},{33,17},{49,33},{2,50}... | collective-permute-start | bytes 5308424 | tf_op jit(solution)/shard_map/ppermute | solution.py:61
  202.0 217.5 %reduce-scatter.8.cloned.1.call-start = ((), (), s32[]{:S(2)}) async-start(), calls=%async_computation.17 | async-start | bytes 2654208 | tf_op jit(solution)/shard_map/reduce_scatter | solution.py:982
  378.6 158.2 %reduce-scatter.10.cloned.1.call-start = ((), (), s32[]{:S(2)}) async-start(), calls=%async_computation.18 | async-start | bytes 2985984 | tf_op jit(solution)/shard_map/reduce_scatter | solution.py:1012
  421.2 37.6 %collective-permute-start.33 = (bf16[80,1920]{1,0:T(8,128)(2,1)}, bf16[80,1920]{1,0:T(8,128)(2,1)}, u32[]{:S(2)}, u32[]{:S(2)}) collective-permute-start(bf16[80,1920]{1,0:T(8,128)(2,1)} %constant_dynamic-slice_fusion), channel_id=1, source_target_pairs={{0,2},{2,4},{4,6},{6,0},{1,3},{3,5},{5,7},{7,1},{8,10},{10,12},{12... | collective-permute-start | bytes 921608 | tf_op jit(solution)/shard_map/ppermute | solution.py:61
  422.5 32.5 %collective-permute-start.36 = (bf16[128,1152]{1,0:T(8,128)(2,1)}, bf16[128,1152]{1,0:T(8,128)(2,1)}, u32[]{:S(2)}, u32[]{:S(2)}) collective-permute-start(bf16[128,1152]{1,0:T(8,128)(2,1)} %get-tuple-element.364), channel_id=1, source_target_pairs={{0,48},{16,0},{32,16},{48,32},{1,49},{17,1},{33,17},{49,33},{2,50}... | collective-permute-start | bytes 884744 | tf_op jit(solution)/shard_map/ppermute | solution.py:61
  432.5 58.6 %all-to-all-start.6 = ((bf16[8,64,2304]{2,1,0:T(8,128)(2,1)}), bf16[8,64,2304]{2,1,0:T(8,128)(2,1)S(1)}, u32[]{:S(2)}, u32[]{:S(2)}) async-start(bf16[8,64,2304]{2,1,0:T(8,128)(2,1)} %broadcast_in_dim.137), calls=%async_computation.8 | async-start | bytes 4718592 | tf_op jit(solution)/shard_map/all_to_all | solution.py:118
  462.2 50.4 %collective-permute-start.40 = (bf16[144,1920]{1,0:T(8,128)(2,1)}, bf16[144,1920]{1,0:T(8,128)(2,1)}, u32[]{:S(2)}, u32[]{:S(2)}) collective-permute-start(bf16[144,1920]{1,0:T(8,128)(2,1)} %pad_maximum_fusion.11), channel_id=1, source_target_pairs={{0,1},{1,0},{2,3},{3,2},{4,5},{5,4},{6,7},{7,6},{8,9},{9,8},{10,11... | collective-permute-start | bytes 1658888 | tf_op jit(solution)/shard_map/ppermute | solution.py:61
  464.5 48.1 %collective-permute-start.41 = (bf16[144,1920]{1,0:T(8,128)(2,1)}, bf16[144,1920]{1,0:T(8,128)(2,1)}, u32[]{:S(2)}, u32[]{:S(2)}) collective-permute-start(bf16[144,1920]{1,0:T(8,128)(2,1)} %pad_maximum_fusion.12), channel_id=1, source_target_pairs={{0,6},{2,0},{4,2},{6,4},{1,7},{3,1},{5,3},{7,5},{8,14},{10,8},{12,... | collective-permute-start | bytes 1658888 | tf_op jit(solution)/shard_map/ppermute | solution.py:61
  491.1 45.7 %all-to-all-start.7 = ((bf16[8,144,432]{2,1,0:T(8,128)(2,1)}), bf16[8,144,432]{2,1,0:T(8,128)(2,1)S(1)}, u32[]{:S(2)}, u32[]{:S(2)}) async-start(bf16[8,144,432]{2,1,0:T(8,128)(2,1)} %bitcast.85), calls=%async_computation.9 | async-start | bytes 2359296 | tf_op jit(solution)/shard_map/all_to_all | solution.py:122
  551.6 86.6 %all-to-all-start.8 = ((bf16[8,256,1152]{2,1,0:T(8,128)(2,1)}), bf16[8,256,1152]{2,1,0:T(8,128)(2,1)}, u32[]{:S(2)}, u32[]{:S(2)}) async-start(bf16[8,256,1152]{2,1,0:T(8,128)(2,1)} %bitcast.71), calls=%async_computation.11 | async-start | bytes 9437184 | tf_op jit(solution)/shard_map/all_to_all | solution.py:122
  556.2 82.0 %reduce-scatter.12.cloned.1.call-start = ((), (), s32[]{:S(2)}) async-start(), calls=%async_computation.19 | async-start | bytes 1290240 | tf_op jit(solution)/shard_map/reduce_scatter | solution.py:1063
  562.3 101.0 %reduce-scatter.14.cloned.1.call-start = ((), (), s32[]{:S(2)}) async-start(), calls=%async_computation.20 | async-start | bytes 1556480 | tf_op jit(solution)/shard_map/reduce_scatter | solution.py:1041
  565.5 55.6 %collective-permute-start.55 = (bf16[144,1920]{1,0:T(8,128)(2,1)}, bf16[144,1920]{1,0:T(8,128)(2,1)S(1)}, u32[]{:S(2)}, u32[]{:S(2)}) collective-permute-start(bf16[144,1920]{1,0:T(8,128)(2,1)} %get-tuple-element.331), channel_id=1, source_target_pairs={{0,6},{2,0},{4,2},{6,4},{1,7},{3,1},{5,3},{7,5},{8,14},{10,8},{12,... | collective-permute-start | bytes 1658888 | tf_op jit(solution)/shard_map/ppermute | solution.py:61
  568.3 53.8 %collective-permute-start.54 = (bf16[144,1920]{1,0:T(8,128)(2,1)}, bf16[144,1920]{1,0:T(8,128)(2,1)S(1)}, u32[]{:S(2)}, u32[]{:S(2)}) collective-permute-start(bf16[144,1920]{1,0:T(8,128)(2,1)} %get-tuple-element.332), channel_id=1, source_target_pairs={{0,1},{1,0},{2,3},{3,2},{4,5},{5,4},{6,7},{7,6},{8,9},{9,8},{10,11... | collective-permute-start | bytes 1658888 | tf_op jit(solution)/shard_map/ppermute | solution.py:61
  569.5 53.1 %collective-permute-start.53 = (bf16[144,1920]{1,0:T(8,128)(2,1)S(1)}, bf16[144,1920]{1,0:T(8,128)(2,1)S(1)}, u32[]{:S(2)}, u32[]{:S(2)}) collective-permute-start(bf16[144,1920]{1,0:T(8,128)(2,1)S(1)} %get-tuple-element.330), channel_id=1, source_target_pairs={{0,2},{2,4},{4,6},{6,0},{1,3},{3,5},{5,7},{7,1},{8,10},{10,12},{12... | collective-permute-start | bytes 1658888 | tf_op jit(solution)/shard_map/ppermute | solution.py:61
  647.5 45.4 %collective-permute-start.38 = (bf16[256,1152]{1,0:T(8,128)(2,1)S(1)}, bf16[256,1152]{1,0:T(8,128)(2,1)}, u32[]{:S(2)}, u32[]{:S(2)}) collective-permute-start(bf16[256,1152]{1,0:T(8,128)(2,1)S(1)} %copy-done.35), channel_id=1, source_target_pairs={{0,48},{16,0},{32,16},{48,32},{1,49},{17,1},{33,17},{49,33},{2,50}... | collective-permute-start | bytes 1769480 | tf_op jit(solution)/shard_map/ppermute | solution.py:61
  659.9 35.4 %collective-permute-start.67 = (bf16[144,1152]{1,0:T(8,128)(2,1)S(1)}, bf16[144,1152]{1,0:T(8,128)(2,1)S(1)}, u32[]{:S(2)}, u32[]{:S(2)}) collective-permute-start(bf16[144,1152]{1,0:T(8,128)(2,1)S(1)} %add.498.refs_0_), channel_id=1, source_target_pairs={{0,16},{16,32},{32,48},{48,0},{1,17},{17,33},{33,49},{49,1},{2,18}... | collective-permute-start | bytes 995336 | tf_op jit(solution)/shard_map/ppermute | solution.py:61
  662.1 34.5 %collective-permute-start.68 = (bf16[144,1152]{1,0:T(8,128)(2,1)S(1)}, bf16[144,1152]{1,0:T(8,128)(2,1)}, u32[]{:S(2)}, u32[]{:S(2)}) collective-permute-start(bf16[144,1152]{1,0:T(8,128)(2,1)S(1)} %add.498.refs_0_), channel_id=1, source_target_pairs={{0,32},{16,48},{32,0},{48,16},{1,33},{17,49},{33,1},{49,17},{2,34}... | collective-permute-start | bytes 995336 | tf_op jit(solution)/shard_map/ppermute | solution.py:61
  685.2 36.2 %collective-permute-start.65 = (bf16[448,1152]{1,0:T(8,128)(2,1)}, bf16[448,1152]{1,0:T(8,128)(2,1)}, u32[]{:S(2)}, u32[]{:S(2)}) collective-permute-start(bf16[448,1152]{1,0:T(8,128)(2,1)} %shard_map.400), channel_id=1, source_target_pairs={{0,8},{8,0},{1,9},{9,1},{2,10},{10,2},{3,11},{11,3},{4,12},{12,4},... | collective-permute-start | bytes 3096584 | tf_op jit(solution)/shard_map/ppermute | solution.py:61
  (132 other events, 1774.7 us)
Sparse Core Ops, SparseCore 0:
  10.6 75.6 all-gather.1
  124.9 50.1 reduce-scatter.5
  356.7 62.8 reduce-scatter.7
  425.4 106.8 reduce-scatter.9
  562.4 23.2 reduce-scatter.11
  625.4 26.0 reduce-scatter.13

commit v13 on v10

--- a/solution.py
+++ b/solution.py
@@ -1009,7 +1009,6 @@
     kv_own, square, grad_qkv = lax.optimization_barrier((kv_own, square, grad_qkv))
     s_lo, s_hi, s20 = reduce_first(square_chunk)
     kv_all = every_peer(kv_own)
-    hidden_grad = lax.psum_scatter(after(hidden_sum, kv_own), FS, scatter_dimension=0, tiled=True)
     out_minus, out_plus = reduce_z(after(out_far, grad_qkv), out_m, out_p)
     grad_qkv = self_backward(
         1, seg_col, seg_row, total1, qkv, after(grad_heads, kv_own), (grad_qkv,)
@@ -1024,8 +1023,8 @@
     heads_part = peers_parts(heads_own)
     square_parts = reduce_third(square_chunk, s20, s11, s31)
     part, sums_one = first_part(after(grad_qkv, heads_own), heads_w, plain_all)
-    part, heads_part, kv_all, hidden_grad, *square_parts = lax.optimization_barrier(
-        (part, heads_part, kv_all, hidden_grad, *square_parts)
+    part, heads_part, kv_all, *square_parts = lax.optimization_barrier(
+        (part, heads_part, kv_all, *square_parts)
     )
     sent = peers_parts(part)
 
@@ -1061,12 +1060,13 @@
 
     late = half(core) + shift(half(1 - core), "c", 1)
     late = lax.psum_scatter(late, "z", scatter_dimension=0, tiled=True)
-    hidden_grad = after(hidden_grad, part)
+    part, norms, late = lax.optimization_barrier((sent, norms, late))
+    hidden_parts = peers_parts(after(hidden_sum, part))
+    hidden_grad = sum_parts(hidden_parts).astype(bf16)
     hidden_grad = hidden_grad + shift(hidden_grad, "xh", 1)
-    part, norms, late = lax.optimization_barrier((sent, norms, late))
     early = after(early, part)
     early = early + shift(early, "xh", 1)
-    hidden_grad = in_order(*neighbours(after(hidden_grad, part)))
+    hidden_grad = in_order(*neighbours(hidden_grad))
     grad_w_up, grad_w_down = sort_hidden(core_index, hidden_grad, shift(hidden_grad, "c", 1))
 
     norms = sum_over(norms, "y", "xl", "xh")
@@ -1109,7 +1109,7 @@
         [],
     )[0]
     grad_text = lax.all_to_all(
-        after(text_part, part), FS, split_axis=0, concat_axis=1, tiled=True
+        after(text_part, hidden_parts), FS, split_axis=0, concat_axis=1, tiled=True
     )
     grad_text = grad_text[:CAP_TOK].astype(f32)
     return (

time: 744 us -> 736 us (0.989)
  waiting for transfers between devices: 210 us -> 183 us
  starting transfers between devices: 135 us -> 150 us
    ppermute x71, waiting for transfers between devices: 134 us -> 109 us  [shift(): return lax.ppermute(x, axis, [(i, (i + by) % n) for i in range(n)])]
    ppermute x71, starting transfers between devices: 92.6 us -> 103 us  [shift(): return lax.ppermute(x, axis, [(i, (i + by) % n) for i in range(n)])]
    all_to_all x3 -> x4, starting transfers between devices: 12.4 us -> 17.1 us  [peers_parts(): return lax.all_to_all(x, axes, 0, 0, tiled=True)]
    all_to_all x3 -> x4, waiting for transfers between devices: 46.4 us -> 46.2 us  [peers_parts(): return lax.all_to_all(x, axes, 0, 0, tiled=True)]
  transfers between devices with their start and end apart: 87 -> 87, of which waited for: 34 -> 34; matrix products, arithmetic and copies ran while one was open for 13% -> 15% of each run, Pallas kernels for 23% -> 23%
where the time goes in v13:
time: 736 us; the launch traced here: 726 us
  Pallas kernels  240 us (33%)
  waiting for transfers between devices  183 us (25%)
  starting transfers between devices  150 us (20%)
  local copies, waits for them, and re-layouts  66.9 us (9%)
  other arithmetic  51.7 us (7%)
  matrix products  18.3 us (2%)
  between operations  15.6 us (2%)
    ppermute x71, waiting for transfers between devices, shift(): return lax.ppermute(x, axis, [(i, (i + by) % n) for i in range(n)])  109 us
    ppermute x71, starting transfers between devices, shift(): return lax.ppermute(x, axis, [(i, (i + by) % n) for i in range(n)])  103 us
    pallas_call x7, Pallas kernels, call(): pl.pallas_call(body, in_specs=[pl.BlockSpec(memory_space=spaces[where]) f...  51.9 us
    all_to_all x4, waiting for transfers between devices, peers_parts(): return lax.all_to_all(x, axes, 0, 0, tiled=True)  46.2 us
    pallas_call x2, Pallas kernels, self_backward(): pl.pallas_call(functools.partial(self_backward_body, head), grid=(ROW //...  37.4 us
    pallas_call x3, Pallas kernels, mlp(): pl.pallas_call(functools.partial(mlp_body, parts, count), in_specs=[pl.Bl...  28.6 us
    pallas_call x2, Pallas kernels, self_forward(): pl.pallas_call(self_forward_body, grid=(ROW // TOK,), in_specs=[pl.BlockS...  24.3 us
    pallas_call x2, Pallas kernels, mlp_grad(): pl.pallas_call(functools.partial(mlp_grad_body, which), grid=(3,), in_spe...  17.6 us
  transfers between devices with their start and end apart: 87, of which 34 were waited for; matrix products, arithmetic and copies ran while one was open for 15% of the time, Pallas kernels for 23%

profile of v13, /device:TPU:1, one launch (start us, length us, event | category | flops | bytes accessed | tf_op | source)
XLA Modules:
  0.0 726.1 jit_solution(4584680376628572928)
XLA Ops:
  18.8 9.6 %collective-permute-done.refs_1_ = bf16[256,1152]{1,0:T(8,128)(2,1)} collective-permute-done((bf16[256,1152]{1,0:T(8,128)(2,1)S(1)}, bf16[256,1152]{1,0:T(8,128)(2,1)}, u32[]{:S(2)}, u32[]{:S(2)}) %collective-permute-start) | collective-permute-done | bytes 589856 | tf_op jit(solution)/shard_map/ppermute | solution.py:61
  42.6 8.6 %collective-permute-done.3.refs_4_ = bf16[256,1152]{1,0:T(8,128)(2,1)S(1)} collective-permute-done((bf16[256,1152]{1,0:T(8,128)(2,1)}, bf16[256,1152]{1,0:T(8,128)(2,1)S(1)}, u32[]{:S(2)}, u32[]{:S(2)}) %collective-permute-start.3) | collective-permute-done | bytes 589856 | tf_op jit(solution)/shard_map/ppermute | solution.py:61
  51.3 10.7 %collective-permute-done.5.refs_6_ = bf16[256,1152]{1,0:T(8,128)(2,1)S(1)} collective-permute-done((bf16[256,1152]{1,0:T(8,128)(2,1)}, bf16[256,1152]{1,0:T(8,128)(2,1)S(1)}, u32[]{:S(2)}, u32[]{:S(2)}) %collective-permute-start.5) | collective-permute-done | bytes 589856 | tf_op jit(solution)/shard_map/ppermute | solution.py:61
  66.0 21.1 %all-to-all-done = bf16[8,144,432]{2,1,0:T(8,128)(2,1)S(1)} async-done(((bf16[8,144,432]{2,1,0:T(8,128)(2,1)}), bf16[8,144,432]{2,1,0:T(8,128)(2,1)S(1)}, u32[]{:S(2)}, u32[]{:S(2)}) %all-to-all-start) | async-done | bytes 995360 | tf_op jit(solution)/shard_map/all_to_all | solution.py:122
  103.6 8.1 %convolution_convert_fusion.q.kv = bf16[2048,768]{1,0:T(8,128)(2,1)} fusion(bf16[2048,1152]{1,0:T(8,128)(2,1)} %get-tuple-element.150.x, bf16[1152,768]{1,0:T(8,128)(2,1)S(1)} %copy-done.19), kind=kOutput, calls=%fused_computation.1 | convolution fusion | flops 3625451520 | bytes 9633792 | tf_op jit(solution)/shard_map/dot_general | solution.py:40
  126.3 12.1 %shard_map.377 = (bf16[2048,72]{1,0:T(8,128)(2,1)}, f32[1,2048]{1,0:T(1,128)}) custom-call(s32[2048,1]{1,0:T(8,128)} %copy.114.seg_q.seg_k, s32[1,2048]{1,0:T(1,128)} %bitcast.90, bf16[2048,768]{1,0:T(8,128)(2,1)} %convolution_convert_fusion.q.kv, bf16[2048,768]{1,0:T(8,128)(2,1)} %convolution_convert_fusion.q.kv), custom_call_target="tpu_custom_call" | custom-call | tf_op jit(solution)/shard_map/pallas_call | solution.py:283
  138.5 12.1 %shard_map.378 = (bf16[2048,72]{1,0:T(8,128)(2,1)}, f32[1,2048]{1,0:T(1,128)}) custom-call(s32[2048,1]{1,0:T(8,128)} %copy.114.seg_q.seg_k, s32[1,2048]{1,0:T(1,128)} %bitcast.91, bf16[2048,768]{1,0:T(8,128)(2,1)} %convolution_convert_fusion.q.kv, bf16[2048,768]{1,0:T(8,128)(2,1)} %convolution_convert_fusion.q.kv), custom_call_target="tpu_custom_call" | custom-call | tf_op jit(solution)/shard_map/pallas_call | solution.py:283
  220.1 8.4 %shard_map.381 = (bf16[512,1152]{1,0:T(8,128)(2,1)}, bf16[512,1152]{1,0:T(8,128)(2,1)}) custom-call(s32[1]{0:T(128)} %bitcast.core, bf16[512,1152]{1,0:T(8,128)(2,1)} %bitcast.28.context, bf16[1152,3072]{1,0:T(8,128)(2,1)} %shard_map.379.mine, bf16[1152,3072]{1,0:T(8,128)(2,1)} %collective-permute-done.12.other), custom_call_target="tpu_custom_call" | custom-call | tf_op jit(solution)/shard_map/pallas_call | solution.py:573
  228.5 11.7 %shard_map.382.mixed = bf16[256,1152]{1,0:T(8,128)(2,1)} custom-call(s32[256,1]{1,0:T(8,128)} %copy.118.cap_q, s32[1,512]{1,0:T(1,128)} %and_select_fusion.1.cap_t, bf16[256,1152]{1,0:T(8,128)(2,1)} %get-tuple-element.168.q, bf16[512,1152]{1,0:T(8,128)(2,1)} %get-tuple-element.172.k, bf16[512,1152]{1,0:T(8,128)(2,1)} %get-tuple-element.173.v), custom_call_target="tpu_custom_call" | custom-call | tf_op jit(solution)/shard_map/pallas_call | solution.py:374
  256.7 8.2 %shard_map.384 = (bf16[256,1152]{1,0:T(8,128)(2,1)}, bf16[256,1152]{1,0:T(8,128)(2,1)}, bf16[256,1152]{1,0:T(8,128)(2,1)}, bf16[256,1152]{1,0:T(8,128)(2,1)}) custom-call(s32[1]{0:T(128)} %bitcast.core, bf16[256,1152]{1,0:T(8,128)(2,1)} %get-tuple-element.175.refs_0_, bf16[256,1152]{1,0:T(8,128)(2,1)} %copy-done.4, bf16[1152,1152]{1,0:T(8,128)(2,1)} %bitcast.63, ...), custom_call_target="tpu_custom_call" | custom-call | tf_op jit(solution)/shard_map/pallas_call | solution.py:480
  270.8 12.3 %shard_map.385 = (bf16[256,1152]{1,0:T(8,128)(2,1)}, bf16[256,1152]{1,0:T(8,128)(2,1)}, bf16[256,1152]{1,0:T(8,128)(2,1)}, bf16[256,1152]{1,0:T(8,128)(2,1)}, bf...) custom-call(s32[1]{0:T(128)} %bitcast.core, ...), custom_call_target="tpu_custom_call" | custom-call | tf_op jit(solution)/shard_map/pallas_call | solution.py:480
  283.9 8.2 %shard_map.386 = (bf16[256,1152]{1,0:T(8,128)(2,1)}, bf16[256,1152]{1,0:T(8,128)(2,1)}, bf16[256,1152]{1,0:T(8,128)(2,1)}, bf16[256,1152]{1,0:T(8,128)(2,1)}) custom-call(s32[1]{0:T(128)} %bitcast.core, bf16[128,1152]{1,0:T(8,128)(2,1)} %copy-done.26, bf16[128,1152]{1,0:T(8,128)(2,1)} %copy-done.28, bf16[128,1152]{1,0:T(8,128)(2,1)} %copy-done.24, ...), custom_call_target="tpu_custom_call" | custom-call | tf_op jit(solution)/shard_map/pallas_call | solution.py:480
  296.8 8.7 %shard_map.387 = bf16[1152,1152]{1,0:T(8,128)(2,1)} custom-call(s32[1]{0:T(128)} %bitcast.core, bf16[256,1152]{1,0:T(8,128)(2,1)} %get-tuple-element.175.refs_0_, bf16[256,1152]{1,0:T(8,128)(2,1)} %copy-done.6, bf16[256,1152]{1,0:T(8,128)(2,1)} %collective-permute-done.16.refs_1_.refs_2_, bf16[256,1152]{1,0:T(8,128)(2,1)} %copy-done.11, ...), custom_call_target="tpu_custom_call" | custom-call | tf_op jit(solution)/shard_map/pallas_call | solution.py:514
  314.5 8.9 %shard_map.388 = bf16[1152,1152]{1,0:T(8,128)(2,1)} custom-call(s32[1]{0:T(128)} %bitcast.core, bf16[256,1152]{1,0:T(8,128)(2,1)} %get-tuple-element.175.refs_0_, bf16[256,1152]{1,0:T(8,128)(2,1)} %copy-done.6, bf16[256,1152]{1,0:T(8,128)(2,1)} %collective-permute-done.16.refs_1_.refs_2_, bf16[256,1152]{1,0:T(8,128)(2,1)} %copy-done.11, ...), custom_call_target="tpu_custom_call" | custom-call | tf_op jit(solution)/shard_map/pallas_call | solution.py:514
  340.9 15.5 %shard_map.390 = (bf16[256,1152]{1,0:T(8,128)(2,1)}, bf16[512,2304]{1,0:T(8,128)(2,1)}) custom-call(s32[512,1]{1,0:T(8,128)} %fusion.36.cap_t, s32[1,256]{1,0:T(1,128)} %bitcast.97, bf16[256,1152]{1,0:T(8,128)(2,1)} %get-tuple-element.168.q, bf16[512,1152]{1,0:T(8,128)(2,1)} %get-tuple-element.172.k, bf16[512,1152]{1,0:T(8,128)(2,1)} %get-tuple-element.173.v, ...), custom_call_target="tpu_custom_call" | custom-call | tf_op jit(solution)/shard_map/pallas_call | solution.py:402
  387.8 8.1 %all-to-all-done.5 = bf16[256,8,144]{0,2,1:T(8,128)(2,1)S(1)} async-done(((bf16[256,8,144]{0,2,1:T(8,128)(2,1)}), bf16[256,8,144]{0,2,1:T(8,128)(2,1)S(1)}, u32[]{:S(2)}, u32[]{:S(2)}) %all-to-all-start.5) | async-done | bytes 589856 | tf_op jit(solution)/shard_map/all_to_all | solution.py:993
  397.2 18.7 %shard_map.392.refs_0_ = bf16[2048,768]{1,0:T(8,128)(2,1)} custom-call(s32[2048,1]{1,0:T(8,128)} %copy.114.seg_q.seg_k, s32[1,2048]{1,0:T(1,128)} %bitcast.92, f32[1,2048]{1,0:T(1,128)} %get-tuple-element.218.total, bf16[2048,768]{1,0:T(8,128)(2,1)} %convolution_convert_fusion.q.kv, bf16[2048,768]{1,0:T(8,128)(2,1)} %convolution_convert_fusion.q.kv, ...), custom_call_target="tpu_custom_call" | custom-call | tf_op jit(solution)/shard_map/pallas_call | solution.py:335
  435.9 18.6 %shard_map.393.g = bf16[2048,768]{1,0:T(8,128)(2,1)} custom-call(s32[2048,1]{1,0:T(8,128)} %copy.114.seg_q.seg_k, s32[1,2048]{1,0:T(1,128)} %bitcast.93, f32[1,2048]{1,0:T(1,128)} %get-tuple-element.226.total, bf16[2048,768]{1,0:T(8,128)(2,1)} %convolution_convert_fusion.q.kv, ...), custom_call_target="tpu_custom_call", output_to_operand_aliasing={{}: (6, {})} | custom-call | tf_op jit(solution)/shard_map/pallas_call | solution.py:335
  486.4 10.8 %shard_map.395 = (bf16[2048,1152]{1,0:T(8,128)(2,1)}, f32[8,1152]{1,0:T(8,128)}) custom-call(bf16[2048,768]{1,0:T(8,128)(2,1)} %shard_map.393.g, bf16[1152,768]{1,0:T(8,128)(2,1)} %shard_map.376.w, bf16[2048,1152]{1,0:T(8,128)(2,1)} %get-tuple-element.236.plain), custom_call_target="tpu_custom_call" | custom-call | flops 12650000384 | tf_op jit(solution)/shard_map/pallas_call | solution.py:676
  497.2 8.9 %collective-permute-done.42 = bf16[144,1920]{1,0:T(8,128)(2,1)S(1)} collective-permute-done((bf16[144,1920]{1,0:T(8,128)(2,1)}, bf16[144,1920]{1,0:T(8,128)(2,1)S(1)}, u32[]{:S(2)}, u32[]{:S(2)}) %collective-permute-start.42) | collective-permute-done | bytes 552992 | tf_op jit(solution)/shard_map/ppermute | solution.py:61
  507.7 11.7 %shard_map.396 = (bf16[512,512]{1,0:T(8,128)(2,1)}, bf16[512,1152]{1,0:T(8,128)(2,1)}, bf16[144,2304]{1,0:T(8,128)(2,1)}) custom-call(s32[1]{0:T(128)} %bitcast.core, bf16[512,2304]{1,0:T(8,128)(2,1)} %bitcast.69, bf16[512,144]{1,0:T(8,128)(2,1)} %constant_dynamic-slice_fusion.5.cols, bf16[512,512]{1,0:T(8,128)(2,1)} %bitcast.83, bf16[512,1152]{1,0:T(8,128)(2,1)} %w_text.1, ...), custom_call_target="tpu_custom_call" | custom-call | tf_op jit(solution)/shard_map/pallas_call | solution.py:573
  550.1 8.0 %reduce-scatter.9.cloned.1.call-done = bf16[112,1152]{1,0:T(8,128)(2,1)} async-done(((bf16[448,1152]{1,0:T(8,128)(2,1)}), bf16[112,1152]{1,0:T(8,128)(2,1)}) %reduce-scatter.9.cloned.1.call-update) | async-done | bytes 258064 | tf_op jit(solution)/shard_map/reduce_scatter | solution.py:1062
  558.1 25.1 %all-to-all-done.8 = bf16[8,256,1152]{2,1,0:T(8,128)(2,1)} async-done(((bf16[8,256,1152]{2,1,0:T(8,128)(2,1)}), bf16[8,256,1152]{2,1,0:T(8,128)(2,1)}, u32[]{:S(2)}, u32[]{:S(2)}) %all-to-all-start.8) | async-done | bytes 4718624 | tf_op jit(solution)/shard_map/all_to_all | solution.py:122
  633.8 16.0 %collective-permute-done.53 = f32[8,1152]{1,0:T(8,128)S(1)} collective-permute-done((f32[8,1152]{1,0:T(8,128)S(1)}, f32[8,1152]{1,0:T(8,128)S(1)}, u32[]{:S(2)}, u32[]{:S(2)}) %collective-permute-start.53) | collective-permute-done | bytes 36896 | tf_op jit(solution)/shard_map/ppermute | solution.py:61
  (462 shorter events, 420.5 us)
Async XLA Ops:
  7.2 92.0 %all-gather.2.cloned.1.call-start = ((), (), s32[]{:S(2)}) async-start(), calls=%async_computation.15 | async-start | bytes 1990656 | tf_op jit(solution)/shard_map/all_gather | solution.py:830
  35.4 26.6 %collective-permute-start.5 = (bf16[256,1152]{1,0:T(8,128)(2,1)}, bf16[256,1152]{1,0:T(8,128)(2,1)S(1)}, u32[]{:S(2)}, u32[]{:S(2)}) collective-permute-start(bf16[256,1152]{1,0:T(8,128)(2,1)} %collective-permute-done.1.refs_2_), channel_id=1, source_target_pairs={{0,1},{1,0},{2,3},{3,2},{4,5},{5,4},{6,7},{7,6},{8,9},{9,8},{10,11... | collective-permute-start | bytes 1769480 | tf_op jit(solution)/shard_map/ppermute | solution.py:61
  35.4 51.7 %all-to-all-start = ((bf16[8,144,432]{2,1,0:T(8,128)(2,1)}), bf16[8,144,432]{2,1,0:T(8,128)(2,1)S(1)}, u32[]{:S(2)}, u32[]{:S(2)}) async-start(bf16[8,144,432]{2,1,0:T(8,128)(2,1)} %bitcast.74), calls=%async_computation | async-start | bytes 2359296 | tf_op jit(solution)/shard_map/all_to_all | solution.py:122
  62.8 28.5 %collective-permute-start.6 = (bf16[128,1152]{1,0:T(8,128)(2,1)}, bf16[128,1152]{1,0:T(8,128)(2,1)}, u32[]{:S(2)}, u32[]{:S(2)}) collective-permute-start(bf16[128,1152]{1,0:T(8,128)(2,1)} %slice.200), channel_id=1, source_target_pairs={{0,6},{2,0},{4,2},{6,4},{1,7},{3,1},{5,3},{7,5},{8,14},{10,8},{12,... | collective-permute-start | bytes 884744 | tf_op jit(solution)/shard_map/ppermute | solution.py:61
  63.8 27.5 %collective-permute-start.7 = (bf16[128,1152]{1,0:T(8,128)(2,1)}, bf16[128,1152]{1,0:T(8,128)(2,1)}, u32[]{:S(2)}, u32[]{:S(2)}) collective-permute-start(bf16[128,1152]{1,0:T(8,128)(2,1)} %slice.201), channel_id=1, source_target_pairs={{0,2},{2,4},{4,6},{6,0},{1,3},{3,5},{5,7},{7,1},{8,10},{10,12},{12... | collective-permute-start | bytes 884744 | tf_op jit(solution)/shard_map/ppermute | solution.py:61
  113.6 44.9 %all-to-all-start.2 = ((bf16[8,144,1152]{2,1,0:T(8,128)(2,1)}), bf16[8,144,1152]{2,1,0:T(8,128)(2,1)S(1)}, u32[]{:S(2)}, u32[]{:S(2)}) async-start(bf16[8,144,1152]{2,1,0:T(8,128)(2,1)} %broadcast_in_dim.121), calls=%async_computation.2 | async-start | bytes 5308416 | tf_op jit(solution)/shard_map/all_to_all | solution.py:118
  118.4 56.7 %reduce-scatter.5.cloned.1.call-start = ((), (), s32[]{:S(2)}) async-start(), calls=%async_computation.16 | async-start | bytes 1327104 | tf_op jit(solution)/shard_map/reduce_scatter | solution.py:871
  118.4 39.5 %collective-permute-start.8 = (bf16[1152,768]{1,0:T(8,128)(2,1)}, bf16[1152,768]{1,0:T(8,128)(2,1)}, u32[]{:S(2)}, u32[]{:S(2)}) collective-permute-start(bf16[1152,768]{1,0:T(8,128)(2,1)} %all-gather.2.cloned.1.call-done.own), channel_id=1, source_target_pairs={{0,16},{16,32},{32,48},{48,0},{1,17},{17,33},{33,49},{49,1},{2,18}... | collective-permute-start | bytes 5308424 | tf_op jit(solution)/shard_map/ppermute | solution.py:61
  120.2 38.3 %collective-permute-start.9 = (bf16[1152,768]{1,0:T(8,128)(2,1)}, bf16[1152,768]{1,0:T(8,128)(2,1)}, u32[]{:S(2)}, u32[]{:S(2)}) collective-permute-start(bf16[1152,768]{1,0:T(8,128)(2,1)} %all-gather.2.cloned.1.call-done.own), channel_id=1, source_target_pairs={{0,48},{16,0},{32,16},{48,32},{1,49},{17,1},{33,17},{49,33},{2,50}... | collective-permute-start | bytes 5308424 | tf_op jit(solution)/shard_map/ppermute | solution.py:61
  202.1 217.3 %reduce-scatter.7.cloned.1.call-start = ((), (), s32[]{:S(2)}) async-start(), calls=%async_computation.17 | async-start | bytes 2654208 | tf_op jit(solution)/shard_map/reduce_scatter | solution.py:982
  421.2 37.3 %collective-permute-start.33 = (bf16[80,1920]{1,0:T(8,128)(2,1)}, bf16[80,1920]{1,0:T(8,128)(2,1)}, u32[]{:S(2)}, u32[]{:S(2)}) collective-permute-start(bf16[80,1920]{1,0:T(8,128)(2,1)} %constant_dynamic-slice_fusion), channel_id=1, source_target_pairs={{0,2},{2,4},{4,6},{6,0},{1,3},{3,5},{5,7},{7,1},{8,10},{10,12},{12... | collective-permute-start | bytes 921608 | tf_op jit(solution)/shard_map/ppermute | solution.py:61
  422.2 32.3 %collective-permute-start.36 = (bf16[128,1152]{1,0:T(8,128)(2,1)}, bf16[128,1152]{1,0:T(8,128)(2,1)}, u32[]{:S(2)}, u32[]{:S(2)}) collective-permute-start(bf16[128,1152]{1,0:T(8,128)(2,1)} %get-tuple-element.362), channel_id=1, source_target_pairs={{0,48},{16,0},{32,16},{48,32},{1,49},{17,1},{33,17},{49,33},{2,50}... | collective-permute-start | bytes 884744 | tf_op jit(solution)/shard_map/ppermute | solution.py:61
  426.6 31.9 %collective-permute-start.34 = (bf16[64,1920]{1,0:T(8,128)(2,1)}, bf16[64,1920]{1,0:T(8,128)(2,1)}, u32[]{:S(2)}, u32[]{:S(2)}) collective-permute-start(bf16[64,1920]{1,0:T(8,128)(2,1)} %constant_dynamic-slice_fusion.9), channel_id=1, source_target_pairs={{0,6},{2,0},{4,2},{6,4},{1,7},{3,1},{5,3},{7,5},{8,14},{10,8},{12,... | collective-permute-start | bytes 737288 | tf_op jit(solution)/shard_map/ppermute | solution.py:61
  430.3 28.1 %collective-permute-start.35 = (bf16[144,1920]{1,0:T(8,128)(2,1)S(1)}, bf16[144,1920]{1,0:T(8,128)(2,1)}, u32[]{:S(2)}, u32[]{:S(2)}) collective-permute-start(bf16[144,1920]{1,0:T(8,128)(2,1)S(1)} %constant_dynamic-slice_fusion.8), channel_id=1, source_target_pairs={{0,2},{2,4},{4,6},{6,0},{1,3},{3,5},{5,7},{7,1},{8,10},{10,12},{12... | collective-permute-start | bytes 1658888 | tf_op jit(solution)/shard_map/ppermute | solution.py:61
  432.1 42.0 %all-to-all-start.6 = ((bf16[8,64,2304]{2,1,0:T(8,128)(2,1)}), bf16[8,64,2304]{2,1,0:T(8,128)(2,1)S(1)}, u32[]{:S(2)}, u32[]{:S(2)}) async-start(bf16[8,64,2304]{2,1,0:T(8,128)(2,1)} %broadcast_in_dim.137), calls=%async_computation.8 | async-start | bytes 4718592 | tf_op jit(solution)/shard_map/all_to_all | solution.py:118
  474.7 33.0 %all-to-all-start.7 = ((bf16[8,144,432]{2,1,0:T(8,128)(2,1)}), bf16[8,144,432]{2,1,0:T(8,128)(2,1)S(1)}, u32[]{:S(2)}, u32[]{:S(2)}) async-start(bf16[8,144,432]{2,1,0:T(8,128)(2,1)} %bitcast.87), calls=%async_computation.9 | async-start | bytes 2359296 | tf_op jit(solution)/shard_map/all_to_all | solution.py:122
  523.4 59.8 %all-to-all-start.8 = ((bf16[8,256,1152]{2,1,0:T(8,128)(2,1)}), bf16[8,256,1152]{2,1,0:T(8,128)(2,1)}, u32[]{:S(2)}, u32[]{:S(2)}) async-start(bf16[8,256,1152]{2,1,0:T(8,128)(2,1)} %bitcast.73), calls=%async_computation.10 | async-start | bytes 9437184 | tf_op jit(solution)/shard_map/all_to_all | solution.py:122
  528.0 30.1 %reduce-scatter.9.cloned.1.call-start = ((), (), s32[]{:S(2)}) async-start(), calls=%async_computation.18 | async-start | bytes 1290240 | tf_op jit(solution)/shard_map/reduce_scatter | solution.py:1062
  533.4 74.7 %reduce-scatter.11.cloned.1.call-start = ((), (), s32[]{:S(2)}) async-start(), calls=%async_computation.19 | async-start | bytes 1556480 | tf_op jit(solution)/shard_map/reduce_scatter | solution.py:1040
  585.7 27.4 %all-to-all-start.9 = ((bf16[8,64,512]{2,1,0:T(8,128)(2,1)}), bf16[8,64,512]{2,1,0:T(8,128)(2,1)S(1)}, u32[]{:S(2)}, u32[]{:S(2)}) async-start(bf16[8,64,512]{2,1,0:T(8,128)(2,1)} %bitcast.42), calls=%async_computation.12 | async-start | bytes 1048576 | tf_op jit(solution)/shard_map/all_to_all | solution.py:1111
  596.6 30.9 %collective-permute-start.39 = (bf16[256,1152]{1,0:T(8,128)(2,1)}, bf16[256,1152]{1,0:T(8,128)(2,1)}, u32[]{:S(2)}, u32[]{:S(2)}) collective-permute-start(bf16[256,1152]{1,0:T(8,128)(2,1)} %pad_maximum_fusion.10), channel_id=1, source_target_pairs={{0,16},{16,32},{32,48},{48,0},{1,17},{17,33},{33,49},{49,1},{2,18}... | collective-permute-start | bytes 1769480 | tf_op jit(solution)/shard_map/ppermute | solution.py:61
  598.0 30.6 %collective-permute-start.38 = (bf16[256,1152]{1,0:T(8,128)(2,1)}, bf16[256,1152]{1,0:T(8,128)(2,1)}, u32[]{:S(2)}, u32[]{:S(2)}) collective-permute-start(bf16[256,1152]{1,0:T(8,128)(2,1)} %pad_maximum_fusion.9), channel_id=1, source_target_pairs={{0,48},{16,0},{32,16},{48,32},{1,49},{17,1},{33,17},{49,33},{2,50}... | collective-permute-start | bytes 1769480 | tf_op jit(solution)/shard_map/ppermute | solution.py:61
  613.1 61.7 %all-to-all-start.10 = ((bf16[8,144,1152]{2,1,0:T(8,128)(2,1)}), bf16[8,144,1152]{2,1,0:T(8,128)(2,1)S(1)}, u32[]{:S(2)}, u32[]{:S(2)}) async-start(bf16[8,144,1152]{2,1,0:T(8,128)(2,1)} %bitcast.68), calls=%async_computation.14 | async-start | bytes 5308416 | tf_op jit(solution)/shard_map/all_to_all | solution.py:122
  617.9 51.6 %collective-permute-start.65 = (bf16[448,1152]{1,0:T(8,128)(2,1)}, bf16[448,1152]{1,0:T(8,128)(2,1)}, u32[]{:S(2)}, u32[]{:S(2)}) collective-permute-start(bf16[448,1152]{1,0:T(8,128)(2,1)} %shard_map.400), channel_id=1, source_target_pairs={{0,8},{8,0},{1,9},{9,1},{2,10},{10,2},{3,11},{11,3},{4,12},{12,4},... | collective-permute-start | bytes 3096584 | tf_op jit(solution)/shard_map/ppermute | solution.py:61
  (136 other events, 1589.5 us)
Sparse Core Ops, SparseCore 0:
  10.6 75.6 all-gather.1
  124.8 50.2 reduce-scatter.4
  356.5 62.8 reduce-scatter.6
  533.5 24.5 reduce-scatter.8
  561.1 23.7 reduce-scatter.10
